TPU v7x, 32 devices: a whole 2x2x4 slice. The times are simulated.
32 devices in a mesh: mode: 8 (over z, y), slab: 4 (over x, core).
Axes of the slice: x: 2, y: 2, z: 4, core: 2. Of those that a mesh axis runs over, the one named last changes fastest.
Arguments:
- guess: float32 [1024, 128, 128], P('mode', 'slab'), may hold values from -6 to 6
- right_side: float32 [1024, 128, 128], P('mode', 'slab'), may hold values from -6 to 6
- mean_coef: float32 [128, 128], P('slab'), may hold values from 0.5 to 2
- field_coef: float32 [3, 128, 128], P(None, 'slab'), may hold values from -2.5 to 2.5
- coupling: bfloat16 [8, 16, 128, 128], replicated, may hold values from -0.0625 to 0.0625
- coupling_list: int32 [8, 16], replicated, may hold values from 0 to 23, as said below
- pair_count: int32 [8], replicated, may hold values from 4 to 16, as said below
Outputs:
- solution: float32 [1024, 128, 128], P('mode', 'slab')
- residual: float32 [1024, 128, 128], P('mode', 'slab')
Inputs may be any that keep to these rules, and one draw needn't show every extreme that they name: `coupling_list`: each row holds 16 distinct entries; entry e couples its row's mode block to mode block e // 3 through coefficient field e % 3. Only the first pair_count entries of a row are live. `pair_count`: number of live entries of each mode block's row.
All inputs are finite; a program needn't handle non-finite values.
Results may differ from a plain program's by a relative error of at most 0.0012.
Values may be sent and summed in bfloat16 or wider, within the bound.
No kernel may reach another device: no remote copies, remote signals or barrier semaphores. Data moves between devices by JAX's collectives and lax.ppermute only.
A program may use at most 256 MiB of HBM per device.

v0:
```python
import math

import jax
import jax.numpy as jnp
from jax import lax
from jax.sharding import PartitionSpec as P

FIELDS = 3
MAXC = 16
NX = 128
NY = 128
ITERS = 2


relaxation = 0.6


def with_halo(block, sides, width):
    for axis, dim in sides:
        count = lax.axis_size(axis)
        forward = [(i, i + 1) for i in range(count - 1)]
        backward = [(target, source) for source, target in forward]
        low = lax.ppermute(
            lax.slice_in_dim(block, block.shape[dim] - width, None, axis=dim), axis, forward
        )
        high = lax.ppermute(lax.slice_in_dim(block, 0, width, axis=dim), axis, backward)
        block = jnp.concatenate([low, block, high], axis=dim)
    return block


def operate(padded, coef_pad):
    center = coef_pad[..., 1:-1, :]
    field = padded[..., 1:-1, :]
    result = 0.5 * (center + coef_pad[..., :-2, :]) * (field - padded[..., :-2, :])
    result = result + 0.5 * (center + coef_pad[..., 2:, :]) * (field - padded[..., 2:, :])
    side_coef = jnp.pad(center, [(0, 0)] * (center.ndim - 1) + [(1, 1)], mode="edge")
    side_field = jnp.pad(field, [(0, 0)] * (field.ndim - 1) + [(1, 1)])
    result = result + 0.5 * (center + side_coef[..., :-2]) * (field - side_field[..., :-2])
    result = result + 0.5 * (center + side_coef[..., 2:]) * (field - side_field[..., 2:])
    return result


def sine_table(length):
    counter = jnp.arange(length).astype(jnp.float32) + 1.0
    angle = math.pi * counter[:, None] * counter[None, :] / (length + 1)
    return math.sqrt(2.0 / (length + 1)) * jnp.sin(angle)


def eigen_table(first, second):
    along_first = 2.0 * jnp.cos(
        math.pi * (jnp.arange(first).astype(jnp.float32) + 1.0) / (first + 1)
    )
    along_second = 2.0 * jnp.cos(
        math.pi * (jnp.arange(second).astype(jnp.float32) + 1.0) / (second + 1)
    )
    return 4.0 - along_first[:, None] - along_second[None, :]


def whole_solve(whole):
    highest = lax.Precision.HIGHEST
    rows_table = sine_table(NX)
    cols_table = sine_table(NY)
    spectral = jnp.einsum("px,mxy->mpy", rows_table, whole, precision=highest)
    spectral = jnp.einsum("mpy,yq->mpq", spectral, cols_table, precision=highest)
    spectral = spectral / eigen_table(NX, NY)
    spatial = jnp.einsum("xp,mpq->mxq", rows_table, spectral, precision=highest)
    return jnp.einsum("mxq,qy->mxy", spatial, cols_table, precision=highest)


def mean_solve(resid):
    whole = lax.all_to_all(resid, "slab", split_axis=0, concat_axis=1, tiled=True)
    spatial = whole_solve(whole)
    return lax.all_to_all(spatial, "slab", split_axis=1, concat_axis=0, tiled=True)


def local(guess, right_side, mean_coef, field_coef, coupling, coupling_list, pair_count):
    highest = lax.Precision.HIGHEST
    modes_dev, rows, cols = guess.shape
    blocks = coupling.shape[0]
    coefs = jnp.concatenate([mean_coef[None], field_coef], 0)
    partner = coupling_list // FIELDS
    field_index = coupling_list % FIELDS
    live_mask = jnp.arange(MAXC)[None, :] < pair_count[:, None]
    onehot = (
        (field_index[:, :, None] == jnp.arange(FIELDS)[None, None, :]) & live_mask[:, :, None]
    ).astype(jnp.float32)
    coef_halo = with_halo(coefs, (("slab", 1),), 1)
    at_top = lax.axis_index("slab") == 0
    at_bottom = lax.axis_index("slab") == lax.axis_size("slab") - 1
    upper = jnp.where(at_top, coefs[:, :1], coef_halo[:, :1])
    lower = jnp.where(at_bottom, coefs[:, -1:], coef_halo[:, -1:])
    coef_rows = jnp.concatenate([upper, coefs, lower], 1)
    field_rows = coef_rows[1:, None]
    solution = guess
    residual = right_side
    for sweep in range(ITERS):
        state_pad = with_halo(solution, (("slab", 1),), 1)
        mean_part = operate(state_pad, coef_rows[0])
        flat_state = solution.astype(jnp.bfloat16).reshape(modes_dev, rows * cols)
        strip_state = lax.all_to_all(flat_state, "mode", split_axis=1, concat_axis=0, tiled=True)
        strip_state = strip_state.reshape(blocks, modes_dev, -1)
        gathered = strip_state[partner]
        products = jnp.einsum(
            "ikab,ikbc->ikac", coupling, gathered, preferred_element_type=jnp.float32
        )
        grouped = jnp.einsum("ikf,ikac->fiac", onehot, products, precision=highest)
        grouped = grouped.reshape(FIELDS, blocks * modes_dev, -1)
        owner_sums = lax.all_to_all(grouped, "mode", split_axis=1, concat_axis=2, tiled=True)
        owner_sums = owner_sums.reshape(FIELDS, modes_dev, rows, cols)
        sums_pad = with_halo(owner_sums, (("slab", 2),), 1)
        coupled = jnp.sum(operate(sums_pad, field_rows), axis=0)
        residual = right_side - mean_part - coupled
        solution = solution + relaxation * mean_solve(residual)
    return (solution, residual)


def solution(mesh):
    placed = (
        P("mode", "slab", None),
        P("mode", "slab", None),
        P("slab", None),
        P(None, "slab", None),
        P(),
        P(),
        P(),
    )
    return jax.shard_map(
        local,
        mesh=mesh,
        in_specs=placed,
        out_specs=(P("mode", "slab", None), P("mode", "slab", None)),
        check_vma=False,
    )
```

profile of v0, /device:TPU:0, one launch (start us, length us, event | category | flops | bytes accessed | tf_op | source)
XLA Modules:
  0.0 880.4 jit_solution(5252664588937341672)
XLA Ops:
  4.2 7.3 all-to-all-start
  11.6 25.6 %all-to-all-done = bf16[128,8,512]{2,0,1:T(8,128)(2,1)S(1)} async-done(((bf16[128,8,512]{2,0,1:T(8,128)(2,1)}), bf16[128,8,512]{2,0,1:T(8,128)(2,1)S(1)}, u32[]{:S(2)}, u32[]{:S(2)}) %all-to-all-start) | async-done | bytes 1048608 | tf_op jit(solution)/shard_map/all_to_all | solution.py:100
  37.2 8.3 gather_fusion
  45.6 22.4 %convolution_bitcast_fusion.1 = f32[8,16,128,512]{2,3,1,0:T(8,128)} fusion(bf16[8,16,128,512]{3,2,1,0:T(8,128)(2,1)} %bitcast.101, bf16[8,16,128,128]{3,2,1,0:T(8,128)(2,1)} %param.11), kind=kOutput, calls=%fused_computation.3 | convolution fusion | flops 2147483648 | bytes 54525952 | tf_op jit(solution)/shard_map/ikab,ikbc->ikac/dot_general | solution.py:103
  68.0 33.9 %copy.177 = f32[8,16,128,512]{3,1,2,0:T(8,128)} copy(f32[8,16,128,512]{2,3,1,0:T(8,128)} %convolution_bitcast_fusion.1) | data formatting | bytes 67108864 | tf_op jit(solution)/shard_map/ikab,ikbc->ikac/dot_general | solution.py:103
  101.8 19.6 %fusion.152 = f32[8,128,512,3]{2,3,1,0:T(4,128)} fusion(f32[8,16,128,512]{3,1,2,0:T(8,128)} %copy.177, s32[8,16]{1,0:T(8,128)S(1)} %get-tuple-element.35, pred[8,16]{1,0:T(8,128)(4,1)S(1)} %iota_compare_fusion.1), kind=kOutput, calls=%fused_computation.200 | convolution fusion | flops 301990656 | bytes 39846528 | tf_op jit(solution)/shard_map/ikf,ikac->fiac/dot_general | solution.py:106
  121.4 5.1 all-to-all-start.1
  129.2 4.8 collective-permute-start.1
  138.9 169.6 %all-to-all-done.1 = f32[3,1024,512]{2,0,1:T(4,128)} async-done(((f32[3,1024,512]{2,0,1:T(4,128)}), f32[3,1024,512]{2,0,1:T(4,128)}, u32[]{:S(2)}, u32[]{:S(2)}) %all-to-all-start.1) | async-done | bytes 6291488 | tf_op jit(solution)/shard_map/all_to_all | solution.py:108
  308.5 8.1 copy.178
  316.6 6.6 copy.179
  329.6 11.7 %fusion.4 = f32[128,32,128]{0,2,1:T(8,128)S(1)} fusion(f32[3,128,32,128]{1,3,2,0:T(8,128)} %bitcast.107, f32[3,128,1,128]{1,3,2,0:T(8,128)S(1)} %collective-permute-done.5, f32[3,128,1,128]{1,3,2,0:T(8,128)S(1)} %collective-permute-done.4, f32[3,32,128]{2,1,0:T(8,128)S(1)} %get-tuple-element.30, f32[3,32,128]{2,1,0:T(8,128)S(1)} %get-tuple-element.29, ...), kind=kLoop, calls=%fused_computation.12 | loop fusion | flops 21495808 | bytes 8978432 | tf_op jit(solution)/shard_map/reduce_sum | solution.py:111
  341.3 4.7 fusion.29
  349.1 6.3 all-to-all-start.2
  355.5 25.7 %all-to-all-done.2 = f32[128,32,128]{2,1,0:T(8,128)} async-done(((f32[128,32,128]{2,1,0:T(8,128)}), f32[128,32,128]{2,1,0:T(8,128)}, u32[]{:S(2)}, u32[]{:S(2)}) %all-to-all-start.2) | async-done | bytes 2097184 | tf_op jit(solution)/shard_map/all_to_all | solution.py:71
  390.2 5.0 fusion.58
  395.2 15.2 %copy.214 = f32[32,128,128]{2,0,1:T(8,128)} copy(f32[32,128,128]{1,2,0:T(8,128)} %fusion.58) | data formatting | bytes 4194304 | tf_op jit(solution)/shard_map/xp,mpq->mxq/transpose | solution.py:66
  410.4 3.7 fusion.72
  414.2 28.2 %all_to_all.116 = f32[32,128,128]{2,0,1:T(8,128)S(1)} all-to-all(f32[32,128,128]{2,0,1:T(8,128)S(1)} %fusion.72), channel_id=1, replica_groups=mesh['mode'=8,'slab'=4] {'slab'}, dimensions={1} | all-to-all | bytes 4194304 | tf_op jit(solution)/shard_map/all_to_all | solution.py:73
  452.0 28.9 %all_to_all.117 = bf16[128,8,512]{2,0,1:T(8,128)(2,1)S(1)} all-to-all(bf16[128,8,512]{2,0,1:T(8,128)(2,1)S(1)} %copy.192), channel_id=1, replica_groups=mesh['mode'=8,'slab'=4] {'mode'}, dimensions={1} | all-to-all | bytes 2097152 | tf_op jit(solution)/shard_map/all_to_all | solution.py:100
  480.9 8.3 gather_fusion.1
  489.3 22.4 %convolution_bitcast_fusion = f32[8,16,128,512]{2,3,1,0:T(8,128)} fusion(bf16[8,16,128,512]{3,2,1,0:T(8,128)(2,1)} %bitcast.100, bf16[8,16,128,128]{3,2,1,0:T(8,128)(2,1)} %param.11), kind=kOutput, calls=%fused_computation.2 | convolution fusion | flops 2147483648 | bytes 54525952 | tf_op jit(solution)/shard_map/ikab,ikbc->ikac/dot_general | solution.py:103
  511.7 33.9 %copy.194 = f32[8,16,128,512]{3,1,2,0:T(8,128)} copy(f32[8,16,128,512]{2,3,1,0:T(8,128)} %convolution_bitcast_fusion) | data formatting | bytes 67108864 | tf_op jit(solution)/shard_map/ikab,ikbc->ikac/dot_general | solution.py:103
  545.6 17.2 %fusion.150 = f32[8,128,512,3]{2,3,1,0:T(4,128)S(1)} fusion(f32[8,16,128,512]{3,1,2,0:T(8,128)} %copy.194, s32[8,16]{1,0:T(8,128)S(1)} %get-tuple-element.35, pred[8,16]{1,0:T(8,128)(4,1)S(1)} %iota_compare_fusion.1), kind=kOutput, calls=%fused_computation.199 | convolution fusion | flops 301990656 | bytes 39846528 | tf_op jit(solution)/shard_map/ikf,ikac->fiac/dot_general | solution.py:106
  562.8 186.4 %all_to_all.118 = f32[3,1024,512]{2,0,1:T(4,128)S(1)} all-to-all(f32[3,1024,512]{2,0,1:T(4,128)S(1)} %bitcast.103), channel_id=1, replica_groups=mesh['mode'=8,'slab'=4] {'mode'}, dimensions={1} | all-to-all | bytes 12582912 | tf_op jit(solution)/shard_map/all_to_all | solution.py:108
  749.1 4.5 copy.195
  753.7 6.8 copy.196
  770.4 12.4 %fusion.11 = f32[128,32,128]{0,2,1:T(8,128)S(1)} fusion(f32[3,128,32,128]{1,3,2,0:T(8,128)} %bitcast.105, f32[3,128,1,128]{1,3,2,0:T(8,128)S(1)} %collective-permute-done.9, f32[3,128,1,128]{1,3,2,0:T(8,128)S(1)} %collective-permute-done.8, f32[3,32,128]{2,1,0:T(8,128)S(1)} %get-tuple-element.30, f32[3,32,128]{2,1,0:T(8,128)S(1)} %get-tuple-element.29, ...), kind=kLoop, calls=%fused_computation.19 | loop fusion | flops 21495808 | bytes 8978432 | tf_op jit(solution)/shard_map/reduce_sum | solution.py:111
  782.9 4.7 fusion.37
  790.6 29.5 %all_to_all.119 = f32[128,32,128]{2,1,0:T(8,128)S(1)} all-to-all(f32[128,32,128]{2,1,0:T(8,128)} %copy.197), channel_id=1, replica_groups=mesh['mode'=8,'slab'=4] {'slab'}, dimensions={0} | all-to-all | bytes 4194304 | tf_op jit(solution)/shard_map/all_to_all | solution.py:71
  827.6 5.0 fusion.61
  839.7 28.2 %all_to_all.120 = f32[32,128,128]{2,0,1:T(8,128)S(1)} all-to-all(f32[32,128,128]{2,0,1:T(8,128)S(1)} %fusion.66), channel_id=1, replica_groups=mesh['mode'=8,'slab'=4] {'slab'}, dimensions={1} | all-to-all | bytes 4194304 | tf_op jit(solution)/shard_map/all_to_all | solution.py:73
  (78 shorter events, 79.0 us)
Async XLA Ops:
  2.8 8.6 copy-start.5
  2.8 8.7 copy-start.6
  4.2 33.0 %all-to-all-start = ((bf16[128,8,512]{2,0,1:T(8,128)(2,1)}), bf16[128,8,512]{2,0,1:T(8,128)(2,1)S(1)}, u32[]{:S(2)}, u32[]{:S(2)}) async-start(bf16[128,8,512]{2,0,1:T(8,128)(2,1)} %copy.175), calls=%async_computation | async-start | bytes 2097152 | tf_op jit(solution)/shard_map/all_to_all | solution.py:100
  121.4 5.1 copy-start.3
  121.4 5.1 copy-start.4
  121.4 187.1 %all-to-all-start.1 = ((f32[3,1024,512]{2,0,1:T(4,128)}), f32[3,1024,512]{2,0,1:T(4,128)}, u32[]{:S(2)}, u32[]{:S(2)}) async-start(f32[3,1024,512]{2,0,1:T(4,128)} %bitcast.102), calls=%async_computation.1 | async-start | bytes 16777216 | tf_op jit(solution)/shard_map/all_to_all | solution.py:108
  126.5 7.5 collective-permute-start
  127.9 213.4 %collective-permute-start.3 = (f32[128,1,128]{0,2,1:T(8,128)S(1)}, f32[128,1,128]{0,2,1:T(8,128)S(1)}, u32[]{:S(2)}, u32[]{:S(2)}) collective-permute-start(f32[128,1,128]{0,2,1:T(8,128)S(1)} %get-tuple-element.21), channel_id=1, source_target_pairs={{1,0},{2,1},{3,2},{5,4},{6,5},{7,6},{9,8},{10,9},{11,10},{13,12},{... | collective-permute-start | bytes 196616 | tf_op jit(solution)/shard_map/ppermute | solution.py:26
  129.2 212.1 %collective-permute-start.1 = (f32[128,1,128]{0,2,1:T(8,128)S(1)}, f32[128,1,128]{0,2,1:T(8,128)S(1)}, u32[]{:S(2)}, u32[]{:S(2)}) collective-permute-start(f32[128,1,128]{0,2,1:T(8,128)S(1)} %get-tuple-element.20), channel_id=1, source_target_pairs={{0,1},{1,2},{2,3},{4,5},{5,6},{6,7},{8,9},{9,10},{10,11},{12,13},{... | collective-permute-start | bytes 196616 | tf_op jit(solution)/shard_map/ppermute | solution.py:23
  134.0 4.6 collective-permute-start.2
  324.2 4.4 collective-permute-start.5
  325.5 4.1 collective-permute-start.4
  329.6 11.7 %copy-start.1 = (f32[128,32,128]{0,2,1:T(8,128)S(1)}, f32[128,32,128]{0,2,1:T(8,128)}, u32[]{:S(2)}) copy-start(f32[128,32,128]{0,2,1:T(8,128)} %copy.173) | copy-start | bytes 6291460
  349.1 32.1 %all-to-all-start.2 = ((f32[128,32,128]{2,1,0:T(8,128)}), f32[128,32,128]{2,1,0:T(8,128)}, u32[]{:S(2)}, u32[]{:S(2)}) async-start(f32[128,32,128]{2,1,0:T(8,128)} %copy.180), calls=%async_computation.2 | async-start | bytes 4194304 | tf_op jit(solution)/shard_map/all_to_all | solution.py:71
  753.7 12.2 %copy-start = (f32[128,32,128]{0,2,1:T(8,128)S(1)}, f32[128,32,128]{0,2,1:T(8,128)}, u32[]{:S(2)}) copy-start(f32[128,32,128]{0,2,1:T(8,128)} %get-tuple-element.11) | copy-start | bytes 6291460
  761.5 8.9 %collective-permute-start.9 = (f32[3,128,1,128]{1,3,2,0:T(8,128)S(1)}, f32[3,128,1,128]{1,3,2,0:T(8,128)S(1)}, u32[]{:S(2)}, u32[]{:S(2)}) collective-permute-start(f32[3,128,1,128]{1,3,2,0:T(8,128)S(1)} %get-tuple-element.15), channel_id=1, source_target_pairs={{1,0},{2,1},{3,2},{5,4},{6,5},{7,6},{9,8},{10,9},{11,10},{13,12},{... | collective-permute-start | bytes 589832 | tf_op jit(solution)/shard_map/ppermute | solution.py:26
  762.8 7.6 collective-permute-start.8
  765.9 17.0 %collective-permute-start.7 = (f32[128,1,128]{0,2,1:T(8,128)S(1)}, f32[128,1,128]{0,2,1:T(8,128)S(1)}, u32[]{:S(2)}, u32[]{:S(2)}) collective-permute-start(f32[128,1,128]{0,2,1:T(8,128)S(1)} %get-tuple-element.19), channel_id=1, source_target_pairs={{1,0},{2,1},{3,2},{5,4},{6,5},{7,6},{9,8},{10,9},{11,10},{13,12},{... | collective-permute-start | bytes 196616 | tf_op jit(solution)/shard_map/ppermute | solution.py:26
  767.2 15.7 %copy-start.2 = (f32[128,32,128]{0,2,1:T(8,128)S(1)}, f32[128,32,128]{0,2,1:T(8,128)}, u32[]{:S(2)}) copy-start(f32[128,32,128]{0,2,1:T(8,128)} %copy.173) | copy-start | bytes 6291460
  767.2 15.7 %collective-permute-start.6 = (f32[128,1,128]{0,2,1:T(8,128)S(1)}, f32[128,1,128]{0,2,1:T(8,128)S(1)}, u32[]{:S(2)}, u32[]{:S(2)}) collective-permute-start(f32[128,1,128]{0,2,1:T(8,128)S(1)} %get-tuple-element.18), channel_id=1, source_target_pairs={{0,1},{1,2},{2,3},{4,5},{5,6},{6,7},{8,9},{9,10},{10,11},{12,13},{... | collective-permute-start | bytes 196616 | tf_op jit(solution)/shard_map/ppermute | solution.py:23
where the time goes:
time: 890 us; the launch traced here: 880 us
  blocking collectives  301 us (34%)
  waiting for transfers between devices  222 us (25%)
  local copies, waits for them, and re-layouts  158 us (18%)
  matrix products  113 us (13%)
  other arithmetic  43.4 us (5%)
  starting transfers between devices  40.7 us (5%)
    all_to_all x1, blocking collectives, local(): lax.all_to_all(grouped, 'mode', split_axis=1, concat_axis=2, tiled=True)  186 us
    all_to_all x1, waiting for transfers between devices, local(): lax.all_to_all(grouped, 'mode', split_axis=1, concat_axis=2, tiled=True)  170 us
    dot_general x2, local copies, waits for them, and re-layouts, local(): jnp.einsum('ikab,ikbc->ikac', coupling, gathered, preferred_element_type=...  67.8 us
    all_to_all x2, blocking collectives, mean_solve(): lax.all_to_all(spatial, 'slab', split_axis=1, concat_axis=0, tiled=True)  56.3 us
    dot_general x2, matrix products, local(): jnp.einsum('ikab,ikbc->ikac', coupling, gathered, preferred_element_type=...  44.8 us
    dot_general x2, matrix products, local(): grouped = jnp.einsum('ikf,ikac->fiac', onehot, products, precision=highest)  36.8 us
    all_to_all x1, blocking collectives, mean_solve(): lax.all_to_all(resid, 'slab', split_axis=0, concat_axis=1, tiled=True)  29.5 us
    all_to_all x1, blocking collectives, local(): lax.all_to_all(flat_state, 'mode', split_axis=1, concat_axis=0, tiled=True)  28.9 us
  transfers between devices with their start and end apart: 13, of which 4 were waited for; matrix products, arithmetic and copies ran while one was open for 5% of the time, Pallas kernels for 0%

commit v1 on v0

v1 whole, which is shorter than its diff:
```python
import functools
import math

import jax
import jax.numpy as jnp
from jax import lax
from jax.experimental import pallas as pl
from jax.experimental.pallas import tpu as pltpu
from jax.sharding import PartitionSpec as P

ITERS = 2
RELAXATION = 0.6
MIB = 1 << 20


def sine_table(length):
    counter = jnp.arange(length).astype(jnp.float32) + 1.0
    angle = math.pi * counter[:, None] * counter[None, :] / (length + 1)
    return math.sqrt(2.0 / (length + 1)) * jnp.sin(angle)


def eigen_table(first, second):
    along_first = 2.0 * jnp.cos(
        math.pi * (jnp.arange(first).astype(jnp.float32) + 1.0) / (first + 1)
    )
    along_second = 2.0 * jnp.cos(
        math.pi * (jnp.arange(second).astype(jnp.float32) + 1.0) / (second + 1)
    )
    return 4.0 - along_first[:, None] - along_second[None, :]


def stencil_weights(coefs):
    padded = jnp.pad(coefs, [(0, 0), (1, 1), (1, 1)], mode="edge")
    up = 0.5 * (coefs + padded[:, :-2, 1:-1])
    down = 0.5 * (coefs + padded[:, 2:, 1:-1])
    left = 0.5 * (coefs + padded[:, 1:-1, :-2])
    right = 0.5 * (coefs + padded[:, 1:-1, 2:])
    nx, ny = coefs.shape[1:]
    row = lax.broadcasted_iota(jnp.int32, (nx, ny), 0)
    col = lax.broadcasted_iota(jnp.int32, (nx, ny), 1)
    centre = up + down + left + right
    return jnp.stack(
        [
            centre,
            jnp.where(row == 0, 0.0, up),
            jnp.where(row == nx - 1, 0.0, down),
            jnp.where(col == 0, 0.0, left),
            jnp.where(col == ny - 1, 0.0, right),
        ],
        axis=1,
    )


def split(value):
    high = value.astype(jnp.bfloat16)
    low = (value - high.astype(jnp.float32)).astype(jnp.bfloat16)
    return high, low


def split_table(value):
    high = lax.reduce_precision(value, 8, 7)
    return high.astype(jnp.bfloat16), (value - high).astype(jnp.bfloat16)


def pack_kernel(strips, rows, height, x_ref, low_ref, high_ref, out_ref):
    modes, cols = low_ref.shape
    for strip in range(strips):
        for r in range(height + 2):
            row = strip * height + r - 1
            if row < 0:
                value = low_ref[...]
            elif row >= rows:
                value = high_ref[...]
            else:
                value = x_ref[pl.ds(row, modes, stride=rows), :]
            out_ref[strip, :, r * cols : (r + 1) * cols] = value.astype(jnp.bfloat16)


def pack_strips(block, low, high, strips):
    modes, rows, cols = block.shape
    height = rows // strips
    return pl.pallas_call(
        functools.partial(pack_kernel, strips, rows, height),
        out_shape=jax.ShapeDtypeStruct((strips, modes, (height + 2) * cols), jnp.bfloat16),
        compiler_params=pltpu.CompilerParams(vmem_limit_bytes=32 * MIB),
    )(block.reshape(modes * rows, cols), low, high)


def dense_kernel(fields, entry_ref, count_ref, coupling_ref, out_ref):
    block = pl.program_id(0)
    width = coupling_ref.shape[-1]
    out_ref[...] = jnp.zeros_like(out_ref)

    def place(k, carry):
        entry = entry_ref[block, k]
        column = pl.multiple_of((entry // fields) * width, width)
        out_ref[0, entry % fields, :, pl.ds(column, width)] = coupling_ref[0, k]
        return carry

    lax.fori_loop(0, count_ref[block], place, 0)


def dense_coupling(coupling, coupling_list, pair_count, fields):
    blocks, entries, width, _ = coupling.shape
    return pl.pallas_call(
        functools.partial(dense_kernel, fields),
        grid_spec=pltpu.PrefetchScalarGridSpec(
            num_scalar_prefetch=2,
            grid=(blocks,),
            in_specs=[pl.BlockSpec((1, entries, width, width), lambda i, *_: (i, 0, 0, 0))],
            out_specs=pl.BlockSpec(
                (1, fields, width, blocks * width), lambda i, *_: (i, 0, 0, 0)
            ),
        ),
        out_shape=jax.ShapeDtypeStruct((blocks, fields, width, blocks * width), coupling.dtype),
        compiler_params=pltpu.CompilerParams(vmem_limit_bytes=32 * MIB),
    )(coupling_list, pair_count, coupling)


def coupled_kernel(height, cols, matrix_ref, state_ref, weight_ref, out_ref, sums_ref):
    fields, width, depth = matrix_ref.shape[1:]
    sums_ref[...] = jnp.dot(
        matrix_ref[0].reshape(fields * width, depth),
        state_ref[...],
        preferred_element_type=jnp.float32,
    )
    for r in range(height):
        total = None
        from_left = None
        from_right = None
        for f in range(fields):
            rows = slice(f * width, (f + 1) * width)
            above = sums_ref[rows, r * cols : (r + 1) * cols]
            here = sums_ref[rows, (r + 1) * cols : (r + 2) * cols]
            below = sums_ref[rows, (r + 2) * cols : (r + 3) * cols]

            def weight(which):
                at = (f * 5 + which) * height + r
                return weight_ref[at : at + 1, :]

            term = weight(0) * here - weight(1) * above - weight(2) * below
            total = term if total is None else total + term
            rightward = weight(4) * here
            leftward = weight(3) * here
            from_left = rightward if from_left is None else from_left + rightward
            from_right = leftward if from_right is None else from_right + leftward
        total = total - pltpu.roll(from_left, 1, 1) - pltpu.roll(from_right, cols - 1, 1)
        out_ref[:, r * cols : (r + 1) * cols] = total


def coupled_sums(matrix, state, weights):
    blocks, fields, width, depth = matrix.shape
    _, five, height, cols = weights.shape
    cells = state.shape[1]
    return pl.pallas_call(
        functools.partial(coupled_kernel, height, cols),
        grid=(blocks,),
        in_specs=[
            pl.BlockSpec((1, fields, width, depth), lambda i: (i, 0, 0, 0)),
            pl.BlockSpec((depth, cells), lambda i: (0, 0)),
            pl.BlockSpec((fields * five * height, cols), lambda i: (0, 0)),
        ],
        out_specs=pl.BlockSpec((width, height * cols), lambda i: (i, 0)),
        out_shape=jax.ShapeDtypeStruct((blocks * width, height * cols), jnp.float32),
        scratch_shapes=[pltpu.VMEM((fields * width, cells), jnp.float32)],
        compiler_params=pltpu.CompilerParams(vmem_limit_bytes=40 * MIB),
    )(matrix, state, weights.reshape(fields * five * height, cols))


TOGETHER = 4
GROUP = 16


def solve(resid, right_ref, left_ref, scale_ref):
    nx, ny = resid[0].shape

    def along_cols(fields):
        high, low = split(jnp.concatenate(fields, axis=0))
        both = jnp.dot(
            jnp.concatenate([high, low], axis=1),
            right_ref[...],
            preferred_element_type=jnp.float32,
        )
        both = both[:, :ny] + both[:, ny:]
        return [both[i * nx : (i + 1) * nx] for i in range(len(fields))]

    def along_rows(wide):
        high, low = split(wide)
        both = jnp.dot(
            left_ref[...],
            jnp.concatenate([high, low], axis=0),
            preferred_element_type=jnp.float32,
        )
        return both[:nx] + both[nx:]

    wide = jnp.concatenate(along_cols(resid), axis=1)
    wide = along_rows(wide)
    scale = scale_ref[...]
    wide = wide * jnp.concatenate([scale] * len(resid), axis=1)
    wide = along_rows(wide)
    return along_cols([wide[:, i * ny : (i + 1) * ny] for i in range(len(resid))])


def sweep_kernel(
    mode_count,
    slab_count,
    last,
    current_ref,
    right_side_ref,
    coupled_ref,
    weight_ref,
    right_ref,
    left_ref,
    scale_ref,
    *refs,
):
    if last:
        solution_ref, residual_ref, turned_ref = refs
    else:
        solution_ref, state_ref, turned_ref = refs
    nx, ny = scale_ref.shape
    group = coupled_ref.shape[1]
    height = nx // (mode_count * slab_count)

    for source in range(mode_count * slab_count):
        first = ((source % slab_count) * mode_count + source // slab_count) * height
        for r in range(height):
            turned_ref[(first + r) * group : (first + r + 1) * group, :] = coupled_ref[
                source, :, r * ny : (r + 1) * ny
            ]

    def several(step, carry):
        values = []
        resid = []
        for i in range(TOGETHER):
            mode = step * TOGETHER + i
            if last:
                here = current_ref[mode]
            else:
                here = current_ref[:, mode].reshape(nx, ny)
            mean = (
                weight_ref[0] * here
                - weight_ref[1] * pltpu.roll(here, 1, 0)
                - weight_ref[2] * pltpu.roll(here, nx - 1, 0)
                - pltpu.roll(weight_ref[4] * here, 1, 1)
                - pltpu.roll(weight_ref[3] * here, ny - 1, 1)
            )
            coupled = turned_ref[pl.ds(mode, nx, stride=group), :]
            value = right_side_ref[:, mode].reshape(nx, ny) - mean - coupled
            if last:
                residual_ref[:, mode] = value.reshape(slab_count, nx // slab_count, ny)
            values.append(here)
            resid.append(value)
        change = solve(resid, right_ref, left_ref, scale_ref)
        for i in range(TOGETHER):
            mode = step * TOGETHER + i
            value = values[i] + change[i]
            if last:
                solution_ref[:, mode] = value.reshape(slab_count, nx // slab_count, ny)
            else:
                solution_ref[mode] = value
                turned_ref[pl.ds(mode, nx, stride=group), :] = value
        return carry

    lax.fori_loop(0, group // TOGETHER, several, 0)

    if not last:
        for target in range(mode_count * slab_count):
            first = ((target % slab_count) * mode_count + target // slab_count) * height
            for r in range(height + 2):
                row = first + r - 1
                if 0 <= row < nx:
                    value = turned_ref[row * group : (row + 1) * group, :].astype(jnp.bfloat16)
                else:
                    value = jnp.zeros((group, ny), jnp.bfloat16)
                state_ref[target, :, r * ny : (r + 1) * ny] = value


def sweep(current, right_side, coupled, weights, tables, mode_count, slab_count, last):
    right, left, scale = tables
    nx, ny = scale.shape
    modes = right_side.shape[1]
    devices = mode_count * slab_count
    height = nx // devices
    whole = lambda a: pl.BlockSpec(a.shape, lambda g: (0,) * a.ndim)
    slabs = pl.BlockSpec((slab_count, GROUP, nx // slab_count, ny), lambda g: (0, g, 0, 0))
    fields = pl.BlockSpec((GROUP, nx, ny), lambda g: (g, 0, 0))
    strips = pl.BlockSpec((devices, GROUP, height * ny), lambda g: (0, g, 0))
    halo_strips = pl.BlockSpec((devices, GROUP, (height + 2) * ny), lambda g: (0, g, 0))
    slabs_shape = jax.ShapeDtypeStruct((slab_count, modes, nx // slab_count, ny), jnp.float32)
    if last:
        out_specs = [slabs, slabs]
        out_shape = [slabs_shape, slabs_shape]
    else:
        out_specs = [fields, halo_strips]
        out_shape = [
            jax.ShapeDtypeStruct((modes, nx, ny), jnp.float32),
            jax.ShapeDtypeStruct((devices, modes, (height + 2) * ny), jnp.bfloat16),
        ]
    return pl.pallas_call(
        functools.partial(sweep_kernel, mode_count, slab_count, last),
        grid=(modes // GROUP,),
        in_specs=[
            fields if last else slabs,
            slabs,
            strips,
            whole(weights),
            whole(right),
            whole(left),
            whole(scale),
        ],
        out_specs=out_specs,
        out_shape=out_shape,
        scratch_shapes=[pltpu.VMEM((nx * GROUP, ny), jnp.float32)],
        compiler_params=pltpu.CompilerParams(vmem_limit_bytes=48 * MIB),
    )(current, right_side, coupled, weights, right, left, scale)


def local(guess, right_side, mean_coef, field_coef, coupling, coupling_list, pair_count):
    mode_count = lax.axis_size("mode")
    slab_count = lax.axis_size("slab")
    both = ("mode", "slab")
    modes, rows, cols = guess.shape
    fields = field_coef.shape[0]
    nx = rows * slab_count
    devices = mode_count * slab_count
    height = nx // devices
    share = modes // slab_count

    forward = [(i, i + 1) for i in range(slab_count - 1)]
    backward = [(i + 1, i) for i in range(slab_count - 1)]
    low = lax.ppermute(guess[:, -1].astype(jnp.bfloat16), "slab", forward)
    high = lax.ppermute(guess[:, 0].astype(jnp.bfloat16), "slab", backward)
    strips = pack_strips(guess, low, high, mode_count)
    state = lax.all_to_all(strips, "mode", 0, 0, tiled=True)
    state = state.reshape(mode_count * modes, (height + 2) * cols)

    def to_fields(block):
        moved = lax.all_to_all(block, "slab", 0, 0, tiled=True)
        return moved.reshape(slab_count, share, rows, cols)

    def to_slabs(block):
        flat = block.reshape(modes, rows, cols)
        return lax.all_to_all(flat, "slab", 0, 0, tiled=True)

    current = to_fields(guess)
    right = to_fields(right_side)

    coefs = jnp.concatenate([mean_coef[None], field_coef], 0)
    coefs = lax.all_gather(coefs, "slab", axis=1, tiled=True)
    weights = stencil_weights(coefs)
    strip = lax.axis_index("slab") * mode_count + lax.axis_index("mode")
    strip_weights = lax.dynamic_slice_in_dim(weights[1:], strip * height, height, axis=2)
    matrix = dense_coupling(coupling, coupling_list, pair_count, fields)

    row_high, row_low = split_table(sine_table(nx))
    col_high, col_low = split_table(sine_table(cols))
    tables = (
        jnp.concatenate(
            [
                jnp.concatenate([col_high, col_low], 1),
                jnp.concatenate([col_high, jnp.zeros_like(col_low)], 1),
            ],
            0,
        ),
        jnp.concatenate(
            [
                jnp.concatenate([row_high, row_high], 1),
                jnp.concatenate([row_low, jnp.zeros_like(row_low)], 1),
            ],
            0,
        ),
        RELAXATION / eigen_table(nx, cols),
    )

    for number in range(ITERS):
        last = number == ITERS - 1
        sums = coupled_sums(matrix, state, strip_weights)
        sums = lax.all_to_all(sums, both, 0, 0, tiled=True)
        sums = sums.reshape(devices, share, height * cols)
        current, other = sweep(
            current, right, sums, weights[0], tables, mode_count, slab_count, last
        )
        if not last:
            state = other.reshape(devices * share, (height + 2) * cols)
            state = lax.all_to_all(state, both, 0, 0, tiled=True)
    return to_slabs(current), to_slabs(other)


def solution(mesh):
    placed = (
        P("mode", "slab", None),
        P("mode", "slab", None),
        P("slab", None),
        P(None, "slab", None),
        P(),
        P(),
        P(),
    )
    return jax.shard_map(
        local,
        mesh=mesh,
        in_specs=placed,
        out_specs=(P("mode", "slab", None), P("mode", "slab", None)),
        check_vma=False,
    )
```

time: 890 us -> 341 us (0.38)
  local copies, waits for them, and re-layouts: 158 us -> 15.4 us
  blocking collectives: 301 us -> 160 us
  waiting for transfers between devices: 222 us -> 89.2 us
  matrix products: 113 us -> 0 us
  Pallas kernels: 0 us -> 44.6 us
  other arithmetic: 43.4 us -> 4.84 us
  starting transfers between devices: 40.7 us -> 25 us
    all_to_all x5 -> x4, blocking collectives: 301 us -> 150 us  [the longest x2 56.4 us: to_slabs(): return lax.all_to_all(flat, 'slab', 0, 0, tiled=True)]
    all_to_all x3 -> x4, waiting for transfers between devices: 221 us -> 88.4 us  [the longest x1 47.4 us: local(): sums = lax.all_to_all(sums, both, 0, 0, tiled=True)]
    dot_general x12 -> x0, matrix products: 113 us -> none  [the longest x2 44.8 us: local(): jnp.einsum('ikab,ikbc->ikac', coupling, gathered, preferred_element_type=...]
    dot_general x2 -> x0, local copies, waits for them, and re-layouts: 67.8 us -> none  [local(): jnp.einsum('ikab,ikbc->ikac', coupling, gathered, preferred_element_type=...]
    pallas_call x0 -> x6, Pallas kernels: none -> 44.6 us  [the longest x2 20.7 us: sweep(): pl.pallas_call(functools.partial(sweep_kernel, mode_count, slab_count, la...]
    all_to_all x8 -> x0, local copies, waits for them, and re-layouts: 29.8 us -> none  [the longest x4 26 us: local(): lax.all_to_all(grouped, 'mode', split_axis=1, concat_axis=2, tiled=True)]
    reduce_sum x2 -> x0, other arithmetic: 24.1 us -> none  [local(): coupled = jnp.sum(operate(sums_pad, field_rows), axis=0)]
    transpose x2 -> x0, local copies, waits for them, and re-layouts: 18.6 us -> none  [whole_solve(): spatial = jnp.einsum('xp,mpq->mxq', rows_table, spectral, precision=highest)]
  transfers between devices with their start and end apart: 13 -> 6, of which waited for: 4 -> 5; matrix products, arithmetic and copies ran while one was open for 5% -> 3% of each run, Pallas kernels for 0% -> 5%
where the time goes in v1:
time: 341 us; the launch traced here: 340 us
  blocking collectives  160 us (47%)
  waiting for transfers between devices  89.2 us (26%)
  Pallas kernels  44.6 us (13%)
  starting transfers between devices  25 us (7%)
  local copies, waits for them, and re-layouts  15.4 us (5%)
  other arithmetic  4.84 us (1%)
    all_to_all x2, blocking collectives, to_slabs(): return lax.all_to_all(flat, 'slab', 0, 0, tiled=True)  56.4 us
    all_to_all x1, blocking collectives, local(): sums = lax.all_to_all(sums, both, 0, 0, tiled=True)  51.7 us
    all_to_all x1, waiting for transfers between devices, local(): sums = lax.all_to_all(sums, both, 0, 0, tiled=True)  47.4 us
    all_to_all x1, blocking collectives, local(): state = lax.all_to_all(state, both, 0, 0, tiled=True)  41.8 us
    all_to_all x1, waiting for transfers between devices, local(): state = lax.all_to_all(strips, 'mode', 0, 0, tiled=True)  25.5 us
    pallas_call x2, Pallas kernels, sweep(): pl.pallas_call(functools.partial(sweep_kernel, mode_count, slab_count, la...  20.7 us
    pallas_call x2, Pallas kernels, coupled_sums(): pl.pallas_call(functools.partial(coupled_kernel, height, cols), grid=(blo...  15.7 us
    all_to_all x2, waiting for transfers between devices, to_fields(): moved = lax.all_to_all(block, 'slab', 0, 0, tiled=True)  15.5 us
  transfers between devices with their start and end apart: 6, of which 5 were waited for; matrix products, arithmetic and copies ran while one was open for 3% of the time, Pallas kernels for 5%

profile of v1, /device:TPU:0, one launch (start us, length us, event | category | flops | bytes accessed | tf_op | source)
XLA Modules:
  0.0 340.1 jit_solution(6323731781237283884)
XLA Ops:
  0.6 4.2 %all-to-all-start.1 = ((f32[128,32,128]{2,1,0:T(8,128)}), f32[128,32,128]{2,1,0:T(8,128)S(1)}, u32[]{:S(2)}, u32[]{:S(2)}) async-start(f32[128,32,128]{2,1,0:T(8,128)} %param.8), calls=%async_computation.1 | async-start | bytes 4194304 | tf_op jit(solution)/shard_map/all_to_all | solution.py:339
  4.8 2.8 copy.15
  7.7 1.3 collective-permute-start.1
  9.0 3.0 collective-permute-start
  12.9 5.1 %shard_map.87 = bf16[8,128,768]{2,1,0:T(8,128)(2,1)} custom-call(f32[4096,128]{1,0:T(8,128)} %bitcast.2.x_ref, bf16[128,128]{1,0:T(8,128)(2,1)S(1)} %collective-permute-done.low_ref, bf16[128,128]{1,0:T(8,128)(2,1)S(1)} %collective-permute-done.1.high_ref), custom_call_target="tpu_custom_call" | custom-call | tf_op jit(solution)/shard_map/pallas_call | solution.py:82
  18.0 12.5 %all-to-all-done.1 = f32[128,32,128]{2,1,0:T(8,128)S(1)} async-done(((f32[128,32,128]{2,1,0:T(8,128)}), f32[128,32,128]{2,1,0:T(8,128)S(1)}, u32[]{:S(2)}, u32[]{:S(2)}) %all-to-all-start.1) | async-done | bytes 2097184 | tf_op jit(solution)/shard_map/all_to_all | solution.py:339
  30.6 1.3 copy-done.6
  31.9 6.7 %all-to-all-start.2 = ((bf16[8,128,768]{2,1,0:T(8,128)(2,1)}), bf16[8,128,768]{2,1,0:T(8,128)(2,1)S(1)}, u32[]{:S(2)}, u32[]{:S(2)}) async-start(bf16[8,128,768]{2,1,0:T(8,128)(2,1)} %shard_map.87), calls=%async_computation.2 | async-start | bytes 3145728 | tf_op jit(solution)/shard_map/all_to_all | solution.py:335
  38.6 10.3 %all_gather.3 = f32[4,128,128]{2,1,0:T(8,128)S(1)} all-gather(f32[4,32,128]{2,1,0:T(8,128)S(1)} %pad_maximum_fusion.11), channel_id=1, replica_groups=mesh['mode'=8,'slab'=4] {'slab'}, dimensions={1}, use_global_device_ids=true | all-gather | bytes 327680 | tf_op jit(solution)/shard_map/all_gather | solution.py:350
  48.9 25.5 %all-to-all-done.2 = bf16[8,128,768]{2,1,0:T(8,128)(2,1)S(1)} async-done(((bf16[8,128,768]{2,1,0:T(8,128)(2,1)}), bf16[8,128,768]{2,1,0:T(8,128)(2,1)S(1)}, u32[]{:S(2)}, u32[]{:S(2)}) %all-to-all-start.2) | async-done | bytes 1572896 | tf_op jit(solution)/shard_map/all_to_all | solution.py:335
  74.4 4.5 %all-to-all-start = ((f32[128,32,128]{2,1,0:T(8,128)}), f32[128,32,128]{2,1,0:T(8,128)}, u32[]{:S(2)}, u32[]{:S(2)}) async-start(f32[128,32,128]{2,1,0:T(8,128)} %param.7), calls=%async_computation | async-start | bytes 4194304 | tf_op jit(solution)/shard_map/all_to_all | solution.py:339
  79.0 1.0 bitcast_dynamic-update-slice_fusion.3
  82.4 0.9 bitcast_dynamic-update-slice_fusion.4
  83.3 1.3 slice.67
  84.7 2.2 copy-done.2
  86.9 3.0 shard_map.86.matrix_ref
  89.9 7.8 %shard_map.88 = f32[1024,512]{1,0:T(8,128)S(1)} custom-call(bf16[8,3,128,1024]{3,2,1,0:T(8,128)(2,1)S(1)} %shard_map.86.matrix_ref, bf16[1024,768]{1,0:T(8,128)(2,1)S(1)} %bitcast.38, f32[60,128]{1,0:T(8,128)S(1)} %reshape.68.weight_ref), custom_call_target="tpu_custom_call" | custom-call | tf_op jit(solution)/shard_map/pallas_call | solution.py:155
  97.7 2.6 copy-done
  100.4 1.3 copy-done.1
  101.7 2.9 all-to-all-done
  104.6 5.3 %all-to-all-start.3 = ((f32[32,32,512]{2,1,0:T(8,128)}), f32[32,32,512]{2,1,0:T(8,128)}, u32[]{:S(2)}, u32[]{:S(2)}) async-start(f32[32,32,512]{2,1,0:T(8,128)} %bitcast.36), calls=%async_computation.3 | async-start | bytes 4194304 | tf_op jit(solution)/shard_map/all_to_all | solution.py:379
  110.4 1.0 slice_bitcast_fusion.weight_ref
  111.4 47.4 %all-to-all-done.3.coupled_ref = f32[32,32,512]{2,1,0:T(8,128)} async-done(((f32[32,32,512]{2,1,0:T(8,128)}), f32[32,32,512]{2,1,0:T(8,128)}, u32[]{:S(2)}, u32[]{:S(2)}) %all-to-all-start.3) | async-done | bytes 2097184 | tf_op jit(solution)/shard_map/all_to_all | solution.py:379
  158.8 10.6 %shard_map.89 = (f32[32,128,128]{2,1,0:T(8,128)S(1)}, bf16[32,32,768]{2,1,0:T(8,128)(2,1)S(1)}) custom-call(f32[4,32,32,128]{3,2,1,0:T(8,128)} %bitcast.current_ref, f32[4,32,32,128]{3,2,1,0:T(8,128)} %bitcast.42, f32[32,32,512]{2,1,0:T(8,128)} %all-to-all-done.3.coupled_ref, f32[5,128,128]{2,1,0:T(8,128)S(1)} %slice_bitcast_fusion.weight_ref, ...), custom_call_target="tpu_custom_call" | custom-call | tf_op jit(solution)/shard_map/pallas_call | solution.py:300
  169.4 41.8 %all_to_all.51 = bf16[32,32,768]{2,1,0:T(8,128)(2,1)S(1)} all-to-all(bf16[32,32,768]{2,1,0:T(8,128)(2,1)S(1)} %get-tuple-element.7), channel_id=1, replica_groups=mesh['mode'=8,'slab'=4] {'mode','slab'}, dimensions={0} | all-to-all | bytes 3145728 | tf_op jit(solution)/shard_map/all_to_all | solution.py:386
  211.3 7.8 %shard_map.90 = f32[1024,512]{1,0:T(8,128)S(1)} custom-call(bf16[8,3,128,1024]{3,2,1,0:T(8,128)(2,1)S(1)} %bitcast.35, bf16[1024,768]{1,0:T(8,128)(2,1)S(1)} %bitcast.39, f32[60,128]{1,0:T(8,128)S(1)} %reshape.68.weight_ref), custom_call_target="tpu_custom_call" | custom-call | tf_op jit(solution)/shard_map/pallas_call | solution.py:155
  219.1 51.7 %all_to_all.52.coupled_ref = f32[32,32,512]{2,1,0:T(8,128)} all-to-all(f32[32,32,512]{2,1,0:T(8,128)S(1)} %bitcast.37), channel_id=1, replica_groups=mesh['mode'=8,'slab'=4] {'mode','slab'}, dimensions={0} | all-to-all | bytes 4194304 | tf_op jit(solution)/shard_map/all_to_all | solution.py:379
  270.8 10.2 %shard_map.91 = (f32[4,32,32,128]{3,2,1,0:T(8,128)S(1)}, f32[4,32,32,128]{3,2,1,0:T(8,128)S(1)}) custom-call(f32[32,128,128]{2,1,0:T(8,128)} %copy-done.3, f32[4,32,32,128]{3,2,1,0:T(8,128)} %bitcast.43, f32[32,32,512]{2,1,0:T(8,128)} %all_to_all.52.coupled_ref, f32[5,128,128]{2,1,0:T(8,128)S(1)} %slice_bitcast_fusion.weight_ref, ...), custom_call_target="tpu_custom_call" | custom-call | tf_op jit(solution)/shard_map/pallas_call | solution.py:300
  281.0 28.3 %all_to_all.53 = f32[128,32,128]{2,1,0:T(8,128)S(1)} all-to-all(f32[128,32,128]{2,1,0:T(8,128)S(1)} %bitcast.41), channel_id=1, replica_groups=mesh['mode'=8,'slab'=4] {'slab'}, dimensions={0} | all-to-all | bytes 4194304 | tf_op jit(solution)/shard_map/all_to_all | solution.py:344
  309.3 28.2 %all_to_all.54 = f32[128,32,128]{2,1,0:T(8,128)S(1)} all-to-all(f32[128,32,128]{2,1,0:T(8,128)S(1)} %bitcast.40), channel_id=1, replica_groups=mesh['mode'=8,'slab'=4] {'slab'}, dimensions={0} | all-to-all | bytes 4194304 | tf_op jit(solution)/shard_map/all_to_all | solution.py:344
  337.4 1.3 copy.22
  338.8 1.3 copy.23
  (38 shorter events, 4.0 us)
Async XLA Ops:
  0.6 29.9 %all-to-all-start.1 = ((f32[128,32,128]{2,1,0:T(8,128)}), f32[128,32,128]{2,1,0:T(8,128)S(1)}, u32[]{:S(2)}, u32[]{:S(2)}) async-start(f32[128,32,128]{2,1,0:T(8,128)} %param.8), calls=%async_computation.1 | async-start | bytes 4194304 | tf_op jit(solution)/shard_map/all_to_all | solution.py:339
  7.7 4.4 %collective-permute-start.1 = (bf16[128,128]{1,0:T(8,128)(2,1)S(1)}, bf16[128,128]{1,0:T(8,128)(2,1)S(1)}, u32[]{:S(2)}, u32[]{:S(2)}) collective-permute-start(bf16[128,128]{1,0:T(8,128)(2,1)S(1)} %get-tuple-element.10), channel_id=1, source_target_pairs={{1,0},{2,1},{3,2},{5,4},{6,5},{7,6},{9,8},{10,9},{11,10},{13,12},{... | collective-permute-start | bytes 98312 | tf_op jit(solution)/shard_map/ppermute | solution.py:333
  9.0 3.9 %collective-permute-start = (bf16[128,128]{1,0:T(8,128)(2,1)S(1)}, bf16[128,128]{1,0:T(8,128)(2,1)S(1)}, u32[]{:S(2)}, u32[]{:S(2)}) collective-permute-start(bf16[128,128]{1,0:T(8,128)(2,1)S(1)} %get-tuple-element.11), channel_id=1, source_target_pairs={{0,1},{1,2},{2,3},{4,5},{5,6},{6,7},{8,9},{9,10},{10,11},{12,13},{... | collective-permute-start | bytes 98312 | tf_op jit(solution)/shard_map/ppermute | solution.py:332
  18.0 20.5 %copy-start.7 = (f32[3,32,128]{2,1,0:T(8,128)S(1)}, f32[3,32,128]{2,1,0:T(8,128)}, u32[]{:S(2)}) copy-start(f32[3,32,128]{2,1,0:T(8,128)} %param.10) | copy-start | bytes 147460
  18.0 20.5 %copy-start.8 = (f32[32,128]{1,0:T(8,128)S(1)}, f32[32,128]{1,0:T(8,128)}, u32[]{:S(2)}) copy-start(f32[32,128]{1,0:T(8,128)} %param.9) | copy-start | bytes 49156
  30.5 1.3 copy-start.6
  31.9 42.5 %all-to-all-start.2 = ((bf16[8,128,768]{2,1,0:T(8,128)(2,1)}), bf16[8,128,768]{2,1,0:T(8,128)(2,1)S(1)}, u32[]{:S(2)}, u32[]{:S(2)}) async-start(bf16[8,128,768]{2,1,0:T(8,128)(2,1)} %shard_map.87), calls=%async_computation.2 | async-start | bytes 3145728 | tf_op jit(solution)/shard_map/all_to_all | solution.py:335
  74.4 30.2 %all-to-all-start = ((f32[128,32,128]{2,1,0:T(8,128)}), f32[128,32,128]{2,1,0:T(8,128)}, u32[]{:S(2)}, u32[]{:S(2)}) async-start(f32[128,32,128]{2,1,0:T(8,128)} %param.7), calls=%async_computation | async-start | bytes 4194304 | tf_op jit(solution)/shard_map/all_to_all | solution.py:339
  82.4 2.2 copy-start.4
  82.4 2.2 copy-start.5
  84.7 2.2 copy-start.2
  97.7 2.6 copy-start
  100.4 1.3 copy-start.1
  104.6 106.6 %slice-start = ((s8[6291456]{0:T(1024)(128)(4,1)}), s8[2097152]{0:T(1024)(128)(4,1)S(1)}, s32[]{:S(2)}) async-start(s8[6291456]{0:T(1024)(128)(4,1)} %bitcast.34), calls=%async_computation.8 | async-start | bytes 4194304
  104.6 54.2 %all-to-all-start.3 = ((f32[32,32,512]{2,1,0:T(8,128)}), f32[32,32,512]{2,1,0:T(8,128)}, u32[]{:S(2)}, u32[]{:S(2)}) async-start(f32[32,32,512]{2,1,0:T(8,128)} %bitcast.36), calls=%async_computation.3 | async-start | bytes 4194304 | tf_op jit(solution)/shard_map/all_to_all | solution.py:379
  158.8 52.4 %slice-start.1 = ((s8[6291456]{0:T(1024)(128)(4,1)}), s8[4194304]{0:T(1024)(128)(4,1)S(1)}, s32[]{:S(2)}) async-start(s8[6291456]{0:T(1024)(128)(4,1)} %bitcast.34), calls=%async_computation.9 | async-start | bytes 8388608
  169.4 41.9 %copy-start.3 = (f32[32,128,128]{2,1,0:T(8,128)}, f32[32,128,128]{2,1,0:T(8,128)S(1)}, u32[]{:S(2)}) copy-start(f32[32,128,128]{2,1,0:T(8,128)S(1)} %get-tuple-element.6.current_ref) | copy-start | bytes 6291460

commit v2 on v1

--- a/solution.py
+++ b/solution.py
@@ -201,27 +201,27 @@
     return along_cols([wide[:, i * ny : (i + 1) * ny] for i in range(len(resid))])
 
 
-def sweep_kernel(
-    mode_count,
-    slab_count,
-    last,
-    current_ref,
-    right_side_ref,
-    coupled_ref,
-    weight_ref,
-    right_ref,
-    left_ref,
-    scale_ref,
-    *refs,
-):
-    if last:
-        solution_ref, residual_ref, turned_ref = refs
-    else:
-        solution_ref, state_ref, turned_ref = refs
-    nx, ny = scale_ref.shape
+def mean_kernel(current_ref, right_side_ref, weight_ref, out_ref):
+    nx, ny = weight_ref.shape[1:]
+
+    def one(mode, carry):
+        here = current_ref[:, mode].reshape(nx, ny)
+        mean = (
+            weight_ref[0] * here
+            - weight_ref[1] * pltpu.roll(here, 1, 0)
+            - weight_ref[2] * pltpu.roll(here, nx - 1, 0)
+            - pltpu.roll(weight_ref[4] * here, 1, 1)
+            - pltpu.roll(weight_ref[3] * here, ny - 1, 1)
+        )
+        value = right_side_ref[:, mode].reshape(nx, ny) - mean
+        out_ref[:, mode] = value.reshape(out_ref.shape[0], -1, ny)
+        return carry
+
+    lax.fori_loop(0, out_ref.shape[1], one, 0)
+
+
+def turn_in(turned_ref, coupled_ref, mode_count, slab_count, height, ny):
     group = coupled_ref.shape[1]
-    height = nx // (mode_count * slab_count)
-
     for source in range(mode_count * slab_count):
         first = ((source % slab_count) * mode_count + source // slab_count) * height
         for r in range(height):
@@ -229,91 +229,184 @@
                 source, :, r * ny : (r + 1) * ny
             ]
 
+
+def step_kernel(
+    mode_count,
+    slab_count,
+    current_ref,
+    base_ref,
+    coupled_ref,
+    right_ref,
+    left_ref,
+    scale_ref,
+    solution_ref,
+    state_ref,
+    turned_ref,
+):
+    nx, ny = scale_ref.shape
+    group = coupled_ref.shape[1]
+    height = nx // (mode_count * slab_count)
+    turn_in(turned_ref, coupled_ref, mode_count, slab_count, height, ny)
+
     def several(step, carry):
-        values = []
+        first = step * TOGETHER
         resid = []
         for i in range(TOGETHER):
-            mode = step * TOGETHER + i
-            if last:
-                here = current_ref[mode]
-            else:
-                here = current_ref[:, mode].reshape(nx, ny)
-            mean = (
-                weight_ref[0] * here
-                - weight_ref[1] * pltpu.roll(here, 1, 0)
-                - weight_ref[2] * pltpu.roll(here, nx - 1, 0)
-                - pltpu.roll(weight_ref[4] * here, 1, 1)
-                - pltpu.roll(weight_ref[3] * here, ny - 1, 1)
-            )
-            coupled = turned_ref[pl.ds(mode, nx, stride=group), :]
-            value = right_side_ref[:, mode].reshape(nx, ny) - mean - coupled
-            if last:
-                residual_ref[:, mode] = value.reshape(slab_count, nx // slab_count, ny)
-            values.append(here)
-            resid.append(value)
+            coupled = turned_ref[pl.ds(first + i, nx, stride=group), :]
+            resid.append(base_ref[:, first + i].reshape(nx, ny) - coupled)
         change = solve(resid, right_ref, left_ref, scale_ref)
         for i in range(TOGETHER):
-            mode = step * TOGETHER + i
-            value = values[i] + change[i]
-            if last:
-                solution_ref[:, mode] = value.reshape(slab_count, nx // slab_count, ny)
+            value = current_ref[:, first + i].reshape(nx, ny) + change[i]
+            solution_ref[:, first + i] = value.reshape(slab_count, nx // slab_count, ny)
+            turned_ref[pl.ds(first + i, nx, stride=group), :] = value
+        return carry
+
+    lax.fori_loop(0, group // TOGETHER, several, 0)
+
+    for target in range(mode_count * slab_count):
+        first = ((target % slab_count) * mode_count + target // slab_count) * height
+        for r in range(height + 2):
+            row = first + r - 1
+            if 0 <= row < nx:
+                value = turned_ref[row * group : (row + 1) * group, :].astype(jnp.bfloat16)
             else:
-                solution_ref[mode] = value
-                turned_ref[pl.ds(mode, nx, stride=group), :] = value
+                value = jnp.zeros((group, ny), jnp.bfloat16)
+            state_ref[target, :, r * ny : (r + 1) * ny] = value
+
+
+def residual_kernel(mode_count, slab_count, base_ref, coupled_ref, out_ref, turned_ref):
+    group = coupled_ref.shape[1]
+    ny = base_ref.shape[-1]
+    nx = turned_ref.shape[0] // group
+    height = nx // (mode_count * slab_count)
+    turn_in(turned_ref, coupled_ref, mode_count, slab_count, height, ny)
+
+    def one(mode, carry):
+        coupled = turned_ref[pl.ds(mode, nx, stride=group), :]
+        out_ref[:, mode] = base_ref[:, mode] - coupled.reshape(slab_count, nx // slab_count, ny)
         return carry
 
-    lax.fori_loop(0, group // TOGETHER, several, 0)
-
-    if not last:
-        for target in range(mode_count * slab_count):
-            first = ((target % slab_count) * mode_count + target // slab_count) * height
-            for r in range(height + 2):
-                row = first + r - 1
-                if 0 <= row < nx:
-                    value = turned_ref[row * group : (row + 1) * group, :].astype(jnp.bfloat16)
-                else:
-                    value = jnp.zeros((group, ny), jnp.bfloat16)
-                state_ref[target, :, r * ny : (r + 1) * ny] = value
-
-
-def sweep(current, right_side, coupled, weights, tables, mode_count, slab_count, last):
-    right, left, scale = tables
-    nx, ny = scale.shape
-    modes = right_side.shape[1]
-    devices = mode_count * slab_count
-    height = nx // devices
-    whole = lambda a: pl.BlockSpec(a.shape, lambda g: (0,) * a.ndim)
-    slabs = pl.BlockSpec((slab_count, GROUP, nx // slab_count, ny), lambda g: (0, g, 0, 0))
-    fields = pl.BlockSpec((GROUP, nx, ny), lambda g: (g, 0, 0))
-    strips = pl.BlockSpec((devices, GROUP, height * ny), lambda g: (0, g, 0))
-    halo_strips = pl.BlockSpec((devices, GROUP, (height + 2) * ny), lambda g: (0, g, 0))
-    slabs_shape = jax.ShapeDtypeStruct((slab_count, modes, nx // slab_count, ny), jnp.float32)
-    if last:
-        out_specs = [slabs, slabs]
-        out_shape = [slabs_shape, slabs_shape]
-    else:
-        out_specs = [fields, halo_strips]
-        out_shape = [
-            jax.ShapeDtypeStruct((modes, nx, ny), jnp.float32),
-            jax.ShapeDtypeStruct((devices, modes, (height + 2) * ny), jnp.bfloat16),
-        ]
+    lax.fori_loop(0, group, one, 0)
+
+
+def correct_kernel(current_ref, resid_ref, right_ref, left_ref, scale_ref, out_ref):
+    nx, ny = scale_ref.shape
+
+    def several(step, carry):
+        first = step * TOGETHER
+        resid = [resid_ref[:, first + i].reshape(nx, ny) for i in range(TOGETHER)]
+        change = solve(resid, right_ref, left_ref, scale_ref)
+        for i in range(TOGETHER):
+            shape = out_ref.shape[:1] + out_ref.shape[2:]
+            out_ref[:, first + i] = current_ref[:, first + i] + change[i].reshape(shape)
+        return carry
+
+    lax.fori_loop(0, out_ref.shape[1] // TOGETHER, several, 0)
+
+
+def whole(array):
+    return pl.BlockSpec(array.shape, lambda g: (0,) * array.ndim)
+
+
+def slabs_of(array):
+    slab_count, _, rows, ny = array.shape
+    return pl.BlockSpec((slab_count, GROUP, rows, ny), lambda g: (0, g, 0, 0))
+
+
+def strips_of(shape):
+    return pl.BlockSpec((shape[0], GROUP, shape[2]), lambda g: (0, g, 0))
+
+
+def per_group(kernel, operands, in_specs, out_shape, out_specs, scratch=(), flops=0):
+    moved = sum(a.size * a.dtype.itemsize for a in operands)
     return pl.pallas_call(
-        functools.partial(sweep_kernel, mode_count, slab_count, last),
-        grid=(modes // GROUP,),
-        in_specs=[
-            fields if last else slabs,
-            slabs,
-            strips,
-            whole(weights),
-            whole(right),
-            whole(left),
-            whole(scale),
-        ],
+        kernel,
+        grid=(operands[0].shape[1] // GROUP,),
+        in_specs=in_specs,
         out_specs=out_specs,
         out_shape=out_shape,
-        scratch_shapes=[pltpu.VMEM((nx * GROUP, ny), jnp.float32)],
+        scratch_shapes=scratch,
+        cost_estimate=pl.CostEstimate(flops=flops, bytes_accessed=2 * moved, transcendentals=0),
         compiler_params=pltpu.CompilerParams(vmem_limit_bytes=48 * MIB),
-    )(current, right_side, coupled, weights, right, left, scale)
+    )(*operands)
+
+
+def mean_part(current, right_side, weights):
+    slabs = slabs_of(current)
+    return per_group(
+        mean_kernel,
+        (current, right_side, weights),
+        [slabs, slabs, whole(weights)],
+        jax.ShapeDtypeStruct(current.shape, jnp.float32),
+        slabs,
+    )
+
+
+def solve_flops(array, tables):
+    nx, ny = tables[2].shape
+    return array.shape[1] * 8 * 3 * nx * ny * (nx + ny) // 2
+
+
+def step(current, base, coupled, tables, mode_count, slab_count):
+    nx, ny = tables[2].shape
+    slabs = slabs_of(current)
+    devices, modes, cells = coupled.shape
+    halo = (devices, modes, cells + 2 * ny)
+    return per_group(
+        functools.partial(step_kernel, mode_count, slab_count),
+        (current, base, coupled, *tables),
+        [slabs, slabs, strips_of(coupled.shape), *map(whole, tables)],
+        [
+            jax.ShapeDtypeStruct(current.shape, jnp.float32),
+            jax.ShapeDtypeStruct(halo, jnp.bfloat16),
+        ],
+        [slabs, strips_of(halo)],
+        [pltpu.VMEM((nx * GROUP, ny), jnp.float32)],
+        solve_flops(current, tables),
+    )
+
+
+def last_residual(base, coupled, mode_count, slab_count):
+    slab, _, rows, ny = base.shape
+    slabs = slabs_of(base)
+    return per_group(
+        functools.partial(residual_kernel, mode_count, slab_count),
+        (base, coupled),
+        [slabs, strips_of(coupled.shape)],
+        jax.ShapeDtypeStruct(base.shape, jnp.float32),
+        slabs,
+        [pltpu.VMEM((slab * rows * GROUP, ny), jnp.float32)],
+    )
+
+
+def correct(current, resid, tables):
+    slabs = slabs_of(current)
+    return per_group(
+        correct_kernel,
+        (current, resid, *tables),
+        [slabs, slabs, *map(whole, tables)],
+        jax.ShapeDtypeStruct(current.shape, jnp.float32),
+        slabs,
+        (),
+        solve_flops(current, tables),
+    )
+
+
+def regroup(block, axis):
+    count = lax.axis_size(axis)
+    here = lax.axis_index(axis)
+    own = lax.dynamic_index_in_dim(block, here, 0)
+    out = lax.dynamic_update_slice_in_dim(jnp.zeros_like(block), own, here, 0)
+    for shift in range(1, count):
+        target = lax.rem(here + shift, count)
+        source = lax.rem(here + count - shift, count)
+        moved = lax.ppermute(
+            lax.dynamic_index_in_dim(block, target, 0),
+            axis,
+            [(i, (i + shift) % count) for i in range(count)],
+        )
+        out = lax.dynamic_update_slice_in_dim(out, moved, source, 0)
+    return out
 
 
 def local(guess, right_side, mean_coef, field_coef, coupling, coupling_list, pair_count):
@@ -336,8 +429,7 @@
     state = state.reshape(mode_count * modes, (height + 2) * cols)
 
     def to_fields(block):
-        moved = lax.all_to_all(block, "slab", 0, 0, tiled=True)
-        return moved.reshape(slab_count, share, rows, cols)
+        return regroup(block.reshape(slab_count, share, rows, cols), "slab")
 
     def to_slabs(block):
         flat = block.reshape(modes, rows, cols)
@@ -374,17 +466,18 @@
     )
 
     for number in range(ITERS):
-        last = number == ITERS - 1
+        base = mean_part(current, right, weights[0])
         sums = coupled_sums(matrix, state, strip_weights)
         sums = lax.all_to_all(sums, both, 0, 0, tiled=True)
         sums = sums.reshape(devices, share, height * cols)
-        current, other = sweep(
-            current, right, sums, weights[0], tables, mode_count, slab_count, last
-        )
-        if not last:
-            state = other.reshape(devices * share, (height + 2) * cols)
+        if number < ITERS - 1:
+            current, state = step(current, base, sums, tables, mode_count, slab_count)
+            state = state.reshape(devices * share, (height + 2) * cols)
             state = lax.all_to_all(state, both, 0, 0, tiled=True)
-    return to_slabs(current), to_slabs(other)
+        else:
+            resid = last_residual(base, sums, mode_count, slab_count)
+            current = correct(current, resid, tables)
+    return to_slabs(current), to_slabs(resid)
 
 
 def solution(mesh):

time: 341 us -> 339 us (level)
  blocking collectives: 160 us -> 80 us
  waiting for transfers between devices: 89.2 us -> 144 us
  local copies, waits for them, and re-layouts: 15.4 us -> 30.8 us
  Pallas kernels: 44.6 us -> 54.4 us
  other arithmetic: 4.84 us -> 1.34 us
    ppermute x0 -> x6, waiting for transfers between devices: none -> 63.2 us  [regroup(): lax.ppermute(lax.dynamic_index_in_dim(block, target, 0), axis, [(i, (i +...]
    all_to_all x1 -> x0, blocking collectives: 51.7 us -> none  [local(): sums = lax.all_to_all(sums, both, 0, 0, tiled=True)]
    all_to_all x2 -> x1, blocking collectives: 56.4 us -> 29.3 us  [to_slabs(): return lax.all_to_all(flat, 'slab', 0, 0, tiled=True)]
    unnamed x25 -> x51, local copies, waits for them, and re-layouts: 12.9 us -> 28.4 us
    pallas_call x2 -> x5, Pallas kernels: 20.7 us -> 31.7 us  [per_group(): pl.pallas_call(kernel, grid=(operands[0].shape[1] // GROUP,), in_specs=in...]
    all_to_all x1 -> x2, waiting for transfers between devices: 47.4 us -> 42.7 us  [local(): sums = lax.all_to_all(sums, both, 0, 0, tiled=True)]
    all_to_all x1, waiting for transfers between devices: 25.5 us -> 20.9 us  [local(): state = lax.all_to_all(strips, 'mode', 0, 0, tiled=True)]
    all_to_all x2 -> x1, starting transfers between devices: 8.69 us -> 4.45 us  [to_slabs(): return lax.all_to_all(flat, 'slab', 0, 0, tiled=True)]
  transfers between devices with their start and end apart: 6 -> 12, of which waited for: 5 -> 7; matrix products, arithmetic and copies ran while one was open for 3% -> 1% of each run, Pallas kernels for 5% -> 6%
where the time goes in v2:
time: 339 us; the launch traced here: 338 us
  waiting for transfers between devices  144 us (42%)
  blocking collectives  80 us (24%)
  Pallas kernels  54.4 us (16%)
  local copies, waits for them, and re-layouts  30.8 us (9%)
  starting transfers between devices  26.9 us (8%)
    ppermute x6, waiting for transfers between devices, regroup(): lax.ppermute(lax.dynamic_index_in_dim(block, target, 0), axis, [(i, (i +...  63.2 us
    all_to_all x1, blocking collectives, local(): state = lax.all_to_all(state, both, 0, 0, tiled=True)  43 us
    all_to_all x2, waiting for transfers between devices, local(): sums = lax.all_to_all(sums, both, 0, 0, tiled=True)  42.7 us
    pallas_call x5, Pallas kernels, per_group(): pl.pallas_call(kernel, grid=(operands[0].shape[1] // GROUP,), in_specs=in...  31.7 us
    all_to_all x1, blocking collectives, to_slabs(): return lax.all_to_all(flat, 'slab', 0, 0, tiled=True)  29.3 us
    unnamed x51, local copies, waits for them, and re-layouts  28.4 us
    all_to_all x1, waiting for transfers between devices, local(): state = lax.all_to_all(strips, 'mode', 0, 0, tiled=True)  20.9 us
    pallas_call x2, Pallas kernels, coupled_sums(): pl.pallas_call(functools.partial(coupled_kernel, height, cols), grid=(blo...  17.1 us
  transfers between devices with their start and end apart: 12, of which 7 were waited for; matrix products, arithmetic and copies ran while one was open for 1% of the time, Pallas kernels for 6%

profile of v2, /device:TPU:0, one launch (start us, length us, event | category | flops | bytes accessed | tf_op | source)
XLA Modules:
  0.0 338.3 jit_solution(1859120185047016950)
XLA Ops:
  0.6 3.0 copy.15
  4.9 3.0 collective-permute-start.6
  8.8 2.4 shard_map.88
  12.3 7.4 %all-to-all-start = ((bf16[8,128,768]{2,1,0:T(8,128)(2,1)}), bf16[8,128,768]{2,1,0:T(8,128)(2,1)}, u32[]{:S(2)}, u32[]{:S(2)}) async-start(bf16[8,128,768]{2,1,0:T(8,128)(2,1)} %copy-done.13), calls=%async_computation | async-start | bytes 3145728 | tf_op jit(solution)/shard_map/all_to_all | solution.py:428
  19.8 7.7 %all_gather.3 = f32[4,128,128]{2,1,0:T(8,128)S(1)} all-gather(f32[4,32,128]{2,1,0:T(8,128)S(1)} %pad_maximum_fusion.11), channel_id=1, replica_groups=mesh['mode'=8,'slab'=4] {'slab'}, dimensions={1}, use_global_device_ids=true | all-gather | bytes 327680 | tf_op jit(solution)/shard_map/all_gather | solution.py:442
  29.8 2.2 copy-done.14
  32.0 3.2 shard_map.87.matrix_ref
  35.2 2.7 copy-done
  37.8 20.9 %all-to-all-done = bf16[8,128,768]{2,1,0:T(8,128)(2,1)} async-done(((bf16[8,128,768]{2,1,0:T(8,128)(2,1)}), bf16[8,128,768]{2,1,0:T(8,128)(2,1)}, u32[]{:S(2)}, u32[]{:S(2)}) %all-to-all-start) | async-done | bytes 1572896 | tf_op jit(solution)/shard_map/all_to_all | solution.py:428
  58.7 2.8 copy-done.1
  61.5 9.3 %shard_map.89 = f32[1024,512]{1,0:T(8,128)S(1)} custom-call(bf16[8,3,128,1024]{3,2,1,0:T(8,128)(2,1)S(1)} %copy-done.1, bf16[1024,768]{1,0:T(8,128)(2,1)} %bitcast.16.state_ref, f32[60,128]{1,0:T(8,128)S(1)} %reshape.68.weight_ref), custom_call_target="tpu_custom_call" | custom-call | tf_op jit(solution)/shard_map/pallas_call | solution.py:155
  70.8 1.4 copy-done.10
  72.2 3.5 %all-to-all-start.1 = ((f32[32,32,512]{2,1,0:T(8,128)}), f32[32,32,512]{2,1,0:T(8,128)}, u32[]{:S(2)}, u32[]{:S(2)}) async-start(f32[32,32,512]{2,1,0:T(8,128)} %bitcast.38), calls=%async_computation.1 | async-start | bytes 4194304 | tf_op jit(solution)/shard_map/all_to_all | solution.py:471
  76.2 1.4 collective-permute-start.2
  78.5 1.6 collective-permute-start.4
  81.8 40.9 %collective-permute-done = f32[1,32,32,128]{3,2,1,0:T(8,128)S(1)} collective-permute-done((f32[1,32,32,128]{3,2,1,0:T(8,128)S(1)}, f32[1,32,32,128]{3,2,1,0:T(8,128)S(1)}, u32[]{:S(2)}, u32[]{:S(2)}) %collective-permute-start) | collective-permute-done | bytes 524320 | tf_op jit(solution)/shard_map/ppermute | solution.py:403
  123.8 21.4 %collective-permute-done.3 = f32[1,32,32,128]{3,2,1,0:T(8,128)S(1)} collective-permute-done((f32[1,32,32,128]{3,2,1,0:T(8,128)S(1)}, f32[1,32,32,128]{3,2,1,0:T(8,128)S(1)}, u32[]{:S(2)}, u32[]{:S(2)}) %collective-permute-start.3) | collective-permute-done | bytes 524320 | tf_op jit(solution)/shard_map/ppermute | solution.py:403
  146.7 5.0 %shard_map.86.base_ref = f32[4,32,32,128]{3,2,1,0:T(8,128)S(1)} custom-call(f32[4,32,32,128]{3,2,1,0:T(8,128)S(1)} %constant_dynamic-update-slice_fusion.3.current_ref, f32[4,32,32,128]{3,2,1,0:T(8,128)} %copy-done.17, f32[5,128,128]{2,1,0:T(8,128)S(1)} %slice_bitcast_fusion.weight_ref), custom_call_target="tpu_custom_call" | custom-call | bytes 9043968 | tf_op jit(solution)/shard_map/pallas_call | solution.py:322
  153.0 1.6 copy-done.3
  154.6 9.7 %shard_map.90 = (f32[4,32,32,128]{3,2,1,0:T(8,128)S(1)}, bf16[32,32,768]{2,1,0:T(8,128)(2,1)S(1)}) custom-call(f32[4,32,32,128]{3,2,1,0:T(8,128)S(1)} %copy-done.3, f32[4,32,32,128]{3,2,1,0:T(8,128)} %copy-done.7, f32[32,32,512]{2,1,0:T(8,128)} %all-to-all-done.1.coupled_ref, bf16[256,256]{1,0:T(8,128)(2,1)S(1)} %get-tuple-element.21.right_ref, ...), custom_call_target="tpu_custom_call" | custom-call | flops 1610612736 | bytes 13238272 | tf_op jit(solution)/shard_map/pallas_call | solution.py:322
  164.3 43.0 %all_to_all.41 = bf16[32,32,768]{2,1,0:T(8,128)(2,1)S(1)} all-to-all(bf16[32,32,768]{2,1,0:T(8,128)(2,1)S(1)} %get-tuple-element.5), channel_id=1, replica_groups=mesh['mode'=8,'slab'=4] {'mode','slab'}, dimensions={0} | all-to-all | bytes 3145728 | tf_op jit(solution)/shard_map/all_to_all | solution.py:476
  207.3 7.8 %shard_map.92 = f32[1024,512]{1,0:T(8,128)S(1)} custom-call(bf16[8,3,128,1024]{3,2,1,0:T(8,128)(2,1)S(1)} %bitcast.35, bf16[1024,768]{1,0:T(8,128)(2,1)S(1)} %bitcast.41, f32[60,128]{1,0:T(8,128)S(1)} %reshape.68.weight_ref), custom_call_target="tpu_custom_call" | custom-call | tf_op jit(solution)/shard_map/pallas_call | solution.py:155
  216.5 3.6 %all-to-all-start.3 = ((f32[32,32,512]{2,1,0:T(8,128)}), f32[32,32,512]{2,1,0:T(8,128)}, u32[]{:S(2)}, u32[]{:S(2)}) async-start(f32[32,32,512]{2,1,0:T(8,128)} %bitcast.39), calls=%async_computation.3 | async-start | bytes 4194304 | tf_op jit(solution)/shard_map/all_to_all | solution.py:471
  220.1 4.8 %shard_map.91.base_ref = f32[4,32,32,128]{3,2,1,0:T(8,128)S(1)} custom-call(f32[4,32,32,128]{3,2,1,0:T(8,128)S(1)} %copy-done.6, f32[4,32,32,128]{3,2,1,0:T(8,128)} %copy-done.17, f32[5,128,128]{2,1,0:T(8,128)S(1)} %slice_bitcast_fusion.weight_ref), custom_call_target="tpu_custom_call" | custom-call | bytes 9043968 | tf_op jit(solution)/shard_map/pallas_call | solution.py:322
  226.3 42.7 %all-to-all-done.3.coupled_ref = f32[32,32,512]{2,1,0:T(8,128)} async-done(((f32[32,32,512]{2,1,0:T(8,128)}), f32[32,32,512]{2,1,0:T(8,128)}, u32[]{:S(2)}, u32[]{:S(2)}) %all-to-all-start.3) | async-done | bytes 2097184 | tf_op jit(solution)/shard_map/all_to_all | solution.py:471
  269.0 1.6 copy-done.9
  270.6 3.8 %shard_map.93.resid_ref = f32[4,32,32,128]{3,2,1,0:T(8,128)} custom-call(f32[4,32,32,128]{3,2,1,0:T(8,128)S(1)} %copy-done.9, f32[32,32,512]{2,1,0:T(8,128)} %all-to-all-done.3.coupled_ref), custom_call_target="tpu_custom_call" | custom-call | bytes 8388608 | tf_op jit(solution)/shard_map/pallas_call | solution.py:322
  274.4 4.5 %all-to-all-start.5 = ((f32[128,32,128]{2,1,0:T(8,128)}), f32[128,32,128]{2,1,0:T(8,128)}, u32[]{:S(2)}, u32[]{:S(2)}) async-start(f32[128,32,128]{2,1,0:T(8,128)} %bitcast.21), calls=%async_computation.5 | async-start | bytes 4194304 | tf_op jit(solution)/shard_map/all_to_all | solution.py:436
  278.9 8.4 %shard_map.94 = f32[4,32,32,128]{3,2,1,0:T(8,128)S(1)} custom-call(f32[4,32,32,128]{3,2,1,0:T(8,128)S(1)} %copy-done.6, f32[4,32,32,128]{3,2,1,0:T(8,128)} %shard_map.93.resid_ref, bf16[256,256]{1,0:T(8,128)(2,1)S(1)} %get-tuple-element.21.right_ref, bf16[256,256]{1,0:T(8,128)(2,1)S(1)} %get-tuple-element.20.left_ref, ...), custom_call_target="tpu_custom_call" | custom-call | flops 1610612736 | bytes 9043968 | tf_op jit(solution)/shard_map/pallas_call | solution.py:322
  288.6 16.0 %all-to-all-done.5 = f32[128,32,128]{2,1,0:T(8,128)} async-done(((f32[128,32,128]{2,1,0:T(8,128)}), f32[128,32,128]{2,1,0:T(8,128)}, u32[]{:S(2)}, u32[]{:S(2)}) %all-to-all-start.5) | async-done | bytes 2097184 | tf_op jit(solution)/shard_map/all_to_all | solution.py:436
  304.6 29.3 %all_to_all.42 = f32[128,32,128]{2,1,0:T(8,128)S(1)} all-to-all(f32[128,32,128]{2,1,0:T(8,128)} %bitcast.40), channel_id=1, replica_groups=mesh['mode'=8,'slab'=4] {'slab'}, dimensions={0} | all-to-all | bytes 4194304 | tf_op jit(solution)/shard_map/all_to_all | solution.py:436
  335.2 3.1 copy.31
  (87 shorter events, 17.6 us)
Async XLA Ops:
  0.6 8.2 %copy-start.4 = (f32[128,32,128]{2,1,0:T(8,128)S(1)}, f32[128,32,128]{2,1,0:T(8,128)}, u32[]{:S(2)}) copy-start(f32[128,32,128]{2,1,0:T(8,128)} %param.7) | copy-start | bytes 6291460
  3.6 4.3 %collective-permute-start.7 = (bf16[128,128]{1,0:T(8,128)(2,1)S(1)}, bf16[128,128]{1,0:T(8,128)(2,1)S(1)}, u32[]{:S(2)}, u32[]{:S(2)}) collective-permute-start(bf16[128,128]{1,0:T(8,128)(2,1)S(1)} %get-tuple-element.14), channel_id=1, source_target_pairs={{1,0},{2,1},{3,2},{5,4},{6,5},{7,6},{9,8},{10,9},{11,10},{13,12},{... | collective-permute-start | bytes 98312 | tf_op jit(solution)/shard_map/ppermute | solution.py:426
  4.9 3.9 %collective-permute-start.6 = (bf16[128,128]{1,0:T(8,128)(2,1)S(1)}, bf16[128,128]{1,0:T(8,128)(2,1)S(1)}, u32[]{:S(2)}, u32[]{:S(2)}) collective-permute-start(bf16[128,128]{1,0:T(8,128)(2,1)S(1)} %get-tuple-element.15), channel_id=1, source_target_pairs={{0,1},{1,2},{2,3},{4,5},{5,6},{6,7},{8,9},{9,10},{10,11},{12,13},{... | collective-permute-start | bytes 98312 | tf_op jit(solution)/shard_map/ppermute | solution.py:425
  12.3 7.4 %copy-start.20 = (f32[3,32,128]{2,1,0:T(8,128)S(1)}, f32[3,32,128]{2,1,0:T(8,128)}, u32[]{:S(2)}) copy-start(f32[3,32,128]{2,1,0:T(8,128)} %param.10) | copy-start | bytes 147460
  12.3 7.4 %copy-start.21 = (f32[32,128]{1,0:T(8,128)S(1)}, f32[32,128]{1,0:T(8,128)}, u32[]{:S(2)}) copy-start(f32[32,128]{1,0:T(8,128)} %param.9) | copy-start | bytes 49156
  12.3 46.4 %all-to-all-start = ((bf16[8,128,768]{2,1,0:T(8,128)(2,1)}), bf16[8,128,768]{2,1,0:T(8,128)(2,1)}, u32[]{:S(2)}, u32[]{:S(2)}) async-start(bf16[8,128,768]{2,1,0:T(8,128)(2,1)} %copy-done.13), calls=%async_computation | async-start | bytes 3145728 | tf_op jit(solution)/shard_map/all_to_all | solution.py:428
  28.1 1.7 copy-start.15
  28.1 1.7 copy-start.16
  29.8 2.2 copy-start.14
  35.2 2.7 copy-start
  58.7 2.8 copy-start.1
  70.8 1.4 copy-start.10
  72.2 80.8 %all-to-all-start.1 = ((f32[32,32,512]{2,1,0:T(8,128)}), f32[32,32,512]{2,1,0:T(8,128)}, u32[]{:S(2)}, u32[]{:S(2)}) async-start(f32[32,32,512]{2,1,0:T(8,128)} %bitcast.38), calls=%async_computation.1 | async-start | bytes 4194304 | tf_op jit(solution)/shard_map/all_to_all | solution.py:471
  76.2 2.1 copy-start.18
  76.2 47.6 %collective-permute-start.2 = (f32[1,32,32,128]{3,2,1,0:T(8,128)S(1)}, f32[1,32,32,128]{3,2,1,0:T(8,128)S(1)}, u32[]{:S(2)}, u32[]{:S(2)}) collective-permute-start(f32[1,32,32,128]{3,2,1,0:T(8,128)S(1)} %get-tuple-element.10), channel_id=1, source_target_pairs={{0,3},{1,0},{2,1},{3,2},{4,7},{5,4},{6,5},{7,6},{8,11},{9,8},{10,9... | collective-permute-start | bytes 1572872 | tf_op jit(solution)/shard_map/ppermute | solution.py:403
  77.6 46.1 %collective-permute-start.1 = (f32[1,32,32,128]{3,2,1,0:T(8,128)S(1)}, f32[1,32,32,128]{3,2,1,0:T(8,128)S(1)}, u32[]{:S(2)}, u32[]{:S(2)}) collective-permute-start(f32[1,32,32,128]{3,2,1,0:T(8,128)S(1)} %get-tuple-element.11), channel_id=1, source_target_pairs={{0,2},{1,3},{2,0},{3,1},{4,6},{5,7},{6,4},{7,5},{8,10},{9,11},{10,... | collective-permute-start | bytes 1572872 | tf_op jit(solution)/shard_map/ppermute | solution.py:403
  77.9 44.8 %collective-permute-start = (f32[1,32,32,128]{3,2,1,0:T(8,128)S(1)}, f32[1,32,32,128]{3,2,1,0:T(8,128)S(1)}, u32[]{:S(2)}, u32[]{:S(2)}) collective-permute-start(f32[1,32,32,128]{3,2,1,0:T(8,128)S(1)} %get-tuple-element.12), channel_id=1, source_target_pairs={{0,1},{1,2},{2,3},{3,0},{4,5},{5,6},{6,7},{7,4},{8,9},{9,10},{10,1... | collective-permute-start | bytes 1572872 | tf_op jit(solution)/shard_map/ppermute | solution.py:403
  78.5 66.7 %collective-permute-start.4 = (f32[1,32,32,128]{3,2,1,0:T(8,128)S(1)}, f32[1,32,32,128]{3,2,1,0:T(8,128)S(1)}, u32[]{:S(2)}, u32[]{:S(2)}) collective-permute-start(f32[1,32,32,128]{3,2,1,0:T(8,128)S(1)} %get-tuple-element.7), channel_id=1, source_target_pairs={{0,2},{1,3},{2,0},{3,1},{4,6},{5,7},{6,4},{7,5},{8,10},{9,11},{10,... | collective-permute-start | bytes 1572872 | tf_op jit(solution)/shard_map/ppermute | solution.py:403
  80.1 65.1 %collective-permute-start.3 = (f32[1,32,32,128]{3,2,1,0:T(8,128)S(1)}, f32[1,32,32,128]{3,2,1,0:T(8,128)S(1)}, u32[]{:S(2)}, u32[]{:S(2)}) collective-permute-start(f32[1,32,32,128]{3,2,1,0:T(8,128)S(1)} %get-tuple-element.8), channel_id=1, source_target_pairs={{0,1},{1,2},{2,3},{3,0},{4,5},{5,6},{6,7},{7,4},{8,9},{9,10},{10,1... | collective-permute-start | bytes 1572872 | tf_op jit(solution)/shard_map/ppermute | solution.py:403
  122.8 22.6 %collective-permute-start.5 = (f32[1,32,32,128]{3,2,1,0:T(8,128)S(1)}, f32[1,32,32,128]{3,2,1,0:T(8,128)S(1)}, u32[]{:S(2)}, u32[]{:S(2)}) collective-permute-start(f32[1,32,32,128]{3,2,1,0:T(8,128)S(1)} %get-tuple-element.6), channel_id=1, source_target_pairs={{0,3},{1,0},{2,1},{3,2},{4,7},{5,4},{6,5},{7,6},{8,11},{9,8},{10,9... | collective-permute-start | bytes 1572872 | tf_op jit(solution)/shard_map/ppermute | solution.py:403
  123.8 21.6 %copy-start.2 = (f32[4,32,32,128]{3,2,1,0:T(8,128)}, f32[4,32,32,128]{3,2,1,0:T(8,128)S(1)}, u32[]{:S(2)}) copy-start(f32[4,32,32,128]{3,2,1,0:T(8,128)S(1)} %constant_dynamic-update-slice_fusion.3.current_ref) | copy-start | bytes 6291460
  145.4 1.3 copy-start.17
  146.7 60.6 %slice-start = ((s8[6291456]{0:T(1024)(128)(4,1)}), s8[2097152]{0:T(1024)(128)(4,1)S(1)}, s32[]{:S(2)}) async-start(s8[6291456]{0:T(1024)(128)(4,1)} %bitcast.34), calls=%async_computation.6 | async-start | bytes 4194304
  153.0 1.6 copy-start.3
  154.6 52.7 %slice-start.1 = ((s8[6291456]{0:T(1024)(128)(4,1)}), s8[4194304]{0:T(1024)(128)(4,1)S(1)}, s32[]{:S(2)}) async-start(s8[6291456]{0:T(1024)(128)(4,1)} %bitcast.34), calls=%async_computation.7 | async-start | bytes 8388608
  164.3 50.8 %copy-start.5 = (f32[4,32,32,128]{3,2,1,0:T(8,128)}, f32[4,32,32,128]{3,2,1,0:T(8,128)S(1)}, u32[]{:S(2)}) copy-start(f32[4,32,32,128]{3,2,1,0:T(8,128)S(1)} %get-tuple-element.4.current_ref) | copy-start | bytes 6291460
  215.2 1.3 copy-start.11
  216.5 3.6 %copy-start.6 = (f32[4,32,32,128]{3,2,1,0:T(8,128)S(1)}, f32[4,32,32,128]{3,2,1,0:T(8,128)}, u32[]{:S(2)}) copy-start(f32[4,32,32,128]{3,2,1,0:T(8,128)} %copy-done.5) | copy-start | bytes 6291460
  216.5 52.5 %all-to-all-start.3 = ((f32[32,32,512]{2,1,0:T(8,128)}), f32[32,32,512]{2,1,0:T(8,128)}, u32[]{:S(2)}, u32[]{:S(2)}) async-start(f32[32,32,512]{2,1,0:T(8,128)} %bitcast.39), calls=%async_computation.3 | async-start | bytes 4194304 | tf_op jit(solution)/shard_map/all_to_all | solution.py:471
  225.0 1.3 copy-start.8
  269.0 1.6 copy-start.9
  274.4 30.2 %all-to-all-start.5 = ((f32[128,32,128]{2,1,0:T(8,128)}), f32[128,32,128]{2,1,0:T(8,128)}, u32[]{:S(2)}, u32[]{:S(2)}) async-start(f32[128,32,128]{2,1,0:T(8,128)} %bitcast.21), calls=%async_computation.5 | async-start | bytes 4194304 | tf_op jit(solution)/shard_map/all_to_all | solution.py:436
  (4 other events, 4.8 us)

commit v3 on v2

--- a/solution.py
+++ b/solution.py
@@ -62,28 +62,23 @@
     return high.astype(jnp.bfloat16), (value - high).astype(jnp.bfloat16)
 
 
-def pack_kernel(strips, rows, height, x_ref, low_ref, high_ref, out_ref):
-    modes, cols = low_ref.shape
+def pack_kernel(rows, height, x_ref, out_ref):
+    strips, modes, cells = out_ref.shape
+    cols = cells // height
     for strip in range(strips):
-        for r in range(height + 2):
-            row = strip * height + r - 1
-            if row < 0:
-                value = low_ref[...]
-            elif row >= rows:
-                value = high_ref[...]
-            else:
-                value = x_ref[pl.ds(row, modes, stride=rows), :]
+        for r in range(height):
+            value = x_ref[pl.ds(strip * height + r, modes, stride=rows), :]
             out_ref[strip, :, r * cols : (r + 1) * cols] = value.astype(jnp.bfloat16)
 
 
-def pack_strips(block, low, high, strips):
+def pack_strips(block, strips):
     modes, rows, cols = block.shape
     height = rows // strips
     return pl.pallas_call(
-        functools.partial(pack_kernel, strips, rows, height),
-        out_shape=jax.ShapeDtypeStruct((strips, modes, (height + 2) * cols), jnp.bfloat16),
+        functools.partial(pack_kernel, rows, height),
+        out_shape=jax.ShapeDtypeStruct((strips, modes, height * cols), jnp.bfloat16),
         compiler_params=pltpu.CompilerParams(vmem_limit_bytes=32 * MIB),
-    )(block.reshape(modes * rows, cols), low, high)
+    )(block.reshape(modes * rows, cols))
 
 
 def dense_kernel(fields, entry_ref, count_ref, coupling_ref, out_ref):
@@ -117,7 +112,12 @@
     )(coupling_list, pair_count, coupling)
 
 
-def coupled_kernel(height, cols, matrix_ref, state_ref, weight_ref, out_ref, sums_ref):
+def weight_row(weight_ref, height, field, which, r):
+    at = (field * 5 + which) * height + r
+    return weight_ref[at : at + 1, :]
+
+
+def inner_kernel(height, cols, matrix_ref, state_ref, weight_ref, out_ref, sums_ref):
     fields, width, depth = matrix_ref.shape[1:]
     sums_ref[...] = jnp.dot(
         matrix_ref[0].reshape(fields * width, depth),
@@ -125,46 +125,82 @@
         preferred_element_type=jnp.float32,
     )
     for r in range(height):
-        total = None
-        from_left = None
-        from_right = None
+        total = 0.0
+        from_left = 0.0
+        from_right = 0.0
         for f in range(fields):
-            rows = slice(f * width, (f + 1) * width)
-            above = sums_ref[rows, r * cols : (r + 1) * cols]
-            here = sums_ref[rows, (r + 1) * cols : (r + 2) * cols]
-            below = sums_ref[rows, (r + 2) * cols : (r + 3) * cols]
-
-            def weight(which):
-                at = (f * 5 + which) * height + r
-                return weight_ref[at : at + 1, :]
-
-            term = weight(0) * here - weight(1) * above - weight(2) * below
-            total = term if total is None else total + term
-            rightward = weight(4) * here
-            leftward = weight(3) * here
-            from_left = rightward if from_left is None else from_left + rightward
-            from_right = leftward if from_right is None else from_right + leftward
+
+            def row(at):
+                return sums_ref[f * width : (f + 1) * width, at * cols : (at + 1) * cols]
+
+            weight = functools.partial(weight_row, weight_ref, height, f)
+            here = row(r)
+            total = total + weight(0, r) * here
+            if r > 0:
+                total = total - weight(1, r) * row(r - 1)
+            if r < height - 1:
+                total = total - weight(2, r) * row(r + 1)
+            from_left = from_left + weight(4, r) * here
+            from_right = from_right + weight(3, r) * here
         total = total - pltpu.roll(from_left, 1, 1) - pltpu.roll(from_right, cols - 1, 1)
         out_ref[:, r * cols : (r + 1) * cols] = total
 
 
-def coupled_sums(matrix, state, weights):
+def border_kernel(height, cols, matrix_ref, above_ref, below_ref, weight_ref, inner_ref, out_ref):
+    fields, width, depth = matrix_ref.shape[1:]
+    matrix = matrix_ref[0].reshape(fields * width, depth)
+    border = jnp.concatenate([above_ref[...], below_ref[...]], axis=1)
+    sums = jnp.dot(matrix, border, preferred_element_type=jnp.float32)
+    for r in range(height):
+        total = inner_ref[:, r * cols : (r + 1) * cols]
+        for f in range(fields):
+            part = sums[f * width : (f + 1) * width]
+            if r == 0:
+                total = total - weight_row(weight_ref, height, f, 1, r) * part[:, :cols]
+            if r == height - 1:
+                total = total - weight_row(weight_ref, height, f, 2, r) * part[:, cols:]
+        out_ref[:, r * cols : (r + 1) * cols] = total
+
+
+def coupled_sums(matrix, state, weights, both):
     blocks, fields, width, depth = matrix.shape
     _, five, height, cols = weights.shape
     cells = state.shape[1]
+    weights = weights.reshape(fields * five * height, cols)
+    mode_count = lax.axis_size("mode")
+    slab_count = lax.axis_size("slab")
+    place = [
+        (t % mode_count) * slab_count + t // mode_count for t in range(mode_count * slab_count)
+    ]
+    onward = list(zip(place[:-1], place[1:]))
+    above = lax.ppermute(state[:, -cols:], both, onward)
+    below = lax.ppermute(state[:, :cols], both, [(b, a) for a, b in onward])
+    matrix_spec = pl.BlockSpec((1, fields, width, depth), lambda i: (i, 0, 0, 0))
+    weight_spec = pl.BlockSpec(weights.shape, lambda i: (0, 0))
+    sums_spec = pl.BlockSpec((width, cells), lambda i: (i, 0))
+    sums_shape = jax.ShapeDtypeStruct((blocks * width, cells), jnp.float32)
+    params = pltpu.CompilerParams(vmem_limit_bytes=40 * MIB)
+    inner = pl.pallas_call(
+        functools.partial(inner_kernel, height, cols),
+        grid=(blocks,),
+        in_specs=[matrix_spec, pl.BlockSpec((depth, cells), lambda i: (0, 0)), weight_spec],
+        out_specs=sums_spec,
+        out_shape=sums_shape,
+        scratch_shapes=[pltpu.VMEM((fields * width, cells), jnp.float32)],
+        cost_estimate=pl.CostEstimate(
+            flops=2 * matrix.size * cells, bytes_accessed=2 * matrix.size, transcendentals=0
+        ),
+        compiler_params=params,
+    )(matrix, state, weights)
+    border_spec = pl.BlockSpec((depth, cols), lambda i: (0, 0))
     return pl.pallas_call(
-        functools.partial(coupled_kernel, height, cols),
+        functools.partial(border_kernel, height, cols),
         grid=(blocks,),
-        in_specs=[
-            pl.BlockSpec((1, fields, width, depth), lambda i: (i, 0, 0, 0)),
-            pl.BlockSpec((depth, cells), lambda i: (0, 0)),
-            pl.BlockSpec((fields * five * height, cols), lambda i: (0, 0)),
-        ],
-        out_specs=pl.BlockSpec((width, height * cols), lambda i: (i, 0)),
-        out_shape=jax.ShapeDtypeStruct((blocks * width, height * cols), jnp.float32),
-        scratch_shapes=[pltpu.VMEM((fields * width, cells), jnp.float32)],
-        compiler_params=pltpu.CompilerParams(vmem_limit_bytes=40 * MIB),
-    )(matrix, state, weights.reshape(fields * five * height, cols))
+        in_specs=[matrix_spec, border_spec, border_spec, weight_spec, sums_spec],
+        out_specs=sums_spec,
+        out_shape=sums_shape,
+        compiler_params=params,
+    )(matrix, above, below, weights, inner)
 
 
 TOGETHER = 4
@@ -265,12 +301,9 @@
 
     for target in range(mode_count * slab_count):
         first = ((target % slab_count) * mode_count + target // slab_count) * height
-        for r in range(height + 2):
-            row = first + r - 1
-            if 0 <= row < nx:
-                value = turned_ref[row * group : (row + 1) * group, :].astype(jnp.bfloat16)
-            else:
-                value = jnp.zeros((group, ny), jnp.bfloat16)
+        for r in range(height):
+            row = first + r
+            value = turned_ref[row * group : (row + 1) * group, :].astype(jnp.bfloat16)
             state_ref[target, :, r * ny : (r + 1) * ny] = value
 
 
@@ -350,17 +383,15 @@
 def step(current, base, coupled, tables, mode_count, slab_count):
     nx, ny = tables[2].shape
     slabs = slabs_of(current)
-    devices, modes, cells = coupled.shape
-    halo = (devices, modes, cells + 2 * ny)
     return per_group(
         functools.partial(step_kernel, mode_count, slab_count),
         (current, base, coupled, *tables),
         [slabs, slabs, strips_of(coupled.shape), *map(whole, tables)],
         [
             jax.ShapeDtypeStruct(current.shape, jnp.float32),
-            jax.ShapeDtypeStruct(halo, jnp.bfloat16),
+            jax.ShapeDtypeStruct(coupled.shape, jnp.bfloat16),
         ],
-        [slabs, strips_of(halo)],
+        [slabs, strips_of(coupled.shape)],
         [pltpu.VMEM((nx * GROUP, ny), jnp.float32)],
         solve_flops(current, tables),
     )
@@ -420,13 +451,9 @@
     height = nx // devices
     share = modes // slab_count
 
-    forward = [(i, i + 1) for i in range(slab_count - 1)]
-    backward = [(i + 1, i) for i in range(slab_count - 1)]
-    low = lax.ppermute(guess[:, -1].astype(jnp.bfloat16), "slab", forward)
-    high = lax.ppermute(guess[:, 0].astype(jnp.bfloat16), "slab", backward)
-    strips = pack_strips(guess, low, high, mode_count)
+    strips = pack_strips(guess, mode_count)
     state = lax.all_to_all(strips, "mode", 0, 0, tiled=True)
-    state = state.reshape(mode_count * modes, (height + 2) * cols)
+    state = state.reshape(mode_count * modes, height * cols)
 
     def to_fields(block):
         return regroup(block.reshape(slab_count, share, rows, cols), "slab")
@@ -435,7 +462,7 @@
         flat = block.reshape(modes, rows, cols)
         return lax.all_to_all(flat, "slab", 0, 0, tiled=True)
 
-    current = to_fields(guess)
+    state, current = lax.optimization_barrier((state, to_fields(guess)))
     right = to_fields(right_side)
 
     coefs = jnp.concatenate([mean_coef[None], field_coef], 0)
@@ -467,12 +494,12 @@
 
     for number in range(ITERS):
         base = mean_part(current, right, weights[0])
-        sums = coupled_sums(matrix, state, strip_weights)
+        sums = coupled_sums(matrix, state, strip_weights, both)
         sums = lax.all_to_all(sums, both, 0, 0, tiled=True)
         sums = sums.reshape(devices, share, height * cols)
         if number < ITERS - 1:
             current, state = step(current, base, sums, tables, mode_count, slab_count)
-            state = state.reshape(devices * share, (height + 2) * cols)
+            state = state.reshape(devices * share, height * cols)
             state = lax.all_to_all(state, both, 0, 0, tiled=True)
         else:
             resid = last_residual(base, sums, mode_count, slab_count)

time: 339 us -> 333 us (0.982)
  waiting for transfers between devices: 144 us -> 104 us
  starting transfers between devices: 26.9 us -> 40.2 us
  blocking collectives: 80 us -> 86 us
  local copies, waits for them, and re-layouts: 30.8 us -> 36.1 us
  other arithmetic: 1.34 us -> 5.82 us
  Pallas kernels: 54.4 us -> 58.3 us
    ppermute x6, waiting for transfers between devices: 63.2 us -> 42.1 us  [regroup(): lax.ppermute(lax.dynamic_index_in_dim(block, target, 0), axis, [(i, (i +...]
    all_to_all x1, waiting for transfers between devices: 20.9 us -> 0.01 us  [local(): state = lax.all_to_all(strips, 'mode', 0, 0, tiled=True)]
    all_gather x1, blocking collectives: 7.73 us -> 26.1 us  [local(): coefs = lax.all_gather(coefs, 'slab', axis=1, tiled=True)]
    all_to_all x1, blocking collectives: 43 us -> 30.6 us  [local(): state = lax.all_to_all(state, both, 0, 0, tiled=True)]
    ppermute x2 -> x4, starting transfers between devices: 4.32 us -> 11.7 us  [the longest x2 9.13 us: coupled_sums(): above = lax.ppermute(state[:, -cols:], both, onward)]
    all_to_all x2, starting transfers between devices: 7.08 us -> 13 us  [local(): sums = lax.all_to_all(sums, both, 0, 0, tiled=True)]
    pallas_call x3 -> x5, Pallas kernels: 19.5 us -> 23.8 us  [the longest x2 13.4 us: coupled_sums(): pl.pallas_call(functools.partial(inner_kernel, height, cols), grid=(block...]
    unnamed x51 -> x48, local copies, waits for them, and re-layouts: 28.4 us -> 24.8 us
  transfers between devices with their start and end apart: 12 -> 14, of which waited for: 7 -> 6; matrix products, arithmetic and copies ran while one was open for 1% -> 5% of each run, Pallas kernels for 6% -> 10%
where the time goes in v3:
time: 333 us; the launch traced here: 332 us
  waiting for transfers between devices  104 us (31%)
  blocking collectives  86 us (26%)
  Pallas kernels  58.3 us (18%)
  starting transfers between devices  40.2 us (12%)
  local copies, waits for them, and re-layouts  36.1 us (11%)
  other arithmetic  5.82 us (2%)
    all_to_all x2, waiting for transfers between devices, local(): sums = lax.all_to_all(sums, both, 0, 0, tiled=True)  42.7 us
    ppermute x6, waiting for transfers between devices, regroup(): lax.ppermute(lax.dynamic_index_in_dim(block, target, 0), axis, [(i, (i +...  42.1 us
    pallas_call x5, Pallas kernels, per_group(): pl.pallas_call(kernel, grid=(operands[0].shape[1] // GROUP,), in_specs=in...  31.6 us
    all_to_all x1, blocking collectives, local(): state = lax.all_to_all(state, both, 0, 0, tiled=True)  30.6 us
    all_to_all x1, blocking collectives, to_slabs(): return lax.all_to_all(flat, 'slab', 0, 0, tiled=True)  29.3 us
    all_gather x1, blocking collectives, local(): coefs = lax.all_gather(coefs, 'slab', axis=1, tiled=True)  26.1 us
    unnamed x48, local copies, waits for them, and re-layouts  24.8 us
    all_to_all x1, waiting for transfers between devices, to_slabs(): return lax.all_to_all(flat, 'slab', 0, 0, tiled=True)  16 us
  transfers between devices with their start and end apart: 14, of which 6 were waited for; matrix products, arithmetic and copies ran while one was open for 5% of the time, Pallas kernels for 10%

profile of v3, /device:TPU:0, one launch (start us, length us, event | category | flops | bytes accessed | tf_op | source)
XLA Modules:
  0.0 331.9 jit_solution(9703399627855952641)
XLA Ops:
  2.2 2.6 shard_map.86
  4.9 7.3 %all-to-all-start = ((bf16[8,128,512]{2,1,0:T(8,128)(2,1)}), bf16[8,128,512]{2,1,0:T(8,128)(2,1)S(1)}, u32[]{:S(2)}, u32[]{:S(2)}) async-start(bf16[8,128,512]{2,1,0:T(8,128)(2,1)} %shard_map.86), calls=%async_computation | async-start | bytes 2097152 | tf_op jit(solution)/shard_map/all_to_all | solution.py:455
  12.4 2.8 constant_dynamic-slice_fusion.4
  16.9 26.1 %all_gather.3 = f32[4,128,128]{2,1,0:T(8,128)S(1)} all-gather(f32[4,32,128]{2,1,0:T(8,128)S(1)} %pad_maximum_fusion.11), channel_id=1, replica_groups=mesh['mode'=8,'slab'=4] {'slab'}, dimensions={1}, use_global_device_ids=true | all-gather | bytes 327680 | tf_op jit(solution)/shard_map/all_gather | solution.py:469
  46.7 1.9 bitcast_dynamic-update-slice_fusion.4
  48.6 2.2 slice.72
  51.7 2.2 copy-done.13
  53.9 2.9 shard_map.88.matrix_ref
  56.8 2.7 copy-done
  64.2 4.6 %collective-permute-start.6 = (bf16[1024,128]{1,0:T(8,128)(2,1)S(1)}, bf16[1024,128]{1,0:T(8,128)(2,1)S(1)}, u32[]{:S(2)}, u32[]{:S(2)}) collective-permute-start(bf16[1024,128]{1,0:T(8,128)(2,1)S(1)} %get-tuple-element.21), channel_id=1, source_target_pairs={{0,4},{4,8},{8,12},{12,16},{16,20},{20,24},{24,28},{28,1},{1,5},{5... | collective-permute-start | bytes 786440 | tf_op jit(solution)/shard_map/ppermute | solution.py:176
  68.8 2.8 copy-done.1
  71.5 6.7 %shard_map.89.inner_ref = f32[1024,512]{1,0:T(8,128)S(1)} custom-call(bf16[8,3,128,1024]{3,2,1,0:T(8,128)(2,1)S(1)} %copy-done.1, bf16[1024,512]{1,0:T(8,128)(2,1)S(1)} %bitcast.37, f32[60,128]{1,0:T(8,128)S(1)} %reshape.66.weight_ref), custom_call_target="tpu_custom_call" | custom-call | flops 3221225472 | bytes 6291456 | tf_op jit(solution)/shard_map/pallas_call | solution.py:183
  79.3 4.7 %shard_map.90 = f32[1024,512]{1,0:T(8,128)} custom-call(bf16[8,3,128,1024]{3,2,1,0:T(8,128)(2,1)S(1)} %copy-done.1, bf16[1024,128]{1,0:T(8,128)(2,1)S(1)} %collective-permute-done.6.above_ref, bf16[1024,128]{1,0:T(8,128)(2,1)S(1)} %collective-permute-done.7.below_ref, f32[60,128]{1,0:T(8,128)S(1)} %reshape.66.weight_ref, f32[1024,512]{1,0:T(8,128)S(1)} %shard_map.89.inner_ref), custom_call_target="tpu_custom_call" | custom-call | tf_op jit(solution)/shard_map/pallas_call | solution.py:196
  84.0 7.5 %all-to-all-start.1 = ((f32[32,32,512]{2,1,0:T(8,128)}), f32[32,32,512]{2,1,0:T(8,128)}, u32[]{:S(2)}, u32[]{:S(2)}) async-start(f32[32,32,512]{2,1,0:T(8,128)} %bitcast.15), calls=%async_computation.1 | async-start | bytes 4194304 | tf_op jit(solution)/shard_map/all_to_all | solution.py:498
  96.9 41.7 %collective-permute-done.3 = f32[1,32,32,128]{3,2,1,0:T(8,128)S(1)} collective-permute-done((f32[1,32,32,128]{3,2,1,0:T(8,128)S(1)}, f32[1,32,32,128]{3,2,1,0:T(8,128)S(1)}, u32[]{:S(2)}, u32[]{:S(2)}) %collective-permute-start.3) | collective-permute-done | bytes 524320 | tf_op jit(solution)/shard_map/ppermute | solution.py:434
  140.6 5.0 %shard_map.87.base_ref = f32[4,32,32,128]{3,2,1,0:T(8,128)S(1)} custom-call(f32[4,32,32,128]{3,2,1,0:T(8,128)S(1)} %copy-done.3, f32[4,32,32,128]{3,2,1,0:T(8,128)} %copy-done.16, f32[5,128,128]{2,1,0:T(8,128)S(1)} %slice_bitcast_fusion.weight_ref), custom_call_target="tpu_custom_call" | custom-call | bytes 9043968 | tf_op jit(solution)/shard_map/pallas_call | solution.py:355
  146.9 1.6 copy-done.4
  148.4 9.6 %shard_map.91 = (f32[4,32,32,128]{3,2,1,0:T(8,128)S(1)}, bf16[32,32,512]{2,1,0:T(8,128)(2,1)S(1)}) custom-call(f32[4,32,32,128]{3,2,1,0:T(8,128)S(1)} %copy-done.4, f32[4,32,32,128]{3,2,1,0:T(8,128)} %copy-done.7, f32[32,32,512]{2,1,0:T(8,128)} %all-to-all-done.1.coupled_ref, bf16[256,256]{1,0:T(8,128)(2,1)S(1)} %get-tuple-element.27.right_ref, ...), custom_call_target="tpu_custom_call" | custom-call | flops 1610612736 | bytes 13238272 | tf_op jit(solution)/shard_map/pallas_call | solution.py:355
  158.1 30.6 %all_to_all.41 = bf16[32,32,512]{2,1,0:T(8,128)(2,1)S(1)} all-to-all(bf16[32,32,512]{2,1,0:T(8,128)(2,1)S(1)} %get-tuple-element.9), channel_id=1, replica_groups=mesh['mode'=8,'slab'=4] {'mode','slab'}, dimensions={0} | all-to-all | bytes 2097152 | tf_op jit(solution)/shard_map/all_to_all | solution.py:503
  190.0 4.6 %collective-permute-start.8 = (bf16[1024,128]{1,0:T(8,128)(2,1)S(1)}, bf16[1024,128]{1,0:T(8,128)(2,1)S(1)}, u32[]{:S(2)}, u32[]{:S(2)}) collective-permute-start(bf16[1024,128]{1,0:T(8,128)(2,1)S(1)} %get-tuple-element.19), channel_id=1, source_target_pairs={{0,4},{4,8},{8,12},{12,16},{16,20},{20,24},{24,28},{28,1},{1,5},{5... | collective-permute-start | bytes 786440 | tf_op jit(solution)/shard_map/ppermute | solution.py:176
  194.6 6.7 %shard_map.93.inner_ref = f32[1024,512]{1,0:T(8,128)S(1)} custom-call(bf16[8,3,128,1024]{3,2,1,0:T(8,128)(2,1)S(1)} %bitcast.31, bf16[1024,512]{1,0:T(8,128)(2,1)S(1)} %bitcast.39, f32[60,128]{1,0:T(8,128)S(1)} %reshape.66.weight_ref), custom_call_target="tpu_custom_call" | custom-call | flops 3221225472 | bytes 6291456 | tf_op jit(solution)/shard_map/pallas_call | solution.py:183
  201.4 2.5 collective-permute-done.8.above_ref
  203.8 3.0 shard_map.94
  208.2 5.5 %all-to-all-start.3 = ((f32[32,32,512]{2,1,0:T(8,128)}), f32[32,32,512]{2,1,0:T(8,128)}, u32[]{:S(2)}, u32[]{:S(2)}) async-start(f32[32,32,512]{2,1,0:T(8,128)} %bitcast.35), calls=%async_computation.3 | async-start | bytes 4194304 | tf_op jit(solution)/shard_map/all_to_all | solution.py:498
  213.8 4.8 %shard_map.92.base_ref = f32[4,32,32,128]{3,2,1,0:T(8,128)S(1)} custom-call(f32[4,32,32,128]{3,2,1,0:T(8,128)S(1)} %copy-done.6, f32[4,32,32,128]{3,2,1,0:T(8,128)} %copy-done.16, f32[5,128,128]{2,1,0:T(8,128)S(1)} %slice_bitcast_fusion.weight_ref), custom_call_target="tpu_custom_call" | custom-call | bytes 9043968 | tf_op jit(solution)/shard_map/pallas_call | solution.py:355
  219.9 42.7 %all-to-all-done.3.coupled_ref = f32[32,32,512]{2,1,0:T(8,128)} async-done(((f32[32,32,512]{2,1,0:T(8,128)}), f32[32,32,512]{2,1,0:T(8,128)}, u32[]{:S(2)}, u32[]{:S(2)}) %all-to-all-start.3) | async-done | bytes 2097184 | tf_op jit(solution)/shard_map/all_to_all | solution.py:498
  264.2 3.8 %shard_map.95.resid_ref = f32[4,32,32,128]{3,2,1,0:T(8,128)} custom-call(f32[4,32,32,128]{3,2,1,0:T(8,128)S(1)} %copy-done.9, f32[32,32,512]{2,1,0:T(8,128)} %all-to-all-done.3.coupled_ref), custom_call_target="tpu_custom_call" | custom-call | bytes 8388608 | tf_op jit(solution)/shard_map/pallas_call | solution.py:355
  268.0 4.4 %all-to-all-start.5 = ((f32[128,32,128]{2,1,0:T(8,128)}), f32[128,32,128]{2,1,0:T(8,128)}, u32[]{:S(2)}, u32[]{:S(2)}) async-start(f32[128,32,128]{2,1,0:T(8,128)} %bitcast.19), calls=%async_computation.5 | async-start | bytes 4194304 | tf_op jit(solution)/shard_map/all_to_all | solution.py:463
  272.4 8.4 %shard_map.96 = f32[4,32,32,128]{3,2,1,0:T(8,128)S(1)} custom-call(f32[4,32,32,128]{3,2,1,0:T(8,128)S(1)} %copy-done.6, f32[4,32,32,128]{3,2,1,0:T(8,128)} %shard_map.95.resid_ref, bf16[256,256]{1,0:T(8,128)(2,1)S(1)} %get-tuple-element.27.right_ref, bf16[256,256]{1,0:T(8,128)(2,1)S(1)} %get-tuple-element.26.left_ref, ...), custom_call_target="tpu_custom_call" | custom-call | flops 1610612736 | bytes 9043968 | tf_op jit(solution)/shard_map/pallas_call | solution.py:355
  282.2 16.0 %all-to-all-done.5 = f32[128,32,128]{2,1,0:T(8,128)} async-done(((f32[128,32,128]{2,1,0:T(8,128)}), f32[128,32,128]{2,1,0:T(8,128)}, u32[]{:S(2)}, u32[]{:S(2)}) %all-to-all-start.5) | async-done | bytes 2097184 | tf_op jit(solution)/shard_map/all_to_all | solution.py:463
  298.2 29.3 %all_to_all.42 = f32[128,32,128]{2,1,0:T(8,128)S(1)} all-to-all(f32[128,32,128]{2,1,0:T(8,128)} %bitcast.32), channel_id=1, replica_groups=mesh['mode'=8,'slab'=4] {'slab'}, dimensions={0} | all-to-all | bytes 4194304 | tf_op jit(solution)/shard_map/all_to_all | solution.py:463
  328.8 3.1 copy.28
  (91 shorter events, 30.5 us)
Async XLA Ops:
  0.6 1.6 copy-start.11
  4.9 57.9 %all-to-all-start = ((bf16[8,128,512]{2,1,0:T(8,128)(2,1)}), bf16[8,128,512]{2,1,0:T(8,128)(2,1)S(1)}, u32[]{:S(2)}, u32[]{:S(2)}) async-start(bf16[8,128,512]{2,1,0:T(8,128)(2,1)} %shard_map.86), calls=%async_computation | async-start | bytes 2097152 | tf_op jit(solution)/shard_map/all_to_all | solution.py:455
  12.4 4.5 %copy-start.19 = (f32[3,32,128]{2,1,0:T(8,128)S(1)}, f32[3,32,128]{2,1,0:T(8,128)}, u32[]{:S(2)}) copy-start(f32[3,32,128]{2,1,0:T(8,128)} %param.10) | copy-start | bytes 147460
  12.4 4.5 %copy-start.20 = (f32[32,128]{1,0:T(8,128)S(1)}, f32[32,128]{1,0:T(8,128)}, u32[]{:S(2)}) copy-start(f32[32,128]{1,0:T(8,128)} %param.9) | copy-start | bytes 49156
  15.2 46.5 %collective-permute-start.2 = (f32[1,32,32,128]{3,2,1,0:T(8,128)}, f32[1,32,32,128]{3,2,1,0:T(8,128)}, u32[]{:S(2)}, u32[]{:S(2)}) collective-permute-start(f32[1,32,32,128]{3,2,1,0:T(8,128)} %get-tuple-element.14), channel_id=1, source_target_pairs={{0,3},{1,0},{2,1},{3,2},{4,7},{5,4},{6,5},{7,6},{8,11},{9,8},{10,9... | collective-permute-start | bytes 1572872 | tf_op jit(solution)/shard_map/ppermute | solution.py:434
  15.8 44.8 %collective-permute-start.1 = (f32[1,32,32,128]{3,2,1,0:T(8,128)}, f32[1,32,32,128]{3,2,1,0:T(8,128)}, u32[]{:S(2)}, u32[]{:S(2)}) collective-permute-start(f32[1,32,32,128]{3,2,1,0:T(8,128)} %get-tuple-element.15), channel_id=1, source_target_pairs={{0,2},{1,3},{2,0},{3,1},{4,6},{5,7},{6,4},{7,5},{8,10},{9,11},{10,... | collective-permute-start | bytes 1572872 | tf_op jit(solution)/shard_map/ppermute | solution.py:434
  16.7 42.8 %collective-permute-start = (f32[1,32,32,128]{3,2,1,0:T(8,128)}, f32[1,32,32,128]{3,2,1,0:T(8,128)}, u32[]{:S(2)}, u32[]{:S(2)}) collective-permute-start(f32[1,32,32,128]{3,2,1,0:T(8,128)} %get-tuple-element.16), channel_id=1, source_target_pairs={{0,1},{1,2},{2,3},{3,0},{4,5},{5,6},{6,7},{7,4},{8,9},{9,10},{10,1... | collective-permute-start | bytes 1572872 | tf_op jit(solution)/shard_map/ppermute | solution.py:434
  45.1 6.6 %copy-start.14 = (s32[8,16]{1,0:T(8,128)S(1)}, s32[8,16]{1,0:T(8,128)}, u32[]{:S(2)}) copy-start(s32[8,16]{1,0:T(8,128)} %entry_ref.1) | copy-start | bytes 1540
  45.1 6.6 %copy-start.15 = (s32[8]{0:T(128)S(1)}, s32[8]{0:T(128)}, u32[]{:S(2)}) copy-start(s32[8]{0:T(128)} %count_ref.1) | copy-start | bytes 100
  51.7 2.2 copy-start.13
  56.8 2.7 copy-start
  62.8 15.4 %copy-start.2 = (f32[4,32,32,128]{3,2,1,0:T(8,128)}, f32[4,32,32,128]{3,2,1,0:T(8,128)S(1)}, u32[]{:S(2)}) copy-start(f32[4,32,32,128]{3,2,1,0:T(8,128)S(1)} %constant_dynamic-update-slice_fusion.3.current_ref) | copy-start | bytes 6291460
  62.9 15.4 %collective-permute-start.7 = (bf16[1024,128]{1,0:T(8,128)(2,1)S(1)}, bf16[1024,128]{1,0:T(8,128)(2,1)S(1)}, u32[]{:S(2)}, u32[]{:S(2)}) collective-permute-start(bf16[1024,128]{1,0:T(8,128)(2,1)S(1)} %get-tuple-element.20), channel_id=1, source_target_pairs={{4,0},{8,4},{12,8},{16,12},{20,16},{24,20},{28,24},{1,28},{5,1},{9... | collective-permute-start | bytes 786440 | tf_op jit(solution)/shard_map/ppermute | solution.py:177
  64.2 15.1 %collective-permute-start.6 = (bf16[1024,128]{1,0:T(8,128)(2,1)S(1)}, bf16[1024,128]{1,0:T(8,128)(2,1)S(1)}, u32[]{:S(2)}, u32[]{:S(2)}) collective-permute-start(bf16[1024,128]{1,0:T(8,128)(2,1)S(1)} %get-tuple-element.21), channel_id=1, source_target_pairs={{0,4},{4,8},{8,12},{12,16},{16,20},{20,24},{24,28},{28,1},{1,5},{5... | collective-permute-start | bytes 786440 | tf_op jit(solution)/shard_map/ppermute | solution.py:176
  68.7 2.8 copy-start.1
  84.0 62.9 %all-to-all-start.1 = ((f32[32,32,512]{2,1,0:T(8,128)}), f32[32,32,512]{2,1,0:T(8,128)}, u32[]{:S(2)}, u32[]{:S(2)}) async-start(f32[32,32,512]{2,1,0:T(8,128)} %bitcast.15), calls=%async_computation.1 | async-start | bytes 4194304 | tf_op jit(solution)/shard_map/all_to_all | solution.py:498
  91.4 1.6 copy-start.18
  93.2 45.9 %collective-permute-start.5 = (f32[1,32,32,128]{3,2,1,0:T(8,128)S(1)}, f32[1,32,32,128]{3,2,1,0:T(8,128)S(1)}, u32[]{:S(2)}, u32[]{:S(2)}) collective-permute-start(f32[1,32,32,128]{3,2,1,0:T(8,128)S(1)} %get-tuple-element.10), channel_id=1, source_target_pairs={{0,3},{1,0},{2,1},{3,2},{4,7},{5,4},{6,5},{7,6},{8,11},{9,8},{10,9... | collective-permute-start | bytes 1572872 | tf_op jit(solution)/shard_map/ppermute | solution.py:434
  94.7 44.4 %collective-permute-start.4 = (f32[1,32,32,128]{3,2,1,0:T(8,128)S(1)}, f32[1,32,32,128]{3,2,1,0:T(8,128)S(1)}, u32[]{:S(2)}, u32[]{:S(2)}) collective-permute-start(f32[1,32,32,128]{3,2,1,0:T(8,128)S(1)} %get-tuple-element.11), channel_id=1, source_target_pairs={{0,2},{1,3},{2,0},{3,1},{4,6},{5,7},{6,4},{7,5},{8,10},{9,11},{10,... | collective-permute-start | bytes 1572872 | tf_op jit(solution)/shard_map/ppermute | solution.py:434
  95.1 43.5 %collective-permute-start.3 = (f32[1,32,32,128]{3,2,1,0:T(8,128)S(1)}, f32[1,32,32,128]{3,2,1,0:T(8,128)S(1)}, u32[]{:S(2)}, u32[]{:S(2)}) collective-permute-start(f32[1,32,32,128]{3,2,1,0:T(8,128)S(1)} %get-tuple-element.12), channel_id=1, source_target_pairs={{0,1},{1,2},{2,3},{3,0},{4,5},{5,6},{6,7},{7,4},{8,9},{9,10},{10,1... | collective-permute-start | bytes 1572872 | tf_op jit(solution)/shard_map/ppermute | solution.py:434
  95.4 45.1 %copy-start.3 = (f32[4,32,32,128]{3,2,1,0:T(8,128)S(1)}, f32[4,32,32,128]{3,2,1,0:T(8,128)}, u32[]{:S(2)}) copy-start(f32[4,32,32,128]{3,2,1,0:T(8,128)} %copy-done.2) | copy-start | bytes 6291460
  140.6 54.1 %slice-start = ((s8[6291456]{0:T(1024)(128)(4,1)}), s8[2097152]{0:T(1024)(128)(4,1)S(1)}, s32[]{:S(2)}) async-start(s8[6291456]{0:T(1024)(128)(4,1)} %bitcast.30), calls=%async_computation.6 | async-start | bytes 4194304
  146.8 1.6 copy-start.4
  148.4 46.2 %slice-start.1 = ((s8[6291456]{0:T(1024)(128)(4,1)}), s8[4194304]{0:T(1024)(128)(4,1)S(1)}, s32[]{:S(2)}) async-start(s8[6291456]{0:T(1024)(128)(4,1)} %bitcast.30), calls=%async_computation.7 | async-start | bytes 8388608
  158.1 43.3 %copy-start.5 = (f32[4,32,32,128]{3,2,1,0:T(8,128)}, f32[4,32,32,128]{3,2,1,0:T(8,128)S(1)}, u32[]{:S(2)}) copy-start(f32[4,32,32,128]{3,2,1,0:T(8,128)S(1)} %get-tuple-element.8.current_ref) | copy-start | bytes 6291460
  188.7 12.6 %collective-permute-start.9 = (bf16[1024,128]{1,0:T(8,128)(2,1)S(1)}, bf16[1024,128]{1,0:T(8,128)(2,1)S(1)}, u32[]{:S(2)}, u32[]{:S(2)}) collective-permute-start(bf16[1024,128]{1,0:T(8,128)(2,1)S(1)} %get-tuple-element.18), channel_id=1, source_target_pairs={{4,0},{8,4},{12,8},{16,12},{20,16},{24,20},{28,24},{1,28},{5,1},{9... | collective-permute-start | bytes 786440 | tf_op jit(solution)/shard_map/ppermute | solution.py:177
  190.0 13.8 %collective-permute-start.8 = (bf16[1024,128]{1,0:T(8,128)(2,1)S(1)}, bf16[1024,128]{1,0:T(8,128)(2,1)S(1)}, u32[]{:S(2)}, u32[]{:S(2)}) collective-permute-start(bf16[1024,128]{1,0:T(8,128)(2,1)S(1)} %get-tuple-element.19), channel_id=1, source_target_pairs={{0,4},{4,8},{8,12},{12,16},{16,20},{20,24},{24,28},{28,1},{1,5},{5... | collective-permute-start | bytes 786440 | tf_op jit(solution)/shard_map/ppermute | solution.py:176
  206.9 1.4 copy-start.12
  208.2 5.5 %copy-start.6 = (f32[4,32,32,128]{3,2,1,0:T(8,128)S(1)}, f32[4,32,32,128]{3,2,1,0:T(8,128)}, u32[]{:S(2)}) copy-start(f32[4,32,32,128]{3,2,1,0:T(8,128)} %copy-done.5) | copy-start | bytes 6291460
  208.2 54.4 %all-to-all-start.3 = ((f32[32,32,512]{2,1,0:T(8,128)}), f32[32,32,512]{2,1,0:T(8,128)}, u32[]{:S(2)}, u32[]{:S(2)}) async-start(f32[32,32,512]{2,1,0:T(8,128)} %bitcast.35), calls=%async_computation.3 | async-start | bytes 4194304 | tf_op jit(solution)/shard_map/all_to_all | solution.py:498
  262.6 1.6 copy-start.9
  268.0 30.2 %all-to-all-start.5 = ((f32[128,32,128]{2,1,0:T(8,128)}), f32[128,32,128]{2,1,0:T(8,128)}, u32[]{:S(2)}, u32[]{:S(2)}) async-start(f32[128,32,128]{2,1,0:T(8,128)} %bitcast.19), calls=%async_computation.5 | async-start | bytes 4194304 | tf_op jit(solution)/shard_map/all_to_all | solution.py:463
  (5 other events, 6.3 us)

commit v4 on v3

v4 whole, which is shorter than its diff:
```python
import functools
import math

import jax
import jax.numpy as jnp
from jax import lax
from jax.experimental import pallas as pl
from jax.experimental.pallas import tpu as pltpu
from jax.sharding import PartitionSpec as P

RELAXATION = 0.6
MIB = 1 << 20


def sine_table(length):
    counter = jnp.arange(length).astype(jnp.float32) + 1.0
    angle = math.pi * counter[:, None] * counter[None, :] / (length + 1)
    return math.sqrt(2.0 / (length + 1)) * jnp.sin(angle)


def eigen_table(first, second):
    along_first = 2.0 * jnp.cos(
        math.pi * (jnp.arange(first).astype(jnp.float32) + 1.0) / (first + 1)
    )
    along_second = 2.0 * jnp.cos(
        math.pi * (jnp.arange(second).astype(jnp.float32) + 1.0) / (second + 1)
    )
    return 4.0 - along_first[:, None] - along_second[None, :]


def stencil_weights(coef):
    nx, ny = coef.shape
    row = lax.broadcasted_iota(jnp.int32, (nx, ny), 0)
    col = lax.broadcasted_iota(jnp.int32, (nx, ny), 1)
    sides = (
        (pltpu.roll(coef, 1, 0), row == 0),
        (pltpu.roll(coef, nx - 1, 0), row == nx - 1),
        (pltpu.roll(coef, 1, 1), col == 0),
        (pltpu.roll(coef, ny - 1, 1), col == ny - 1),
    )
    centre = 0.0
    weights = []
    for other, outside in sides:
        weight = 0.5 * (coef + jnp.where(outside, coef, other))
        centre = centre + weight
        weights.append(jnp.where(outside, 0.0, weight))
    return [centre] + weights


def weights_kernel(strip_ref, coef_ref, mean_ref, strip_weight_ref, full_ref):
    _, nx, ny = mean_ref.shape
    fields = coef_ref.shape[1] - 1
    height = strip_weight_ref.shape[0] // (5 * fields)
    for which, weight in enumerate(stencil_weights(coef_ref[:, 0].reshape(nx, ny))):
        mean_ref[which] = weight
    for f in range(fields):
        for which, weight in enumerate(stencil_weights(coef_ref[:, f + 1].reshape(nx, ny))):
            full_ref[...] = weight
            for r in range(height):
                at = (f * 5 + which) * height + r
                strip_weight_ref[at : at + 1, :] = full_ref[
                    pl.ds(strip_ref[0] * height + r, 1), :
                ]


def all_weights(moved, strip, coefs, height):
    slab_count, entries, rows, ny = moved.shape
    nx = slab_count * rows
    last = entries // coefs - 1
    fields = coefs - 1
    return pl.pallas_call(
        weights_kernel,
        grid_spec=pltpu.PrefetchScalarGridSpec(
            num_scalar_prefetch=1,
            grid=(1,),
            in_specs=[pl.BlockSpec((slab_count, coefs, rows, ny), lambda i, *_: (0, last, 0, 0))],
            out_specs=[
                pl.BlockSpec((5, nx, ny), lambda i, *_: (0, 0, 0)),
                pl.BlockSpec((fields * 5 * height, ny), lambda i, *_: (0, 0)),
            ],
            scratch_shapes=[pltpu.VMEM((nx, ny), jnp.float32)],
        ),
        out_shape=[
            jax.ShapeDtypeStruct((5, nx, ny), jnp.float32),
            jax.ShapeDtypeStruct((fields * 5 * height, ny), jnp.float32),
        ],
        compiler_params=pltpu.CompilerParams(vmem_limit_bytes=32 * MIB),
    )(strip.reshape(1), moved)


def split(value):
    high = value.astype(jnp.bfloat16)
    low = (value - high.astype(jnp.float32)).astype(jnp.bfloat16)
    return high, low


def split_table(value):
    high = lax.reduce_precision(value, 8, 7)
    return high.astype(jnp.bfloat16), (value - high).astype(jnp.bfloat16)


LOW = 32
FIRST_POWER = 7
SUM_POWER = 5
SOLUTION_POWER = 4


def encode(value, power):
    square = value * value
    if power == 4:
        result = square * (value * jnp.abs(value))
    elif power == 5:
        result = square * square * value
    else:
        result = (square * square) * (square * value)
    return result.astype(jnp.bfloat16)


def decode(code, power):
    code = code.astype(jnp.float32)
    size = jnp.abs(code)
    value = jnp.exp(jnp.log(size) * (1.0 / power))
    value = jnp.where(size > 0.0, value, 0.0)
    return jnp.where(code < 0.0, -value, value)


def code_scales(nx, ny, entries, width):
    guess_max, mean_max, field_max, coupling_max = 6.0, 2.0, 2.5, 0.0625
    gain = 8.0 * field_max * entries * width * coupling_max * 1.01
    inverse = (min(nx, ny) + 1) ** 2 / 8.0

    def bound(iterate):
        return guess_max + (8.0 * mean_max + gain) * iterate

    change = RELAXATION * inverse * 1.01
    second = guess_max + change * bound(guess_max)
    third = second + change * bound(second)

    def scale(limit, power):
        return 0.8 * 2.0 ** (127.0 / power) / limit

    first = math.sqrt(2.0 * ny) * gain * guess_max
    return (
        min(1.0, scale(first, FIRST_POWER)),
        min(1.0, scale(bound(second), SUM_POWER)),
        min(1.0, scale(third, SOLUTION_POWER)),
    )


def pack_kernel(rows, height, x_ref, out_ref):
    strips, modes, cells = out_ref.shape
    cols = cells // height
    for strip in range(strips):
        for r in range(height):
            value = x_ref[pl.ds(strip * height + r, modes, stride=rows), :]
            out_ref[strip, :, r * cols : (r + 1) * cols] = value.astype(jnp.bfloat16)


def pack_strips(block, strips):
    modes, rows, cols = block.shape
    height = rows // strips
    return pl.pallas_call(
        functools.partial(pack_kernel, rows, height),
        out_shape=jax.ShapeDtypeStruct((strips, modes, height * cols), jnp.bfloat16),
        compiler_params=pltpu.CompilerParams(vmem_limit_bytes=32 * MIB),
    )(block.reshape(modes * rows, cols))


def dense_kernel(fields, entry_ref, count_ref, coupling_ref, out_ref):
    block = pl.program_id(0)
    width = coupling_ref.shape[-1]
    out_ref[...] = jnp.zeros_like(out_ref)

    def place(k, carry):
        entry = entry_ref[block, k]
        column = pl.multiple_of((entry // fields) * width, width)
        out_ref[0, entry % fields, :, pl.ds(column, width)] = coupling_ref[0, k]
        return carry

    lax.fori_loop(0, count_ref[block], place, 0)


def dense_coupling(coupling, coupling_list, pair_count, fields):
    blocks, entries, width, _ = coupling.shape
    return pl.pallas_call(
        functools.partial(dense_kernel, fields),
        grid_spec=pltpu.PrefetchScalarGridSpec(
            num_scalar_prefetch=2,
            grid=(blocks,),
            in_specs=[pl.BlockSpec((1, entries, width, width), lambda i, *_: (i, 0, 0, 0))],
            out_specs=pl.BlockSpec(
                (1, fields, width, blocks * width), lambda i, *_: (i, 0, 0, 0)
            ),
        ),
        out_shape=jax.ShapeDtypeStruct((blocks, fields, width, blocks * width), coupling.dtype),
        compiler_params=pltpu.CompilerParams(vmem_limit_bytes=32 * MIB),
    )(coupling_list, pair_count, coupling)


def low_tiles(height, cols):
    return -(-height * LOW // cols)


def along_cols(fields, right_ref):
    size, ny = fields[0].shape
    high, low = split(jnp.concatenate(fields, axis=0))
    both = jnp.dot(
        jnp.concatenate([high, low], axis=1), right_ref[...], preferred_element_type=jnp.float32
    )
    both = both[:, :ny] + both[:, ny:]
    return [both[i * size : (i + 1) * size] for i in range(len(fields))]


def along_rows(wide, left_ref):
    nx = wide.shape[0]
    high, low = split(wide)
    both = jnp.dot(
        left_ref[...], jnp.concatenate([high, low], axis=0), preferred_element_type=jnp.float32
    )
    return both[:nx] + both[nx:]


def weight_row(weight_ref, height, field, which, r):
    at = (field * 5 + which) * height + r
    return weight_ref[at : at + 1, :]


def inner_kernel(height, cols, matrix_ref, state_ref, weight_ref, out_ref, sums_ref):
    fields, width, depth = matrix_ref.shape[1:]
    sums_ref[...] = jnp.dot(
        matrix_ref[0].reshape(fields * width, depth),
        state_ref[...],
        preferred_element_type=jnp.float32,
    )
    for r in range(height):
        total = 0.0
        from_left = 0.0
        from_right = 0.0
        for f in range(fields):

            def row(at):
                return sums_ref[f * width : (f + 1) * width, at * cols : (at + 1) * cols]

            weight = functools.partial(weight_row, weight_ref, height, f)
            here = row(r)
            total = total + weight(0, r) * here
            if r > 0:
                total = total - weight(1, r) * row(r - 1)
            if r < height - 1:
                total = total - weight(2, r) * row(r + 1)
            from_left = from_left + weight(4, r) * here
            from_right = from_right + weight(3, r) * here
        total = total - pltpu.roll(from_left, 1, 1) - pltpu.roll(from_right, cols - 1, 1)
        out_ref[:, r * cols : (r + 1) * cols] = total


def border_kernel(
    height,
    cols,
    first,
    scale,
    matrix_ref,
    above_ref,
    below_ref,
    weight_ref,
    inner_ref,
    right_ref,
    out_ref,
):
    fields, width, depth = matrix_ref.shape[1:]
    matrix = matrix_ref[0].reshape(fields * width, depth)
    border = jnp.concatenate([above_ref[...], below_ref[...]], axis=1)
    sums = jnp.dot(matrix, border, preferred_element_type=jnp.float32)
    rows = []
    for r in range(height):
        total = inner_ref[:, r * cols : (r + 1) * cols]
        for f in range(fields):
            part = sums[f * width : (f + 1) * width]
            if r == 0:
                total = total - weight_row(weight_ref, height, f, 1, r) * part[:, :cols]
            if r == height - 1:
                total = total - weight_row(weight_ref, height, f, 2, r) * part[:, cols:]
        rows.append(total)
    if not first:
        for r in range(height):
            out_ref[:, r * cols : (r + 1) * cols] = encode(rows[r] * scale, SUM_POWER)
        return
    rows = along_cols(rows, right_ref)
    low_col = lax.broadcasted_iota(jnp.int32, (width, cols), 1) < LOW
    for r in range(height):
        value = rows[r] * scale
        code = encode(value, FIRST_POWER)
        out_ref[:, r * cols : (r + 1) * cols] = code
        rest = jnp.where(low_col, value - decode(code, FIRST_POWER), 0.0)
        place = r % (cols // LOW)
        rest = pltpu.roll(rest, place * LOW, 1) if place else rest
        packed = rest if place == 0 else packed + rest
        if place == cols // LOW - 1 or r == height - 1:
            at = (height + r // (cols // LOW)) * cols
            out_ref[:, at : at + cols] = packed.astype(jnp.bfloat16)


def coupled_sums(matrix, state, weights, right, first, scale, both):
    blocks, fields, width, depth = matrix.shape
    cells = state.shape[1]
    height = weights.shape[0] // (5 * fields)
    cols = cells // height
    mode_count = lax.axis_size("mode")
    slab_count = lax.axis_size("slab")
    place = [
        (t % mode_count) * slab_count + t // mode_count for t in range(mode_count * slab_count)
    ]
    onward = list(zip(place[:-1], place[1:]))
    above = lax.ppermute(state[:, -cols:], both, onward)
    below = lax.ppermute(state[:, :cols], both, [(b, a) for a, b in onward])
    matrix_spec = pl.BlockSpec((1, fields, width, depth), lambda i: (i, 0, 0, 0))
    weight_spec = pl.BlockSpec(weights.shape, lambda i: (0, 0))
    sums_spec = pl.BlockSpec((width, cells), lambda i: (i, 0))
    params = pltpu.CompilerParams(vmem_limit_bytes=40 * MIB)
    inner = pl.pallas_call(
        functools.partial(inner_kernel, height, cols),
        grid=(blocks,),
        in_specs=[matrix_spec, pl.BlockSpec((depth, cells), lambda i: (0, 0)), weight_spec],
        out_specs=sums_spec,
        out_shape=jax.ShapeDtypeStruct((blocks * width, cells), jnp.float32),
        scratch_shapes=[pltpu.VMEM((fields * width, cells), jnp.float32)],
        cost_estimate=pl.CostEstimate(
            flops=2 * matrix.size * cells, bytes_accessed=2 * matrix.size, transcendentals=0
        ),
        compiler_params=params,
    )(matrix, state, weights)
    border_spec = pl.BlockSpec((depth, cols), lambda i: (0, 0))
    sent = cells + (low_tiles(height, cols) * cols if first else 0)
    return pl.pallas_call(
        functools.partial(border_kernel, height, cols, first, scale),
        grid=(blocks,),
        in_specs=[
            matrix_spec,
            border_spec,
            border_spec,
            weight_spec,
            sums_spec,
            pl.BlockSpec(right.shape, lambda i: (0, 0)),
        ],
        out_specs=pl.BlockSpec((width, sent), lambda i: (i, 0)),
        out_shape=jax.ShapeDtypeStruct((blocks * width, sent), jnp.bfloat16),
        compiler_params=params,
    )(matrix, above, below, weights, inner, right)


TOGETHER = 4
GROUP = 16


def solve(spectral, right_ref, left_ref, scale_ref):
    ny = spectral[0].shape[1]
    wide = along_rows(jnp.concatenate(spectral, axis=1), left_ref)
    wide = wide * jnp.concatenate([scale_ref[...]] * len(spectral), axis=1)
    wide = along_rows(wide, left_ref)
    return along_cols([wide[:, i * ny : (i + 1) * ny] for i in range(len(spectral))], right_ref)


def mean_kernel(first, current_ref, right_side_ref, weight_ref, right_ref, out_ref):
    nx, ny = weight_ref.shape[1:]

    def several(number, carry):
        values = []
        for i in range(TOGETHER):
            mode = number * TOGETHER + i
            here = current_ref[:, mode].reshape(nx, ny)
            mean = (
                weight_ref[0] * here
                - weight_ref[1] * pltpu.roll(here, 1, 0)
                - weight_ref[2] * pltpu.roll(here, nx - 1, 0)
                - pltpu.roll(weight_ref[4] * here, 1, 1)
                - pltpu.roll(weight_ref[3] * here, ny - 1, 1)
            )
            values.append(right_side_ref[:, mode].reshape(nx, ny) - mean)
        if first:
            values = along_cols(values, right_ref)
        for i in range(TOGETHER):
            out_ref[:, number * TOGETHER + i] = values[i].reshape(out_ref.shape[0], -1, ny)
        return carry

    lax.fori_loop(0, out_ref.shape[1] // TOGETHER, several, 0)


def turn_in(turned_ref, coupled_ref, mode_count, slab_count, height, first, scale):
    group = coupled_ref.shape[1]
    ny = turned_ref.shape[1]
    low_col = lax.broadcasted_iota(jnp.int32, (group, ny), 1) < LOW
    for source in range(mode_count * slab_count):
        start = ((source % slab_count) * mode_count + source // slab_count) * height
        for r in range(height):
            code = coupled_ref[source, :, r * ny : (r + 1) * ny]
            value = decode(code, FIRST_POWER if first else SUM_POWER)
            if first:
                at = (height + r // (ny // LOW)) * ny
                rest = coupled_ref[source, :, at : at + ny].astype(jnp.float32)
                place = r % (ny // LOW)
                rest = pltpu.roll(rest, ny - place * LOW, 1) if place else rest
                value = value + jnp.where(low_col, rest, 0.0)
            turned_ref[(start + r) * group : (start + r + 1) * group, :] = value * (1.0 / scale)


def step_kernel(
    mode_count,
    slab_count,
    code_scale,
    current_ref,
    base_ref,
    coupled_ref,
    right_ref,
    left_ref,
    scale_ref,
    solution_ref,
    state_ref,
    turned_ref,
):
    nx, ny = scale_ref.shape
    group = coupled_ref.shape[1]
    height = nx // (mode_count * slab_count)
    turn_in(turned_ref, coupled_ref, mode_count, slab_count, height, True, code_scale)

    def several(number, carry):
        start = number * TOGETHER
        resid = []
        for i in range(TOGETHER):
            coupled = turned_ref[pl.ds(start + i, nx, stride=group), :]
            resid.append(base_ref[:, start + i].reshape(nx, ny) - coupled)
        change = solve(resid, right_ref, left_ref, scale_ref)
        for i in range(TOGETHER):
            value = current_ref[:, start + i].reshape(nx, ny) + change[i]
            solution_ref[:, start + i] = value.reshape(slab_count, nx // slab_count, ny)
            turned_ref[pl.ds(start + i, nx, stride=group), :] = value
        return carry

    lax.fori_loop(0, group // TOGETHER, several, 0)

    for target in range(mode_count * slab_count):
        start = ((target % slab_count) * mode_count + target // slab_count) * height
        for r in range(height):
            row = start + r
            value = turned_ref[row * group : (row + 1) * group, :].astype(jnp.bfloat16)
            state_ref[target, :, r * ny : (r + 1) * ny] = value


def residual_kernel(
    mode_count, slab_count, code_scale, base_ref, coupled_ref, out_ref, code_ref, turned_ref
):
    group = coupled_ref.shape[1]
    ny = base_ref.shape[-1]
    nx = turned_ref.shape[0] // group
    height = nx // (mode_count * slab_count)
    turn_in(turned_ref, coupled_ref, mode_count, slab_count, height, False, code_scale)

    def one(mode, carry):
        coupled = turned_ref[pl.ds(mode, nx, stride=group), :]
        value = base_ref[:, mode] - coupled.reshape(slab_count, nx // slab_count, ny)
        out_ref[:, mode] = value
        code_ref[:, mode] = encode(value * code_scale, SUM_POWER)
        return carry

    lax.fori_loop(0, group, one, 0)


def correct_kernel(code_scale, current_ref, resid_ref, right_ref, left_ref, scale_ref, out_ref):
    nx, ny = scale_ref.shape

    def several(number, carry):
        start = number * TOGETHER
        resid = [resid_ref[:, start + i].reshape(nx, ny) for i in range(TOGETHER)]
        change = solve(along_cols(resid, right_ref), right_ref, left_ref, scale_ref)
        for i in range(TOGETHER):
            shape = out_ref.shape[:1] + out_ref.shape[2:]
            value = current_ref[:, start + i] + change[i].reshape(shape)
            out_ref[:, start + i] = encode(value * code_scale, SOLUTION_POWER)
        return carry

    lax.fori_loop(0, out_ref.shape[1] // TOGETHER, several, 0)


def whole(array):
    return pl.BlockSpec(array.shape, lambda g: (0,) * array.ndim)


def slabs_of(array):
    slab_count, _, rows, ny = array.shape
    return pl.BlockSpec((slab_count, GROUP, rows, ny), lambda g: (0, g, 0, 0))


def strips_of(shape):
    return pl.BlockSpec((shape[0], GROUP, shape[2]), lambda g: (0, g, 0))


def per_group(kernel, groups, operands, in_specs, out_shape, out_specs, scratch=(), flops=0):
    moved = sum(a.size * a.dtype.itemsize for a in operands)
    return pl.pallas_call(
        kernel,
        grid=(groups,),
        in_specs=in_specs,
        out_specs=out_specs,
        out_shape=out_shape,
        scratch_shapes=scratch,
        cost_estimate=pl.CostEstimate(flops=flops, bytes_accessed=2 * moved, transcendentals=0),
        compiler_params=pltpu.CompilerParams(vmem_limit_bytes=48 * MIB),
    )(*operands)


def mean_part(current, right_side, weights, right, first):
    slabs = slabs_of(right_side)
    return per_group(
        functools.partial(mean_kernel, first),
        right_side.shape[1] // GROUP,
        (current, right_side, weights, right),
        [slabs, slabs, whole(weights), whole(right)],
        jax.ShapeDtypeStruct(right_side.shape, jnp.float32),
        slabs,
    )


def solve_flops(array, tables):
    nx, ny = tables[2].shape
    return array.shape[1] * 8 * 3 * nx * ny * (nx + ny) // 2


def step(current, base, coupled, tables, mode_count, slab_count, code_scale):
    nx, ny = tables[2].shape
    slabs = slabs_of(base)
    devices, modes, _ = coupled.shape
    state = (devices, modes, nx // devices * ny)
    return per_group(
        functools.partial(step_kernel, mode_count, slab_count, code_scale),
        modes // GROUP,
        (current, base, coupled, *tables),
        [slabs, slabs, strips_of(coupled.shape), *map(whole, tables)],
        [
            jax.ShapeDtypeStruct(base.shape, jnp.float32),
            jax.ShapeDtypeStruct(state, jnp.bfloat16),
        ],
        [slabs, strips_of(state)],
        [pltpu.VMEM((nx * GROUP, ny), jnp.float32)],
        solve_flops(base, tables),
    )


def last_residual(base, coupled, mode_count, slab_count, code_scale):
    slab, modes, rows, ny = base.shape
    slabs = slabs_of(base)
    return per_group(
        functools.partial(residual_kernel, mode_count, slab_count, code_scale),
        modes // GROUP,
        (base, coupled),
        [slabs, strips_of(coupled.shape)],
        [
            jax.ShapeDtypeStruct(base.shape, jnp.float32),
            jax.ShapeDtypeStruct(base.shape, jnp.bfloat16),
        ],
        [slabs, slabs],
        [pltpu.VMEM((slab * rows * GROUP, ny), jnp.float32)],
    )


def correct(current, resid, tables, code_scale):
    slabs = slabs_of(resid)
    return per_group(
        functools.partial(correct_kernel, code_scale),
        resid.shape[1] // GROUP,
        (current, resid, *tables),
        [slabs, slabs, *map(whole, tables)],
        jax.ShapeDtypeStruct(resid.shape, jnp.bfloat16),
        slabs,
        (),
        solve_flops(resid, tables),
    )


def regroup(block, axis, same=None):
    count = lax.axis_size(axis)
    here = lax.axis_index(axis)

    def part(target):
        chosen = lax.dynamic_index_in_dim(block, target, 0)
        return chosen if same is None else jnp.concatenate([chosen, same[None]], axis=1)

    own = part(here)
    out = jnp.zeros((count,) + own.shape[1:], own.dtype)
    out = lax.dynamic_update_slice_in_dim(out, own, here, 0)
    for shift in range(1, count):
        target = lax.rem(here + shift, count)
        source = lax.rem(here + count - shift, count)
        moved = lax.ppermute(part(target), axis, [(i, (i + shift) % count) for i in range(count)])
        out = lax.dynamic_update_slice_in_dim(out, moved, source, 0)
    return out


def local(guess, right_side, mean_coef, field_coef, coupling, coupling_list, pair_count):
    mode_count = lax.axis_size("mode")
    slab_count = lax.axis_size("slab")
    both = ("mode", "slab")
    modes, rows, cols = guess.shape
    fields = field_coef.shape[0]
    nx = rows * slab_count
    devices = mode_count * slab_count
    height = nx // devices
    share = modes // slab_count

    strips = pack_strips(guess, mode_count)
    state = lax.all_to_all(strips, "mode", 0, 0, tiled=True)
    state = state.reshape(mode_count * modes, height * cols)

    def to_slabs(block):
        flat = block.reshape(modes, rows, cols)
        return lax.all_to_all(flat, "slab", 0, 0, tiled=True)

    coefs = jnp.concatenate([mean_coef[None], field_coef], 0)
    current = regroup(guess.reshape(slab_count, share, rows, cols), "slab", coefs)
    state, current = lax.optimization_barrier((state, current))
    right_side = regroup(right_side.reshape(slab_count, share, rows, cols), "slab")

    strip = lax.axis_index("slab") * mode_count + lax.axis_index("mode")
    mean_weights, strip_weights = all_weights(current, strip, fields + 1, height)
    matrix = dense_coupling(coupling, coupling_list, pair_count, fields)

    row_high, row_low = split_table(sine_table(nx))
    col_high, col_low = split_table(sine_table(cols))
    tables = (
        jnp.concatenate(
            [
                jnp.concatenate([col_high, col_low], 1),
                jnp.concatenate([col_high, jnp.zeros_like(col_low)], 1),
            ],
            0,
        ),
        jnp.concatenate(
            [
                jnp.concatenate([row_high, row_high], 1),
                jnp.concatenate([row_low, jnp.zeros_like(row_low)], 1),
            ],
            0,
        ),
        RELAXATION / eigen_table(nx, cols),
    )

    first_scale, sum_scale, solution_scale = code_scales(nx, cols, coupling.shape[1], modes)

    def exchanged_sums(state, first, scale):
        sums = coupled_sums(matrix, state, strip_weights, tables[0], first, scale, both)
        sums = lax.all_to_all(sums, both, 0, 0, tiled=True)
        return sums.reshape(devices, share, -1)

    base = mean_part(current, right_side, mean_weights, tables[0], True)
    sums = exchanged_sums(state, True, first_scale)
    current, state = step(current, base, sums, tables, mode_count, slab_count, first_scale)
    state = state.reshape(devices * share, height * cols)
    state = lax.all_to_all(state, both, 0, 0, tiled=True)

    base = mean_part(current, right_side, mean_weights, tables[0], False)
    sums = exchanged_sums(state, False, sum_scale)
    resid, code = last_residual(base, sums, mode_count, slab_count, sum_scale)
    resid_out = decode(to_slabs(code), SUM_POWER) * (1.0 / sum_scale)
    code = correct(current, resid, tables, solution_scale)
    return decode(to_slabs(code), SOLUTION_POWER) * (1.0 / solution_scale), resid_out


def solution(mesh):
    placed = (
        P("mode", "slab", None),
        P("mode", "slab", None),
        P("slab", None),
        P(None, "slab", None),
        P(),
        P(),
        P(),
    )
    return jax.shard_map(
        local,
        mesh=mesh,
        in_specs=placed,
        out_specs=(P("mode", "slab", None), P("mode", "slab", None)),
        check_vma=False,
    )
```

time: 333 us -> 268 us (0.80)
  blocking collectives: 86 us -> 49.2 us
  waiting for transfers between devices: 104 us -> 80.4 us
  local copies, waits for them, and re-layouts: 36.1 us -> 25.2 us
  starting transfers between devices: 40.2 us -> 45 us
    all_gather x1 -> x0, blocking collectives: 26.1 us -> none  [local(): coefs = lax.all_gather(coefs, 'slab', axis=1, tiled=True)]
    all_to_all x2, waiting for transfers between devices: 42.7 us -> 20.8 us  [exchanged_sums(): sums = lax.all_to_all(sums, both, 0, 0, tiled=True)]
    all_to_all x1, blocking collectives: 29.3 us -> 17 us  [to_slabs(): return lax.all_to_all(flat, 'slab', 0, 0, tiled=True)]
    unnamed x48 -> x60, local copies, waits for them, and re-layouts: 24.8 us -> 19.8 us
    mul x0 -> x2, other arithmetic: none -> 4.41 us  [the longest x1 2.21 us: local(): decode(to_slabs(code), SOLUTION_POWER) * (1.0 / solution_scale)]
    all_to_all x1, waiting for transfers between devices: 16 us -> 12.2 us  [to_slabs(): return lax.all_to_all(flat, 'slab', 0, 0, tiled=True)]
    dynamic_slice x3 -> x2, local copies, waits for them, and re-layouts: 3.79 us -> 0.37 us  [part(): chosen = lax.dynamic_index_in_dim(block, target, 0)]
    unnamed x5 -> x2, other arithmetic: 3.42 us -> 0.01 us
  transfers between devices with their start and end apart: 14 -> 14, of which waited for: 6 -> 8; matrix products, arithmetic and copies ran while one was open for 5% -> 4% of each run, Pallas kernels for 10% -> 9%
where the time goes in v4:
time: 268 us; the launch traced here: 267 us
  waiting for transfers between devices  80.4 us (30%)
  Pallas kernels  59 us (22%)
  blocking collectives  49.2 us (18%)
  starting transfers between devices  45 us (17%)
  local copies, waits for them, and re-layouts  25.2 us (9%)
  other arithmetic  7.42 us (3%)
    ppermute x6, waiting for transfers between devices, regroup(): lax.ppermute(part(target), axis, [(i, (i + shift) % count) for i in range...  44.9 us
    all_to_all x1, blocking collectives, local(): state = lax.all_to_all(state, both, 0, 0, tiled=True)  32.2 us
    pallas_call x5, Pallas kernels, per_group(): pl.pallas_call(kernel, grid=(groups,), in_specs=in_specs, out_specs=out_s...  28.2 us
    all_to_all x2, waiting for transfers between devices, exchanged_sums(): sums = lax.all_to_all(sums, both, 0, 0, tiled=True)  20.8 us
    unnamed x60, local copies, waits for them, and re-layouts  19.8 us
    all_to_all x1, blocking collectives, to_slabs(): return lax.all_to_all(flat, 'slab', 0, 0, tiled=True)  17 us
    all_to_all x2, starting transfers between devices, exchanged_sums(): sums = lax.all_to_all(sums, both, 0, 0, tiled=True)  16.2 us
    pallas_call x2, Pallas kernels, coupled_sums(): pl.pallas_call(functools.partial(inner_kernel, height, cols), grid=(block...  13.4 us
  transfers between devices with their start and end apart: 14, of which 8 were waited for; matrix products, arithmetic and copies ran while one was open for 4% of the time, Pallas kernels for 9%

profile of v4, /device:TPU:0, one launch (start us, length us, event | category | flops | bytes accessed | tf_op | source)
XLA Modules:
  0.0 267.3 jit_solution(16945911575198699335)
XLA Ops:
  2.2 2.6 shard_map.86
  4.9 7.3 %all-to-all-start = ((bf16[8,128,512]{2,1,0:T(8,128)(2,1)}), bf16[8,128,512]{2,1,0:T(8,128)(2,1)S(1)}, u32[]{:S(2)}, u32[]{:S(2)}) async-start(bf16[8,128,512]{2,1,0:T(8,128)(2,1)} %shard_map.86), calls=%async_computation | async-start | bytes 2097152 | tf_op jit(solution)/shard_map/all_to_all | solution.py:609
  16.9 2.2 copy-done.9
  19.1 2.8 %shard_map.89.matrix_ref = bf16[8,3,128,1024]{3,2,1,0:T(8,128)(2,1)S(1)} custom-call(s32[8,16]{1,0:T(8,128)S(1)} %copy-done.21, s32[8]{0:T(128)S(1)} %copy-done.22, bf16[8,16,128,128]{3,2,1,0:T(8,128)(2,1)S(1)} %copy-done.9), custom_call_target="tpu_custom_call" | custom-call | tf_op jit(solution)/shard_map/pallas_call | solution.py:185
  21.9 2.6 copy-done
  25.6 3.8 %collective-permute-done = f32[1,36,32,128]{3,2,1,0:T(8,128)} collective-permute-done((f32[1,36,32,128]{3,2,1,0:T(8,128)}, f32[1,36,32,128]{3,2,1,0:T(8,128)}, u32[]{:S(2)}, u32[]{:S(2)}) %collective-permute-start) | collective-permute-done | bytes 589856 | tf_op jit(solution)/shard_map/ppermute | solution.py:592
  33.1 8.5 %collective-permute-done.2 = f32[1,36,32,128]{3,2,1,0:T(8,128)} collective-permute-done((f32[1,36,32,128]{3,2,1,0:T(8,128)}, f32[1,36,32,128]{3,2,1,0:T(8,128)}, u32[]{:S(2)}, u32[]{:S(2)}) %collective-permute-start.2) | collective-permute-done | bytes 589856 | tf_op jit(solution)/shard_map/ppermute | solution.py:592
  41.6 2.1 constant_dynamic-update-slice_fusion.3.coef_ref.current_ref
  45.0 4.6 %collective-permute-start.6 = (bf16[1024,128]{1,0:T(8,128)(2,1)S(1)}, bf16[1024,128]{1,0:T(8,128)(2,1)S(1)}, u32[]{:S(2)}, u32[]{:S(2)}) collective-permute-start(bf16[1024,128]{1,0:T(8,128)(2,1)S(1)} %get-tuple-element.29), channel_id=1, source_target_pairs={{0,4},{4,8},{8,12},{12,16},{16,20},{20,24},{24,28},{28,1},{1,5},{5... | collective-permute-start | bytes 786440 | tf_op jit(solution)/shard_map/ppermute | solution.py:314
  52.3 2.8 %copy-done.1 = bf16[8,3,128,1024]{3,2,1,0:T(8,128)(2,1)S(1)} copy-done((bf16[8,3,128,1024]{3,2,1,0:T(8,128)(2,1)S(1)}, bf16[8,3,128,1024]{3,2,1,0:T(8,128)(2,1)}, u32[]{:S(2)}) %copy-start.1) | copy-done | bytes 6291480
  55.1 6.7 %shard_map.90.inner_ref = f32[1024,512]{1,0:T(8,128)S(1)} custom-call(bf16[8,3,128,1024]{3,2,1,0:T(8,128)(2,1)S(1)} %copy-done.1, bf16[1024,512]{1,0:T(8,128)(2,1)S(1)} %bitcast.20, f32[60,128]{1,0:T(8,128)S(1)} %get-tuple-element.13.weight_ref), custom_call_target="tpu_custom_call" | custom-call | flops 3221225472 | bytes 6291456 | tf_op jit(solution)/shard_map/pallas_call | solution.py:320
  61.8 7.2 %shard_map.91 = bf16[1024,640]{1,0:T(8,128)(2,1)} custom-call(bf16[8,3,128,1024]{3,2,1,0:T(8,128)(2,1)S(1)} %bitcast.14, bf16[1024,128]{1,0:T(8,128)(2,1)S(1)} %collective-permute-done.6.above_ref, bf16[1024,128]{1,0:T(8,128)(2,1)S(1)} %collective-permute-done.7.below_ref, f32[60,128]{1,0:T(8,128)S(1)} %get-tuple-element.13.weight_ref, ...), custom_call_target="tpu_custom_call" | custom-call | tf_op jit(solution)/shard_map/pallas_call | solution.py:334
  69.0 10.8 %all-to-all-start.1 = ((bf16[32,32,640]{2,1,0:T(8,128)(2,1)}), bf16[32,32,640]{2,1,0:T(8,128)(2,1)S(1)}, u32[]{:S(2)}, u32[]{:S(2)}) async-start(bf16[32,32,640]{2,1,0:T(8,128)(2,1)} %bitcast.7), calls=%async_computation.1 | async-start | bytes 2621440 | tf_op jit(solution)/shard_map/all_to_all | solution.py:649
  84.3 21.4 %collective-permute-done.3 = f32[1,32,32,128]{3,2,1,0:T(8,128)S(1)} collective-permute-done((f32[1,32,32,128]{3,2,1,0:T(8,128)S(1)}, f32[1,32,32,128]{3,2,1,0:T(8,128)S(1)}, u32[]{:S(2)}, u32[]{:S(2)}) %collective-permute-start.3) | collective-permute-done | bytes 524320 | tf_op jit(solution)/shard_map/ppermute | solution.py:592
  106.7 10.3 %collective-permute-done.5 = f32[1,32,32,128]{3,2,1,0:T(8,128)S(1)} collective-permute-done((f32[1,32,32,128]{3,2,1,0:T(8,128)S(1)}, f32[1,32,32,128]{3,2,1,0:T(8,128)S(1)}, u32[]{:S(2)}, u32[]{:S(2)}) %collective-permute-start.5) | collective-permute-done | bytes 524320 | tf_op jit(solution)/shard_map/ppermute | solution.py:592
  117.1 4.2 %shard_map.88.base_ref = f32[4,32,32,128]{3,2,1,0:T(8,128)S(1)} custom-call(f32[4,36,32,128]{3,2,1,0:T(8,128)} %constant_dynamic-update-slice_fusion.3.coef_ref.current_ref, f32[4,32,32,128]{3,2,1,0:T(8,128)S(1)} %constant_dynamic-update-slice_fusion.2.right_side_ref, f32[5,128,128]{2,1,0:T(8,128)S(1)} %copy-done.13, ...), custom_call_target="tpu_custom_call" | custom-call | bytes 9830400 | tf_op jit(solution)/shard_map/pallas_call | solution.py:498
  125.8 9.0 %shard_map.92 = (f32[4,32,32,128]{3,2,1,0:T(8,128)S(1)}, bf16[32,32,512]{2,1,0:T(8,128)(2,1)S(1)}) custom-call(f32[4,36,32,128]{3,2,1,0:T(8,128)} %constant_dynamic-update-slice_fusion.3.coef_ref.current_ref, f32[4,32,32,128]{3,2,1,0:T(8,128)} %copy-done.5, bf16[32,32,640]{2,1,0:T(8,128)(2,1)S(1)} %all-to-all-done.1.coupled_ref, ...), custom_call_target="tpu_custom_call" | custom-call | flops 1610612736 | bytes 12189696 | tf_op jit(solution)/shard_map/pallas_call | solution.py:498
  134.7 32.2 %all_to_all.41 = bf16[32,32,512]{2,1,0:T(8,128)(2,1)S(1)} all-to-all(bf16[32,32,512]{2,1,0:T(8,128)(2,1)S(1)} %get-tuple-element.15), channel_id=1, replica_groups=mesh['mode'=8,'slab'=4] {'mode','slab'}, dimensions={0} | all-to-all | bytes 2097152 | tf_op jit(solution)/shard_map/all_to_all | solution.py:656
  168.2 4.6 %collective-permute-start.8 = (bf16[1024,128]{1,0:T(8,128)(2,1)S(1)}, bf16[1024,128]{1,0:T(8,128)(2,1)S(1)}, u32[]{:S(2)}, u32[]{:S(2)}) collective-permute-start(bf16[1024,128]{1,0:T(8,128)(2,1)S(1)} %get-tuple-element.27), channel_id=1, source_target_pairs={{0,4},{4,8},{8,12},{12,16},{16,20},{20,24},{24,28},{28,1},{1,5},{5... | collective-permute-start | bytes 786440 | tf_op jit(solution)/shard_map/ppermute | solution.py:314
  172.8 6.7 %shard_map.94.inner_ref = f32[1024,512]{1,0:T(8,128)S(1)} custom-call(bf16[8,3,128,1024]{3,2,1,0:T(8,128)(2,1)S(1)} %bitcast.16, bf16[1024,512]{1,0:T(8,128)(2,1)S(1)} %bitcast.22, f32[60,128]{1,0:T(8,128)S(1)} %copy-done.20), custom_call_target="tpu_custom_call" | custom-call | flops 3221225472 | bytes 6291456 | tf_op jit(solution)/shard_map/pallas_call | solution.py:320
  179.6 2.5 collective-permute-done.8.above_ref
  182.0 4.6 %shard_map.95 = bf16[1024,512]{1,0:T(8,128)(2,1)} custom-call(bf16[8,3,128,1024]{3,2,1,0:T(8,128)(2,1)S(1)} %bitcast.16, bf16[1024,128]{1,0:T(8,128)(2,1)S(1)} %collective-permute-done.8.above_ref, bf16[1024,128]{1,0:T(8,128)(2,1)S(1)} %collective-permute-done.9.below_ref, f32[60,128]{1,0:T(8,128)S(1)} %copy-done.20, f32[1024,512]{1,0:T(8,128)S(1)} %shard_map.94.inner_ref, ...), custom_call_target="tpu_custom_call" | custom-call | tf_op jit(solution)/shard_map/pallas_call | solution.py:334
  186.6 5.4 %all-to-all-start.3 = ((bf16[32,32,512]{2,1,0:T(8,128)(2,1)}), bf16[32,32,512]{2,1,0:T(8,128)(2,1)S(1)}, u32[]{:S(2)}, u32[]{:S(2)}) async-start(bf16[32,32,512]{2,1,0:T(8,128)(2,1)} %bitcast.9), calls=%async_computation.3 | async-start | bytes 2097152 | tf_op jit(solution)/shard_map/all_to_all | solution.py:649
  193.0 3.1 %shard_map.93.base_ref = f32[4,32,32,128]{3,2,1,0:T(8,128)S(1)} custom-call(f32[4,32,32,128]{3,2,1,0:T(8,128)S(1)} %copy-done.11, f32[4,32,32,128]{3,2,1,0:T(8,128)} %copy-done.4, f32[5,128,128]{2,1,0:T(8,128)S(1)} %copy-done.14, bf16[256,256]{1,0:T(8,128)(2,1)S(1)} %get-tuple-element.31.right_ref), custom_call_target="tpu_custom_call" | custom-call | bytes 9306112 | tf_op jit(solution)/shard_map/pallas_call | solution.py:498
  197.4 20.8 %all-to-all-done.3.coupled_ref = bf16[32,32,512]{2,1,0:T(8,128)(2,1)S(1)} async-done(((bf16[32,32,512]{2,1,0:T(8,128)(2,1)}), bf16[32,32,512]{2,1,0:T(8,128)(2,1)S(1)}, u32[]{:S(2)}, u32[]{:S(2)}) %all-to-all-start.3) | async-done | bytes 1048608 | tf_op jit(solution)/shard_map/all_to_all | solution.py:649
  218.2 4.6 %shard_map.96 = (f32[4,32,32,128]{3,2,1,0:T(8,128)S(1)}, bf16[4,32,32,128]{3,2,1,0:T(8,128)(2,1)}) custom-call(f32[4,32,32,128]{3,2,1,0:T(8,128)} %copy-done.6, bf16[32,32,512]{2,1,0:T(8,128)(2,1)S(1)} %all-to-all-done.3.coupled_ref), custom_call_target="tpu_custom_call" | custom-call | bytes 6291456 | tf_op jit(solution)/shard_map/pallas_call | solution.py:498
  222.8 7.4 %shard_map.97 = bf16[4,32,32,128]{3,2,1,0:T(8,128)(2,1)S(1)} custom-call(f32[4,32,32,128]{3,2,1,0:T(8,128)S(1)} %copy-done.11, f32[4,32,32,128]{3,2,1,0:T(8,128)S(1)} %get-tuple-element.16.resid_ref, bf16[256,256]{1,0:T(8,128)(2,1)S(1)} %get-tuple-element.31.right_ref, bf16[256,256]{1,0:T(8,128)(2,1)S(1)} %copy-done.16, f32[128,128]{1,0:T(8,128)S(1)} %copy-done.18), custom_call_target="tpu_custom_call" | custom-call | flops 1610612736 | bytes 9043968 | tf_op jit(solution)/shard_map/pallas_call | solution.py:498
  230.2 17.0 %all_to_all.42 = bf16[128,32,128]{2,1,0:T(8,128)(2,1)S(1)} all-to-all(bf16[128,32,128]{2,1,0:T(8,128)(2,1)S(1)} %bitcast.23), channel_id=1, replica_groups=mesh['mode'=8,'slab'=4] {'slab'}, dimensions={0} | all-to-all | bytes 2097152 | tf_op jit(solution)/shard_map/all_to_all | solution.py:614
  247.2 3.5 %all-to-all-start.5 = ((bf16[128,32,128]{2,1,0:T(8,128)(2,1)}), bf16[128,32,128]{2,1,0:T(8,128)(2,1)S(1)}, u32[]{:S(2)}, u32[]{:S(2)}) async-start(bf16[128,32,128]{2,1,0:T(8,128)(2,1)} %bitcast.11), calls=%async_computation.5 | async-start | bytes 2097152 | tf_op jit(solution)/shard_map/all_to_all | solution.py:614
  250.7 2.2 fusion.10
  252.9 12.2 %all-to-all-done.5 = bf16[128,32,128]{2,1,0:T(8,128)(2,1)S(1)} async-done(((bf16[128,32,128]{2,1,0:T(8,128)(2,1)}), bf16[128,32,128]{2,1,0:T(8,128)(2,1)S(1)}, u32[]{:S(2)}, u32[]{:S(2)}) %all-to-all-start.5) | async-done | bytes 1048608 | tf_op jit(solution)/shard_map/all_to_all | solution.py:614
  265.1 2.2 fusion.11
  (93 shorter events, 28.5 us)
Async XLA Ops:
  2.2 9.9 %copy-start.24 = (f32[3,32,128]{2,1,0:T(8,128)S(1)}, f32[3,32,128]{2,1,0:T(8,128)}, u32[]{:S(2)}) copy-start(f32[3,32,128]{2,1,0:T(8,128)} %param.10) | copy-start | bytes 147460
  2.2 9.9 %copy-start.25 = (f32[32,128]{1,0:T(8,128)S(1)}, f32[32,128]{1,0:T(8,128)}, u32[]{:S(2)}) copy-start(f32[32,128]{1,0:T(8,128)} %param.9) | copy-start | bytes 49156
  2.2 10.0 %copy-start.8 = (f32[128,32,128]{2,1,0:T(8,128)S(1)}, f32[128,32,128]{2,1,0:T(8,128)}, u32[]{:S(2)}) copy-start(f32[128,32,128]{2,1,0:T(8,128)} %param.7) | copy-start | bytes 6291460
  4.9 38.8 %all-to-all-start = ((bf16[8,128,512]{2,1,0:T(8,128)(2,1)}), bf16[8,128,512]{2,1,0:T(8,128)(2,1)S(1)}, u32[]{:S(2)}, u32[]{:S(2)}) async-start(bf16[8,128,512]{2,1,0:T(8,128)(2,1)} %shard_map.86), calls=%async_computation | async-start | bytes 2097152 | tf_op jit(solution)/shard_map/all_to_all | solution.py:609
  12.7 4.2 %copy-start.21 = (s32[8,16]{1,0:T(8,128)S(1)}, s32[8,16]{1,0:T(8,128)}, u32[]{:S(2)}) copy-start(s32[8,16]{1,0:T(8,128)} %entry_ref.1) | copy-start | bytes 1540
  12.7 4.2 %copy-start.22 = (s32[8]{0:T(128)S(1)}, s32[8]{0:T(128)}, u32[]{:S(2)}) copy-start(s32[8]{0:T(128)} %count_ref.1) | copy-start | bytes 100
  14.0 15.4 %collective-permute-start = (f32[1,36,32,128]{3,2,1,0:T(8,128)}, f32[1,36,32,128]{3,2,1,0:T(8,128)}, u32[]{:S(2)}, u32[]{:S(2)}) collective-permute-start(f32[1,36,32,128]{3,2,1,0:T(8,128)} %get-tuple-element.33), channel_id=1, source_target_pairs={{0,1},{1,2},{2,3},{3,0},{4,5},{5,6},{6,7},{7,4},{8,9},{9,10},{10,1... | collective-permute-start | bytes 1769480 | tf_op jit(solution)/shard_map/ppermute | solution.py:592
  14.0 16.5 %collective-permute-start.1 = (f32[1,36,32,128]{3,2,1,0:T(8,128)}, f32[1,36,32,128]{3,2,1,0:T(8,128)}, u32[]{:S(2)}, u32[]{:S(2)}) collective-permute-start(f32[1,36,32,128]{3,2,1,0:T(8,128)} %get-tuple-element.34), channel_id=1, source_target_pairs={{0,2},{1,3},{2,0},{3,1},{4,6},{5,7},{6,4},{7,5},{8,10},{9,11},{10,... | collective-permute-start | bytes 1769480 | tf_op jit(solution)/shard_map/ppermute | solution.py:592
  15.5 26.1 %collective-permute-start.2 = (f32[1,36,32,128]{3,2,1,0:T(8,128)}, f32[1,36,32,128]{3,2,1,0:T(8,128)}, u32[]{:S(2)}, u32[]{:S(2)}) collective-permute-start(f32[1,36,32,128]{3,2,1,0:T(8,128)} %get-tuple-element.32), channel_id=1, source_target_pairs={{0,3},{1,0},{2,1},{3,2},{4,7},{5,4},{6,5},{7,6},{8,11},{9,8},{10,9... | collective-permute-start | bytes 1769480 | tf_op jit(solution)/shard_map/ppermute | solution.py:592
  41.5 20.2 %slice-start = ((s8[6291456]{0:T(1024)(128)(4,1)}), s8[2097152]{0:T(1024)(128)(4,1)S(1)}, s32[]{:S(2)}) async-start(s8[6291456]{0:T(1024)(128)(4,1)} %bitcast.13), calls=%async_computation.6 | async-start | bytes 4194304
  43.7 18.1 %collective-permute-start.7 = (bf16[1024,128]{1,0:T(8,128)(2,1)S(1)}, bf16[1024,128]{1,0:T(8,128)(2,1)S(1)}, u32[]{:S(2)}, u32[]{:S(2)}) collective-permute-start(bf16[1024,128]{1,0:T(8,128)(2,1)S(1)} %get-tuple-element.28), channel_id=1, source_target_pairs={{4,0},{8,4},{12,8},{16,12},{20,16},{24,20},{28,24},{1,28},{5,1},{9... | collective-permute-start | bytes 786440 | tf_op jit(solution)/shard_map/ppermute | solution.py:315
  45.0 16.8 %collective-permute-start.6 = (bf16[1024,128]{1,0:T(8,128)(2,1)S(1)}, bf16[1024,128]{1,0:T(8,128)(2,1)S(1)}, u32[]{:S(2)}, u32[]{:S(2)}) collective-permute-start(bf16[1024,128]{1,0:T(8,128)(2,1)S(1)} %get-tuple-element.29), channel_id=1, source_target_pairs={{0,4},{4,8},{8,12},{12,16},{16,20},{20,24},{24,28},{28,1},{1,5},{5... | collective-permute-start | bytes 786440 | tf_op jit(solution)/shard_map/ppermute | solution.py:314
  52.3 9.5 %copy-start.19 = (f32[60,128]{1,0:T(8,128)}, f32[60,128]{1,0:T(8,128)S(1)}, u32[]{:S(2)}) copy-start(f32[60,128]{1,0:T(8,128)S(1)} %get-tuple-element.13.weight_ref) | copy-start | bytes 92164
  52.3 2.8 %copy-start.1 = (bf16[8,3,128,1024]{3,2,1,0:T(8,128)(2,1)S(1)}, bf16[8,3,128,1024]{3,2,1,0:T(8,128)(2,1)}, u32[]{:S(2)}) copy-start(bf16[8,3,128,1024]{3,2,1,0:T(8,128)(2,1)} %copy-done) | copy-start | bytes 18874372
  55.1 6.7 %slice-start.1 = ((s8[6291456]{0:T(1024)(128)(4,1)}), s8[4194304]{0:T(1024)(128)(4,1)S(1)}, s32[]{:S(2)}) async-start(s8[6291456]{0:T(1024)(128)(4,1)} %bitcast.13), calls=%async_computation.7 | async-start | bytes 8388608
  69.0 11.1 %copy-start.23 = (f32[128,32,128]{2,1,0:T(8,128)S(1)}, f32[128,32,128]{2,1,0:T(8,128)}, u32[]{:S(2)}) copy-start(f32[128,32,128]{2,1,0:T(8,128)} %param.8) | copy-start | bytes 6291460
  69.0 55.0 %all-to-all-start.1 = ((bf16[32,32,640]{2,1,0:T(8,128)(2,1)}), bf16[32,32,640]{2,1,0:T(8,128)(2,1)S(1)}, u32[]{:S(2)}, u32[]{:S(2)}) async-start(bf16[32,32,640]{2,1,0:T(8,128)(2,1)} %bitcast.7), calls=%async_computation.1 | async-start | bytes 2621440 | tf_op jit(solution)/shard_map/all_to_all | solution.py:649
  80.3 36.8 %copy-start.13 = (f32[5,128,128]{2,1,0:T(8,128)S(1)}, f32[5,128,128]{2,1,0:T(8,128)}, u32[]{:S(2)}) copy-start(f32[5,128,128]{2,1,0:T(8,128)} %copy-done.12) | copy-start | bytes 983044
  80.3 25.4 %collective-permute-start.3 = (f32[1,32,32,128]{3,2,1,0:T(8,128)S(1)}, f32[1,32,32,128]{3,2,1,0:T(8,128)S(1)}, u32[]{:S(2)}, u32[]{:S(2)}) collective-permute-start(f32[1,32,32,128]{3,2,1,0:T(8,128)S(1)} %get-tuple-element.20), channel_id=1, source_target_pairs={{0,1},{1,2},{2,3},{3,0},{4,5},{5,6},{6,7},{7,4},{8,9},{9,10},{10,1... | collective-permute-start | bytes 1572872 | tf_op jit(solution)/shard_map/ppermute | solution.py:592
  80.6 26.1 %collective-permute-start.4 = (f32[1,32,32,128]{3,2,1,0:T(8,128)S(1)}, f32[1,32,32,128]{3,2,1,0:T(8,128)S(1)}, u32[]{:S(2)}, u32[]{:S(2)}) collective-permute-start(f32[1,32,32,128]{3,2,1,0:T(8,128)S(1)} %get-tuple-element.19), channel_id=1, source_target_pairs={{0,2},{1,3},{2,0},{3,1},{4,6},{5,7},{6,4},{7,5},{8,10},{9,11},{10,... | collective-permute-start | bytes 1572872 | tf_op jit(solution)/shard_map/ppermute | solution.py:592
  82.3 34.8 %collective-permute-start.5 = (f32[1,32,32,128]{3,2,1,0:T(8,128)S(1)}, f32[1,32,32,128]{3,2,1,0:T(8,128)S(1)}, u32[]{:S(2)}, u32[]{:S(2)}) collective-permute-start(f32[1,32,32,128]{3,2,1,0:T(8,128)S(1)} %get-tuple-element.18), channel_id=1, source_target_pairs={{0,3},{1,0},{2,1},{3,2},{4,7},{5,4},{6,5},{7,6},{8,11},{9,8},{10,9... | collective-permute-start | bytes 1572872 | tf_op jit(solution)/shard_map/ppermute | solution.py:592
  117.1 55.7 %slice-start.2 = ((s8[6291456]{0:T(1024)(128)(4,1)}), s8[2097152]{0:T(1024)(128)(4,1)S(1)}, s32[]{:S(2)}) async-start(s8[6291456]{0:T(1024)(128)(4,1)} %bitcast.15), calls=%async_computation.8 | async-start | bytes 4194304
  125.8 47.1 %slice-start.3 = ((s8[6291456]{0:T(1024)(128)(4,1)}), s8[4194304]{0:T(1024)(128)(4,1)S(1)}, s32[]{:S(2)}) async-start(s8[6291456]{0:T(1024)(128)(4,1)} %bitcast.15), calls=%async_computation.9 | async-start | bytes 8388608
  134.7 44.8 %copy-start.10 = (f32[4,32,32,128]{3,2,1,0:T(8,128)}, f32[4,32,32,128]{3,2,1,0:T(8,128)S(1)}, u32[]{:S(2)}) copy-start(f32[4,32,32,128]{3,2,1,0:T(8,128)S(1)} %get-tuple-element.14.current_ref) | copy-start | bytes 6291460
  134.7 38.1 %copy-start.20 = (f32[60,128]{1,0:T(8,128)S(1)}, f32[60,128]{1,0:T(8,128)}, u32[]{:S(2)}) copy-start(f32[60,128]{1,0:T(8,128)} %copy-done.19) | copy-start | bytes 92164
  166.9 12.6 %collective-permute-start.9 = (bf16[1024,128]{1,0:T(8,128)(2,1)S(1)}, bf16[1024,128]{1,0:T(8,128)(2,1)S(1)}, u32[]{:S(2)}, u32[]{:S(2)}) collective-permute-start(bf16[1024,128]{1,0:T(8,128)(2,1)S(1)} %get-tuple-element.26), channel_id=1, source_target_pairs={{4,0},{8,4},{12,8},{16,12},{20,16},{24,20},{28,24},{1,28},{5,1},{9... | collective-permute-start | bytes 786440 | tf_op jit(solution)/shard_map/ppermute | solution.py:315
  168.2 13.8 %collective-permute-start.8 = (bf16[1024,128]{1,0:T(8,128)(2,1)S(1)}, bf16[1024,128]{1,0:T(8,128)(2,1)S(1)}, u32[]{:S(2)}, u32[]{:S(2)}) collective-permute-start(bf16[1024,128]{1,0:T(8,128)(2,1)S(1)} %get-tuple-element.27), channel_id=1, source_target_pairs={{0,4},{4,8},{8,12},{12,16},{16,20},{20,24},{24,28},{28,1},{1,5},{5... | collective-permute-start | bytes 786440 | tf_op jit(solution)/shard_map/ppermute | solution.py:314
  186.6 5.4 %copy-start.11 = (f32[4,32,32,128]{3,2,1,0:T(8,128)S(1)}, f32[4,32,32,128]{3,2,1,0:T(8,128)}, u32[]{:S(2)}) copy-start(f32[4,32,32,128]{3,2,1,0:T(8,128)} %copy-done.10) | copy-start | bytes 6291460
  186.6 31.6 %all-to-all-start.3 = ((bf16[32,32,512]{2,1,0:T(8,128)(2,1)}), bf16[32,32,512]{2,1,0:T(8,128)(2,1)S(1)}, u32[]{:S(2)}, u32[]{:S(2)}) async-start(bf16[32,32,512]{2,1,0:T(8,128)(2,1)} %bitcast.9), calls=%async_computation.3 | async-start | bytes 2097152 | tf_op jit(solution)/shard_map/all_to_all | solution.py:649
  197.4 25.4 %copy-start.16 = (bf16[256,256]{1,0:T(8,128)(2,1)S(1)}, bf16[256,256]{1,0:T(8,128)(2,1)}, u32[]{:S(2)}) copy-start(bf16[256,256]{1,0:T(8,128)(2,1)} %get-tuple-element.30.left_ref) | copy-start | bytes 393220
  197.4 25.4 %copy-start.18 = (f32[128,128]{1,0:T(8,128)S(1)}, f32[128,128]{1,0:T(8,128)}, u32[]{:S(2)}) copy-start(f32[128,128]{1,0:T(8,128)} %subtract_divide_fusion.scale_ref) | copy-start | bytes 196612
  247.2 18.0 %all-to-all-start.5 = ((bf16[128,32,128]{2,1,0:T(8,128)(2,1)}), bf16[128,32,128]{2,1,0:T(8,128)(2,1)S(1)}, u32[]{:S(2)}, u32[]{:S(2)}) async-start(bf16[128,32,128]{2,1,0:T(8,128)(2,1)} %bitcast.11), calls=%async_computation.5 | async-start | bytes 2097152 | tf_op jit(solution)/shard_map/all_to_all | solution.py:614
  (12 other events, 17.0 us)

commit v5 on v4

--- a/solution.py
+++ b/solution.py
@@ -63,17 +63,16 @@
                 ]
 
 
-def all_weights(moved, strip, coefs, height):
-    slab_count, entries, rows, ny = moved.shape
+def all_weights(coefs, strip, height):
+    slab_count, entries, rows, ny = coefs.shape
     nx = slab_count * rows
-    last = entries // coefs - 1
-    fields = coefs - 1
+    fields = entries - 1
     return pl.pallas_call(
         weights_kernel,
         grid_spec=pltpu.PrefetchScalarGridSpec(
             num_scalar_prefetch=1,
             grid=(1,),
-            in_specs=[pl.BlockSpec((slab_count, coefs, rows, ny), lambda i, *_: (0, last, 0, 0))],
+            in_specs=[pl.BlockSpec(coefs.shape, lambda i, *_: (0, 0, 0, 0))],
             out_specs=[
                 pl.BlockSpec((5, nx, ny), lambda i, *_: (0, 0, 0)),
                 pl.BlockSpec((fields * 5 * height, ny), lambda i, *_: (0, 0)),
@@ -85,7 +84,7 @@
             jax.ShapeDtypeStruct((fields * 5 * height, ny), jnp.float32),
         ],
         compiler_params=pltpu.CompilerParams(vmem_limit_bytes=32 * MIB),
-    )(strip.reshape(1), moved)
+    )(strip.reshape(1), coefs)
 
 
 def split(value):
@@ -310,7 +309,7 @@
     place = [
         (t % mode_count) * slab_count + t // mode_count for t in range(mode_count * slab_count)
     ]
-    onward = list(zip(place[:-1], place[1:]))
+    onward = list(zip(place, place[1:] + place[:1]))
     above = lax.ppermute(state[:, -cols:], both, onward)
     below = lax.ppermute(state[:, :cols], both, [(b, a) for a, b in onward])
     matrix_spec = pl.BlockSpec((1, fields, width, depth), lambda i: (i, 0, 0, 0))
@@ -348,7 +347,7 @@
     )(matrix, above, below, weights, inner, right)
 
 
-TOGETHER = 4
+TOGETHER = 8
 GROUP = 16
 
 
@@ -575,23 +574,34 @@
     )
 
 
-def regroup(block, axis, same=None):
+def collect(parts, axis):
     count = lax.axis_size(axis)
     here = lax.axis_index(axis)
-
-    def part(target):
-        chosen = lax.dynamic_index_in_dim(block, target, 0)
-        return chosen if same is None else jnp.concatenate([chosen, same[None]], axis=1)
-
-    own = part(here)
-    out = jnp.zeros((count,) + own.shape[1:], own.dtype)
-    out = lax.dynamic_update_slice_in_dim(out, own, here, 0)
+    out = jnp.zeros((count,) + parts[0].shape[1:], parts[0].dtype)
+    for shift, part in enumerate(parts):
+        source = lax.rem(here + count - shift, count)
+        out = lax.dynamic_update_slice_in_dim(out, part, source, 0)
+    return out
+
+
+def onwards(part, axis, shift):
+    count = lax.axis_size(axis)
+    return lax.ppermute(part, axis, [(i, (i + shift) % count) for i in range(count)])
+
+
+def regroup(block, axis):
+    count = lax.axis_size(axis)
+    here = lax.axis_index(axis)
+    parts = [lax.dynamic_index_in_dim(block, here, 0)]
     for shift in range(1, count):
         target = lax.rem(here + shift, count)
-        source = lax.rem(here + count - shift, count)
-        moved = lax.ppermute(part(target), axis, [(i, (i + shift) % count) for i in range(count)])
-        out = lax.dynamic_update_slice_in_dim(out, moved, source, 0)
-    return out
+        parts.append(onwards(lax.dynamic_index_in_dim(block, target, 0), axis, shift))
+    return collect(parts, axis)
+
+
+def spread(block, axis):
+    count = lax.axis_size(axis)
+    return collect([block[None]] + [onwards(block[None], axis, i) for i in range(1, count)], axis)
 
 
 def local(guess, right_side, mean_coef, field_coef, coupling, coupling_list, pair_count):
@@ -614,12 +624,12 @@
         return lax.all_to_all(flat, "slab", 0, 0, tiled=True)
 
     coefs = jnp.concatenate([mean_coef[None], field_coef], 0)
-    current = regroup(guess.reshape(slab_count, share, rows, cols), "slab", coefs)
-    state, current = lax.optimization_barrier((state, current))
+    coefs = spread(coefs, "slab")
+    current = regroup(guess.reshape(slab_count, share, rows, cols), "slab")
     right_side = regroup(right_side.reshape(slab_count, share, rows, cols), "slab")
 
     strip = lax.axis_index("slab") * mode_count + lax.axis_index("mode")
-    mean_weights, strip_weights = all_weights(current, strip, fields + 1, height)
+    mean_weights, strip_weights = all_weights(coefs, strip, height)
     matrix = dense_coupling(coupling, coupling_list, pair_count, fields)
 
     row_high, row_low = split_table(sine_table(nx))
@@ -644,22 +654,22 @@
 
     first_scale, sum_scale, solution_scale = code_scales(nx, cols, coupling.shape[1], modes)
 
-    def exchanged_sums(state, first, scale):
-        sums = coupled_sums(matrix, state, strip_weights, tables[0], first, scale, both)
-        sums = lax.all_to_all(sums, both, 0, 0, tiled=True)
-        return sums.reshape(devices, share, -1)
-
+    sums = coupled_sums(matrix, state, strip_weights, tables[0], True, first_scale, both)
+    sums, current, right_side = lax.optimization_barrier((sums, current, right_side))
+    sums = lax.all_to_all(sums, both, 0, 0, tiled=True).reshape(devices, share, -1)
     base = mean_part(current, right_side, mean_weights, tables[0], True)
-    sums = exchanged_sums(state, True, first_scale)
     current, state = step(current, base, sums, tables, mode_count, slab_count, first_scale)
     state = state.reshape(devices * share, height * cols)
     state = lax.all_to_all(state, both, 0, 0, tiled=True)
 
     base = mean_part(current, right_side, mean_weights, tables[0], False)
-    sums = exchanged_sums(state, False, sum_scale)
+    sums = coupled_sums(matrix, state, strip_weights, tables[0], False, sum_scale, both)
+    sums = lax.all_to_all(sums, both, 0, 0, tiled=True).reshape(devices, share, -1)
     resid, code = last_residual(base, sums, mode_count, slab_count, sum_scale)
-    resid_out = decode(to_slabs(code), SUM_POWER) * (1.0 / sum_scale)
+    moved = to_slabs(code)
     code = correct(current, resid, tables, solution_scale)
+    code, moved = lax.optimization_barrier((code, moved))
+    resid_out = decode(moved, SUM_POWER) * (1.0 / sum_scale)
     return decode(to_slabs(code), SOLUTION_POWER) * (1.0 / solution_scale), resid_out
 
 

time: 268 us -> 257 us (0.959)
  blocking collectives: 49.2 us -> 29.6 us
  waiting for transfers between devices: 80.4 us -> 94.8 us
  starting transfers between devices: 45 us -> 38.6 us
  local copies, waits for them, and re-layouts: 25.2 us -> 31.1 us
  Pallas kernels: 59 us -> 54.1 us
    all_to_all x2, waiting for transfers between devices: 20.8 us -> 46 us  [local(): lax.all_to_all(sums, both, 0, 0, tiled=True).reshape(devices, share, -1)]
    ppermute x6 -> x9, waiting for transfers between devices: 44.9 us -> 24 us  [onwards(): lax.ppermute(part, axis, [(i, (i + shift) % count) for i in range(count)])]
    all_to_all x1 -> x0, blocking collectives: 17 us -> none  [to_slabs(): return lax.all_to_all(flat, 'slab', 0, 0, tiled=True)]
    ppermute x2, starting transfers between devices: 9.12 us -> 0.01 us  [coupled_sums(): above = lax.ppermute(state[:, -cols:], both, onward)]
    all_to_all x2, starting transfers between devices: 16.2 us -> 7.32 us  [local(): lax.all_to_all(sums, both, 0, 0, tiled=True).reshape(devices, share, -1)]
    ppermute x2, starting transfers between devices: 2.58 us -> 8.82 us  [coupled_sums(): below = lax.ppermute(state[:, :cols], both, [(b, a) for a, b in onward])]
    all_to_all x1 -> x2, waiting for transfers between devices: 12.2 us -> 18.4 us  [to_slabs(): return lax.all_to_all(flat, 'slab', 0, 0, tiled=True)]
    pallas_call x5, Pallas kernels: 28.2 us -> 23.4 us  [per_group(): pl.pallas_call(kernel, grid=(groups,), in_specs=in_specs, out_specs=out_s...]
  transfers between devices with their start and end apart: 14 -> 18, of which waited for: 8 -> 11; matrix products, arithmetic and copies ran while one was open for 4% -> 7% of each run, Pallas kernels for 9% -> 12%
where the time goes in v5:
time: 257 us; the launch traced here: 256 us
  waiting for transfers between devices  94.8 us (37%)
  Pallas kernels  54.1 us (21%)
  starting transfers between devices  38.6 us (15%)
  local copies, waits for them, and re-layouts  31.1 us (12%)
  blocking collectives  29.6 us (12%)
  other arithmetic  6.93 us (3%)
    all_to_all x2, waiting for transfers between devices, local(): lax.all_to_all(sums, both, 0, 0, tiled=True).reshape(devices, share, -1)  46 us
    all_to_all x1, blocking collectives, local(): state = lax.all_to_all(state, both, 0, 0, tiled=True)  29.6 us
    ppermute x9, waiting for transfers between devices, onwards(): lax.ppermute(part, axis, [(i, (i + shift) % count) for i in range(count)])  24 us
    pallas_call x5, Pallas kernels, per_group(): pl.pallas_call(kernel, grid=(groups,), in_specs=in_specs, out_specs=out_s...  23.4 us
    all_to_all x2, waiting for transfers between devices, to_slabs(): return lax.all_to_all(flat, 'slab', 0, 0, tiled=True)  18.4 us
    unnamed x50, local copies, waits for them, and re-layouts  18.3 us
    pallas_call x2, Pallas kernels, coupled_sums(): pl.pallas_call(functools.partial(inner_kernel, height, cols), grid=(block...  13.4 us
    pallas_call x2, Pallas kernels, coupled_sums(): pl.pallas_call(functools.partial(border_kernel, height, cols, first, scal...  11.7 us
  transfers between devices with their start and end apart: 18, of which 11 were waited for; matrix products, arithmetic and copies ran while one was open for 7% of the time, Pallas kernels for 12%

profile of v5, /device:TPU:0, one launch (start us, length us, event | category | flops | bytes accessed | tf_op | source)
XLA Modules:
  0.0 256.2 jit_solution(7798967963227726444)
XLA Ops:
  1.4 2.9 %collective-permute-start.3 = (f32[1,4,32,128]{3,2,1,0:T(8,128)S(1)}, f32[1,4,32,128]{3,2,1,0:T(8,128)}, u32[]{:S(2)}, u32[]{:S(2)}) collective-permute-start(f32[1,4,32,128]{3,2,1,0:T(8,128)S(1)} %maximum_bitcast_fusion), channel_id=1, source_target_pairs={{0,2},{1,3},{2,0},{3,1},{4,6},{5,7},{6,4},{7,5},{8,10},{9,11},{10,... | collective-permute-start | bytes 196616 | tf_op jit(solution)/shard_map/ppermute | solution.py:589
  7.7 2.6 %shard_map.87 = bf16[8,128,512]{2,1,0:T(8,128)(2,1)} custom-call(f32[4096,128]{1,0:T(8,128)S(1)} %bitcast.20), custom_call_target="tpu_custom_call" | custom-call | tf_op jit(solution)/shard_map/pallas_call | solution.py:161
  10.4 5.8 %all-to-all-start = ((bf16[8,128,512]{2,1,0:T(8,128)(2,1)}), bf16[8,128,512]{2,1,0:T(8,128)(2,1)S(1)}, u32[]{:S(2)}, u32[]{:S(2)}) async-start(bf16[8,128,512]{2,1,0:T(8,128)(2,1)} %shard_map.87), calls=%async_computation | async-start | bytes 2097152 | tf_op jit(solution)/shard_map/all_to_all | solution.py:619
  16.5 2.7 %constant_dynamic-slice_fusion.2 = (f32[1,32,32,128]{3,2,1,0:T(8,128)}, f32[1,32,32,128]{3,2,1,0:T(8,128)}, f32[1,32,32,128]{3,2,1,0:T(8,128)}, f32[4,32,32,128]{3,2,1,0:T(8,128)S(1)}) fusion(f32[4,32,32,128]{3,2,1,0:T(8,128)} %bitcast.19, s32[]{:T(128)S(6)} %select_n.46, s32[]{:T(128)S(6)} %select_n.47, s32[]{:T(128)S(6)} %select_n.48, ...), kind=kLoop, calls=%fused_computation.39 | loop fusion | bytes 4194324 | tf_op jit(solution)/shard_map/jit(dynamic_index_in_dim)/dynamic_slice | solution.py:598
  21.9 2.6 %shard_map.86.matrix_ref = bf16[8,3,128,1024]{3,2,1,0:T(8,128)(2,1)S(1)} custom-call(s32[8,16]{1,0:T(8,128)S(1)} %copy-done.13, s32[8]{0:T(128)S(1)} %copy-done.14, bf16[8,16,128,128]{3,2,1,0:T(8,128)(2,1)S(1)} %copy-done.6), custom_call_target="tpu_custom_call" | custom-call | tf_op jit(solution)/shard_map/pallas_call | solution.py:184
  35.4 5.4 %collective-permute-done.5 = f32[1,32,32,128]{3,2,1,0:T(8,128)} collective-permute-done((f32[1,32,32,128]{3,2,1,0:T(8,128)}, f32[1,32,32,128]{3,2,1,0:T(8,128)}, u32[]{:S(2)}, u32[]{:S(2)}) %collective-permute-start.5) | collective-permute-done | bytes 524320 | tf_op jit(solution)/shard_map/ppermute | solution.py:589
  44.9 7.0 %collective-permute-done.8 = f32[1,32,32,128]{3,2,1,0:T(8,128)S(1)} collective-permute-done((f32[1,32,32,128]{3,2,1,0:T(8,128)S(1)}, f32[1,32,32,128]{3,2,1,0:T(8,128)S(1)}, u32[]{:S(2)}, u32[]{:S(2)}) %collective-permute-start.8) | collective-permute-done | bytes 524320 | tf_op jit(solution)/shard_map/ppermute | solution.py:589
  52.7 4.0 %collective-permute-done.9 = f32[1,32,32,128]{3,2,1,0:T(8,128)S(1)} collective-permute-done((f32[1,32,32,128]{3,2,1,0:T(8,128)S(1)}, f32[1,32,32,128]{3,2,1,0:T(8,128)S(1)}, u32[]{:S(2)}, u32[]{:S(2)}) %collective-permute-start.9) | collective-permute-done | bytes 524320 | tf_op jit(solution)/shard_map/ppermute | solution.py:589
  57.6 7.0 %collective-permute-done.10 = f32[1,32,32,128]{3,2,1,0:T(8,128)S(1)} collective-permute-done((f32[1,32,32,128]{3,2,1,0:T(8,128)S(1)}, f32[1,32,32,128]{3,2,1,0:T(8,128)S(1)}, u32[]{:S(2)}, u32[]{:S(2)}) %collective-permute-start.10) | collective-permute-done | bytes 524320 | tf_op jit(solution)/shard_map/ppermute | solution.py:589
  65.4 5.8 %collective-permute-start.1 = (bf16[1024,128]{1,0:T(8,128)(2,1)S(1)}, bf16[1024,128]{1,0:T(8,128)(2,1)S(1)}, u32[]{:S(2)}, u32[]{:S(2)}) collective-permute-start(bf16[1024,128]{1,0:T(8,128)(2,1)S(1)} %get-tuple-element.34), channel_id=1, source_target_pairs={{4,0},{8,4},{12,8},{16,12},{20,16},{24,20},{28,24},{1,28},{5,1},{9... | collective-permute-start | bytes 786440 | tf_op jit(solution)/shard_map/ppermute | solution.py:314
  71.3 2.8 %copy-done.1 = bf16[8,3,128,1024]{3,2,1,0:T(8,128)(2,1)S(1)} copy-done((bf16[8,3,128,1024]{3,2,1,0:T(8,128)(2,1)S(1)}, bf16[8,3,128,1024]{3,2,1,0:T(8,128)(2,1)}, u32[]{:S(2)}) %copy-start.1) | copy-done | bytes 6291480
  74.1 6.7 %shard_map.89.inner_ref = f32[1024,512]{1,0:T(8,128)S(1)} custom-call(bf16[8,3,128,1024]{3,2,1,0:T(8,128)(2,1)S(1)} %copy-done.1, bf16[1024,512]{1,0:T(8,128)(2,1)S(1)} %bitcast.22, f32[60,128]{1,0:T(8,128)S(1)} %get-tuple-element.13.weight_ref), custom_call_target="tpu_custom_call" | custom-call | flops 3221225472 | bytes 6291456 | tf_op jit(solution)/shard_map/pallas_call | solution.py:319
  82.0 7.2 %shard_map.90 = bf16[1024,640]{1,0:T(8,128)(2,1)} custom-call(bf16[8,3,128,1024]{3,2,1,0:T(8,128)(2,1)S(1)} %bitcast.16, bf16[1024,128]{1,0:T(8,128)(2,1)S(1)} %collective-permute-done.above_ref, bf16[1024,128]{1,0:T(8,128)(2,1)S(1)} %collective-permute-done.1.below_ref, f32[60,128]{1,0:T(8,128)S(1)} %get-tuple-element.13.weight_ref, ...), custom_call_target="tpu_custom_call" | custom-call | tf_op jit(solution)/shard_map/pallas_call | solution.py:333
  89.2 4.6 %all-to-all-start.1 = ((bf16[32,32,640]{2,1,0:T(8,128)(2,1)}), bf16[32,32,640]{2,1,0:T(8,128)(2,1)}, u32[]{:S(2)}, u32[]{:S(2)}) async-start(bf16[32,32,640]{2,1,0:T(8,128)(2,1)} %bitcast.7), calls=%async_computation.1 | async-start | bytes 2621440 | tf_op jit(solution)/shard_map/all_to_all | solution.py:659
  95.6 3.5 %shard_map.91.base_ref = f32[4,32,32,128]{3,2,1,0:T(8,128)S(1)} custom-call(f32[4,32,32,128]{3,2,1,0:T(8,128)S(1)} %copy-done.4, f32[4,32,32,128]{3,2,1,0:T(8,128)} %constant_dynamic-update-slice_fusion.2.right_side_ref, f32[5,128,128]{2,1,0:T(8,128)S(1)} %copy-done.12, bf16[256,256]{1,0:T(8,128)(2,1)S(1)} %get-tuple-element.37.right_ref), custom_call_target="tpu_custom_call" | custom-call | bytes 9306112 | tf_op jit(solution)/shard_map/pallas_call | solution.py:497
  100.4 25.5 %all-to-all-done.1.coupled_ref = bf16[32,32,640]{2,1,0:T(8,128)(2,1)} async-done(((bf16[32,32,640]{2,1,0:T(8,128)(2,1)}), bf16[32,32,640]{2,1,0:T(8,128)(2,1)}, u32[]{:S(2)}, u32[]{:S(2)}) %all-to-all-start.1) | async-done | bytes 1310752 | tf_op jit(solution)/shard_map/all_to_all | solution.py:659
  125.9 7.2 %shard_map.92 = (f32[4,32,32,128]{3,2,1,0:T(8,128)S(1)}, bf16[32,32,512]{2,1,0:T(8,128)(2,1)S(1)}) custom-call(f32[4,32,32,128]{3,2,1,0:T(8,128)} %copy-done.3, f32[4,32,32,128]{3,2,1,0:T(8,128)} %copy-done.10, bf16[32,32,640]{2,1,0:T(8,128)(2,1)} %all-to-all-done.1.coupled_ref, bf16[256,256]{1,0:T(8,128)(2,1)S(1)} %get-tuple-element.37.right_ref, ...), custom_call_target="tpu_custom_call" | custom-call | flops 1610612736 | bytes 11665408 | tf_op jit(solution)/shard_map/pallas_call | solution.py:497
  133.1 29.6 %all_to_all.41 = bf16[32,32,512]{2,1,0:T(8,128)(2,1)S(1)} all-to-all(bf16[32,32,512]{2,1,0:T(8,128)(2,1)S(1)} %get-tuple-element.19), channel_id=1, replica_groups=mesh['mode'=8,'slab'=4] {'mode','slab'}, dimensions={0} | all-to-all | bytes 2097152 | tf_op jit(solution)/shard_map/all_to_all | solution.py:663
  162.8 3.0 %collective-permute-start.12 = (bf16[1024,128]{1,0:T(8,128)(2,1)S(1)}, bf16[1024,128]{1,0:T(8,128)(2,1)S(1)}, u32[]{:S(2)}, u32[]{:S(2)}) collective-permute-start(bf16[1024,128]{1,0:T(8,128)(2,1)S(1)} %get-tuple-element.32), channel_id=1, source_target_pairs={{4,0},{8,4},{12,8},{16,12},{20,16},{24,20},{28,24},{1,28},{5,1},{9... | collective-permute-start | bytes 786440 | tf_op jit(solution)/shard_map/ppermute | solution.py:314
  165.8 6.7 %shard_map.94.inner_ref = f32[1024,512]{1,0:T(8,128)S(1)} custom-call(bf16[8,3,128,1024]{3,2,1,0:T(8,128)(2,1)S(1)} %bitcast.18, bf16[1024,512]{1,0:T(8,128)(2,1)S(1)} %bitcast.24, f32[60,128]{1,0:T(8,128)S(1)} %get-tuple-element.13.weight_ref), custom_call_target="tpu_custom_call" | custom-call | flops 3221225472 | bytes 6291456 | tf_op jit(solution)/shard_map/pallas_call | solution.py:319
  172.5 5.2 %collective-permute-done.11.above_ref = bf16[1024,128]{1,0:T(8,128)(2,1)S(1)} collective-permute-done((bf16[1024,128]{1,0:T(8,128)(2,1)S(1)}, bf16[1024,128]{1,0:T(8,128)(2,1)S(1)}, u32[]{:S(2)}, u32[]{:S(2)}) %collective-permute-start.11) | collective-permute-done | bytes 262176 | tf_op jit(solution)/shard_map/ppermute | solution.py:313
  177.7 4.6 %shard_map.95 = bf16[1024,512]{1,0:T(8,128)(2,1)} custom-call(bf16[8,3,128,1024]{3,2,1,0:T(8,128)(2,1)S(1)} %bitcast.18, bf16[1024,128]{1,0:T(8,128)(2,1)S(1)} %collective-permute-done.11.above_ref, bf16[1024,128]{1,0:T(8,128)(2,1)S(1)} %collective-permute-done.12.below_ref, f32[60,128]{1,0:T(8,128)S(1)} %get-tuple-element.13.weight_ref, ...), custom_call_target="tpu_custom_call" | custom-call | tf_op jit(solution)/shard_map/pallas_call | solution.py:333
  182.3 2.7 %all-to-all-start.3 = ((bf16[32,32,512]{2,1,0:T(8,128)(2,1)}), bf16[32,32,512]{2,1,0:T(8,128)(2,1)S(1)}, u32[]{:S(2)}, u32[]{:S(2)}) async-start(bf16[32,32,512]{2,1,0:T(8,128)(2,1)} %bitcast.9), calls=%async_computation.3 | async-start | bytes 2097152 | tf_op jit(solution)/shard_map/all_to_all | solution.py:667
  186.6 2.8 %shard_map.93.base_ref = f32[4,32,32,128]{3,2,1,0:T(8,128)S(1)} custom-call(f32[4,32,32,128]{3,2,1,0:T(8,128)S(1)} %copy-done.8, f32[4,32,32,128]{3,2,1,0:T(8,128)} %constant_dynamic-update-slice_fusion.2.right_side_ref, f32[5,128,128]{2,1,0:T(8,128)S(1)} %copy-done.12, bf16[256,256]{1,0:T(8,128)(2,1)S(1)} %get-tuple-element.37.right_ref), custom_call_target="tpu_custom_call" | custom-call | bytes 9306112 | tf_op jit(solution)/shard_map/pallas_call | solution.py:497
  190.8 20.5 %all-to-all-done.3.coupled_ref = bf16[32,32,512]{2,1,0:T(8,128)(2,1)S(1)} async-done(((bf16[32,32,512]{2,1,0:T(8,128)(2,1)}), bf16[32,32,512]{2,1,0:T(8,128)(2,1)S(1)}, u32[]{:S(2)}, u32[]{:S(2)}) %all-to-all-start.3) | async-done | bytes 1048608 | tf_op jit(solution)/shard_map/all_to_all | solution.py:667
  211.2 4.6 %shard_map.96 = (f32[4,32,32,128]{3,2,1,0:T(8,128)S(1)}, bf16[4,32,32,128]{3,2,1,0:T(8,128)(2,1)}) custom-call(f32[4,32,32,128]{3,2,1,0:T(8,128)} %copy-done.2, bf16[32,32,512]{2,1,0:T(8,128)(2,1)S(1)} %all-to-all-done.3.coupled_ref), custom_call_target="tpu_custom_call" | custom-call | bytes 6291456 | tf_op jit(solution)/shard_map/pallas_call | solution.py:497
  217.1 4.6 %all-to-all-start.4 = ((bf16[128,32,128]{2,1,0:T(8,128)(2,1)}), bf16[128,32,128]{2,1,0:T(8,128)(2,1)}, u32[]{:S(2)}, u32[]{:S(2)}) async-start(bf16[128,32,128]{2,1,0:T(8,128)(2,1)} %bitcast.10), calls=%async_computation.4 | async-start | bytes 2097152 | tf_op jit(solution)/shard_map/all_to_all | solution.py:624
  223.3 5.4 %shard_map.97 = bf16[4,32,32,128]{3,2,1,0:T(8,128)(2,1)} custom-call(f32[4,32,32,128]{3,2,1,0:T(8,128)S(1)} %copy-done.9, f32[4,32,32,128]{3,2,1,0:T(8,128)S(1)} %copy-done.16, bf16[256,256]{1,0:T(8,128)(2,1)S(1)} %get-tuple-element.37.right_ref, bf16[256,256]{1,0:T(8,128)(2,1)S(1)} %get-tuple-element.36.left_ref, f32[128,128]{1,0:T(8,128)S(1)} %subtract_divide_fusion.scale_ref), custom_call_target="tpu_custom_call" | custom-call | flops 1610612736 | bytes 9043968 | tf_op jit(solution)/shard_map/pallas_call | solution.py:497
  228.7 7.4 %all-to-all-done.4 = bf16[128,32,128]{2,1,0:T(8,128)(2,1)} async-done(((bf16[128,32,128]{2,1,0:T(8,128)(2,1)}), bf16[128,32,128]{2,1,0:T(8,128)(2,1)}, u32[]{:S(2)}, u32[]{:S(2)}) %all-to-all-start.4) | async-done | bytes 1048608 | tf_op jit(solution)/shard_map/all_to_all | solution.py:624
  236.0 3.5 %all-to-all-start.5 = ((bf16[128,32,128]{2,1,0:T(8,128)(2,1)}), bf16[128,32,128]{2,1,0:T(8,128)(2,1)S(1)}, u32[]{:S(2)}, u32[]{:S(2)}) async-start(bf16[128,32,128]{2,1,0:T(8,128)(2,1)} %bitcast.11), calls=%async_computation.5 | async-start | bytes 2097152 | tf_op jit(solution)/shard_map/all_to_all | solution.py:624
  239.6 3.4 %fusion.11 = f32[128,32,128]{2,1,0:T(8,128)} fusion(bf16[128,32,128]{2,1,0:T(8,128)(2,1)} %all-to-all-done.4), kind=kLoop, calls=%fused_computation.17 | loop fusion | flops 4718592 | bytes 3145728 | tf_op jit(solution)/shard_map/mul | solution.py:672
  243.0 11.0 %all-to-all-done.5 = bf16[128,32,128]{2,1,0:T(8,128)(2,1)S(1)} async-done(((bf16[128,32,128]{2,1,0:T(8,128)(2,1)}), bf16[128,32,128]{2,1,0:T(8,128)(2,1)S(1)}, u32[]{:S(2)}, u32[]{:S(2)}) %all-to-all-start.5) | async-done | bytes 1048608 | tf_op jit(solution)/shard_map/all_to_all | solution.py:624
  (94 shorter events, 36.9 us)
Async XLA Ops:
  1.4 30.4 %collective-permute-start.3 = (f32[1,4,32,128]{3,2,1,0:T(8,128)S(1)}, f32[1,4,32,128]{3,2,1,0:T(8,128)}, u32[]{:S(2)}, u32[]{:S(2)}) collective-permute-start(f32[1,4,32,128]{3,2,1,0:T(8,128)S(1)} %maximum_bitcast_fusion), channel_id=1, source_target_pairs={{0,2},{1,3},{2,0},{3,1},{4,6},{5,7},{6,4},{7,5},{8,10},{9,11},{10,... | collective-permute-start | bytes 196616 | tf_op jit(solution)/shard_map/ppermute | solution.py:589
  4.4 24.6 %collective-permute-start.2 = (f32[1,4,32,128]{3,2,1,0:T(8,128)S(1)}, f32[1,4,32,128]{3,2,1,0:T(8,128)}, u32[]{:S(2)}, u32[]{:S(2)}) collective-permute-start(f32[1,4,32,128]{3,2,1,0:T(8,128)S(1)} %maximum_bitcast_fusion), channel_id=1, source_target_pairs={{0,1},{1,2},{2,3},{3,0},{4,5},{5,6},{6,7},{7,4},{8,9},{9,10},{10,1... | collective-permute-start | bytes 196616 | tf_op jit(solution)/shard_map/ppermute | solution.py:589
  4.4 28.3 %collective-permute-start.4 = (f32[1,4,32,128]{3,2,1,0:T(8,128)S(1)}, f32[1,4,32,128]{3,2,1,0:T(8,128)}, u32[]{:S(2)}, u32[]{:S(2)}) collective-permute-start(f32[1,4,32,128]{3,2,1,0:T(8,128)S(1)} %maximum_bitcast_fusion), channel_id=1, source_target_pairs={{0,3},{1,0},{2,1},{3,2},{4,7},{5,4},{6,5},{7,6},{8,11},{9,8},{10,9... | collective-permute-start | bytes 196616 | tf_op jit(solution)/shard_map/ppermute | solution.py:589
  10.4 55.0 %all-to-all-start = ((bf16[8,128,512]{2,1,0:T(8,128)(2,1)}), bf16[8,128,512]{2,1,0:T(8,128)(2,1)S(1)}, u32[]{:S(2)}, u32[]{:S(2)}) async-start(bf16[8,128,512]{2,1,0:T(8,128)(2,1)} %shard_map.87), calls=%async_computation | async-start | bytes 2097152 | tf_op jit(solution)/shard_map/all_to_all | solution.py:619
  16.4 3.3 %copy-start.13 = (s32[8,16]{1,0:T(8,128)S(1)}, s32[8,16]{1,0:T(8,128)}, u32[]{:S(2)}) copy-start(s32[8,16]{1,0:T(8,128)} %entry_ref.1) | copy-start | bytes 1540
  16.5 3.3 %copy-start.14 = (s32[8]{0:T(128)S(1)}, s32[8]{0:T(128)}, u32[]{:S(2)}) copy-start(s32[8]{0:T(128)} %count_ref.1) | copy-start | bytes 100
  19.2 22.7 %collective-permute-start.6 = (f32[1,32,32,128]{3,2,1,0:T(8,128)}, f32[1,32,32,128]{3,2,1,0:T(8,128)}, u32[]{:S(2)}, u32[]{:S(2)}) collective-permute-start(f32[1,32,32,128]{3,2,1,0:T(8,128)} %get-tuple-element.29), channel_id=1, source_target_pairs={{0,2},{1,3},{2,0},{3,1},{4,6},{5,7},{6,4},{7,5},{8,10},{9,11},{10,... | collective-permute-start | bytes 1572872 | tf_op jit(solution)/shard_map/ppermute | solution.py:589
  19.7 21.1 %collective-permute-start.5 = (f32[1,32,32,128]{3,2,1,0:T(8,128)}, f32[1,32,32,128]{3,2,1,0:T(8,128)}, u32[]{:S(2)}, u32[]{:S(2)}) collective-permute-start(f32[1,32,32,128]{3,2,1,0:T(8,128)} %get-tuple-element.30), channel_id=1, source_target_pairs={{0,1},{1,2},{2,3},{3,0},{4,5},{5,6},{6,7},{7,4},{8,9},{9,10},{10,1... | collective-permute-start | bytes 1572872 | tf_op jit(solution)/shard_map/ppermute | solution.py:589
  19.7 2.2 copy-start.6
  24.5 4.1 %copy-start = (bf16[8,3,128,1024]{3,2,1,0:T(8,128)(2,1)}, bf16[8,3,128,1024]{3,2,1,0:T(8,128)(2,1)S(1)}, u32[]{:S(2)}) copy-start(bf16[8,3,128,1024]{3,2,1,0:T(8,128)(2,1)S(1)} %shard_map.86.matrix_ref) | copy-start | bytes 18874372
  24.5 3.1 %copy-start.17 = (f32[128,32,128]{2,1,0:T(8,128)S(1)}, f32[128,32,128]{2,1,0:T(8,128)}, u32[]{:S(2)}) copy-start(f32[128,32,128]{2,1,0:T(8,128)} %param.8) | copy-start | bytes 6291460
  29.2 14.3 %collective-permute-start.7 = (f32[1,32,32,128]{3,2,1,0:T(8,128)S(1)}, f32[1,32,32,128]{3,2,1,0:T(8,128)S(1)}, u32[]{:S(2)}, u32[]{:S(2)}) collective-permute-start(f32[1,32,32,128]{3,2,1,0:T(8,128)S(1)} %copy-done.18), channel_id=1, source_target_pairs={{0,3},{1,0},{2,1},{3,2},{4,7},{5,4},{6,5},{7,6},{8,11},{9,8},{10,9... | collective-permute-start | bytes 1572872 | tf_op jit(solution)/shard_map/ppermute | solution.py:589
  31.8 20.1 %collective-permute-start.8 = (f32[1,32,32,128]{3,2,1,0:T(8,128)S(1)}, f32[1,32,32,128]{3,2,1,0:T(8,128)S(1)}, u32[]{:S(2)}, u32[]{:S(2)}) collective-permute-start(f32[1,32,32,128]{3,2,1,0:T(8,128)S(1)} %get-tuple-element.26), channel_id=1, source_target_pairs={{0,1},{1,2},{2,3},{3,0},{4,5},{5,6},{6,7},{7,4},{8,9},{9,10},{10,1... | collective-permute-start | bytes 1572872 | tf_op jit(solution)/shard_map/ppermute | solution.py:589
  32.7 24.0 %collective-permute-start.9 = (f32[1,32,32,128]{3,2,1,0:T(8,128)S(1)}, f32[1,32,32,128]{3,2,1,0:T(8,128)S(1)}, u32[]{:S(2)}, u32[]{:S(2)}) collective-permute-start(f32[1,32,32,128]{3,2,1,0:T(8,128)S(1)} %get-tuple-element.25), channel_id=1, source_target_pairs={{0,2},{1,3},{2,0},{3,1},{4,6},{5,7},{6,4},{7,5},{8,10},{9,11},{10,... | collective-permute-start | bytes 1572872 | tf_op jit(solution)/shard_map/ppermute | solution.py:589
  35.4 17.3 %copy-start.11 = (f32[5,128,128]{2,1,0:T(8,128)}, f32[5,128,128]{2,1,0:T(8,128)S(1)}, u32[]{:S(2)}) copy-start(f32[5,128,128]{2,1,0:T(8,128)S(1)} %get-tuple-element.16.weight_ref) | copy-start | bytes 983044
  40.8 23.8 %collective-permute-start.10 = (f32[1,32,32,128]{3,2,1,0:T(8,128)S(1)}, f32[1,32,32,128]{3,2,1,0:T(8,128)S(1)}, u32[]{:S(2)}, u32[]{:S(2)}) collective-permute-start(f32[1,32,32,128]{3,2,1,0:T(8,128)S(1)} %get-tuple-element.24), channel_id=1, source_target_pairs={{0,3},{1,0},{2,1},{3,2},{4,7},{5,4},{6,5},{7,6},{8,11},{9,8},{10,9... | collective-permute-start | bytes 1572872 | tf_op jit(solution)/shard_map/ppermute | solution.py:589
  51.9 30.1 %slice-start = ((s8[6291456]{0:T(1024)(128)(4,1)}), s8[2097152]{0:T(1024)(128)(4,1)S(1)}, s32[]{:S(2)}) async-start(s8[6291456]{0:T(1024)(128)(4,1)} %bitcast.15), calls=%async_computation.6 | async-start | bytes 4194304
  65.4 15.3 %collective-permute-start.1 = (bf16[1024,128]{1,0:T(8,128)(2,1)S(1)}, bf16[1024,128]{1,0:T(8,128)(2,1)S(1)}, u32[]{:S(2)}, u32[]{:S(2)}) collective-permute-start(bf16[1024,128]{1,0:T(8,128)(2,1)S(1)} %get-tuple-element.34), channel_id=1, source_target_pairs={{4,0},{8,4},{12,8},{16,12},{20,16},{24,20},{28,24},{1,28},{5,1},{9... | collective-permute-start | bytes 786440 | tf_op jit(solution)/shard_map/ppermute | solution.py:314
  71.3 10.8 %collective-permute-start = (bf16[1024,128]{1,0:T(8,128)(2,1)S(1)}, bf16[1024,128]{1,0:T(8,128)(2,1)S(1)}, u32[]{:S(2)}, u32[]{:S(2)}) collective-permute-start(bf16[1024,128]{1,0:T(8,128)(2,1)S(1)} %get-tuple-element.35), channel_id=1, source_target_pairs={{0,4},{4,8},{8,12},{12,16},{16,20},{20,24},{24,28},{28,1},{1,5},{5... | collective-permute-start | bytes 786440 | tf_op jit(solution)/shard_map/ppermute | solution.py:313
  71.3 2.8 %copy-start.1 = (bf16[8,3,128,1024]{3,2,1,0:T(8,128)(2,1)S(1)}, bf16[8,3,128,1024]{3,2,1,0:T(8,128)(2,1)}, u32[]{:S(2)}) copy-start(bf16[8,3,128,1024]{3,2,1,0:T(8,128)(2,1)} %copy-done) | copy-start | bytes 18874372
  74.1 8.0 %slice-start.1 = ((s8[6291456]{0:T(1024)(128)(4,1)}), s8[4194304]{0:T(1024)(128)(4,1)S(1)}, s32[]{:S(2)}) async-start(s8[6291456]{0:T(1024)(128)(4,1)} %bitcast.15), calls=%async_computation.7 | async-start | bytes 8388608
  89.2 4.8 %copy-start.12 = (f32[5,128,128]{2,1,0:T(8,128)S(1)}, f32[5,128,128]{2,1,0:T(8,128)}, u32[]{:S(2)}) copy-start(f32[5,128,128]{2,1,0:T(8,128)} %copy-done.11) | copy-start | bytes 983044
  89.2 36.7 %all-to-all-start.1 = ((bf16[32,32,640]{2,1,0:T(8,128)(2,1)}), bf16[32,32,640]{2,1,0:T(8,128)(2,1)}, u32[]{:S(2)}, u32[]{:S(2)}) async-start(bf16[32,32,640]{2,1,0:T(8,128)(2,1)} %bitcast.7), calls=%async_computation.1 | async-start | bytes 2621440 | tf_op jit(solution)/shard_map/all_to_all | solution.py:659
  95.5 70.2 %slice-start.2 = ((s8[6291456]{0:T(1024)(128)(4,1)}), s8[2097152]{0:T(1024)(128)(4,1)S(1)}, s32[]{:S(2)}) async-start(s8[6291456]{0:T(1024)(128)(4,1)} %bitcast.17), calls=%async_computation.8 | async-start | bytes 4194304
  125.9 39.8 %slice-start.3 = ((s8[6291456]{0:T(1024)(128)(4,1)}), s8[4194304]{0:T(1024)(128)(4,1)S(1)}, s32[]{:S(2)}) async-start(s8[6291456]{0:T(1024)(128)(4,1)} %bitcast.17), calls=%async_computation.9 | async-start | bytes 8388608
  133.1 39.4 %copy-start.7 = (f32[4,32,32,128]{3,2,1,0:T(8,128)}, f32[4,32,32,128]{3,2,1,0:T(8,128)S(1)}, u32[]{:S(2)}) copy-start(f32[4,32,32,128]{3,2,1,0:T(8,128)S(1)} %get-tuple-element.18.current_ref) | copy-start | bytes 6291460
  162.8 9.7 %collective-permute-start.12 = (bf16[1024,128]{1,0:T(8,128)(2,1)S(1)}, bf16[1024,128]{1,0:T(8,128)(2,1)S(1)}, u32[]{:S(2)}, u32[]{:S(2)}) collective-permute-start(bf16[1024,128]{1,0:T(8,128)(2,1)S(1)} %get-tuple-element.32), channel_id=1, source_target_pairs={{4,0},{8,4},{12,8},{16,12},{20,16},{24,20},{28,24},{1,28},{5,1},{9... | collective-permute-start | bytes 786440 | tf_op jit(solution)/shard_map/ppermute | solution.py:314
  165.7 11.9 %collective-permute-start.11 = (bf16[1024,128]{1,0:T(8,128)(2,1)S(1)}, bf16[1024,128]{1,0:T(8,128)(2,1)S(1)}, u32[]{:S(2)}, u32[]{:S(2)}) collective-permute-start(bf16[1024,128]{1,0:T(8,128)(2,1)S(1)} %get-tuple-element.33), channel_id=1, source_target_pairs={{0,4},{4,8},{8,12},{12,16},{16,20},{20,24},{24,28},{28,1},{1,5},{5... | collective-permute-start | bytes 786440 | tf_op jit(solution)/shard_map/ppermute | solution.py:313
  182.3 29.0 %all-to-all-start.3 = ((bf16[32,32,512]{2,1,0:T(8,128)(2,1)}), bf16[32,32,512]{2,1,0:T(8,128)(2,1)S(1)}, u32[]{:S(2)}, u32[]{:S(2)}) async-start(bf16[32,32,512]{2,1,0:T(8,128)(2,1)} %bitcast.9), calls=%async_computation.3 | async-start | bytes 2097152 | tf_op jit(solution)/shard_map/all_to_all | solution.py:667
  217.1 4.6 %copy-start.16 = (f32[4,32,32,128]{3,2,1,0:T(8,128)S(1)}, f32[4,32,32,128]{3,2,1,0:T(8,128)}, u32[]{:S(2)}) copy-start(f32[4,32,32,128]{3,2,1,0:T(8,128)} %copy-done.15) | copy-start | bytes 6291460
  217.1 18.9 %all-to-all-start.4 = ((bf16[128,32,128]{2,1,0:T(8,128)(2,1)}), bf16[128,32,128]{2,1,0:T(8,128)(2,1)}, u32[]{:S(2)}, u32[]{:S(2)}) async-start(bf16[128,32,128]{2,1,0:T(8,128)(2,1)} %bitcast.10), calls=%async_computation.4 | async-start | bytes 2097152 | tf_op jit(solution)/shard_map/all_to_all | solution.py:624
  236.0 18.0 %all-to-all-start.5 = ((bf16[128,32,128]{2,1,0:T(8,128)(2,1)}), bf16[128,32,128]{2,1,0:T(8,128)(2,1)S(1)}, u32[]{:S(2)}, u32[]{:S(2)}) async-start(bf16[128,32,128]{2,1,0:T(8,128)(2,1)} %bitcast.11), calls=%async_computation.5 | async-start | bytes 2097152 | tf_op jit(solution)/shard_map/all_to_all | solution.py:624
  (11 other events, 15.9 us)

commit v6 on v5

--- a/solution.py
+++ b/solution.py
@@ -9,7 +9,8 @@
 from jax.sharding import PartitionSpec as P
 
 RELAXATION = 0.6
-MIB = 1 << 20
+VMEM_BYTES = 60 << 20
+UNROLL = 4
 
 
 def sine_table(length):
@@ -83,7 +84,7 @@
             jax.ShapeDtypeStruct((5, nx, ny), jnp.float32),
             jax.ShapeDtypeStruct((fields * 5 * height, ny), jnp.float32),
         ],
-        compiler_params=pltpu.CompilerParams(vmem_limit_bytes=32 * MIB),
+        compiler_params=pltpu.CompilerParams(vmem_limit_bytes=VMEM_BYTES),
     )(strip.reshape(1), coefs)
 
 
@@ -160,8 +161,11 @@
     height = rows // strips
     return pl.pallas_call(
         functools.partial(pack_kernel, rows, height),
+        grid=(modes // GROUP,),
+        in_specs=[pl.BlockSpec((GROUP * rows, cols), lambda g: (g, 0))],
+        out_specs=pl.BlockSpec((strips, GROUP, height * cols), lambda g: (0, g, 0)),
         out_shape=jax.ShapeDtypeStruct((strips, modes, height * cols), jnp.bfloat16),
-        compiler_params=pltpu.CompilerParams(vmem_limit_bytes=32 * MIB),
+        compiler_params=pltpu.CompilerParams(vmem_limit_bytes=VMEM_BYTES),
     )(block.reshape(modes * rows, cols))
 
 
@@ -192,7 +196,7 @@
             ),
         ),
         out_shape=jax.ShapeDtypeStruct((blocks, fields, width, blocks * width), coupling.dtype),
-        compiler_params=pltpu.CompilerParams(vmem_limit_bytes=32 * MIB),
+        compiler_params=pltpu.CompilerParams(vmem_limit_bytes=VMEM_BYTES),
     )(coupling_list, pair_count, coupling)
 
 
@@ -224,33 +228,35 @@
     return weight_ref[at : at + 1, :]
 
 
-def inner_kernel(height, cols, matrix_ref, state_ref, weight_ref, out_ref, sums_ref):
-    fields, width, depth = matrix_ref.shape[1:]
-    sums_ref[...] = jnp.dot(
-        matrix_ref[0].reshape(fields * width, depth),
-        state_ref[...],
-        preferred_element_type=jnp.float32,
-    )
-    for r in range(height):
-        total = 0.0
-        from_left = 0.0
-        from_right = 0.0
-        for f in range(fields):
-
-            def row(at):
-                return sums_ref[f * width : (f + 1) * width, at * cols : (at + 1) * cols]
-
-            weight = functools.partial(weight_row, weight_ref, height, f)
-            here = row(r)
-            total = total + weight(0, r) * here
-            if r > 0:
-                total = total - weight(1, r) * row(r - 1)
-            if r < height - 1:
-                total = total - weight(2, r) * row(r + 1)
-            from_left = from_left + weight(4, r) * here
-            from_right = from_right + weight(3, r) * here
-        total = total - pltpu.roll(from_left, 1, 1) - pltpu.roll(from_right, cols - 1, 1)
-        out_ref[:, r * cols : (r + 1) * cols] = total
+def inner_kernel(height, cols, matrix_ref, state_ref, weight_ref, out_ref, *sums_refs):
+    blocks, fields, width, depth = matrix_ref.shape
+    for block in range(blocks):
+        sums_ref = sums_refs[block % len(sums_refs)]
+        sums_ref[...] = jnp.dot(
+            matrix_ref[block].reshape(fields * width, depth),
+            state_ref[...],
+            preferred_element_type=jnp.float32,
+        )
+        for r in range(height):
+            total = 0.0
+            from_left = 0.0
+            from_right = 0.0
+            for f in range(fields):
+
+                def row(at):
+                    return sums_ref[f * width : (f + 1) * width, at * cols : (at + 1) * cols]
+
+                weight = functools.partial(weight_row, weight_ref, height, f)
+                here = row(r)
+                total = total + weight(0, r) * here
+                if r > 0:
+                    total = total - weight(1, r) * row(r - 1)
+                if r < height - 1:
+                    total = total - weight(2, r) * row(r + 1)
+                from_left = from_left + weight(4, r) * here
+                from_right = from_right + weight(3, r) * here
+            total = total - pltpu.roll(from_left, 1, 1) - pltpu.roll(from_right, cols - 1, 1)
+            out_ref[block * width : (block + 1) * width, r * cols : (r + 1) * cols] = total
 
 
 def border_kernel(
@@ -266,37 +272,40 @@
     right_ref,
     out_ref,
 ):
-    fields, width, depth = matrix_ref.shape[1:]
-    matrix = matrix_ref[0].reshape(fields * width, depth)
+    blocks, fields, width, depth = matrix_ref.shape
     border = jnp.concatenate([above_ref[...], below_ref[...]], axis=1)
-    sums = jnp.dot(matrix, border, preferred_element_type=jnp.float32)
-    rows = []
-    for r in range(height):
-        total = inner_ref[:, r * cols : (r + 1) * cols]
-        for f in range(fields):
-            part = sums[f * width : (f + 1) * width]
-            if r == 0:
-                total = total - weight_row(weight_ref, height, f, 1, r) * part[:, :cols]
-            if r == height - 1:
-                total = total - weight_row(weight_ref, height, f, 2, r) * part[:, cols:]
-        rows.append(total)
-    if not first:
+    low_col = lax.broadcasted_iota(jnp.int32, (width, cols), 1) < LOW
+    for block in range(blocks):
+        matrix = matrix_ref[block].reshape(fields * width, depth)
+        sums = jnp.dot(matrix, border, preferred_element_type=jnp.float32)
+        modes = slice(block * width, (block + 1) * width)
+        rows = []
         for r in range(height):
-            out_ref[:, r * cols : (r + 1) * cols] = encode(rows[r] * scale, SUM_POWER)
-        return
-    rows = along_cols(rows, right_ref)
-    low_col = lax.broadcasted_iota(jnp.int32, (width, cols), 1) < LOW
-    for r in range(height):
-        value = rows[r] * scale
-        code = encode(value, FIRST_POWER)
-        out_ref[:, r * cols : (r + 1) * cols] = code
-        rest = jnp.where(low_col, value - decode(code, FIRST_POWER), 0.0)
-        place = r % (cols // LOW)
-        rest = pltpu.roll(rest, place * LOW, 1) if place else rest
-        packed = rest if place == 0 else packed + rest
-        if place == cols // LOW - 1 or r == height - 1:
-            at = (height + r // (cols // LOW)) * cols
-            out_ref[:, at : at + cols] = packed.astype(jnp.bfloat16)
+            total = inner_ref[modes, r * cols : (r + 1) * cols]
+            for f in range(fields):
+                part = sums[f * width : (f + 1) * width]
+                if r == 0:
+                    total = total - weight_row(weight_ref, height, f, 1, r) * part[:, :cols]
+                if r == height - 1:
+                    total = total - weight_row(weight_ref, height, f, 2, r) * part[:, cols:]
+            rows.append(total)
+        if not first:
+            for r in range(height):
+                code = encode(rows[r] * scale, SUM_POWER)
+                out_ref[modes, r * cols : (r + 1) * cols] = code
+            continue
+        rows = along_cols(rows, right_ref)
+        for r in range(height):
+            value = rows[r] * scale
+            code = encode(value, FIRST_POWER)
+            out_ref[modes, r * cols : (r + 1) * cols] = code
+            rest = jnp.where(low_col, value - decode(code, FIRST_POWER), 0.0)
+            place = r % (cols // LOW)
+            rest = pltpu.roll(rest, place * LOW, 1) if place else rest
+            packed = rest if place == 0 else packed + rest
+            if place == cols // LOW - 1 or r == height - 1:
+                at = (height + r // (cols // LOW)) * cols
+                out_ref[modes, at : at + cols] = packed.astype(jnp.bfloat16)
 
 
 def coupled_sums(matrix, state, weights, right, first, scale, both):
@@ -312,17 +321,18 @@
     onward = list(zip(place, place[1:] + place[:1]))
     above = lax.ppermute(state[:, -cols:], both, onward)
     below = lax.ppermute(state[:, :cols], both, [(b, a) for a, b in onward])
-    matrix_spec = pl.BlockSpec((1, fields, width, depth), lambda i: (i, 0, 0, 0))
+    unroll = math.gcd(blocks, UNROLL)
+    matrix_spec = pl.BlockSpec((unroll, fields, width, depth), lambda i: (i, 0, 0, 0))
     weight_spec = pl.BlockSpec(weights.shape, lambda i: (0, 0))
-    sums_spec = pl.BlockSpec((width, cells), lambda i: (i, 0))
-    params = pltpu.CompilerParams(vmem_limit_bytes=40 * MIB)
+    sums_spec = pl.BlockSpec((unroll * width, cells), lambda i: (i, 0))
+    params = pltpu.CompilerParams(vmem_limit_bytes=VMEM_BYTES)
     inner = pl.pallas_call(
         functools.partial(inner_kernel, height, cols),
-        grid=(blocks,),
+        grid=(blocks // unroll,),
         in_specs=[matrix_spec, pl.BlockSpec((depth, cells), lambda i: (0, 0)), weight_spec],
         out_specs=sums_spec,
         out_shape=jax.ShapeDtypeStruct((blocks * width, cells), jnp.float32),
-        scratch_shapes=[pltpu.VMEM((fields * width, cells), jnp.float32)],
+        scratch_shapes=[pltpu.VMEM((fields * width, cells), jnp.float32)] * 2,
         cost_estimate=pl.CostEstimate(
             flops=2 * matrix.size * cells, bytes_accessed=2 * matrix.size, transcendentals=0
         ),
@@ -332,7 +342,7 @@
     sent = cells + (low_tiles(height, cols) * cols if first else 0)
     return pl.pallas_call(
         functools.partial(border_kernel, height, cols, first, scale),
-        grid=(blocks,),
+        grid=(blocks // unroll,),
         in_specs=[
             matrix_spec,
             border_spec,
@@ -341,13 +351,13 @@
             sums_spec,
             pl.BlockSpec(right.shape, lambda i: (0, 0)),
         ],
-        out_specs=pl.BlockSpec((width, sent), lambda i: (i, 0)),
+        out_specs=pl.BlockSpec((unroll * width, sent), lambda i: (i, 0)),
         out_shape=jax.ShapeDtypeStruct((blocks * width, sent), jnp.bfloat16),
         compiler_params=params,
     )(matrix, above, below, weights, inner, right)
 
 
-TOGETHER = 8
+TOGETHER = 16
 GROUP = 16
 
 
@@ -502,7 +512,7 @@
         out_shape=out_shape,
         scratch_shapes=scratch,
         cost_estimate=pl.CostEstimate(flops=flops, bytes_accessed=2 * moved, transcendentals=0),
-        compiler_params=pltpu.CompilerParams(vmem_limit_bytes=48 * MIB),
+        compiler_params=pltpu.CompilerParams(vmem_limit_bytes=VMEM_BYTES),
     )(*operands)
 
 
@@ -589,14 +599,18 @@
     return lax.ppermute(part, axis, [(i, (i + shift) % count) for i in range(count)])
 
 
-def regroup(block, axis):
+def regroup_parts(block, axis):
     count = lax.axis_size(axis)
     here = lax.axis_index(axis)
     parts = [lax.dynamic_index_in_dim(block, here, 0)]
     for shift in range(1, count):
         target = lax.rem(here + shift, count)
         parts.append(onwards(lax.dynamic_index_in_dim(block, target, 0), axis, shift))
-    return collect(parts, axis)
+    return parts
+
+
+def regroup(block, axis):
+    return collect(regroup_parts(block, axis), axis)
 
 
 def spread(block, axis):
@@ -616,6 +630,8 @@
     share = modes // slab_count
 
     strips = pack_strips(guess, mode_count)
+    coefs = jnp.concatenate([mean_coef[None], field_coef], 0)
+    strips, coefs = lax.optimization_barrier((strips, coefs))
     state = lax.all_to_all(strips, "mode", 0, 0, tiled=True)
     state = state.reshape(mode_count * modes, height * cols)
 
@@ -623,10 +639,10 @@
         flat = block.reshape(modes, rows, cols)
         return lax.all_to_all(flat, "slab", 0, 0, tiled=True)
 
-    coefs = jnp.concatenate([mean_coef[None], field_coef], 0)
     coefs = spread(coefs, "slab")
     current = regroup(guess.reshape(slab_count, share, rows, cols), "slab")
-    right_side = regroup(right_side.reshape(slab_count, share, rows, cols), "slab")
+    state, current, right_side = lax.optimization_barrier((state, current, right_side))
+    right_parts = regroup_parts(right_side.reshape(slab_count, share, rows, cols), "slab")
 
     strip = lax.axis_index("slab") * mode_count + lax.axis_index("mode")
     mean_weights, strip_weights = all_weights(coefs, strip, height)
@@ -655,8 +671,9 @@
     first_scale, sum_scale, solution_scale = code_scales(nx, cols, coupling.shape[1], modes)
 
     sums = coupled_sums(matrix, state, strip_weights, tables[0], True, first_scale, both)
-    sums, current, right_side = lax.optimization_barrier((sums, current, right_side))
+    sums, *right_parts[1::2] = lax.optimization_barrier((sums, *right_parts[1::2]))
     sums = lax.all_to_all(sums, both, 0, 0, tiled=True).reshape(devices, share, -1)
+    right_side = collect(right_parts, "slab")
     base = mean_part(current, right_side, mean_weights, tables[0], True)
     current, state = step(current, base, sums, tables, mode_count, slab_count, first_scale)
     state = state.reshape(devices * share, height * cols)
@@ -666,10 +683,9 @@
     sums = coupled_sums(matrix, state, strip_weights, tables[0], False, sum_scale, both)
     sums = lax.all_to_all(sums, both, 0, 0, tiled=True).reshape(devices, share, -1)
     resid, code = last_residual(base, sums, mode_count, slab_count, sum_scale)
-    moved = to_slabs(code)
+    moved = regroup(code, "slab").reshape(modes, rows, cols)
+    resid_out = decode(moved, SUM_POWER) * (1.0 / sum_scale)
     code = correct(current, resid, tables, solution_scale)
-    code, moved = lax.optimization_barrier((code, moved))
-    resid_out = decode(moved, SUM_POWER) * (1.0 / sum_scale)
     return decode(to_slabs(code), SOLUTION_POWER) * (1.0 / solution_scale), resid_out
 
 

time: 257 us -> 243 us (0.946)
  waiting for transfers between devices: 94.8 us -> 65.3 us
  Pallas kernels: 54.1 us -> 73.8 us
  local copies, waits for them, and re-layouts: 31.1 us -> 21.6 us
  blocking collectives: 29.6 us -> 32.2 us
    all_to_all x2, waiting for transfers between devices: 46 us -> 22.3 us  [local(): lax.all_to_all(sums, both, 0, 0, tiled=True).reshape(devices, share, -1)]
    unnamed x50 -> x28, local copies, waits for them, and re-layouts: 18.3 us -> 8 us
    all_to_all x2 -> x1, waiting for transfers between devices: 18.4 us -> 10.4 us  [to_slabs(): return lax.all_to_all(flat, 'slab', 0, 0, tiled=True)]
    pallas_call x1, Pallas kernels: 2.59 us -> 8.7 us  [dense_coupling(): pl.pallas_call(functools.partial(dense_kernel, fields), grid_spec=pltpu.P...]
    ppermute x2, waiting for transfers between devices: 6.45 us -> 0.5 us  [coupled_sums(): above = lax.ppermute(state[:, -cols:], both, onward)]
    ppermute x9 -> x12, waiting for transfers between devices: 24 us -> 29.3 us  [onwards(): lax.ppermute(part, axis, [(i, (i + shift) % count) for i in range(count)])]
    all_to_all x2 -> x1, starting transfers between devices: 8.09 us -> 3.51 us  [to_slabs(): return lax.all_to_all(flat, 'slab', 0, 0, tiled=True)]
    ppermute x2, starting transfers between devices: 0.01 us -> 3.57 us  [coupled_sums(): above = lax.ppermute(state[:, -cols:], both, onward)]
  transfers between devices with their start and end apart: 18 -> 20, of which waited for: 11 -> 8; matrix products, arithmetic and copies ran while one was open for 7% -> 6% of each run, Pallas kernels for 12% -> 21%
where the time goes in v6:
time: 243 us; the launch traced here: 242 us
  Pallas kernels  73.8 us (30%)
  waiting for transfers between devices  65.3 us (27%)
  starting transfers between devices  41 us (17%)
  blocking collectives  32.2 us (13%)
  local copies, waits for them, and re-layouts  21.6 us (9%)
  other arithmetic  6.77 us (3%)
    all_to_all x1, blocking collectives, local(): state = lax.all_to_all(state, both, 0, 0, tiled=True)  32.2 us
    ppermute x12, waiting for transfers between devices, onwards(): lax.ppermute(part, axis, [(i, (i + shift) % count) for i in range(count)])  29.3 us
    pallas_call x5, Pallas kernels, per_group(): pl.pallas_call(kernel, grid=(groups,), in_specs=in_specs, out_specs=out_s...  26 us
    all_to_all x2, waiting for transfers between devices, local(): lax.all_to_all(sums, both, 0, 0, tiled=True).reshape(devices, share, -1)  22.3 us
    pallas_call x2, Pallas kernels, coupled_sums(): pl.pallas_call(functools.partial(inner_kernel, height, cols), grid=(block...  16.4 us
    pallas_call x2, Pallas kernels, coupled_sums(): pl.pallas_call(functools.partial(border_kernel, height, cols, first, scal...  14.7 us
    ppermute x12, starting transfers between devices, onwards(): lax.ppermute(part, axis, [(i, (i + shift) % count) for i in range(count)])  12.1 us
    all_to_all x1, waiting for transfers between devices, to_slabs(): return lax.all_to_all(flat, 'slab', 0, 0, tiled=True)  10.4 us
  transfers between devices with their start and end apart: 20, of which 8 were waited for; matrix products, arithmetic and copies ran while one was open for 6% of the time, Pallas kernels for 21%

profile of v6, /device:TPU:0, one launch (start us, length us, event | category | flops | bytes accessed | tf_op | source)
XLA Modules:
  0.0 241.6 jit_solution(10747252051471100194)
XLA Ops:
  0.6 5.9 %shard_map.86 = bf16[8,128,512]{2,1,0:T(8,128)(2,1)} custom-call(f32[4096,128]{1,0:T(8,128)} %bitcast.16), custom_call_target="tpu_custom_call" | custom-call | tf_op jit(solution)/shard_map/pallas_call | solution.py:162
  6.6 7.3 %all-to-all-start = ((bf16[8,128,512]{2,1,0:T(8,128)(2,1)}), bf16[8,128,512]{2,1,0:T(8,128)(2,1)S(1)}, u32[]{:S(2)}, u32[]{:S(2)}) async-start(bf16[8,128,512]{2,1,0:T(8,128)(2,1)} %shard_map.86), calls=%async_computation | async-start | bytes 2097152 | tf_op jit(solution)/shard_map/all_to_all | solution.py:635
  13.9 1.6 collective-permute-start.6
  17.1 2.7 %constant_dynamic-slice_fusion.5 = (f32[1,32,32,128]{3,2,1,0:T(8,128)}, f32[1,32,32,128]{3,2,1,0:T(8,128)}, f32[1,32,32,128]{3,2,1,0:T(8,128)}, f32[4,32,32,128]{3,2,1,0:T(8,128)S(1)}) fusion(f32[4,32,32,128]{3,2,1,0:T(8,128)} %bitcast.17, s32[]{:T(128)S(6)} %select_n.57, s32[]{:T(128)S(6)} %select_n.58, s32[]{:T(128)S(6)} %select_n.56, ...), kind=kLoop, calls=%fused_computation.50 | loop fusion | bytes 4194324 | tf_op jit(solution)/shard_map/jit(dynamic_index_in_dim)/dynamic_slice | solution.py:608
  21.5 8.7 %shard_map.87.matrix_ref = bf16[8,3,128,1024]{3,2,1,0:T(8,128)(2,1)} custom-call(s32[8,16]{1,0:T(8,128)} %entry_ref.1, s32[8]{0:T(128)} %count_ref.1, bf16[8,16,128,128]{3,2,1,0:T(8,128)(2,1)} %coupling_ref.1), custom_call_target="tpu_custom_call" | custom-call | tf_op jit(solution)/shard_map/pallas_call | solution.py:188
  34.0 1.9 shard_map.88
  38.2 5.5 %collective-permute-done.2 = f32[1,32,32,128]{3,2,1,0:T(8,128)S(1)} collective-permute-done((f32[1,32,32,128]{3,2,1,0:T(8,128)}, f32[1,32,32,128]{3,2,1,0:T(8,128)S(1)}, u32[]{:S(2)}, u32[]{:S(2)}) %collective-permute-start.2) | collective-permute-done | bytes 524320 | tf_op jit(solution)/shard_map/ppermute | solution.py:599
  47.6 2.2 collective-permute-start.8
  50.7 2.0 collective-permute-start.3
  52.8 3.3 %collective-permute-start.4 = (bf16[1024,128]{1,0:T(8,128)(2,1)S(1)}, bf16[1024,128]{1,0:T(8,128)(2,1)S(1)}, u32[]{:S(2)}, u32[]{:S(2)}) collective-permute-start(bf16[1024,128]{1,0:T(8,128)(2,1)S(1)} %get-tuple-element.44), channel_id=1, source_target_pairs={{4,0},{8,4},{12,8},{16,12},{20,16},{24,20},{28,24},{1,28},{5,1},{9... | collective-permute-start | bytes 786440 | tf_op jit(solution)/shard_map/ppermute | solution.py:323
  56.1 8.2 %shard_map.89.inner_ref = f32[1024,512]{1,0:T(8,128)} custom-call(bf16[8,3,128,1024]{3,2,1,0:T(8,128)(2,1)} %shard_map.87.matrix_ref, bf16[1024,512]{1,0:T(8,128)(2,1)} %bitcast.21, f32[60,128]{1,0:T(8,128)} %get-tuple-element.21.weight_ref), custom_call_target="tpu_custom_call" | custom-call | flops 3221225472 | bytes 6291456 | tf_op jit(solution)/shard_map/pallas_call | solution.py:329
  64.8 1.9 collective-permute-done.4.below_ref
  67.4 9.2 %shard_map.90 = bf16[1024,640]{1,0:T(8,128)(2,1)} custom-call(bf16[8,3,128,1024]{3,2,1,0:T(8,128)(2,1)} %shard_map.87.matrix_ref, bf16[1024,128]{1,0:T(8,128)(2,1)} %copy-done.9, bf16[1024,128]{1,0:T(8,128)(2,1)} %copy-done.11, f32[60,128]{1,0:T(8,128)} %get-tuple-element.21.weight_ref, f32[1024,512]{1,0:T(8,128)} %shard_map.89.inner_ref, ...), custom_call_target="tpu_custom_call" | custom-call | tf_op jit(solution)/shard_map/pallas_call | solution.py:343
  76.6 3.7 %all-to-all-start.1 = ((bf16[32,32,640]{2,1,0:T(8,128)(2,1)}), bf16[32,32,640]{2,1,0:T(8,128)(2,1)S(1)}, u32[]{:S(2)}, u32[]{:S(2)}) async-start(bf16[32,32,640]{2,1,0:T(8,128)(2,1)} %bitcast.18), calls=%async_computation.1 | async-start | bytes 2621440 | tf_op jit(solution)/shard_map/all_to_all | solution.py:675
  80.2 1.8 collective-permute-start.10
  83.9 22.7 %collective-permute-done.10 = f32[1,32,32,128]{3,2,1,0:T(8,128)S(1)} collective-permute-done((f32[1,32,32,128]{3,2,1,0:T(8,128)}, f32[1,32,32,128]{3,2,1,0:T(8,128)S(1)}, u32[]{:S(2)}, u32[]{:S(2)}) %collective-permute-start.10) | collective-permute-done | bytes 524320 | tf_op jit(solution)/shard_map/ppermute | solution.py:599
  109.1 4.3 %shard_map.91.base_ref = f32[4,32,32,128]{3,2,1,0:T(8,128)} custom-call(f32[4,32,32,128]{3,2,1,0:T(8,128)} %copy-done.1, f32[4,32,32,128]{3,2,1,0:T(8,128)} %copy-done, f32[5,128,128]{2,1,0:T(8,128)} %get-tuple-element.24.weight_ref, bf16[256,256]{1,0:T(8,128)(2,1)} %get-tuple-element.47.right_ref), custom_call_target="tpu_custom_call" | custom-call | bytes 9306112 | tf_op jit(solution)/shard_map/pallas_call | solution.py:507
  114.4 7.2 %shard_map.92 = (f32[4,32,32,128]{3,2,1,0:T(8,128)}, bf16[32,32,512]{2,1,0:T(8,128)(2,1)}) custom-call(f32[4,32,32,128]{3,2,1,0:T(8,128)} %copy-done.1, f32[4,32,32,128]{3,2,1,0:T(8,128)} %shard_map.91.base_ref, bf16[32,32,640]{2,1,0:T(8,128)(2,1)} %copy-done.6, bf16[256,256]{1,0:T(8,128)(2,1)} %get-tuple-element.47.right_ref, ...), custom_call_target="tpu_custom_call" | custom-call | flops 1610612736 | bytes 11665408 | tf_op jit(solution)/shard_map/pallas_call | solution.py:507
  121.6 32.2 %all_to_all.36 = bf16[32,32,512]{2,1,0:T(8,128)(2,1)S(1)} all-to-all(bf16[32,32,512]{2,1,0:T(8,128)(2,1)} %get-tuple-element.27), channel_id=1, replica_groups=mesh['mode'=8,'slab'=4] {'mode','slab'}, dimensions={0} | all-to-all | bytes 2097152 | tf_op jit(solution)/shard_map/all_to_all | solution.py:680
  155.4 3.9 %collective-permute-start.12 = (bf16[1024,128]{1,0:T(8,128)(2,1)S(1)}, bf16[1024,128]{1,0:T(8,128)(2,1)S(1)}, u32[]{:S(2)}, u32[]{:S(2)}) collective-permute-start(bf16[1024,128]{1,0:T(8,128)(2,1)S(1)} %get-tuple-element.42), channel_id=1, source_target_pairs={{4,0},{8,4},{12,8},{16,12},{20,16},{24,20},{28,24},{1,28},{5,1},{9... | collective-permute-start | bytes 786440 | tf_op jit(solution)/shard_map/ppermute | solution.py:323
  159.3 8.2 %shard_map.94.inner_ref = f32[1024,512]{1,0:T(8,128)} custom-call(bf16[8,3,128,1024]{3,2,1,0:T(8,128)(2,1)} %shard_map.87.matrix_ref, bf16[1024,512]{1,0:T(8,128)(2,1)} %bitcast.23, f32[60,128]{1,0:T(8,128)} %get-tuple-element.21.weight_ref), custom_call_target="tpu_custom_call" | custom-call | flops 3221225472 | bytes 6291456 | tf_op jit(solution)/shard_map/pallas_call | solution.py:329
  169.1 5.6 %shard_map.95 = bf16[1024,512]{1,0:T(8,128)(2,1)} custom-call(bf16[8,3,128,1024]{3,2,1,0:T(8,128)(2,1)} %shard_map.87.matrix_ref, bf16[1024,128]{1,0:T(8,128)(2,1)} %copy-done.8, bf16[1024,128]{1,0:T(8,128)(2,1)} %copy-done.10, f32[60,128]{1,0:T(8,128)} %get-tuple-element.21.weight_ref, f32[1024,512]{1,0:T(8,128)} %shard_map.94.inner_ref, ...), custom_call_target="tpu_custom_call" | custom-call | tf_op jit(solution)/shard_map/pallas_call | solution.py:343
  174.7 3.7 %all-to-all-start.3 = ((bf16[32,32,512]{2,1,0:T(8,128)(2,1)}), bf16[32,32,512]{2,1,0:T(8,128)(2,1)S(1)}, u32[]{:S(2)}, u32[]{:S(2)}) async-start(bf16[32,32,512]{2,1,0:T(8,128)(2,1)} %bitcast.19), calls=%async_computation.3 | async-start | bytes 2097152 | tf_op jit(solution)/shard_map/all_to_all | solution.py:684
  178.4 3.9 %shard_map.93.base_ref = f32[4,32,32,128]{3,2,1,0:T(8,128)} custom-call(f32[4,32,32,128]{3,2,1,0:T(8,128)} %get-tuple-element.26.current_ref, f32[4,32,32,128]{3,2,1,0:T(8,128)} %copy-done, f32[5,128,128]{2,1,0:T(8,128)} %get-tuple-element.24.weight_ref, bf16[256,256]{1,0:T(8,128)(2,1)} %get-tuple-element.47.right_ref), custom_call_target="tpu_custom_call" | custom-call | bytes 9306112 | tf_op jit(solution)/shard_map/pallas_call | solution.py:507
  182.4 22.3 %all-to-all-done.3.coupled_ref = bf16[32,32,512]{2,1,0:T(8,128)(2,1)S(1)} async-done(((bf16[32,32,512]{2,1,0:T(8,128)(2,1)}), bf16[32,32,512]{2,1,0:T(8,128)(2,1)S(1)}, u32[]{:S(2)}, u32[]{:S(2)}) %all-to-all-start.3) | async-done | bytes 1048608 | tf_op jit(solution)/shard_map/all_to_all | solution.py:684
  205.7 4.9 %shard_map.96 = (f32[4,32,32,128]{3,2,1,0:T(8,128)}, bf16[4,32,32,128]{3,2,1,0:T(8,128)(2,1)}) custom-call(f32[4,32,32,128]{3,2,1,0:T(8,128)} %shard_map.93.base_ref, bf16[32,32,512]{2,1,0:T(8,128)(2,1)} %copy-done.2), custom_call_target="tpu_custom_call" | custom-call | bytes 6291456 | tf_op jit(solution)/shard_map/pallas_call | solution.py:507
  210.7 2.0 constant_dynamic-slice_fusion.8
  215.7 5.8 %shard_map.97 = bf16[4,32,32,128]{3,2,1,0:T(8,128)(2,1)} custom-call(f32[4,32,32,128]{3,2,1,0:T(8,128)} %get-tuple-element.26.current_ref, f32[4,32,32,128]{3,2,1,0:T(8,128)} %get-tuple-element.28.resid_ref, bf16[256,256]{1,0:T(8,128)(2,1)} %get-tuple-element.47.right_ref, bf16[256,256]{1,0:T(8,128)(2,1)} %get-tuple-element.46.left_ref, ...), custom_call_target="tpu_custom_call" | custom-call | flops 1610612736 | bytes 9043968 | tf_op jit(solution)/shard_map/pallas_call | solution.py:507
  221.4 3.5 %all-to-all-start.4 = ((bf16[128,32,128]{2,1,0:T(8,128)(2,1)}), bf16[128,32,128]{2,1,0:T(8,128)(2,1)S(1)}, u32[]{:S(2)}, u32[]{:S(2)}) async-start(bf16[128,32,128]{2,1,0:T(8,128)(2,1)} %bitcast.25), calls=%async_computation.4 | async-start | bytes 2097152 | tf_op jit(solution)/shard_map/all_to_all | solution.py:640
  227.2 1.8 fusion.11
  229.0 10.4 %all-to-all-done.4 = bf16[128,32,128]{2,1,0:T(8,128)(2,1)S(1)} async-done(((bf16[128,32,128]{2,1,0:T(8,128)(2,1)}), bf16[128,32,128]{2,1,0:T(8,128)(2,1)S(1)}, u32[]{:S(2)}, u32[]{:S(2)}) %all-to-all-start.4) | async-done | bytes 1048608 | tf_op jit(solution)/shard_map/all_to_all | solution.py:640
  239.4 2.2 fusion.10
  (81 shorter events, 30.2 us)
Async XLA Ops:
  0.6 6.0 %copy-start.13 = (f32[32,128]{1,0:T(8,128)S(1)}, f32[32,128]{1,0:T(8,128)}, u32[]{:S(2)}) copy-start(f32[32,128]{1,0:T(8,128)} %param.9) | copy-start | bytes 49156
  0.6 6.0 %copy-start.12 = (f32[3,32,128]{2,1,0:T(8,128)S(1)}, f32[3,32,128]{2,1,0:T(8,128)}, u32[]{:S(2)}) copy-start(f32[3,32,128]{2,1,0:T(8,128)} %param.10) | copy-start | bytes 147460
  6.6 37.1 %all-to-all-start = ((bf16[8,128,512]{2,1,0:T(8,128)(2,1)}), bf16[8,128,512]{2,1,0:T(8,128)(2,1)S(1)}, u32[]{:S(2)}, u32[]{:S(2)}) async-start(bf16[8,128,512]{2,1,0:T(8,128)(2,1)} %shard_map.86), calls=%async_computation | async-start | bytes 2097152 | tf_op jit(solution)/shard_map/all_to_all | solution.py:635
  13.9 16.3 %collective-permute-start.5 = (f32[1,4,32,128]{3,2,1,0:T(8,128)S(1)}, f32[1,4,32,128]{3,2,1,0:T(8,128)}, u32[]{:S(2)}, u32[]{:S(2)}) collective-permute-start(f32[1,4,32,128]{3,2,1,0:T(8,128)S(1)} %bitcast.26), channel_id=1, source_target_pairs={{0,1},{1,2},{2,3},{3,0},{4,5},{5,6},{6,7},{7,4},{8,9},{9,10},{10,1... | collective-permute-start | bytes 196616 | tf_op jit(solution)/shard_map/ppermute | solution.py:599
  13.9 18.5 %collective-permute-start.6 = (f32[1,4,32,128]{3,2,1,0:T(8,128)S(1)}, f32[1,4,32,128]{3,2,1,0:T(8,128)}, u32[]{:S(2)}, u32[]{:S(2)}) collective-permute-start(f32[1,4,32,128]{3,2,1,0:T(8,128)S(1)} %bitcast.27), channel_id=1, source_target_pairs={{0,2},{1,3},{2,0},{3,1},{4,6},{5,7},{6,4},{7,5},{8,10},{9,11},{10,... | collective-permute-start | bytes 196616 | tf_op jit(solution)/shard_map/ppermute | solution.py:599
  15.5 17.8 %collective-permute-start.7 = (f32[1,4,32,128]{3,2,1,0:T(8,128)S(1)}, f32[1,4,32,128]{3,2,1,0:T(8,128)S(1)}, u32[]{:S(2)}, u32[]{:S(2)}) collective-permute-start(f32[1,4,32,128]{3,2,1,0:T(8,128)S(1)} %bitcast.28), channel_id=1, source_target_pairs={{0,3},{1,0},{2,1},{3,2},{4,7},{5,4},{6,5},{7,6},{8,11},{9,8},{10,9... | collective-permute-start | bytes 196616 | tf_op jit(solution)/shard_map/ppermute | solution.py:599
  19.8 16.2 %collective-permute-start = (f32[1,32,32,128]{3,2,1,0:T(8,128)}, f32[1,32,32,128]{3,2,1,0:T(8,128)}, u32[]{:S(2)}, u32[]{:S(2)}) collective-permute-start(f32[1,32,32,128]{3,2,1,0:T(8,128)} %get-tuple-element.36), channel_id=1, source_target_pairs={{0,1},{1,2},{2,3},{3,0},{4,5},{5,6},{6,7},{7,4},{8,9},{9,10},{10,1... | collective-permute-start | bytes 1572872 | tf_op jit(solution)/shard_map/ppermute | solution.py:599
  19.8 17.2 %collective-permute-start.1 = (f32[1,32,32,128]{3,2,1,0:T(8,128)}, f32[1,32,32,128]{3,2,1,0:T(8,128)}, u32[]{:S(2)}, u32[]{:S(2)}) collective-permute-start(f32[1,32,32,128]{3,2,1,0:T(8,128)} %get-tuple-element.35), channel_id=1, source_target_pairs={{0,2},{1,3},{2,0},{3,1},{4,6},{5,7},{6,4},{7,5},{8,10},{9,11},{10,... | collective-permute-start | bytes 1572872 | tf_op jit(solution)/shard_map/ppermute | solution.py:599
  30.2 13.5 %collective-permute-start.2 = (f32[1,32,32,128]{3,2,1,0:T(8,128)}, f32[1,32,32,128]{3,2,1,0:T(8,128)S(1)}, u32[]{:S(2)}, u32[]{:S(2)}) collective-permute-start(f32[1,32,32,128]{3,2,1,0:T(8,128)} %get-tuple-element.34), channel_id=1, source_target_pairs={{0,3},{1,0},{2,1},{3,2},{4,7},{5,4},{6,5},{7,6},{8,11},{9,8},{10,9... | collective-permute-start | bytes 1572872 | tf_op jit(solution)/shard_map/ppermute | solution.py:599
  43.7 1.3 copy-start.1
  43.7 6.3 %copy-start.3 = (bf16[8,128,512]{2,1,0:T(8,128)(2,1)}, bf16[8,128,512]{2,1,0:T(8,128)(2,1)S(1)}, u32[]{:S(2)}) copy-start(bf16[8,128,512]{2,1,0:T(8,128)(2,1)S(1)} %all-to-all-done) | copy-start | bytes 3145732
  43.7 2.7 %copy-start.5 = (f32[128,32,128]{2,1,0:T(8,128)S(1)}, f32[128,32,128]{2,1,0:T(8,128)}, u32[]{:S(2)}) copy-start(f32[128,32,128]{2,1,0:T(8,128)} %param.8) | copy-start | bytes 6291460
  47.6 28.9 %collective-permute-start.8 = (f32[1,32,32,128]{3,2,1,0:T(8,128)}, f32[1,32,32,128]{3,2,1,0:T(8,128)}, u32[]{:S(2)}, u32[]{:S(2)}) collective-permute-start(f32[1,32,32,128]{3,2,1,0:T(8,128)} %get-tuple-element.32), channel_id=1, source_target_pairs={{0,1},{1,2},{2,3},{3,0},{4,5},{5,6},{6,7},{7,4},{8,9},{9,10},{10,1... | collective-permute-start | bytes 1572872 | tf_op jit(solution)/shard_map/ppermute | solution.py:599
  49.8 26.7 %collective-permute-start.9 = (f32[1,32,32,128]{3,2,1,0:T(8,128)S(1)}, f32[1,32,32,128]{3,2,1,0:T(8,128)}, u32[]{:S(2)}, u32[]{:S(2)}) collective-permute-start(f32[1,32,32,128]{3,2,1,0:T(8,128)S(1)} %get-tuple-element.31), channel_id=1, source_target_pairs={{0,3},{1,0},{2,1},{3,2},{4,7},{5,4},{6,5},{7,6},{8,11},{9,8},{10,9... | collective-permute-start | bytes 1572872 | tf_op jit(solution)/shard_map/ppermute | solution.py:599
  50.7 14.1 %collective-permute-start.3 = (bf16[1024,128]{1,0:T(8,128)(2,1)}, bf16[1024,128]{1,0:T(8,128)(2,1)S(1)}, u32[]{:S(2)}, u32[]{:S(2)}) collective-permute-start(bf16[1024,128]{1,0:T(8,128)(2,1)} %get-tuple-element.45), channel_id=1, source_target_pairs={{0,4},{4,8},{8,12},{12,16},{16,20},{20,24},{24,28},{28,1},{1,5},{5... | collective-permute-start | bytes 786440 | tf_op jit(solution)/shard_map/ppermute | solution.py:322
  52.8 13.9 %collective-permute-start.4 = (bf16[1024,128]{1,0:T(8,128)(2,1)S(1)}, bf16[1024,128]{1,0:T(8,128)(2,1)S(1)}, u32[]{:S(2)}, u32[]{:S(2)}) collective-permute-start(bf16[1024,128]{1,0:T(8,128)(2,1)S(1)} %get-tuple-element.44), channel_id=1, source_target_pairs={{4,0},{8,4},{12,8},{16,12},{20,16},{24,20},{28,24},{1,28},{5,1},{9... | collective-permute-start | bytes 786440 | tf_op jit(solution)/shard_map/ppermute | solution.py:323
  64.8 1.9 copy-start.9
  76.6 36.8 %all-to-all-start.1 = ((bf16[32,32,640]{2,1,0:T(8,128)(2,1)}), bf16[32,32,640]{2,1,0:T(8,128)(2,1)S(1)}, u32[]{:S(2)}, u32[]{:S(2)}) async-start(bf16[32,32,640]{2,1,0:T(8,128)(2,1)} %bitcast.18), calls=%async_computation.1 | async-start | bytes 2621440 | tf_op jit(solution)/shard_map/all_to_all | solution.py:675
  80.2 26.4 %collective-permute-start.10 = (f32[1,32,32,128]{3,2,1,0:T(8,128)}, f32[1,32,32,128]{3,2,1,0:T(8,128)S(1)}, u32[]{:S(2)}, u32[]{:S(2)}) collective-permute-start(f32[1,32,32,128]{3,2,1,0:T(8,128)} %get-tuple-element.30), channel_id=1, source_target_pairs={{0,2},{1,3},{2,0},{3,1},{4,6},{5,7},{6,4},{7,5},{8,10},{9,11},{10,... | collective-permute-start | bytes 1572872 | tf_op jit(solution)/shard_map/ppermute | solution.py:599
  107.8 1.3 copy-start
  113.4 1.1 copy-start.6
  153.8 5.4 %copy-start.4 = (bf16[32,32,512]{2,1,0:T(8,128)(2,1)}, bf16[32,32,512]{2,1,0:T(8,128)(2,1)S(1)}, u32[]{:S(2)}) copy-start(bf16[32,32,512]{2,1,0:T(8,128)(2,1)S(1)} %all_to_all.36) | copy-start | bytes 3145732
  153.9 13.6 %collective-permute-start.11 = (bf16[1024,128]{1,0:T(8,128)(2,1)S(1)}, bf16[1024,128]{1,0:T(8,128)(2,1)S(1)}, u32[]{:S(2)}, u32[]{:S(2)}) collective-permute-start(bf16[1024,128]{1,0:T(8,128)(2,1)S(1)} %get-tuple-element.43), channel_id=1, source_target_pairs={{0,4},{4,8},{8,12},{12,16},{16,20},{20,24},{24,28},{28,1},{1,5},{5... | collective-permute-start | bytes 786440 | tf_op jit(solution)/shard_map/ppermute | solution.py:322
  155.4 13.0 %collective-permute-start.12 = (bf16[1024,128]{1,0:T(8,128)(2,1)S(1)}, bf16[1024,128]{1,0:T(8,128)(2,1)S(1)}, u32[]{:S(2)}, u32[]{:S(2)}) collective-permute-start(bf16[1024,128]{1,0:T(8,128)(2,1)S(1)} %get-tuple-element.42), channel_id=1, source_target_pairs={{4,0},{8,4},{12,8},{16,12},{20,16},{24,20},{28,24},{1,28},{5,1},{9... | collective-permute-start | bytes 786440 | tf_op jit(solution)/shard_map/ppermute | solution.py:323
  167.5 0.9 copy-start.8
  168.4 0.7 copy-start.10
  174.7 30.0 %all-to-all-start.3 = ((bf16[32,32,512]{2,1,0:T(8,128)(2,1)}), bf16[32,32,512]{2,1,0:T(8,128)(2,1)S(1)}, u32[]{:S(2)}, u32[]{:S(2)}) async-start(bf16[32,32,512]{2,1,0:T(8,128)(2,1)} %bitcast.19), calls=%async_computation.3 | async-start | bytes 2097152 | tf_op jit(solution)/shard_map/all_to_all | solution.py:684
  204.7 1.0 copy-start.2
  212.7 12.2 %collective-permute-start.13 = (bf16[1,32,32,128]{3,2,1,0:T(8,128)(2,1)}, bf16[1,32,32,128]{3,2,1,0:T(8,128)(2,1)S(1)}, u32[]{:S(2)}, u32[]{:S(2)}) collective-permute-start(bf16[1,32,32,128]{3,2,1,0:T(8,128)(2,1)} %get-tuple-element.40), channel_id=1, source_target_pairs={{0,1},{1,2},{2,3},{3,0},{4,5},{5,6},{6,7},{7,4},{8,9},{9,10},{10,1... | collective-permute-start | bytes 786440 | tf_op jit(solution)/shard_map/ppermute | solution.py:599
  212.7 12.3 %collective-permute-start.14 = (bf16[1,32,32,128]{3,2,1,0:T(8,128)(2,1)S(1)}, bf16[1,32,32,128]{3,2,1,0:T(8,128)(2,1)S(1)}, u32[]{:S(2)}, u32[]{:S(2)}) collective-permute-start(bf16[1,32,32,128]{3,2,1,0:T(8,128)(2,1)S(1)} %get-tuple-element.39), channel_id=1, source_target_pairs={{0,2},{1,3},{2,0},{3,1},{4,6},{5,7},{6,4},{7,5},{8,10},{9,11},{10,... | collective-permute-start | bytes 786440 | tf_op jit(solution)/shard_map/ppermute | solution.py:599
  214.2 11.9 %collective-permute-start.15 = (bf16[1,32,32,128]{3,2,1,0:T(8,128)(2,1)S(1)}, bf16[1,32,32,128]{3,2,1,0:T(8,128)(2,1)S(1)}, u32[]{:S(2)}, u32[]{:S(2)}) collective-permute-start(bf16[1,32,32,128]{3,2,1,0:T(8,128)(2,1)S(1)} %get-tuple-element.38), channel_id=1, source_target_pairs={{0,3},{1,0},{2,1},{3,2},{4,7},{5,4},{6,5},{7,6},{8,11},{9,8},{10,9... | collective-permute-start | bytes 786440 | tf_op jit(solution)/shard_map/ppermute | solution.py:599
  221.4 18.0 %all-to-all-start.4 = ((bf16[128,32,128]{2,1,0:T(8,128)(2,1)}), bf16[128,32,128]{2,1,0:T(8,128)(2,1)S(1)}, u32[]{:S(2)}, u32[]{:S(2)}) async-start(bf16[128,32,128]{2,1,0:T(8,128)(2,1)} %bitcast.25), calls=%async_computation.4 | async-start | bytes 2097152 | tf_op jit(solution)/shard_map/all_to_all | solution.py:640
  (2 other events, 1.4 us)

commit v7 on v6

--- a/solution.py
+++ b/solution.py
@@ -10,6 +10,7 @@
 
 RELAXATION = 0.6
 VMEM_BYTES = 60 << 20
+SHARED_VMEM_BYTES = 32 << 20
 UNROLL = 4
 
 
@@ -84,7 +85,7 @@
             jax.ShapeDtypeStruct((5, nx, ny), jnp.float32),
             jax.ShapeDtypeStruct((fields * 5 * height, ny), jnp.float32),
         ],
-        compiler_params=pltpu.CompilerParams(vmem_limit_bytes=VMEM_BYTES),
+        compiler_params=pltpu.CompilerParams(vmem_limit_bytes=SHARED_VMEM_BYTES),
     )(strip.reshape(1), coefs)
 
 
@@ -161,9 +162,9 @@
     height = rows // strips
     return pl.pallas_call(
         functools.partial(pack_kernel, rows, height),
-        grid=(modes // GROUP,),
-        in_specs=[pl.BlockSpec((GROUP * rows, cols), lambda g: (g, 0))],
-        out_specs=pl.BlockSpec((strips, GROUP, height * cols), lambda g: (0, g, 0)),
+        grid=(2,),
+        in_specs=[pl.BlockSpec((modes // 2 * rows, cols), lambda g: (g, 0))],
+        out_specs=pl.BlockSpec((strips, modes // 2, height * cols), lambda g: (0, g, 0)),
         out_shape=jax.ShapeDtypeStruct((strips, modes, height * cols), jnp.bfloat16),
         compiler_params=pltpu.CompilerParams(vmem_limit_bytes=VMEM_BYTES),
     )(block.reshape(modes * rows, cols))
@@ -196,7 +197,7 @@
             ),
         ),
         out_shape=jax.ShapeDtypeStruct((blocks, fields, width, blocks * width), coupling.dtype),
-        compiler_params=pltpu.CompilerParams(vmem_limit_bytes=VMEM_BYTES),
+        compiler_params=pltpu.CompilerParams(vmem_limit_bytes=SHARED_VMEM_BYTES),
     )(coupling_list, pair_count, coupling)
 
 
@@ -228,15 +229,14 @@
     return weight_ref[at : at + 1, :]
 
 
-def inner_kernel(height, cols, matrix_ref, state_ref, weight_ref, out_ref, *sums_refs):
+def inner_kernel(height, cols, matrix_ref, state_ref, weight_ref, out_ref, sums_ref):
     blocks, fields, width, depth = matrix_ref.shape
+    sums_ref[...] = jnp.dot(
+        matrix_ref[...].reshape(blocks * fields * width, depth),
+        state_ref[...],
+        preferred_element_type=jnp.float32,
+    )
     for block in range(blocks):
-        sums_ref = sums_refs[block % len(sums_refs)]
-        sums_ref[...] = jnp.dot(
-            matrix_ref[block].reshape(fields * width, depth),
-            state_ref[...],
-            preferred_element_type=jnp.float32,
-        )
         for r in range(height):
             total = 0.0
             from_left = 0.0
@@ -244,7 +244,8 @@
             for f in range(fields):
 
                 def row(at):
-                    return sums_ref[f * width : (f + 1) * width, at * cols : (at + 1) * cols]
+                    start = (block * fields + f) * width
+                    return sums_ref[start : start + width, at * cols : (at + 1) * cols]
 
                 weight = functools.partial(weight_row, weight_ref, height, f)
                 here = row(r)
@@ -275,15 +276,15 @@
     blocks, fields, width, depth = matrix_ref.shape
     border = jnp.concatenate([above_ref[...], below_ref[...]], axis=1)
     low_col = lax.broadcasted_iota(jnp.int32, (width, cols), 1) < LOW
+    matrix = matrix_ref[...].reshape(blocks * fields * width, depth)
+    sums = jnp.dot(matrix, border, preferred_element_type=jnp.float32)
     for block in range(blocks):
-        matrix = matrix_ref[block].reshape(fields * width, depth)
-        sums = jnp.dot(matrix, border, preferred_element_type=jnp.float32)
         modes = slice(block * width, (block + 1) * width)
         rows = []
         for r in range(height):
             total = inner_ref[modes, r * cols : (r + 1) * cols]
             for f in range(fields):
-                part = sums[f * width : (f + 1) * width]
+                part = sums[(block * fields + f) * width : (block * fields + f + 1) * width]
                 if r == 0:
                     total = total - weight_row(weight_ref, height, f, 1, r) * part[:, :cols]
                 if r == height - 1:
@@ -325,14 +326,14 @@
     matrix_spec = pl.BlockSpec((unroll, fields, width, depth), lambda i: (i, 0, 0, 0))
     weight_spec = pl.BlockSpec(weights.shape, lambda i: (0, 0))
     sums_spec = pl.BlockSpec((unroll * width, cells), lambda i: (i, 0))
-    params = pltpu.CompilerParams(vmem_limit_bytes=VMEM_BYTES)
+    params = pltpu.CompilerParams(vmem_limit_bytes=SHARED_VMEM_BYTES)
     inner = pl.pallas_call(
         functools.partial(inner_kernel, height, cols),
         grid=(blocks // unroll,),
         in_specs=[matrix_spec, pl.BlockSpec((depth, cells), lambda i: (0, 0)), weight_spec],
         out_specs=sums_spec,
         out_shape=jax.ShapeDtypeStruct((blocks * width, cells), jnp.float32),
-        scratch_shapes=[pltpu.VMEM((fields * width, cells), jnp.float32)] * 2,
+        scratch_shapes=[pltpu.VMEM((unroll * fields * width, cells), jnp.float32)],
         cost_estimate=pl.CostEstimate(
             flops=2 * matrix.size * cells, bytes_accessed=2 * matrix.size, transcendentals=0
         ),
@@ -455,8 +456,9 @@
 
 
 def residual_kernel(
-    mode_count, slab_count, code_scale, base_ref, coupled_ref, out_ref, code_ref, turned_ref
+    mode_count, slab_count, code_scale, here_ref, base_ref, coupled_ref, out_ref, *refs
 ):
+    *code_refs, turned_ref = refs
     group = coupled_ref.shape[1]
     ny = base_ref.shape[-1]
     nx = turned_ref.shape[0] // group
@@ -465,12 +467,13 @@
 
     def one(mode, carry):
         coupled = turned_ref[pl.ds(mode, nx, stride=group), :]
-        value = base_ref[:, mode] - coupled.reshape(slab_count, nx // slab_count, ny)
-        out_ref[:, mode] = value
-        code_ref[:, mode] = encode(value * code_scale, SUM_POWER)
+        out_ref[:, mode] = base_ref[:, mode] - coupled.reshape(slab_count, nx // slab_count, ny)
         return carry
 
     lax.fori_loop(0, group, one, 0)
+    for shift, code_ref in enumerate(code_refs):
+        slab = lax.rem(here_ref[0] + shift, slab_count)
+        code_ref[0] = encode(out_ref[slab] * code_scale, SUM_POWER)
 
 
 def correct_kernel(code_scale, current_ref, resid_ref, right_ref, left_ref, scale_ref, out_ref):
@@ -555,19 +558,26 @@
 
 def last_residual(base, coupled, mode_count, slab_count, code_scale):
     slab, modes, rows, ny = base.shape
-    slabs = slabs_of(base)
-    return per_group(
+    slabs = pl.BlockSpec((slab, GROUP, rows, ny), lambda g, *_: (0, g, 0, 0))
+    part = pl.BlockSpec((1, GROUP, rows, ny), lambda g, *_: (0, g, 0, 0))
+    devices, _, cells = coupled.shape
+    out, *parts = pl.pallas_call(
         functools.partial(residual_kernel, mode_count, slab_count, code_scale),
-        modes // GROUP,
-        (base, coupled),
-        [slabs, strips_of(coupled.shape)],
-        [
-            jax.ShapeDtypeStruct(base.shape, jnp.float32),
-            jax.ShapeDtypeStruct(base.shape, jnp.bfloat16),
-        ],
-        [slabs, slabs],
-        [pltpu.VMEM((slab * rows * GROUP, ny), jnp.float32)],
-    )
+        grid_spec=pltpu.PrefetchScalarGridSpec(
+            num_scalar_prefetch=1,
+            grid=(modes // GROUP,),
+            in_specs=[slabs, pl.BlockSpec((devices, GROUP, cells), lambda g, *_: (0, g, 0))],
+            out_specs=[slabs] + [part] * slab,
+            scratch_shapes=[pltpu.VMEM((slab * rows * GROUP, ny), jnp.float32)],
+        ),
+        out_shape=[jax.ShapeDtypeStruct(base.shape, jnp.float32)]
+        + [jax.ShapeDtypeStruct((1, modes, rows, ny), jnp.bfloat16)] * slab,
+        cost_estimate=pl.CostEstimate(
+            flops=0, bytes_accessed=2 * base.size * 4, transcendentals=0
+        ),
+        compiler_params=pltpu.CompilerParams(vmem_limit_bytes=VMEM_BYTES),
+    )(lax.axis_index("slab").reshape(1), base, coupled)
+    return out, parts
 
 
 def correct(current, resid, tables, code_scale):
@@ -599,18 +609,16 @@
     return lax.ppermute(part, axis, [(i, (i + shift) % count) for i in range(count)])
 
 
-def regroup_parts(block, axis):
+def parts_of(block, axis):
     count = lax.axis_size(axis)
     here = lax.axis_index(axis)
-    parts = [lax.dynamic_index_in_dim(block, here, 0)]
-    for shift in range(1, count):
-        target = lax.rem(here + shift, count)
-        parts.append(onwards(lax.dynamic_index_in_dim(block, target, 0), axis, shift))
-    return parts
-
-
-def regroup(block, axis):
-    return collect(regroup_parts(block, axis), axis)
+    return [
+        lax.dynamic_index_in_dim(block, lax.rem(here + shift, count), 0) for shift in range(count)
+    ]
+
+
+def moved_parts(parts, axis):
+    return [parts[0]] + [onwards(parts[i], axis, i) for i in range(1, len(parts))]
 
 
 def spread(block, axis):
@@ -640,9 +648,11 @@
         return lax.all_to_all(flat, "slab", 0, 0, tiled=True)
 
     coefs = spread(coefs, "slab")
-    current = regroup(guess.reshape(slab_count, share, rows, cols), "slab")
-    state, current, right_side = lax.optimization_barrier((state, current, right_side))
-    right_parts = regroup_parts(right_side.reshape(slab_count, share, rows, cols), "slab")
+    guess_parts = parts_of(guess.reshape(slab_count, share, rows, cols), "slab")
+    current = collect(moved_parts(guess_parts, "slab"), "slab")
+    right_parts = parts_of(right_side.reshape(slab_count, share, rows, cols), "slab")
+    state, current, right_parts = lax.optimization_barrier((state, current, right_parts))
+    right_side = collect(moved_parts(right_parts, "slab"), "slab")
 
     strip = lax.axis_index("slab") * mode_count + lax.axis_index("mode")
     mean_weights, strip_weights = all_weights(coefs, strip, height)
@@ -671,9 +681,8 @@
     first_scale, sum_scale, solution_scale = code_scales(nx, cols, coupling.shape[1], modes)
 
     sums = coupled_sums(matrix, state, strip_weights, tables[0], True, first_scale, both)
-    sums, *right_parts[1::2] = lax.optimization_barrier((sums, *right_parts[1::2]))
+    sums, right_side = lax.optimization_barrier((sums, right_side))
     sums = lax.all_to_all(sums, both, 0, 0, tiled=True).reshape(devices, share, -1)
-    right_side = collect(right_parts, "slab")
     base = mean_part(current, right_side, mean_weights, tables[0], True)
     current, state = step(current, base, sums, tables, mode_count, slab_count, first_scale)
     state = state.reshape(devices * share, height * cols)
@@ -682,8 +691,8 @@
     base = mean_part(current, right_side, mean_weights, tables[0], False)
     sums = coupled_sums(matrix, state, strip_weights, tables[0], False, sum_scale, both)
     sums = lax.all_to_all(sums, both, 0, 0, tiled=True).reshape(devices, share, -1)
-    resid, code = last_residual(base, sums, mode_count, slab_count, sum_scale)
-    moved = regroup(code, "slab").reshape(modes, rows, cols)
+    resid, parts = last_residual(base, sums, mode_count, slab_count, sum_scale)
+    moved = collect(moved_parts(parts, "slab"), "slab").reshape(modes, rows, cols)
     resid_out = decode(moved, SUM_POWER) * (1.0 / sum_scale)
     code = correct(current, resid, tables, solution_scale)
     return decode(to_slabs(code), SOLUTION_POWER) * (1.0 / solution_scale), resid_out

time: 243 us -> 232 us (0.955)
  Pallas kernels: 73.8 us -> 51.3 us
  local copies, waits for them, and re-layouts: 21.6 us -> 27.6 us
  waiting for transfers between devices: 65.3 us -> 71.3 us
    all_to_all x2, waiting for transfers between devices: 22.3 us -> 49.4 us  [local(): lax.all_to_all(sums, both, 0, 0, tiled=True).reshape(devices, share, -1)]
    ppermute x12, waiting for transfers between devices: 29.3 us -> 10.4 us  [onwards(): lax.ppermute(part, axis, [(i, (i + shift) % count) for i in range(count)])]
    unnamed x28 -> x42, local copies, waits for them, and re-layouts: 8 us -> 15.5 us
    pallas_call x2, Pallas kernels: 14.7 us -> 8.13 us  [coupled_sums(): pl.pallas_call(functools.partial(border_kernel, height, cols, first, scal...]
    pallas_call x1, Pallas kernels: 8.7 us -> 2.66 us  [dense_coupling(): pl.pallas_call(functools.partial(dense_kernel, fields), grid_spec=pltpu.P...]
    pallas_call x2, Pallas kernels: 16.4 us -> 10.7 us  [coupled_sums(): pl.pallas_call(functools.partial(inner_kernel, height, cols), grid=(block...]
    pallas_call x5 -> x4, Pallas kernels: 26 us -> 21.1 us  [per_group(): pl.pallas_call(kernel, grid=(groups,), in_specs=in_specs, out_specs=out_s...]
    dynamic_slice x3 -> x2, local copies, waits for them, and re-layouts: 5.89 us -> 2.72 us  [parts_of(): lax.dynamic_index_in_dim(block, lax.rem(here + shift, count), 0)]
  transfers between devices with their start and end apart: 20 -> 20, of which waited for: 8 -> 8; matrix products, arithmetic and copies ran while one was open for 6% -> 7% of each run, Pallas kernels for 21% -> 14%
where the time goes in v7:
time: 232 us; the launch traced here: 231 us
  waiting for transfers between devices  71.3 us (31%)
  Pallas kernels  51.3 us (22%)
  starting transfers between devices  43.2 us (19%)
  blocking collectives  29.8 us (13%)
  local copies, waits for them, and re-layouts  27.6 us (12%)
  other arithmetic  6.72 us (3%)
    all_to_all x2, waiting for transfers between devices, local(): lax.all_to_all(sums, both, 0, 0, tiled=True).reshape(devices, share, -1)  49.4 us
    all_to_all x1, blocking collectives, local(): state = lax.all_to_all(state, both, 0, 0, tiled=True)  29.8 us
    pallas_call x4, Pallas kernels, per_group(): pl.pallas_call(kernel, grid=(groups,), in_specs=in_specs, out_specs=out_s...  21.1 us
    unnamed x42, local copies, waits for them, and re-layouts  15.5 us
    ppermute x12, starting transfers between devices, onwards(): lax.ppermute(part, axis, [(i, (i + shift) % count) for i in range(count)])  11.2 us
    pallas_call x2, Pallas kernels, coupled_sums(): pl.pallas_call(functools.partial(inner_kernel, height, cols), grid=(block...  10.7 us
    all_to_all x1, waiting for transfers between devices, to_slabs(): return lax.all_to_all(flat, 'slab', 0, 0, tiled=True)  10.5 us
    ppermute x12, waiting for transfers between devices, onwards(): lax.ppermute(part, axis, [(i, (i + shift) % count) for i in range(count)])  10.4 us
  transfers between devices with their start and end apart: 20, of which 8 were waited for; matrix products, arithmetic and copies ran while one was open for 7% of the time, Pallas kernels for 14%

profile of v7, /device:TPU:0, one launch (start us, length us, event | category | flops | bytes accessed | tf_op | source)
XLA Modules:
  0.0 231.0 jit_solution(11545312116301805665)
XLA Ops:
  0.6 3.3 %shard_map.86 = bf16[8,128,512]{2,1,0:T(8,128)(2,1)} custom-call(f32[4096,128]{1,0:T(8,128)} %bitcast.23), custom_call_target="tpu_custom_call" | custom-call | tf_op jit(solution)/shard_map/pallas_call | solution.py:163
  4.0 7.4 %all-to-all-start = ((bf16[8,128,512]{2,1,0:T(8,128)(2,1)}), bf16[8,128,512]{2,1,0:T(8,128)(2,1)S(1)}, u32[]{:S(2)}, u32[]{:S(2)}) async-start(bf16[8,128,512]{2,1,0:T(8,128)(2,1)} %shard_map.86), calls=%async_computation | async-start | bytes 2097152 | tf_op jit(solution)/shard_map/all_to_all | solution.py:643
  14.4 1.6 broadcast.88.clone
  20.4 2.2 copy-done.4
  22.6 2.7 %shard_map.87.matrix_ref = bf16[8,3,128,1024]{3,2,1,0:T(8,128)(2,1)S(1)} custom-call(s32[8,16]{1,0:T(8,128)S(1)} %copy-done.8, s32[8]{0:T(128)S(1)} %copy-done.9, bf16[8,16,128,128]{3,2,1,0:T(8,128)(2,1)S(1)} %copy-done.4), custom_call_target="tpu_custom_call" | custom-call | tf_op jit(solution)/shard_map/pallas_call | solution.py:189
  25.3 2.7 %copy-done = bf16[8,3,128,1024]{3,2,1,0:T(8,128)(2,1)} copy-done((bf16[8,3,128,1024]{3,2,1,0:T(8,128)(2,1)}, bf16[8,3,128,1024]{3,2,1,0:T(8,128)(2,1)S(1)}, u32[]{:S(2)}) %copy-start) | copy-done | bytes 6291480
  33.1 7.9 %collective-permute-done.2 = f32[1,32,32,128]{3,2,1,0:T(8,128)S(1)} collective-permute-done((f32[1,32,32,128]{3,2,1,0:T(8,128)S(1)}, f32[1,32,32,128]{3,2,1,0:T(8,128)S(1)}, u32[]{:S(2)}, u32[]{:S(2)}) %collective-permute-start.2) | collective-permute-done | bytes 524320 | tf_op jit(solution)/shard_map/ppermute | solution.py:609
  41.9 1.9 collective-permute-start.8
  45.2 2.1 collective-permute-start.3
  47.3 3.3 %collective-permute-start.4 = (bf16[1024,128]{1,0:T(8,128)(2,1)S(1)}, bf16[1024,128]{1,0:T(8,128)(2,1)S(1)}, u32[]{:S(2)}, u32[]{:S(2)}) collective-permute-start(bf16[1024,128]{1,0:T(8,128)(2,1)S(1)} %get-tuple-element.50), channel_id=1, source_target_pairs={{4,0},{8,4},{12,8},{16,12},{20,16},{24,20},{28,24},{1,28},{5,1},{9... | collective-permute-start | bytes 786440 | tf_op jit(solution)/shard_map/ppermute | solution.py:324
  53.0 2.8 %copy-done.1 = bf16[8,3,128,1024]{3,2,1,0:T(8,128)(2,1)S(1)} copy-done((bf16[8,3,128,1024]{3,2,1,0:T(8,128)(2,1)S(1)}, bf16[8,3,128,1024]{3,2,1,0:T(8,128)(2,1)}, u32[]{:S(2)}) %copy-start.1) | copy-done | bytes 6291480
  55.8 5.4 %shard_map.89.inner_ref = f32[1024,512]{1,0:T(8,128)S(1)} custom-call(bf16[8,3,128,1024]{3,2,1,0:T(8,128)(2,1)S(1)} %copy-done.1, bf16[1024,512]{1,0:T(8,128)(2,1)S(1)} %bitcast.20, f32[60,128]{1,0:T(8,128)S(1)} %get-tuple-element.25.weight_ref), custom_call_target="tpu_custom_call" | custom-call | flops 3221225472 | bytes 6291456 | tf_op jit(solution)/shard_map/pallas_call | solution.py:330
  61.2 5.1 %shard_map.90 = bf16[1024,640]{1,0:T(8,128)(2,1)} custom-call(bf16[8,3,128,1024]{3,2,1,0:T(8,128)(2,1)S(1)} %bitcast.18, bf16[1024,128]{1,0:T(8,128)(2,1)S(1)} %collective-permute-done.3.above_ref, bf16[1024,128]{1,0:T(8,128)(2,1)S(1)} %collective-permute-done.4.below_ref, f32[60,128]{1,0:T(8,128)S(1)} %get-tuple-element.25.weight_ref, ...), custom_call_target="tpu_custom_call" | custom-call | tf_op jit(solution)/shard_map/pallas_call | solution.py:344
  68.9 7.1 %all-to-all-start.1 = ((bf16[32,32,640]{2,1,0:T(8,128)(2,1)}), bf16[32,32,640]{2,1,0:T(8,128)(2,1)S(1)}, u32[]{:S(2)}, u32[]{:S(2)}) async-start(bf16[32,32,640]{2,1,0:T(8,128)(2,1)} %bitcast.7), calls=%async_computation.1 | async-start | bytes 2621440 | tf_op jit(solution)/shard_map/all_to_all | solution.py:685
  76.8 4.2 %shard_map.91.base_ref = f32[4,32,32,128]{3,2,1,0:T(8,128)} custom-call(f32[4,32,32,128]{3,2,1,0:T(8,128)} %constant_dynamic-update-slice_fusion.11.current_ref, f32[4,32,32,128]{3,2,1,0:T(8,128)} %constant_dynamic-update-slice_fusion.3.right_side_ref, f32[5,128,128]{2,1,0:T(8,128)} %copy-done.7, bf16[256,256]{1,0:T(8,128)(2,1)} %copy-done.5), custom_call_target="tpu_custom_call" | custom-call | bytes 9306112 | tf_op jit(solution)/shard_map/pallas_call | solution.py:510
  81.0 27.1 %all-to-all-done.1.coupled_ref = bf16[32,32,640]{2,1,0:T(8,128)(2,1)S(1)} async-done(((bf16[32,32,640]{2,1,0:T(8,128)(2,1)}), bf16[32,32,640]{2,1,0:T(8,128)(2,1)S(1)}, u32[]{:S(2)}, u32[]{:S(2)}) %all-to-all-start.1) | async-done | bytes 1310752 | tf_op jit(solution)/shard_map/all_to_all | solution.py:685
  109.2 7.2 %shard_map.92 = (f32[4,32,32,128]{3,2,1,0:T(8,128)}, bf16[32,32,512]{2,1,0:T(8,128)(2,1)}) custom-call(f32[4,32,32,128]{3,2,1,0:T(8,128)} %constant_dynamic-update-slice_fusion.11.current_ref, f32[4,32,32,128]{3,2,1,0:T(8,128)} %shard_map.91.base_ref, bf16[32,32,640]{2,1,0:T(8,128)(2,1)} %copy-done.14, bf16[256,256]{1,0:T(8,128)(2,1)} %copy-done.5, ...), custom_call_target="tpu_custom_call" | custom-call | flops 1610612736 | bytes 11665408 | tf_op jit(solution)/shard_map/pallas_call | solution.py:510
  116.4 29.8 %all_to_all.36 = bf16[32,32,512]{2,1,0:T(8,128)(2,1)S(1)} all-to-all(bf16[32,32,512]{2,1,0:T(8,128)(2,1)} %get-tuple-element.34), channel_id=1, replica_groups=mesh['mode'=8,'slab'=4] {'mode','slab'}, dimensions={0} | all-to-all | bytes 2097152 | tf_op jit(solution)/shard_map/all_to_all | solution.py:689
  147.8 3.9 %collective-permute-start.12 = (bf16[1024,128]{1,0:T(8,128)(2,1)S(1)}, bf16[1024,128]{1,0:T(8,128)(2,1)S(1)}, u32[]{:S(2)}, u32[]{:S(2)}) collective-permute-start(bf16[1024,128]{1,0:T(8,128)(2,1)S(1)} %get-tuple-element.48), channel_id=1, source_target_pairs={{4,0},{8,4},{12,8},{16,12},{20,16},{24,20},{28,24},{1,28},{5,1},{9... | collective-permute-start | bytes 786440 | tf_op jit(solution)/shard_map/ppermute | solution.py:324
  151.6 2.8 %copy-done.2 = bf16[8,3,128,1024]{3,2,1,0:T(8,128)(2,1)S(1)} copy-done((bf16[8,3,128,1024]{3,2,1,0:T(8,128)(2,1)S(1)}, bf16[8,3,128,1024]{3,2,1,0:T(8,128)(2,1)}, u32[]{:S(2)}) %copy-start.2) | copy-done | bytes 6291480
  154.4 5.4 %shard_map.94.inner_ref = f32[1024,512]{1,0:T(8,128)S(1)} custom-call(bf16[8,3,128,1024]{3,2,1,0:T(8,128)(2,1)S(1)} %copy-done.2, bf16[1024,512]{1,0:T(8,128)(2,1)S(1)} %bitcast.22, f32[60,128]{1,0:T(8,128)S(1)} %get-tuple-element.25.weight_ref), custom_call_target="tpu_custom_call" | custom-call | flops 3221225472 | bytes 6291456 | tf_op jit(solution)/shard_map/pallas_call | solution.py:330
  160.8 2.8 %copy-done.3 = bf16[8,3,128,1024]{3,2,1,0:T(8,128)(2,1)S(1)} copy-done((bf16[8,3,128,1024]{3,2,1,0:T(8,128)(2,1)S(1)}, bf16[8,3,128,1024]{3,2,1,0:T(8,128)(2,1)}, u32[]{:S(2)}) %copy-start.3) | copy-done | bytes 6291480
  163.6 3.0 %shard_map.95 = bf16[1024,512]{1,0:T(8,128)(2,1)} custom-call(bf16[8,3,128,1024]{3,2,1,0:T(8,128)(2,1)S(1)} %copy-done.3, bf16[1024,128]{1,0:T(8,128)(2,1)S(1)} %collective-permute-done.11.above_ref, bf16[1024,128]{1,0:T(8,128)(2,1)S(1)} %collective-permute-done.12.below_ref, f32[60,128]{1,0:T(8,128)S(1)} %get-tuple-element.25.weight_ref, ...), custom_call_target="tpu_custom_call" | custom-call | tf_op jit(solution)/shard_map/pallas_call | solution.py:344
  166.5 3.0 %all-to-all-start.3 = ((bf16[32,32,512]{2,1,0:T(8,128)(2,1)}), bf16[32,32,512]{2,1,0:T(8,128)(2,1)S(1)}, u32[]{:S(2)}, u32[]{:S(2)}) async-start(bf16[32,32,512]{2,1,0:T(8,128)(2,1)} %bitcast.10), calls=%async_computation.3 | async-start | bytes 2097152 | tf_op jit(solution)/shard_map/all_to_all | solution.py:693
  169.6 3.9 %shard_map.93.base_ref = f32[4,32,32,128]{3,2,1,0:T(8,128)} custom-call(f32[4,32,32,128]{3,2,1,0:T(8,128)} %get-tuple-element.33.current_ref, f32[4,32,32,128]{3,2,1,0:T(8,128)} %constant_dynamic-update-slice_fusion.3.right_side_ref, f32[5,128,128]{2,1,0:T(8,128)} %copy-done.7, bf16[256,256]{1,0:T(8,128)(2,1)} %copy-done.5), custom_call_target="tpu_custom_call" | custom-call | bytes 9306112 | tf_op jit(solution)/shard_map/pallas_call | solution.py:510
  173.5 22.3 %all-to-all-done.3.coupled_ref = bf16[32,32,512]{2,1,0:T(8,128)(2,1)S(1)} async-done(((bf16[32,32,512]{2,1,0:T(8,128)(2,1)}), bf16[32,32,512]{2,1,0:T(8,128)(2,1)S(1)}, u32[]{:S(2)}, u32[]{:S(2)}) %all-to-all-start.3) | async-done | bytes 1048608 | tf_op jit(solution)/shard_map/all_to_all | solution.py:693
  196.8 5.1 %shard_map.96 = (f32[4,32,32,128]{3,2,1,0:T(8,128)}, bf16[1,32,32,128]{3,2,1,0:T(8,128)(2,1)}, bf16[1,32,32,128]{3,2,1,0:T(8,128)(2,1)}, bf16[1,32,32,128]{3,2,1,0:T(8,128)(2,1)}, bf16[1,32,32,128]{3,2,1,0:T(8,128)(2,1)}) custom-call(s32[1]{0:T(128)} %bitcast.8.here_ref, f32[4,32,32,128]{3,2,1,0:T(8,128)} %shard_map.93.base_ref, bf16[32,32,512]{2,1,0:T(8,128)(2,1)} %copy-done.11), custom_call_target="tpu_custom_call" | custom-call | bytes 4194304 | tf_op jit(solution)/shard_map/pallas_call | solution.py:564
  204.9 5.8 %shard_map.97 = bf16[4,32,32,128]{3,2,1,0:T(8,128)(2,1)} custom-call(f32[4,32,32,128]{3,2,1,0:T(8,128)} %get-tuple-element.33.current_ref, f32[4,32,32,128]{3,2,1,0:T(8,128)} %get-tuple-element.35.resid_ref, bf16[256,256]{1,0:T(8,128)(2,1)} %copy-done.5, bf16[256,256]{1,0:T(8,128)(2,1)} %get-tuple-element.52.left_ref, f32[128,128]{1,0:T(8,128)} %subtract_divide_fusion.scale_ref), custom_call_target="tpu_custom_call" | custom-call | flops 1610612736 | bytes 9043968 | tf_op jit(solution)/shard_map/pallas_call | solution.py:510
  210.7 3.6 %all-to-all-start.4 = ((bf16[128,32,128]{2,1,0:T(8,128)(2,1)}), bf16[128,32,128]{2,1,0:T(8,128)(2,1)S(1)}, u32[]{:S(2)}, u32[]{:S(2)}) async-start(bf16[128,32,128]{2,1,0:T(8,128)(2,1)} %bitcast.26), calls=%async_computation.4 | async-start | bytes 2097152 | tf_op jit(solution)/shard_map/all_to_all | solution.py:648
  216.5 1.8 fusion.11
  218.3 10.5 %all-to-all-done.4 = bf16[128,32,128]{2,1,0:T(8,128)(2,1)S(1)} async-done(((bf16[128,32,128]{2,1,0:T(8,128)(2,1)}), bf16[128,32,128]{2,1,0:T(8,128)(2,1)S(1)}, u32[]{:S(2)}, u32[]{:S(2)}) %all-to-all-start.4) | async-done | bytes 1048608 | tf_op jit(solution)/shard_map/all_to_all | solution.py:648
  228.8 2.2 fusion.10
  (97 shorter events, 30.1 us)
Async XLA Ops:
  0.6 3.3 %copy-start.18 = (f32[32,128]{1,0:T(8,128)S(1)}, f32[32,128]{1,0:T(8,128)}, u32[]{:S(2)}) copy-start(f32[32,128]{1,0:T(8,128)} %param.9) | copy-start | bytes 49156
  0.6 3.3 %copy-start.17 = (f32[3,32,128]{2,1,0:T(8,128)S(1)}, f32[3,32,128]{2,1,0:T(8,128)}, u32[]{:S(2)}) copy-start(f32[3,32,128]{2,1,0:T(8,128)} %param.10) | copy-start | bytes 147460
  4.0 12.0 %copy-start.10 = (f32[128,32,128]{2,1,0:T(8,128)S(1)}, f32[128,32,128]{2,1,0:T(8,128)}, u32[]{:S(2)}) copy-start(f32[128,32,128]{2,1,0:T(8,128)} %param.7) | copy-start | bytes 6291460
  4.0 37.9 %all-to-all-start = ((bf16[8,128,512]{2,1,0:T(8,128)(2,1)}), bf16[8,128,512]{2,1,0:T(8,128)(2,1)S(1)}, u32[]{:S(2)}, u32[]{:S(2)}) async-start(bf16[8,128,512]{2,1,0:T(8,128)(2,1)} %shard_map.86), calls=%async_computation | async-start | bytes 2097152 | tf_op jit(solution)/shard_map/all_to_all | solution.py:643
  11.4 16.5 %collective-permute-start.5 = (f32[1,4,32,128]{3,2,1,0:T(8,128)S(1)}, f32[1,4,32,128]{3,2,1,0:T(8,128)S(1)}, u32[]{:S(2)}, u32[]{:S(2)}) collective-permute-start(f32[1,4,32,128]{3,2,1,0:T(8,128)S(1)} %bitcast.27), channel_id=1, source_target_pairs={{0,1},{1,2},{2,3},{3,0},{4,5},{5,6},{6,7},{7,4},{8,9},{9,10},{10,1... | collective-permute-start | bytes 196616 | tf_op jit(solution)/shard_map/ppermute | solution.py:609
  11.4 18.0 %collective-permute-start.6 = (f32[1,4,32,128]{3,2,1,0:T(8,128)S(1)}, f32[1,4,32,128]{3,2,1,0:T(8,128)S(1)}, u32[]{:S(2)}, u32[]{:S(2)}) collective-permute-start(f32[1,4,32,128]{3,2,1,0:T(8,128)S(1)} %bitcast.28), channel_id=1, source_target_pairs={{0,2},{1,3},{2,0},{3,1},{4,6},{5,7},{6,4},{7,5},{8,10},{9,11},{10,... | collective-permute-start | bytes 196616 | tf_op jit(solution)/shard_map/ppermute | solution.py:609
  13.0 16.4 %collective-permute-start.7 = (f32[1,4,32,128]{3,2,1,0:T(8,128)S(1)}, f32[1,4,32,128]{3,2,1,0:T(8,128)S(1)}, u32[]{:S(2)}, u32[]{:S(2)}) collective-permute-start(f32[1,4,32,128]{3,2,1,0:T(8,128)S(1)} %bitcast.29), channel_id=1, source_target_pairs={{0,3},{1,0},{2,1},{3,2},{4,7},{5,4},{6,5},{7,6},{8,11},{9,8},{10,9... | collective-permute-start | bytes 196616 | tf_op jit(solution)/shard_map/ppermute | solution.py:609
  17.3 13.9 %collective-permute-start = (f32[1,32,32,128]{3,2,1,0:T(8,128)}, f32[1,32,32,128]{3,2,1,0:T(8,128)S(1)}, u32[]{:S(2)}, u32[]{:S(2)}) collective-permute-start(f32[1,32,32,128]{3,2,1,0:T(8,128)} %get-tuple-element.46), channel_id=1, source_target_pairs={{0,1},{1,2},{2,3},{3,0},{4,5},{5,6},{6,7},{7,4},{8,9},{9,10},{10,1... | collective-permute-start | bytes 1572872 | tf_op jit(solution)/shard_map/ppermute | solution.py:609
  17.3 15.0 %collective-permute-start.1 = (f32[1,32,32,128]{3,2,1,0:T(8,128)}, f32[1,32,32,128]{3,2,1,0:T(8,128)S(1)}, u32[]{:S(2)}, u32[]{:S(2)}) collective-permute-start(f32[1,32,32,128]{3,2,1,0:T(8,128)} %get-tuple-element.45), channel_id=1, source_target_pairs={{0,2},{1,3},{2,0},{3,1},{4,6},{5,7},{6,4},{7,5},{8,10},{9,11},{10,... | collective-permute-start | bytes 1572872 | tf_op jit(solution)/shard_map/ppermute | solution.py:609
  20.3 40.9 %copy-start.5 = (bf16[256,256]{1,0:T(8,128)(2,1)}, bf16[256,256]{1,0:T(8,128)(2,1)S(1)}, u32[]{:S(2)}) copy-start(bf16[256,256]{1,0:T(8,128)(2,1)S(1)} %get-tuple-element.53.right_ref) | copy-start | bytes 393220
  22.6 5.4 %copy-start.15 = (f32[1,32,32,128]{3,2,1,0:T(8,128)S(1)}, f32[1,32,32,128]{3,2,1,0:T(8,128)}, u32[]{:S(2)}) copy-start(f32[1,32,32,128]{3,2,1,0:T(8,128)} %get-tuple-element.44) | copy-start | bytes 1572868
  27.9 13.1 %collective-permute-start.2 = (f32[1,32,32,128]{3,2,1,0:T(8,128)S(1)}, f32[1,32,32,128]{3,2,1,0:T(8,128)S(1)}, u32[]{:S(2)}, u32[]{:S(2)}) collective-permute-start(f32[1,32,32,128]{3,2,1,0:T(8,128)S(1)} %copy-done.15), channel_id=1, source_target_pairs={{0,3},{1,0},{2,1},{3,2},{4,7},{5,4},{6,5},{7,6},{8,11},{9,8},{10,9... | collective-permute-start | bytes 1572872 | tf_op jit(solution)/shard_map/ppermute | solution.py:609
  29.7 11.3 %copy-start.7 = (f32[5,128,128]{2,1,0:T(8,128)}, f32[5,128,128]{2,1,0:T(8,128)S(1)}, u32[]{:S(2)}) copy-start(f32[5,128,128]{2,1,0:T(8,128)S(1)} %get-tuple-element.31.weight_ref) | copy-start | bytes 983044
  41.0 20.2 %slice-start = ((s8[6291456]{0:T(1024)(128)(4,1)}), s8[2097152]{0:T(1024)(128)(4,1)S(1)}, s32[]{:S(2)}) async-start(s8[6291456]{0:T(1024)(128)(4,1)} %bitcast.17), calls=%async_computation.5 | async-start | bytes 4194304
  41.9 10.3 %copy-start.13 = (f32[1,32,32,128]{3,2,1,0:T(8,128)S(1)}, f32[1,32,32,128]{3,2,1,0:T(8,128)}, u32[]{:S(2)}) copy-start(f32[1,32,32,128]{3,2,1,0:T(8,128)} %get-tuple-element.26) | copy-start | bytes 1572868
  41.9 24.5 %collective-permute-start.8 = (f32[1,32,32,128]{3,2,1,0:T(8,128)}, f32[1,32,32,128]{3,2,1,0:T(8,128)S(1)}, u32[]{:S(2)}, u32[]{:S(2)}) collective-permute-start(f32[1,32,32,128]{3,2,1,0:T(8,128)} %get-tuple-element.27), channel_id=1, source_target_pairs={{0,1},{1,2},{2,3},{3,0},{4,5},{5,6},{6,7},{7,4},{8,9},{9,10},{10,1... | collective-permute-start | bytes 1572872 | tf_op jit(solution)/shard_map/ppermute | solution.py:609
  43.7 23.5 %collective-permute-start.9 = (f32[1,32,32,128]{3,2,1,0:T(8,128)}, f32[1,32,32,128]{3,2,1,0:T(8,128)S(1)}, u32[]{:S(2)}, u32[]{:S(2)}) collective-permute-start(f32[1,32,32,128]{3,2,1,0:T(8,128)} %get-tuple-element.28), channel_id=1, source_target_pairs={{0,2},{1,3},{2,0},{3,1},{4,6},{5,7},{6,4},{7,5},{8,10},{9,11},{10,... | collective-permute-start | bytes 1572872 | tf_op jit(solution)/shard_map/ppermute | solution.py:609
  44.3 23.8 %collective-permute-start.10 = (f32[1,32,32,128]{3,2,1,0:T(8,128)}, f32[1,32,32,128]{3,2,1,0:T(8,128)S(1)}, u32[]{:S(2)}, u32[]{:S(2)}) collective-permute-start(f32[1,32,32,128]{3,2,1,0:T(8,128)} %get-tuple-element.29), channel_id=1, source_target_pairs={{0,3},{1,0},{2,1},{3,2},{4,7},{5,4},{6,5},{7,6},{8,11},{9,8},{10,9... | collective-permute-start | bytes 1572872 | tf_op jit(solution)/shard_map/ppermute | solution.py:609
  45.2 16.0 %collective-permute-start.3 = (bf16[1024,128]{1,0:T(8,128)(2,1)S(1)}, bf16[1024,128]{1,0:T(8,128)(2,1)S(1)}, u32[]{:S(2)}, u32[]{:S(2)}) collective-permute-start(bf16[1024,128]{1,0:T(8,128)(2,1)S(1)} %get-tuple-element.51), channel_id=1, source_target_pairs={{0,4},{4,8},{8,12},{12,16},{16,20},{20,24},{24,28},{28,1},{1,5},{5... | collective-permute-start | bytes 786440 | tf_op jit(solution)/shard_map/ppermute | solution.py:323
  47.3 13.9 %collective-permute-start.4 = (bf16[1024,128]{1,0:T(8,128)(2,1)S(1)}, bf16[1024,128]{1,0:T(8,128)(2,1)S(1)}, u32[]{:S(2)}, u32[]{:S(2)}) collective-permute-start(bf16[1024,128]{1,0:T(8,128)(2,1)S(1)} %get-tuple-element.50), channel_id=1, source_target_pairs={{4,0},{8,4},{12,8},{16,12},{20,16},{24,20},{28,24},{1,28},{5,1},{9... | collective-permute-start | bytes 786440 | tf_op jit(solution)/shard_map/ppermute | solution.py:324
  55.8 5.4 %slice-start.1 = ((s8[6291456]{0:T(1024)(128)(4,1)}), s8[4194304]{0:T(1024)(128)(4,1)S(1)}, s32[]{:S(2)}) async-start(s8[6291456]{0:T(1024)(128)(4,1)} %bitcast.17), calls=%async_computation.6 | async-start | bytes 8388608
  68.9 39.2 %all-to-all-start.1 = ((bf16[32,32,640]{2,1,0:T(8,128)(2,1)}), bf16[32,32,640]{2,1,0:T(8,128)(2,1)S(1)}, u32[]{:S(2)}, u32[]{:S(2)}) async-start(bf16[32,32,640]{2,1,0:T(8,128)(2,1)} %bitcast.7), calls=%async_computation.1 | async-start | bytes 2621440 | tf_op jit(solution)/shard_map/all_to_all | solution.py:685
  146.2 13.6 %collective-permute-start.11 = (bf16[1024,128]{1,0:T(8,128)(2,1)S(1)}, bf16[1024,128]{1,0:T(8,128)(2,1)S(1)}, u32[]{:S(2)}, u32[]{:S(2)}) collective-permute-start(bf16[1024,128]{1,0:T(8,128)(2,1)S(1)} %get-tuple-element.49), channel_id=1, source_target_pairs={{0,4},{4,8},{8,12},{12,16},{16,20},{20,24},{24,28},{28,1},{1,5},{5... | collective-permute-start | bytes 786440 | tf_op jit(solution)/shard_map/ppermute | solution.py:323
  147.8 13.0 %collective-permute-start.12 = (bf16[1024,128]{1,0:T(8,128)(2,1)S(1)}, bf16[1024,128]{1,0:T(8,128)(2,1)S(1)}, u32[]{:S(2)}, u32[]{:S(2)}) collective-permute-start(bf16[1024,128]{1,0:T(8,128)(2,1)S(1)} %get-tuple-element.48), channel_id=1, source_target_pairs={{4,0},{8,4},{12,8},{16,12},{20,16},{24,20},{28,24},{1,28},{5,1},{9... | collective-permute-start | bytes 786440 | tf_op jit(solution)/shard_map/ppermute | solution.py:324
  154.4 6.4 %copy-start.6 = (bf16[256,256]{1,0:T(8,128)(2,1)S(1)}, bf16[256,256]{1,0:T(8,128)(2,1)}, u32[]{:S(2)}) copy-start(bf16[256,256]{1,0:T(8,128)(2,1)} %copy-done.5) | copy-start | bytes 393220
  160.8 2.8 %copy-start.3 = (bf16[8,3,128,1024]{3,2,1,0:T(8,128)(2,1)S(1)}, bf16[8,3,128,1024]{3,2,1,0:T(8,128)(2,1)}, u32[]{:S(2)}) copy-start(bf16[8,3,128,1024]{3,2,1,0:T(8,128)(2,1)} %copy-done) | copy-start | bytes 18874372
  166.5 29.3 %all-to-all-start.3 = ((bf16[32,32,512]{2,1,0:T(8,128)(2,1)}), bf16[32,32,512]{2,1,0:T(8,128)(2,1)S(1)}, u32[]{:S(2)}, u32[]{:S(2)}) async-start(bf16[32,32,512]{2,1,0:T(8,128)(2,1)} %bitcast.10), calls=%async_computation.3 | async-start | bytes 2097152 | tf_op jit(solution)/shard_map/all_to_all | solution.py:693
  201.9 12.6 %collective-permute-start.13 = (bf16[1,32,32,128]{3,2,1,0:T(8,128)(2,1)}, bf16[1,32,32,128]{3,2,1,0:T(8,128)(2,1)S(1)}, u32[]{:S(2)}, u32[]{:S(2)}) collective-permute-start(bf16[1,32,32,128]{3,2,1,0:T(8,128)(2,1)} %get-tuple-element.37), channel_id=1, source_target_pairs={{0,1},{1,2},{2,3},{3,0},{4,5},{5,6},{6,7},{7,4},{8,9},{9,10},{10,1... | collective-permute-start | bytes 786440 | tf_op jit(solution)/shard_map/ppermute | solution.py:609
  201.9 12.7 %collective-permute-start.14 = (bf16[1,32,32,128]{3,2,1,0:T(8,128)(2,1)}, bf16[1,32,32,128]{3,2,1,0:T(8,128)(2,1)S(1)}, u32[]{:S(2)}, u32[]{:S(2)}) collective-permute-start(bf16[1,32,32,128]{3,2,1,0:T(8,128)(2,1)} %get-tuple-element.38), channel_id=1, source_target_pairs={{0,2},{1,3},{2,0},{3,1},{4,6},{5,7},{6,4},{7,5},{8,10},{9,11},{10,... | collective-permute-start | bytes 786440 | tf_op jit(solution)/shard_map/ppermute | solution.py:609
  203.5 12.0 %collective-permute-start.15 = (bf16[1,32,32,128]{3,2,1,0:T(8,128)(2,1)}, bf16[1,32,32,128]{3,2,1,0:T(8,128)(2,1)S(1)}, u32[]{:S(2)}, u32[]{:S(2)}) collective-permute-start(bf16[1,32,32,128]{3,2,1,0:T(8,128)(2,1)} %get-tuple-element.39), channel_id=1, source_target_pairs={{0,3},{1,0},{2,1},{3,2},{4,7},{5,4},{6,5},{7,6},{8,11},{9,8},{10,9... | collective-permute-start | bytes 786440 | tf_op jit(solution)/shard_map/ppermute | solution.py:609
  210.7 3.8 %copy-start.16 = (bf16[1,32,32,128]{3,2,1,0:T(8,128)(2,1)S(1)}, bf16[1,32,32,128]{3,2,1,0:T(8,128)(2,1)}, u32[]{:S(2)}) copy-start(bf16[1,32,32,128]{3,2,1,0:T(8,128)(2,1)} %get-tuple-element.36) | copy-start | bytes 786436
  210.7 18.1 %all-to-all-start.4 = ((bf16[128,32,128]{2,1,0:T(8,128)(2,1)}), bf16[128,32,128]{2,1,0:T(8,128)(2,1)S(1)}, u32[]{:S(2)}, u32[]{:S(2)}) async-start(bf16[128,32,128]{2,1,0:T(8,128)(2,1)} %bitcast.26), calls=%async_computation.4 | async-start | bytes 2097152 | tf_op jit(solution)/shard_map/all_to_all | solution.py:648
  (9 other events, 19.0 us)

commit v8 on v7

--- a/solution.py
+++ b/solution.py
@@ -9,9 +9,8 @@
 from jax.sharding import PartitionSpec as P
 
 RELAXATION = 0.6
-VMEM_BYTES = 60 << 20
-SHARED_VMEM_BYTES = 32 << 20
-UNROLL = 4
+VMEM_BYTES = 57 << 20
+UNROLL = 2
 
 
 def sine_table(length):
@@ -49,10 +48,18 @@
     return [centre] + weights
 
 
-def weights_kernel(strip_ref, coef_ref, mean_ref, strip_weight_ref, full_ref):
+def in_order(here, shift, count):
+    return lax.rem(here + count - shift, count)
+
+
+def weights_kernel(slabs, place_ref, *refs):
+    part_refs = refs[:slabs]
+    mean_ref, strip_weight_ref, coef_ref, full_ref = refs[slabs:]
     _, nx, ny = mean_ref.shape
     fields = coef_ref.shape[1] - 1
     height = strip_weight_ref.shape[0] // (5 * fields)
+    for shift, part_ref in enumerate(part_refs):
+        coef_ref[in_order(place_ref[0], shift, slabs)] = part_ref[0]
     for which, weight in enumerate(stencil_weights(coef_ref[:, 0].reshape(nx, ny))):
         mean_ref[which] = weight
     for f in range(fields):
@@ -61,32 +68,38 @@
             for r in range(height):
                 at = (f * 5 + which) * height + r
                 strip_weight_ref[at : at + 1, :] = full_ref[
-                    pl.ds(strip_ref[0] * height + r, 1), :
+                    pl.ds(place_ref[1] * height + r, 1), :
                 ]
 
 
-def all_weights(coefs, strip, height):
-    slab_count, entries, rows, ny = coefs.shape
+def all_weights(parts, place, coefs, height):
+    slab_count = len(parts)
+    _, entries, rows, ny = parts[0].shape
     nx = slab_count * rows
-    fields = entries - 1
+    last = entries // coefs - 1
+    fields = coefs - 1
     return pl.pallas_call(
-        weights_kernel,
+        functools.partial(weights_kernel, slab_count),
         grid_spec=pltpu.PrefetchScalarGridSpec(
             num_scalar_prefetch=1,
             grid=(1,),
-            in_specs=[pl.BlockSpec(coefs.shape, lambda i, *_: (0, 0, 0, 0))],
+            in_specs=[pl.BlockSpec((1, coefs, rows, ny), lambda i, *_: (0, last, 0, 0))]
+            * slab_count,
             out_specs=[
                 pl.BlockSpec((5, nx, ny), lambda i, *_: (0, 0, 0)),
                 pl.BlockSpec((fields * 5 * height, ny), lambda i, *_: (0, 0)),
             ],
-            scratch_shapes=[pltpu.VMEM((nx, ny), jnp.float32)],
+            scratch_shapes=[
+                pltpu.VMEM((slab_count, coefs, rows, ny), jnp.float32),
+                pltpu.VMEM((nx, ny), jnp.float32),
+            ],
         ),
         out_shape=[
             jax.ShapeDtypeStruct((5, nx, ny), jnp.float32),
             jax.ShapeDtypeStruct((fields * 5 * height, ny), jnp.float32),
         ],
-        compiler_params=pltpu.CompilerParams(vmem_limit_bytes=SHARED_VMEM_BYTES),
-    )(strip.reshape(1), coefs)
+        compiler_params=pltpu.CompilerParams(vmem_limit_bytes=VMEM_BYTES),
+    )(place, *parts)
 
 
 def split(value):
@@ -197,7 +210,7 @@
             ),
         ),
         out_shape=jax.ShapeDtypeStruct((blocks, fields, width, blocks * width), coupling.dtype),
-        compiler_params=pltpu.CompilerParams(vmem_limit_bytes=SHARED_VMEM_BYTES),
+        compiler_params=pltpu.CompilerParams(vmem_limit_bytes=VMEM_BYTES),
     )(coupling_list, pair_count, coupling)
 
 
@@ -326,7 +339,7 @@
     matrix_spec = pl.BlockSpec((unroll, fields, width, depth), lambda i: (i, 0, 0, 0))
     weight_spec = pl.BlockSpec(weights.shape, lambda i: (0, 0))
     sums_spec = pl.BlockSpec((unroll * width, cells), lambda i: (i, 0))
-    params = pltpu.CompilerParams(vmem_limit_bytes=SHARED_VMEM_BYTES)
+    params = pltpu.CompilerParams(vmem_limit_bytes=VMEM_BYTES)
     inner = pl.pallas_call(
         functools.partial(inner_kernel, height, cols),
         grid=(blocks // unroll,),
@@ -359,6 +372,7 @@
 
 
 TOGETHER = 16
+MEAN_TOGETHER = 8
 GROUP = 16
 
 
@@ -370,29 +384,43 @@
     return along_cols([wide[:, i * ny : (i + 1) * ny] for i in range(len(spectral))], right_ref)
 
 
-def mean_kernel(first, current_ref, right_side_ref, weight_ref, right_ref, out_ref):
+def mean_fields(current_ref, right_side_ref, weight_ref, start):
     nx, ny = weight_ref.shape[1:]
-
-    def several(number, carry):
-        values = []
-        for i in range(TOGETHER):
-            mode = number * TOGETHER + i
-            here = current_ref[:, mode].reshape(nx, ny)
-            mean = (
-                weight_ref[0] * here
-                - weight_ref[1] * pltpu.roll(here, 1, 0)
-                - weight_ref[2] * pltpu.roll(here, nx - 1, 0)
-                - pltpu.roll(weight_ref[4] * here, 1, 1)
-                - pltpu.roll(weight_ref[3] * here, ny - 1, 1)
-            )
-            values.append(right_side_ref[:, mode].reshape(nx, ny) - mean)
-        if first:
-            values = along_cols(values, right_ref)
-        for i in range(TOGETHER):
-            out_ref[:, number * TOGETHER + i] = values[i].reshape(out_ref.shape[0], -1, ny)
-        return carry
-
-    lax.fori_loop(0, out_ref.shape[1] // TOGETHER, several, 0)
+    values = []
+    for mode in range(start, start + MEAN_TOGETHER):
+        here = current_ref[:, mode].reshape(nx, ny)
+        mean = (
+            weight_ref[0] * here
+            - weight_ref[1] * pltpu.roll(here, 1, 0)
+            - weight_ref[2] * pltpu.roll(here, nx - 1, 0)
+            - pltpu.roll(weight_ref[4] * here, 1, 1)
+            - pltpu.roll(weight_ref[3] * here, ny - 1, 1)
+        )
+        values.append(right_side_ref[:, mode].reshape(nx, ny) - mean)
+    return values
+
+
+def first_mean_kernel(slabs, place_ref, *refs):
+    current_parts = refs[:slabs]
+    right_side_parts = refs[slabs : 2 * slabs]
+    weight_ref, right_ref, current_ref, right_side_ref, out_ref = refs[2 * slabs :]
+    for shift in range(slabs):
+        slab = in_order(place_ref[0], shift, slabs)
+        current_ref[slab] = current_parts[shift][0]
+        right_side_ref[slab] = right_side_parts[shift][0]
+    shape = (slabs,) + out_ref.shape[2:]
+    for start in range(0, out_ref.shape[1], MEAN_TOGETHER):
+        values = mean_fields(current_ref, right_side_ref, weight_ref, start)
+        for i, value in enumerate(along_cols(values, right_ref)):
+            out_ref[:, start + i] = value.reshape(shape)
+
+
+def mean_kernel(current_ref, right_side_ref, weight_ref, out_ref):
+    shape = out_ref.shape[:1] + out_ref.shape[2:]
+    for start in range(0, out_ref.shape[1], MEAN_TOGETHER):
+        values = mean_fields(current_ref, right_side_ref, weight_ref, start)
+        for i, value in enumerate(values):
+            out_ref[:, start + i] = value.reshape(shape)
 
 
 def turn_in(turned_ref, coupled_ref, mode_count, slab_count, height, first, scale):
@@ -519,13 +547,36 @@
     )(*operands)
 
 
-def mean_part(current, right_side, weights, right, first):
+def first_mean_part(place, current_parts, right_side_parts, weights, right):
+    slabs = len(right_side_parts)
+    _, modes, rows, ny = right_side_parts[0].shape
+    part = pl.BlockSpec((1, GROUP, rows, ny), lambda g, *_: (0, g, 0, 0))
+    slab = pl.BlockSpec((slabs, GROUP, rows, ny), lambda g, *_: (0, g, 0, 0))
+    shape = jax.ShapeDtypeStruct((slabs, modes, rows, ny), jnp.float32)
+    return pl.pallas_call(
+        functools.partial(first_mean_kernel, slabs),
+        grid_spec=pltpu.PrefetchScalarGridSpec(
+            num_scalar_prefetch=1,
+            grid=(modes // GROUP,),
+            in_specs=[part] * (2 * slabs)
+            + [
+                pl.BlockSpec(weights.shape, lambda g, *_: (0, 0, 0)),
+                pl.BlockSpec(right.shape, lambda g, *_: (0, 0)),
+            ],
+            out_specs=[slab] * 3,
+        ),
+        out_shape=[shape] * 3,
+        compiler_params=pltpu.CompilerParams(vmem_limit_bytes=VMEM_BYTES),
+    )(place, *current_parts, *right_side_parts, weights, right)
+
+
+def mean_part(current, right_side, weights):
     slabs = slabs_of(right_side)
     return per_group(
-        functools.partial(mean_kernel, first),
+        mean_kernel,
         right_side.shape[1] // GROUP,
-        (current, right_side, weights, right),
-        [slabs, slabs, whole(weights), whole(right)],
+        (current, right_side, weights),
+        [slabs, slabs, whole(weights)],
         jax.ShapeDtypeStruct(right_side.shape, jnp.float32),
         slabs,
     )
@@ -621,11 +672,6 @@
     return [parts[0]] + [onwards(parts[i], axis, i) for i in range(1, len(parts))]
 
 
-def spread(block, axis):
-    count = lax.axis_size(axis)
-    return collect([block[None]] + [onwards(block[None], axis, i) for i in range(1, count)], axis)
-
-
 def local(guess, right_side, mean_coef, field_coef, coupling, coupling_list, pair_count):
     mode_count = lax.axis_size("mode")
     slab_count = lax.axis_size("slab")
@@ -638,8 +684,7 @@
     share = modes // slab_count
 
     strips = pack_strips(guess, mode_count)
-    coefs = jnp.concatenate([mean_coef[None], field_coef], 0)
-    strips, coefs = lax.optimization_barrier((strips, coefs))
+    coefs = jnp.concatenate([mean_coef[None], field_coef], 0)[None]
     state = lax.all_to_all(strips, "mode", 0, 0, tiled=True)
     state = state.reshape(mode_count * modes, height * cols)
 
@@ -647,15 +692,16 @@
         flat = block.reshape(modes, rows, cols)
         return lax.all_to_all(flat, "slab", 0, 0, tiled=True)
 
-    coefs = spread(coefs, "slab")
     guess_parts = parts_of(guess.reshape(slab_count, share, rows, cols), "slab")
-    current = collect(moved_parts(guess_parts, "slab"), "slab")
+    guess_parts = [jnp.concatenate([part, coefs], axis=1) for part in guess_parts]
+    guess_parts = moved_parts(guess_parts, "slab")
     right_parts = parts_of(right_side.reshape(slab_count, share, rows, cols), "slab")
-    state, current, right_parts = lax.optimization_barrier((state, current, right_parts))
-    right_side = collect(moved_parts(right_parts, "slab"), "slab")
-
-    strip = lax.axis_index("slab") * mode_count + lax.axis_index("mode")
-    mean_weights, strip_weights = all_weights(coefs, strip, height)
+    state, guess_parts, right_parts = lax.optimization_barrier((state, guess_parts, right_parts))
+    right_parts = moved_parts(right_parts, "slab")
+
+    slab = lax.axis_index("slab")
+    place = jnp.stack([slab, slab * mode_count + lax.axis_index("mode")])
+    mean_weights, strip_weights = all_weights(guess_parts, place, fields + 1, height)
     matrix = dense_coupling(coupling, coupling_list, pair_count, fields)
 
     row_high, row_low = split_table(sine_table(nx))
@@ -681,14 +727,16 @@
     first_scale, sum_scale, solution_scale = code_scales(nx, cols, coupling.shape[1], modes)
 
     sums = coupled_sums(matrix, state, strip_weights, tables[0], True, first_scale, both)
-    sums, right_side = lax.optimization_barrier((sums, right_side))
+    sums, right_parts = lax.optimization_barrier((sums, right_parts))
     sums = lax.all_to_all(sums, both, 0, 0, tiled=True).reshape(devices, share, -1)
-    base = mean_part(current, right_side, mean_weights, tables[0], True)
+    current, right_side, base = first_mean_part(
+        place, guess_parts, right_parts, mean_weights, tables[0]
+    )
     current, state = step(current, base, sums, tables, mode_count, slab_count, first_scale)
     state = state.reshape(devices * share, height * cols)
     state = lax.all_to_all(state, both, 0, 0, tiled=True)
 
-    base = mean_part(current, right_side, mean_weights, tables[0], False)
+    base = mean_part(current, right_side, mean_weights)
     sums = coupled_sums(matrix, state, strip_weights, tables[0], False, sum_scale, both)
     sums = lax.all_to_all(sums, both, 0, 0, tiled=True).reshape(devices, share, -1)
     resid, parts = last_residual(base, sums, mode_count, slab_count, sum_scale)

time: 232 us -> 231 us (level)
  Pallas kernels: 51.3 us -> 74.3 us
  local copies, waits for them, and re-layouts: 27.6 us -> 5.78 us
  starting transfers between devices: 43.2 us -> 38.2 us
    unnamed x42 -> x34, local copies, waits for them, and re-layouts: 15.5 us -> 3.84 us
    pallas_call x1 -> x2, Pallas kernels: 0.29 us -> 8.58 us  [the longest x1 5.97 us: first_mean_part(): pl.pallas_call(functools.partial(first_mean_kernel, slabs), grid_spec=plt...]
    pallas_call x2, Pallas kernels: 10.7 us -> 17.4 us  [coupled_sums(): pl.pallas_call(functools.partial(inner_kernel, height, cols), grid=(block...]
    pallas_call x1, Pallas kernels: 2.66 us -> 8.99 us  [dense_coupling(): pl.pallas_call(functools.partial(dense_kernel, fields), grid_spec=pltpu.P...]
    dynamic_update_slice x15 -> x4, local copies, waits for them, and re-layouts: 6 us -> 0.16 us  [collect(): out = lax.dynamic_update_slice_in_dim(out, part, source, 0)]
    pallas_call x2, Pallas kernels: 8.13 us -> 14 us  [coupled_sums(): pl.pallas_call(functools.partial(border_kernel, height, cols, first, scal...]
    pallas_call x4 -> x3, Pallas kernels: 21.1 us -> 16.8 us  [per_group(): pl.pallas_call(kernel, grid=(groups,), in_specs=in_specs, out_specs=out_s...]
    another operation x2 -> x0, local copies, waits for them, and re-layouts: 3.16 us -> none
  transfers between devices with their start and end apart: 20 -> 17, of which waited for: 8 -> 8; matrix products, arithmetic and copies ran while one was open for 7% -> 4% of each run, Pallas kernels for 14% -> 23%
where the time goes in v8:
time: 231 us; the launch traced here: 229 us
  Pallas kernels  74.3 us (32%)
  waiting for transfers between devices  71.8 us (31%)
  starting transfers between devices  38.2 us (17%)
  blocking collectives  29.8 us (13%)
  other arithmetic  8.66 us (4%)
  local copies, waits for them, and re-layouts  5.78 us (3%)
    all_to_all x2, waiting for transfers between devices, local(): lax.all_to_all(sums, both, 0, 0, tiled=True).reshape(devices, share, -1)  47.6 us
    all_to_all x1, blocking collectives, local(): state = lax.all_to_all(state, both, 0, 0, tiled=True)  29.8 us
    pallas_call x2, Pallas kernels, coupled_sums(): pl.pallas_call(functools.partial(inner_kernel, height, cols), grid=(block...  17.4 us
    pallas_call x3, Pallas kernels, per_group(): pl.pallas_call(kernel, grid=(groups,), in_specs=in_specs, out_specs=out_s...  16.8 us
    pallas_call x2, Pallas kernels, coupled_sums(): pl.pallas_call(functools.partial(border_kernel, height, cols, first, scal...  14 us
    ppermute x9, waiting for transfers between devices, onwards(): lax.ppermute(part, axis, [(i, (i + shift) % count) for i in range(count)])  13.4 us
    all_to_all x1, waiting for transfers between devices, to_slabs(): return lax.all_to_all(flat, 'slab', 0, 0, tiled=True)  10.4 us
    pallas_call x1, Pallas kernels, dense_coupling(): pl.pallas_call(functools.partial(dense_kernel, fields), grid_spec=pltpu.P...  8.99 us
  transfers between devices with their start and end apart: 17, of which 8 were waited for; matrix products, arithmetic and copies ran while one was open for 4% of the time, Pallas kernels for 23%

profile of v8, /device:TPU:0, one launch (start us, length us, event | category | flops | bytes accessed | tf_op | source)
XLA Modules:
  0.0 229.5 jit_solution(12470715433924252312)
XLA Ops:
  0.7 3.5 %shard_map.86 = bf16[8,128,512]{2,1,0:T(8,128)(2,1)} custom-call(f32[4096,128]{1,0:T(8,128)} %bitcast.17), custom_call_target="tpu_custom_call" | custom-call | tf_op jit(solution)/shard_map/pallas_call | solution.py:176
  4.1 7.3 %all-to-all-start = ((bf16[8,128,512]{2,1,0:T(8,128)(2,1)}), bf16[8,128,512]{2,1,0:T(8,128)(2,1)S(1)}, u32[]{:S(2)}, u32[]{:S(2)}) async-start(bf16[8,128,512]{2,1,0:T(8,128)(2,1)} %shard_map.86), calls=%async_computation | async-start | bytes 2097152 | tf_op jit(solution)/shard_map/all_to_all | solution.py:688
  12.9 1.5 collective-permute-start.1
  14.5 1.4 collective-permute-start.2
  15.9 9.0 %shard_map.87.matrix_ref = bf16[8,3,128,1024]{3,2,1,0:T(8,128)(2,1)} custom-call(s32[8,16]{1,0:T(8,128)} %entry_ref.1, s32[8]{0:T(128)} %count_ref.1, bf16[8,16,128,128]{3,2,1,0:T(8,128)(2,1)} %coupling_ref.1), custom_call_target="tpu_custom_call" | custom-call | tf_op jit(solution)/shard_map/pallas_call | solution.py:202
  29.3 11.1 %collective-permute-done.2.refs_3_ = f32[1,36,32,128]{3,2,1,0:T(8,128)S(1)} collective-permute-done((f32[1,36,32,128]{3,2,1,0:T(8,128)S(1)}, f32[1,36,32,128]{3,2,1,0:T(8,128)S(1)}, u32[]{:S(2)}, u32[]{:S(2)}) %collective-permute-start.2) | collective-permute-done | bytes 589856 | tf_op jit(solution)/shard_map/ppermute | solution.py:660
  41.3 1.5 collective-permute-start.6
  42.8 2.1 collective-permute-start.3
  44.9 3.3 %collective-permute-start.4 = (bf16[1024,128]{1,0:T(8,128)(2,1)S(1)}, bf16[1024,128]{1,0:T(8,128)(2,1)S(1)}, u32[]{:S(2)}, u32[]{:S(2)}) collective-permute-start(bf16[1024,128]{1,0:T(8,128)(2,1)S(1)} %get-tuple-element.64), channel_id=1, source_target_pairs={{4,0},{8,4},{12,8},{16,12},{20,16},{24,20},{28,24},{1,28},{5,1},{9... | collective-permute-start | bytes 786440 | tf_op jit(solution)/shard_map/ppermute | solution.py:337
  48.2 2.6 %shard_map.88 = (f32[5,128,128]{2,1,0:T(8,128)}, f32[60,128]{1,0:T(8,128)}) custom-call(s32[2]{0:T(128)} %pad_add_fusion.place_ref, f32[1,36,32,128]{3,2,1,0:T(8,128)} %get-tuple-element.28.refs_0_, f32[1,36,32,128]{3,2,1,0:T(8,128)} %copy-done.2, f32[1,36,32,128]{3,2,1,0:T(8,128)} %copy-done.3, f32[1,36,32,128]{3,2,1,0:T(8,128)} %copy-done.4), custom_call_target="tpu_custom_call" | custom-call | tf_op jit(solution)/shard_map/pallas_call | solution.py:81
  50.8 8.7 %shard_map.89.inner_ref = f32[1024,512]{1,0:T(8,128)} custom-call(bf16[8,3,128,1024]{3,2,1,0:T(8,128)(2,1)} %shard_map.87.matrix_ref, bf16[1024,512]{1,0:T(8,128)(2,1)} %bitcast.22, f32[60,128]{1,0:T(8,128)} %get-tuple-element.33.weight_ref), custom_call_target="tpu_custom_call" | custom-call | flops 3221225472 | bytes 6291456 | tf_op jit(solution)/shard_map/pallas_call | solution.py:343
  60.3 7.8 %shard_map.90 = bf16[1024,640]{1,0:T(8,128)(2,1)} custom-call(bf16[8,3,128,1024]{3,2,1,0:T(8,128)(2,1)} %shard_map.87.matrix_ref, bf16[1024,128]{1,0:T(8,128)(2,1)} %copy-done.10, bf16[1024,128]{1,0:T(8,128)(2,1)} %copy-done.12, f32[60,128]{1,0:T(8,128)} %get-tuple-element.33.weight_ref, f32[1024,512]{1,0:T(8,128)} %shard_map.89.inner_ref, ...), custom_call_target="tpu_custom_call" | custom-call | tf_op jit(solution)/shard_map/pallas_call | solution.py:357
  68.2 4.6 %all-to-all-start.1 = ((bf16[32,32,640]{2,1,0:T(8,128)(2,1)}), bf16[32,32,640]{2,1,0:T(8,128)(2,1)S(1)}, u32[]{:S(2)}, u32[]{:S(2)}) async-start(bf16[32,32,640]{2,1,0:T(8,128)(2,1)} %bitcast.19), calls=%async_computation.1 | async-start | bytes 2621440 | tf_op jit(solution)/shard_map/all_to_all | solution.py:731
  73.6 6.0 %shard_map.91 = (f32[4,32,32,128]{3,2,1,0:T(8,128)}, f32[4,32,32,128]{3,2,1,0:T(8,128)}, f32[4,32,32,128]{3,2,1,0:T(8,128)}) custom-call(s32[2]{0:T(128)} %pad_add_fusion.place_ref, f32[1,36,32,128]{3,2,1,0:T(8,128)} %get-tuple-element.28.refs_0_, f32[1,36,32,128]{3,2,1,0:T(8,128)} %copy-done.2, f32[1,36,32,128]{3,2,1,0:T(8,128)} %copy-done.3, ...), custom_call_target="tpu_custom_call" | custom-call | tf_op jit(solution)/shard_map/pallas_call | solution.py:556
  79.6 25.4 %all-to-all-done.1.coupled_ref = bf16[32,32,640]{2,1,0:T(8,128)(2,1)S(1)} async-done(((bf16[32,32,640]{2,1,0:T(8,128)(2,1)}), bf16[32,32,640]{2,1,0:T(8,128)(2,1)S(1)}, u32[]{:S(2)}, u32[]{:S(2)}) %all-to-all-start.1) | async-done | bytes 1310752 | tf_op jit(solution)/shard_map/all_to_all | solution.py:731
  106.0 7.1 %shard_map.92 = (f32[4,32,32,128]{3,2,1,0:T(8,128)}, bf16[32,32,512]{2,1,0:T(8,128)(2,1)}) custom-call(f32[4,32,32,128]{3,2,1,0:T(8,128)} %get-tuple-element.43.current_ref, f32[4,32,32,128]{3,2,1,0:T(8,128)} %get-tuple-element.44.base_ref, bf16[32,32,640]{2,1,0:T(8,128)(2,1)} %copy-done.8, bf16[256,256]{1,0:T(8,128)(2,1)} %get-tuple-element.67.right_ref.refs_9_, ...), custom_call_target="tpu_custom_call" | custom-call | flops 1610612736 | bytes 11665408 | tf_op jit(solution)/shard_map/pallas_call | solution.py:538
  113.2 29.8 %all_to_all.36 = bf16[32,32,512]{2,1,0:T(8,128)(2,1)S(1)} all-to-all(bf16[32,32,512]{2,1,0:T(8,128)(2,1)} %get-tuple-element.48), channel_id=1, replica_groups=mesh['mode'=8,'slab'=4] {'mode','slab'}, dimensions={0} | all-to-all | bytes 2097152 | tf_op jit(solution)/shard_map/all_to_all | solution.py:737
  143.0 1.5 collective-permute-start.8
  144.6 3.9 %collective-permute-start.9 = (bf16[1024,128]{1,0:T(8,128)(2,1)S(1)}, bf16[1024,128]{1,0:T(8,128)(2,1)S(1)}, u32[]{:S(2)}, u32[]{:S(2)}) collective-permute-start(bf16[1024,128]{1,0:T(8,128)(2,1)S(1)} %get-tuple-element.62), channel_id=1, source_target_pairs={{4,0},{8,4},{12,8},{16,12},{20,16},{24,20},{28,24},{1,28},{5,1},{9... | collective-permute-start | bytes 786440 | tf_op jit(solution)/shard_map/ppermute | solution.py:337
  148.4 8.7 %shard_map.94.inner_ref = f32[1024,512]{1,0:T(8,128)} custom-call(bf16[8,3,128,1024]{3,2,1,0:T(8,128)(2,1)} %shard_map.87.matrix_ref, bf16[1024,512]{1,0:T(8,128)(2,1)} %bitcast.24, f32[60,128]{1,0:T(8,128)} %get-tuple-element.33.weight_ref), custom_call_target="tpu_custom_call" | custom-call | flops 3221225472 | bytes 6291456 | tf_op jit(solution)/shard_map/pallas_call | solution.py:343
  158.5 6.1 %shard_map.95 = bf16[1024,512]{1,0:T(8,128)(2,1)} custom-call(bf16[8,3,128,1024]{3,2,1,0:T(8,128)(2,1)} %shard_map.87.matrix_ref, bf16[1024,128]{1,0:T(8,128)(2,1)} %copy-done.11, bf16[1024,128]{1,0:T(8,128)(2,1)} %copy-done.13, f32[60,128]{1,0:T(8,128)} %get-tuple-element.33.weight_ref, f32[1024,512]{1,0:T(8,128)} %shard_map.94.inner_ref, ...), custom_call_target="tpu_custom_call" | custom-call | tf_op jit(solution)/shard_map/pallas_call | solution.py:357
  164.7 3.6 %all-to-all-start.3 = ((bf16[32,32,512]{2,1,0:T(8,128)(2,1)}), bf16[32,32,512]{2,1,0:T(8,128)(2,1)S(1)}, u32[]{:S(2)}, u32[]{:S(2)}) async-start(bf16[32,32,512]{2,1,0:T(8,128)(2,1)} %bitcast.20), calls=%async_computation.3 | async-start | bytes 2097152 | tf_op jit(solution)/shard_map/all_to_all | solution.py:741
  168.3 3.9 %shard_map.93.base_ref = f32[4,32,32,128]{3,2,1,0:T(8,128)} custom-call(f32[4,32,32,128]{3,2,1,0:T(8,128)} %get-tuple-element.46.current_ref, f32[4,32,32,128]{3,2,1,0:T(8,128)} %get-tuple-element.47.right_side_ref, f32[5,128,128]{2,1,0:T(8,128)} %get-tuple-element.42.refs_8_.weight_ref), custom_call_target="tpu_custom_call" | custom-call | bytes 9043968 | tf_op jit(solution)/shard_map/pallas_call | solution.py:538
  172.2 22.2 %all-to-all-done.3.coupled_ref = bf16[32,32,512]{2,1,0:T(8,128)(2,1)S(1)} async-done(((bf16[32,32,512]{2,1,0:T(8,128)(2,1)}), bf16[32,32,512]{2,1,0:T(8,128)(2,1)S(1)}, u32[]{:S(2)}, u32[]{:S(2)}) %all-to-all-start.3) | async-done | bytes 1048608 | tf_op jit(solution)/shard_map/all_to_all | solution.py:741
  195.4 5.1 %shard_map.96 = (f32[4,32,32,128]{3,2,1,0:T(8,128)}, bf16[1,32,32,128]{3,2,1,0:T(8,128)(2,1)}, bf16[1,32,32,128]{3,2,1,0:T(8,128)(2,1)}, bf16[1,32,32,128]{3,2,1,0:T(8,128)(2,1)}, bf16[1,32,32,128]{3,2,1,0:T(8,128)(2,1)}) custom-call(s32[1]{0:T(128)} %bitcast.here_ref, f32[4,32,32,128]{3,2,1,0:T(8,128)} %shard_map.93.base_ref, bf16[32,32,512]{2,1,0:T(8,128)(2,1)} %copy-done.1), custom_call_target="tpu_custom_call" | custom-call | bytes 4194304 | tf_op jit(solution)/shard_map/pallas_call | solution.py:615
  200.5 1.5 collective-permute-start.11
  202.0 1.4 collective-permute-start.12
  203.4 5.8 %shard_map.97 = bf16[4,32,32,128]{3,2,1,0:T(8,128)(2,1)} custom-call(f32[4,32,32,128]{3,2,1,0:T(8,128)} %get-tuple-element.46.current_ref, f32[4,32,32,128]{3,2,1,0:T(8,128)} %get-tuple-element.49.resid_ref, bf16[256,256]{1,0:T(8,128)(2,1)} %get-tuple-element.67.right_ref.refs_9_, bf16[256,256]{1,0:T(8,128)(2,1)} %get-tuple-element.66.left_ref, ...), custom_call_target="tpu_custom_call" | custom-call | flops 1610612736 | bytes 9043968 | tf_op jit(solution)/shard_map/pallas_call | solution.py:538
  209.2 3.6 %all-to-all-start.4 = ((bf16[128,32,128]{2,1,0:T(8,128)(2,1)}), bf16[128,32,128]{2,1,0:T(8,128)(2,1)S(1)}, u32[]{:S(2)}, u32[]{:S(2)}) async-start(bf16[128,32,128]{2,1,0:T(8,128)(2,1)} %bitcast.26), calls=%async_computation.4 | async-start | bytes 2097152 | tf_op jit(solution)/shard_map/all_to_all | solution.py:693
  215.0 1.8 fusion.11
  216.8 10.4 %all-to-all-done.4 = bf16[128,32,128]{2,1,0:T(8,128)(2,1)S(1)} async-done(((bf16[128,32,128]{2,1,0:T(8,128)(2,1)}), bf16[128,32,128]{2,1,0:T(8,128)(2,1)S(1)}, u32[]{:S(2)}, u32[]{:S(2)}) %all-to-all-start.4) | async-done | bytes 1048608 | tf_op jit(solution)/shard_map/all_to_all | solution.py:693
  227.3 2.2 fusion.10
  (70 shorter events, 14.0 us)
Async XLA Ops:
  0.6 10.8 %copy-start.15 = (f32[3,32,128]{2,1,0:T(8,128)S(1)}, f32[3,32,128]{2,1,0:T(8,128)}, u32[]{:S(2)}) copy-start(f32[3,32,128]{2,1,0:T(8,128)} %param.10) | copy-start | bytes 147460
  0.6 10.8 %copy-start.16 = (f32[32,128]{1,0:T(8,128)S(1)}, f32[32,128]{1,0:T(8,128)}, u32[]{:S(2)}) copy-start(f32[32,128]{1,0:T(8,128)} %param.9) | copy-start | bytes 49156
  0.6 10.8 %copy-start = (f32[128,32,128]{2,1,0:T(8,128)S(1)}, f32[128,32,128]{2,1,0:T(8,128)}, u32[]{:S(2)}) copy-start(f32[128,32,128]{2,1,0:T(8,128)} %param.7) | copy-start | bytes 6291460
  4.1 36.3 %all-to-all-start = ((bf16[8,128,512]{2,1,0:T(8,128)(2,1)}), bf16[8,128,512]{2,1,0:T(8,128)(2,1)S(1)}, u32[]{:S(2)}, u32[]{:S(2)}) async-start(bf16[8,128,512]{2,1,0:T(8,128)(2,1)} %shard_map.86), calls=%async_computation | async-start | bytes 2097152 | tf_op jit(solution)/shard_map/all_to_all | solution.py:688
  12.9 15.3 %collective-permute-start = (f32[1,36,32,128]{3,2,1,0:T(8,128)}, f32[1,36,32,128]{3,2,1,0:T(8,128)S(1)}, u32[]{:S(2)}, u32[]{:S(2)}) collective-permute-start(f32[1,36,32,128]{3,2,1,0:T(8,128)} %get-tuple-element.69), channel_id=1, source_target_pairs={{0,1},{1,2},{2,3},{3,0},{4,5},{5,6},{6,7},{7,4},{8,9},{9,10},{10,1... | collective-permute-start | bytes 1769480 | tf_op jit(solution)/shard_map/ppermute | solution.py:660
  12.9 16.4 %collective-permute-start.1 = (f32[1,36,32,128]{3,2,1,0:T(8,128)}, f32[1,36,32,128]{3,2,1,0:T(8,128)S(1)}, u32[]{:S(2)}, u32[]{:S(2)}) collective-permute-start(f32[1,36,32,128]{3,2,1,0:T(8,128)} %get-tuple-element.70), channel_id=1, source_target_pairs={{0,2},{1,3},{2,0},{3,1},{4,6},{5,7},{6,4},{7,5},{8,10},{9,11},{10,... | collective-permute-start | bytes 1769480 | tf_op jit(solution)/shard_map/ppermute | solution.py:660
  14.5 26.0 %collective-permute-start.2 = (f32[1,36,32,128]{3,2,1,0:T(8,128)S(1)}, f32[1,36,32,128]{3,2,1,0:T(8,128)S(1)}, u32[]{:S(2)}, u32[]{:S(2)}) collective-permute-start(f32[1,36,32,128]{3,2,1,0:T(8,128)S(1)} %get-tuple-element.68), channel_id=1, source_target_pairs={{0,3},{1,0},{2,1},{3,2},{4,7},{5,4},{6,5},{7,6},{8,11},{9,8},{10,9... | collective-permute-start | bytes 1769480 | tf_op jit(solution)/shard_map/ppermute | solution.py:660
  15.9 10.6 %copy-start.7 = (f32[128,32,128]{2,1,0:T(8,128)S(1)}, f32[128,32,128]{2,1,0:T(8,128)}, u32[]{:S(2)}) copy-start(f32[128,32,128]{2,1,0:T(8,128)} %param.8) | copy-start | bytes 6291460
  28.2 20.0 %copy-start.2 = (f32[1,36,32,128]{3,2,1,0:T(8,128)}, f32[1,36,32,128]{3,2,1,0:T(8,128)S(1)}, u32[]{:S(2)}) copy-start(f32[1,36,32,128]{3,2,1,0:T(8,128)S(1)} %collective-permute-done.refs_1_) | copy-start | bytes 1769476
  29.3 18.9 %copy-start.3 = (f32[1,36,32,128]{3,2,1,0:T(8,128)}, f32[1,36,32,128]{3,2,1,0:T(8,128)S(1)}, u32[]{:S(2)}) copy-start(f32[1,36,32,128]{3,2,1,0:T(8,128)S(1)} %collective-permute-done.1.refs_2_) | copy-start | bytes 1769476
  40.4 7.8 %copy-start.4 = (f32[1,36,32,128]{3,2,1,0:T(8,128)}, f32[1,36,32,128]{3,2,1,0:T(8,128)S(1)}, u32[]{:S(2)}) copy-start(f32[1,36,32,128]{3,2,1,0:T(8,128)S(1)} %collective-permute-done.2.refs_3_) | copy-start | bytes 1769476
  40.4 10.4 %copy-start.5 = (bf16[8,128,512]{2,1,0:T(8,128)(2,1)}, bf16[8,128,512]{2,1,0:T(8,128)(2,1)S(1)}, u32[]{:S(2)}) copy-start(bf16[8,128,512]{2,1,0:T(8,128)(2,1)S(1)} %all-to-all-done) | copy-start | bytes 3145732
  40.4 27.7 %collective-permute-start.5 = (f32[1,32,32,128]{3,2,1,0:T(8,128)}, f32[1,32,32,128]{3,2,1,0:T(8,128)S(1)}, u32[]{:S(2)}, u32[]{:S(2)}) collective-permute-start(f32[1,32,32,128]{3,2,1,0:T(8,128)} %get-tuple-element.35), channel_id=1, source_target_pairs={{0,1},{1,2},{2,3},{3,0},{4,5},{5,6},{6,7},{7,4},{8,9},{9,10},{10,1... | collective-permute-start | bytes 1572872 | tf_op jit(solution)/shard_map/ppermute | solution.py:660
  41.3 26.9 %collective-permute-start.6 = (f32[1,32,32,128]{3,2,1,0:T(8,128)}, f32[1,32,32,128]{3,2,1,0:T(8,128)}, u32[]{:S(2)}, u32[]{:S(2)}) collective-permute-start(f32[1,32,32,128]{3,2,1,0:T(8,128)} %get-tuple-element.36), channel_id=1, source_target_pairs={{0,2},{1,3},{2,0},{3,1},{4,6},{5,7},{6,4},{7,5},{8,10},{9,11},{10,... | collective-permute-start | bytes 1572872 | tf_op jit(solution)/shard_map/ppermute | solution.py:660
  42.8 25.4 %collective-permute-start.7 = (f32[1,32,32,128]{3,2,1,0:T(8,128)}, f32[1,32,32,128]{3,2,1,0:T(8,128)}, u32[]{:S(2)}, u32[]{:S(2)}) collective-permute-start(f32[1,32,32,128]{3,2,1,0:T(8,128)} %get-tuple-element.37), channel_id=1, source_target_pairs={{0,3},{1,0},{2,1},{3,2},{4,7},{5,4},{6,5},{7,6},{8,11},{9,8},{10,9... | collective-permute-start | bytes 1572872 | tf_op jit(solution)/shard_map/ppermute | solution.py:660
  42.8 16.7 %collective-permute-start.3 = (bf16[1024,128]{1,0:T(8,128)(2,1)S(1)}, bf16[1024,128]{1,0:T(8,128)(2,1)S(1)}, u32[]{:S(2)}, u32[]{:S(2)}) collective-permute-start(bf16[1024,128]{1,0:T(8,128)(2,1)S(1)} %get-tuple-element.65), channel_id=1, source_target_pairs={{0,4},{4,8},{8,12},{12,16},{16,20},{20,24},{24,28},{28,1},{1,5},{5... | collective-permute-start | bytes 786440 | tf_op jit(solution)/shard_map/ppermute | solution.py:336
  44.9 14.7 %collective-permute-start.4 = (bf16[1024,128]{1,0:T(8,128)(2,1)S(1)}, bf16[1024,128]{1,0:T(8,128)(2,1)S(1)}, u32[]{:S(2)}, u32[]{:S(2)}) collective-permute-start(bf16[1024,128]{1,0:T(8,128)(2,1)S(1)} %get-tuple-element.64), channel_id=1, source_target_pairs={{4,0},{8,4},{12,8},{16,12},{20,16},{24,20},{28,24},{1,28},{5,1},{9... | collective-permute-start | bytes 786440 | tf_op jit(solution)/shard_map/ppermute | solution.py:337
  59.6 0.8 copy-start.12
  68.2 5.4 %copy-start.9 = (f32[1,32,32,128]{3,2,1,0:T(8,128)}, f32[1,32,32,128]{3,2,1,0:T(8,128)S(1)}, u32[]{:S(2)}) copy-start(f32[1,32,32,128]{3,2,1,0:T(8,128)S(1)} %collective-permute-done.5.refs_5_) | copy-start | bytes 1572868
  68.2 36.8 %all-to-all-start.1 = ((bf16[32,32,640]{2,1,0:T(8,128)(2,1)}), bf16[32,32,640]{2,1,0:T(8,128)(2,1)S(1)}, u32[]{:S(2)}, u32[]{:S(2)}) async-start(bf16[32,32,640]{2,1,0:T(8,128)(2,1)} %bitcast.19), calls=%async_computation.1 | async-start | bytes 2621440 | tf_op jit(solution)/shard_map/all_to_all | solution.py:731
  105.0 1.1 copy-start.8
  143.0 5.4 %copy-start.6 = (bf16[32,32,512]{2,1,0:T(8,128)(2,1)}, bf16[32,32,512]{2,1,0:T(8,128)(2,1)S(1)}, u32[]{:S(2)}) copy-start(bf16[32,32,512]{2,1,0:T(8,128)(2,1)S(1)} %all_to_all.36) | copy-start | bytes 3145732
  143.0 14.1 %collective-permute-start.8 = (bf16[1024,128]{1,0:T(8,128)(2,1)S(1)}, bf16[1024,128]{1,0:T(8,128)(2,1)S(1)}, u32[]{:S(2)}, u32[]{:S(2)}) collective-permute-start(bf16[1024,128]{1,0:T(8,128)(2,1)S(1)} %get-tuple-element.63), channel_id=1, source_target_pairs={{0,4},{4,8},{8,12},{12,16},{16,20},{20,24},{24,28},{28,1},{1,5},{5... | collective-permute-start | bytes 786440 | tf_op jit(solution)/shard_map/ppermute | solution.py:336
  144.6 13.0 %collective-permute-start.9 = (bf16[1024,128]{1,0:T(8,128)(2,1)S(1)}, bf16[1024,128]{1,0:T(8,128)(2,1)S(1)}, u32[]{:S(2)}, u32[]{:S(2)}) collective-permute-start(bf16[1024,128]{1,0:T(8,128)(2,1)S(1)} %get-tuple-element.62), channel_id=1, source_target_pairs={{4,0},{8,4},{12,8},{16,12},{20,16},{24,20},{28,24},{1,28},{5,1},{9... | collective-permute-start | bytes 786440 | tf_op jit(solution)/shard_map/ppermute | solution.py:337
  157.8 0.7 copy-start.13
  164.7 29.7 %all-to-all-start.3 = ((bf16[32,32,512]{2,1,0:T(8,128)(2,1)}), bf16[32,32,512]{2,1,0:T(8,128)(2,1)S(1)}, u32[]{:S(2)}, u32[]{:S(2)}) async-start(bf16[32,32,512]{2,1,0:T(8,128)(2,1)} %bitcast.20), calls=%async_computation.3 | async-start | bytes 2097152 | tf_op jit(solution)/shard_map/all_to_all | solution.py:741
  194.4 1.0 copy-start.1
  200.5 12.6 %collective-permute-start.10 = (bf16[1,32,32,128]{3,2,1,0:T(8,128)(2,1)}, bf16[1,32,32,128]{3,2,1,0:T(8,128)(2,1)S(1)}, u32[]{:S(2)}, u32[]{:S(2)}) collective-permute-start(bf16[1,32,32,128]{3,2,1,0:T(8,128)(2,1)} %get-tuple-element.51), channel_id=1, source_target_pairs={{0,1},{1,2},{2,3},{3,0},{4,5},{5,6},{6,7},{7,4},{8,9},{9,10},{10,1... | collective-permute-start | bytes 786440 | tf_op jit(solution)/shard_map/ppermute | solution.py:660
  200.5 12.6 %collective-permute-start.11 = (bf16[1,32,32,128]{3,2,1,0:T(8,128)(2,1)}, bf16[1,32,32,128]{3,2,1,0:T(8,128)(2,1)S(1)}, u32[]{:S(2)}, u32[]{:S(2)}) collective-permute-start(bf16[1,32,32,128]{3,2,1,0:T(8,128)(2,1)} %get-tuple-element.52), channel_id=1, source_target_pairs={{0,2},{1,3},{2,0},{3,1},{4,6},{5,7},{6,4},{7,5},{8,10},{9,11},{10,... | collective-permute-start | bytes 786440 | tf_op jit(solution)/shard_map/ppermute | solution.py:660
  202.0 12.0 %collective-permute-start.12 = (bf16[1,32,32,128]{3,2,1,0:T(8,128)(2,1)}, bf16[1,32,32,128]{3,2,1,0:T(8,128)(2,1)S(1)}, u32[]{:S(2)}, u32[]{:S(2)}) collective-permute-start(bf16[1,32,32,128]{3,2,1,0:T(8,128)(2,1)} %get-tuple-element.53), channel_id=1, source_target_pairs={{0,3},{1,0},{2,1},{3,2},{4,7},{5,4},{6,5},{7,6},{8,11},{9,8},{10,9... | collective-permute-start | bytes 786440 | tf_op jit(solution)/shard_map/ppermute | solution.py:660
  209.2 3.8 %copy-start.14 = (bf16[1,32,32,128]{3,2,1,0:T(8,128)(2,1)S(1)}, bf16[1,32,32,128]{3,2,1,0:T(8,128)(2,1)}, u32[]{:S(2)}) copy-start(bf16[1,32,32,128]{3,2,1,0:T(8,128)(2,1)} %get-tuple-element.50) | copy-start | bytes 786436
  209.2 18.1 %all-to-all-start.4 = ((bf16[128,32,128]{2,1,0:T(8,128)(2,1)}), bf16[128,32,128]{2,1,0:T(8,128)(2,1)S(1)}, u32[]{:S(2)}, u32[]{:S(2)}) async-start(bf16[128,32,128]{2,1,0:T(8,128)(2,1)} %bitcast.26), calls=%async_computation.4 | async-start | bytes 2097152 | tf_op jit(solution)/shard_map/all_to_all | solution.py:693
  (2 other events, 1.4 us)

commit v9 on v8

--- a/solution.py
+++ b/solution.py
@@ -9,8 +9,10 @@
 from jax.sharding import PartitionSpec as P
 
 RELAXATION = 0.6
-VMEM_BYTES = 57 << 20
-UNROLL = 2
+VMEM_BYTES = 60 << 20
+SHARED_VMEM_BYTES = 48 << 20
+COUPLING_VMEM_BYTES = 32 << 20
+UNROLL = 4
 
 
 def sine_table(length):
@@ -72,18 +74,17 @@
                 ]
 
 
-def all_weights(parts, place, coefs, height):
+def all_weights(parts, place, height):
     slab_count = len(parts)
-    _, entries, rows, ny = parts[0].shape
+    _, coefs, rows, ny = parts[0].shape
     nx = slab_count * rows
-    last = entries // coefs - 1
     fields = coefs - 1
     return pl.pallas_call(
         functools.partial(weights_kernel, slab_count),
         grid_spec=pltpu.PrefetchScalarGridSpec(
             num_scalar_prefetch=1,
             grid=(1,),
-            in_specs=[pl.BlockSpec((1, coefs, rows, ny), lambda i, *_: (0, last, 0, 0))]
+            in_specs=[pl.BlockSpec((1, coefs, rows, ny), lambda i, *_: (0, 0, 0, 0))]
             * slab_count,
             out_specs=[
                 pl.BlockSpec((5, nx, ny), lambda i, *_: (0, 0, 0)),
@@ -98,7 +99,7 @@
             jax.ShapeDtypeStruct((5, nx, ny), jnp.float32),
             jax.ShapeDtypeStruct((fields * 5 * height, ny), jnp.float32),
         ],
-        compiler_params=pltpu.CompilerParams(vmem_limit_bytes=VMEM_BYTES),
+        compiler_params=pltpu.CompilerParams(vmem_limit_bytes=COUPLING_VMEM_BYTES),
     )(place, *parts)
 
 
@@ -210,7 +211,7 @@
             ),
         ),
         out_shape=jax.ShapeDtypeStruct((blocks, fields, width, blocks * width), coupling.dtype),
-        compiler_params=pltpu.CompilerParams(vmem_limit_bytes=VMEM_BYTES),
+        compiler_params=pltpu.CompilerParams(vmem_limit_bytes=COUPLING_VMEM_BYTES),
     )(coupling_list, pair_count, coupling)
 
 
@@ -339,7 +340,7 @@
     matrix_spec = pl.BlockSpec((unroll, fields, width, depth), lambda i: (i, 0, 0, 0))
     weight_spec = pl.BlockSpec(weights.shape, lambda i: (0, 0))
     sums_spec = pl.BlockSpec((unroll * width, cells), lambda i: (i, 0))
-    params = pltpu.CompilerParams(vmem_limit_bytes=VMEM_BYTES)
+    params = pltpu.CompilerParams(vmem_limit_bytes=COUPLING_VMEM_BYTES)
     inner = pl.pallas_call(
         functools.partial(inner_kernel, height, cols),
         grid=(blocks // unroll,),
@@ -533,7 +534,9 @@
     return pl.BlockSpec((shape[0], GROUP, shape[2]), lambda g: (0, g, 0))
 
 
-def per_group(kernel, groups, operands, in_specs, out_shape, out_specs, scratch=(), flops=0):
+def per_group(
+    kernel, groups, operands, in_specs, out_shape, out_specs, scratch=(), flops=0, vmem=SHARED_VMEM_BYTES
+):
     moved = sum(a.size * a.dtype.itemsize for a in operands)
     return pl.pallas_call(
         kernel,
@@ -543,7 +546,7 @@
         out_shape=out_shape,
         scratch_shapes=scratch,
         cost_estimate=pl.CostEstimate(flops=flops, bytes_accessed=2 * moved, transcendentals=0),
-        compiler_params=pltpu.CompilerParams(vmem_limit_bytes=VMEM_BYTES),
+        compiler_params=pltpu.CompilerParams(vmem_limit_bytes=vmem),
     )(*operands)
 
 
@@ -566,7 +569,7 @@
             out_specs=[slab] * 3,
         ),
         out_shape=[shape] * 3,
-        compiler_params=pltpu.CompilerParams(vmem_limit_bytes=VMEM_BYTES),
+        compiler_params=pltpu.CompilerParams(vmem_limit_bytes=SHARED_VMEM_BYTES),
     )(place, *current_parts, *right_side_parts, weights, right)
 
 
@@ -626,7 +629,7 @@
         cost_estimate=pl.CostEstimate(
             flops=0, bytes_accessed=2 * base.size * 4, transcendentals=0
         ),
-        compiler_params=pltpu.CompilerParams(vmem_limit_bytes=VMEM_BYTES),
+        compiler_params=pltpu.CompilerParams(vmem_limit_bytes=SHARED_VMEM_BYTES),
     )(lax.axis_index("slab").reshape(1), base, coupled)
     return out, parts
 
@@ -642,6 +645,7 @@
         slabs,
         (),
         solve_flops(resid, tables),
+        VMEM_BYTES,
     )
 
 
@@ -685,6 +689,7 @@
 
     strips = pack_strips(guess, mode_count)
     coefs = jnp.concatenate([mean_coef[None], field_coef], 0)[None]
+    strips, coefs = lax.optimization_barrier((strips, coefs))
     state = lax.all_to_all(strips, "mode", 0, 0, tiled=True)
     state = state.reshape(mode_count * modes, height * cols)
 
@@ -692,16 +697,17 @@
         flat = block.reshape(modes, rows, cols)
         return lax.all_to_all(flat, "slab", 0, 0, tiled=True)
 
+    coef_parts = moved_parts([coefs] * slab_count, "slab")
     guess_parts = parts_of(guess.reshape(slab_count, share, rows, cols), "slab")
-    guess_parts = [jnp.concatenate([part, coefs], axis=1) for part in guess_parts]
     guess_parts = moved_parts(guess_parts, "slab")
     right_parts = parts_of(right_side.reshape(slab_count, share, rows, cols), "slab")
-    state, guess_parts, right_parts = lax.optimization_barrier((state, guess_parts, right_parts))
+    guess_parts, right_parts = lax.optimization_barrier((guess_parts, right_parts))
     right_parts = moved_parts(right_parts, "slab")
 
     slab = lax.axis_index("slab")
     place = jnp.stack([slab, slab * mode_count + lax.axis_index("mode")])
-    mean_weights, strip_weights = all_weights(guess_parts, place, fields + 1, height)
+    coef_parts, coupling = lax.optimization_barrier((coef_parts, coupling))
+    mean_weights, strip_weights = all_weights(coef_parts, place, height)
     matrix = dense_coupling(coupling, coupling_list, pair_count, fields)
 
     row_high, row_low = split_table(sine_table(nx))

time: 231 us -> 233 us (level)
  Pallas kernels: 74.3 us -> 51.4 us
  local copies, waits for them, and re-layouts: 5.78 us -> 18.6 us
  waiting for transfers between devices: 71.8 us -> 83.8 us
  starting transfers between devices: 38.2 us -> 42.4 us
  other arithmetic: 8.66 us -> 5.53 us
    unnamed x34 -> x52, local copies, waits for them, and re-layouts: 3.84 us -> 12.6 us
    ppermute x9 -> x12, waiting for transfers between devices: 13.4 us -> 21.8 us  [onwards(): lax.ppermute(part, axis, [(i, (i + shift) % count) for i in range(count)])]
    pallas_call x2, Pallas kernels: 17.4 us -> 10.7 us  [coupled_sums(): pl.pallas_call(functools.partial(inner_kernel, height, cols), grid=(block...]
    pallas_call x2, Pallas kernels: 14 us -> 8.07 us  [coupled_sums(): pl.pallas_call(functools.partial(border_kernel, height, cols, first, scal...]
    pallas_call x1, Pallas kernels: 8.99 us -> 3.2 us  [dense_coupling(): pl.pallas_call(functools.partial(dense_kernel, fields), grid_spec=pltpu.P...]
    dynamic_slice x2, local copies, waits for them, and re-layouts: 1.55 us -> 5.59 us  [parts_of(): lax.dynamic_index_in_dim(block, lax.rem(here + shift, count), 0)]
    ppermute x2, waiting for transfers between devices: 0.44 us -> 4.28 us  [coupled_sums(): below = lax.ppermute(state[:, :cols], both, [(b, a) for a, b in onward])]
    ppermute x9 -> x12, starting transfers between devices: 8.24 us -> 10.4 us  [onwards(): lax.ppermute(part, axis, [(i, (i + shift) % count) for i in range(count)])]
  transfers between devices with their start and end apart: 17 -> 20, of which waited for: 8 -> 9; matrix products, arithmetic and copies ran while one was open for 4% -> 4% of each run, Pallas kernels for 23% -> 15%
where the time goes in v9:
time: 233 us; the launch traced here: 232 us
  waiting for transfers between devices  83.8 us (36%)
  Pallas kernels  51.4 us (22%)
  starting transfers between devices  42.4 us (18%)
  blocking collectives  29.6 us (13%)
  local copies, waits for them, and re-layouts  18.6 us (8%)
  other arithmetic  5.53 us (2%)
    all_to_all x2, waiting for transfers between devices, local(): lax.all_to_all(sums, both, 0, 0, tiled=True).reshape(devices, share, -1)  45.5 us
    all_to_all x1, blocking collectives, local(): state = lax.all_to_all(state, both, 0, 0, tiled=True)  29.6 us
    ppermute x12, waiting for transfers between devices, onwards(): lax.ppermute(part, axis, [(i, (i + shift) % count) for i in range(count)])  21.8 us
    pallas_call x3, Pallas kernels, per_group(): pl.pallas_call(kernel, grid=(groups,), in_specs=in_specs, out_specs=out_s...  14.9 us
    unnamed x52, local copies, waits for them, and re-layouts  12.6 us
    pallas_call x2, Pallas kernels, coupled_sums(): pl.pallas_call(functools.partial(inner_kernel, height, cols), grid=(block...  10.7 us
    all_to_all x1, waiting for transfers between devices, to_slabs(): return lax.all_to_all(flat, 'slab', 0, 0, tiled=True)  10.7 us
    ppermute x12, starting transfers between devices, onwards(): lax.ppermute(part, axis, [(i, (i + shift) % count) for i in range(count)])  10.4 us
  transfers between devices with their start and end apart: 20, of which 9 were waited for; matrix products, arithmetic and copies ran while one was open for 4% of the time, Pallas kernels for 15%

profile of v9, /device:TPU:0, one launch (start us, length us, event | category | flops | bytes accessed | tf_op | source)
XLA Modules:
  0.0 232.4 jit_solution(8954634170319447872)
XLA Ops:
  0.6 3.3 %shard_map.86 = bf16[8,128,512]{2,1,0:T(8,128)(2,1)} custom-call(f32[4096,128]{1,0:T(8,128)} %bitcast.23), custom_call_target="tpu_custom_call" | custom-call | tf_op jit(solution)/shard_map/pallas_call | solution.py:177
  4.0 7.3 %all-to-all-start = ((bf16[8,128,512]{2,1,0:T(8,128)(2,1)}), bf16[8,128,512]{2,1,0:T(8,128)(2,1)S(1)}, u32[]{:S(2)}, u32[]{:S(2)}) async-start(bf16[8,128,512]{2,1,0:T(8,128)(2,1)} %shard_map.86), calls=%async_computation | async-start | bytes 2097152 | tf_op jit(solution)/shard_map/all_to_all | solution.py:693
  12.8 2.7 %constant_dynamic-slice_fusion.4 = (f32[1,32,32,128]{3,2,1,0:T(8,128)}, f32[1,32,32,128]{3,2,1,0:T(8,128)}, f32[1,32,32,128]{3,2,1,0:T(8,128)}, f32[1,32,32,128]{3,2,1,0:T(8,128)S(1)}) fusion(f32[4,32,32,128]{3,2,1,0:T(8,128)} %bitcast.24, s32[]{:T(128)S(6)} %select_n.40, s32[]{:T(128)S(6)} %select_n.39, s32[]{:T(128)S(6)} %select_n.38, s32[]{:T(128)S(6)} %select_n.37), kind=kLoop, calls=%fused_computation.39 | loop fusion | bytes 4194320 | tf_op jit(solution)/shard_map/jit(dynamic_index_in_dim)/dynamic_slice | solution.py:671
  17.6 2.8 %constant_dynamic-slice_fusion = (f32[1,32,32,128]{3,2,1,0:T(8,128)}, f32[1,32,32,128]{3,2,1,0:T(8,128)}, f32[1,32,32,128]{3,2,1,0:T(8,128)}, f32[1,32,32,128]{3,2,1,0:T(8,128)S(1)}) fusion(f32[4,32,32,128]{3,2,1,0:T(8,128)} %bitcast.25, s32[]{:T(128)S(6)} %select_n.40, s32[]{:T(128)S(6)} %select_n.39, s32[]{:T(128)S(6)} %select_n.38, s32[]{:T(128)S(6)} %select_n.37), kind=kLoop, calls=%fused_computation.35 | loop fusion | bytes 4194320 | tf_op jit(solution)/shard_map/jit(dynamic_index_in_dim)/dynamic_slice | solution.py:671
  22.0 18.0 %collective-permute-done.5.refs_3_ = f32[1,4,32,128]{3,2,1,0:T(8,128)S(1)} collective-permute-done((f32[1,4,32,128]{3,2,1,0:T(8,128)S(1)}, f32[1,4,32,128]{3,2,1,0:T(8,128)S(1)}, u32[]{:S(2)}, u32[]{:S(2)}) %collective-permute-start.5) | collective-permute-done | bytes 65568 | tf_op jit(solution)/shard_map/ppermute | solution.py:664
  40.0 3.2 %shard_map.87.matrix_ref = bf16[8,3,128,1024]{3,2,1,0:T(8,128)(2,1)S(1)} custom-call(s32[8,16]{1,0:T(8,128)S(1)} %copy-done.19, s32[8]{0:T(128)S(1)} %copy-done.20, bf16[8,16,128,128]{3,2,1,0:T(8,128)(2,1)S(1)} %copy-done.4), custom_call_target="tpu_custom_call" | custom-call | tf_op jit(solution)/shard_map/pallas_call | solution.py:203
  43.2 2.6 %copy-done = bf16[8,3,128,1024]{3,2,1,0:T(8,128)(2,1)} copy-done((bf16[8,3,128,1024]{3,2,1,0:T(8,128)(2,1)}, bf16[8,3,128,1024]{3,2,1,0:T(8,128)(2,1)S(1)}, u32[]{:S(2)}) %copy-start) | copy-done | bytes 6291480
  48.3 2.0 collective-permute-start.10
  51.9 2.0 collective-permute-start.6
  53.9 3.6 %collective-permute-start.7 = (bf16[1024,128]{1,0:T(8,128)(2,1)S(1)}, bf16[1024,128]{1,0:T(8,128)(2,1)S(1)}, u32[]{:S(2)}, u32[]{:S(2)}) collective-permute-start(bf16[1024,128]{1,0:T(8,128)(2,1)S(1)} %get-tuple-element.76), channel_id=1, source_target_pairs={{4,0},{8,4},{12,8},{16,12},{20,16},{24,20},{28,24},{1,28},{5,1},{9... | collective-permute-start | bytes 786440 | tf_op jit(solution)/shard_map/ppermute | solution.py:338
  57.5 2.8 %copy-done.1 = bf16[8,3,128,1024]{3,2,1,0:T(8,128)(2,1)S(1)} copy-done((bf16[8,3,128,1024]{3,2,1,0:T(8,128)(2,1)S(1)}, bf16[8,3,128,1024]{3,2,1,0:T(8,128)(2,1)}, u32[]{:S(2)}) %copy-start.1) | copy-done | bytes 6291480
  60.3 5.4 %shard_map.89.inner_ref = f32[1024,512]{1,0:T(8,128)S(1)} custom-call(bf16[8,3,128,1024]{3,2,1,0:T(8,128)(2,1)S(1)} %copy-done.1, bf16[1024,512]{1,0:T(8,128)(2,1)S(1)} %bitcast.20, f32[60,128]{1,0:T(8,128)S(1)} %get-tuple-element.45.weight_ref), custom_call_target="tpu_custom_call" | custom-call | flops 3221225472 | bytes 6291456 | tf_op jit(solution)/shard_map/pallas_call | solution.py:344
  65.7 2.1 collective-permute-done.7.below_ref
  67.8 5.1 %shard_map.90 = bf16[1024,640]{1,0:T(8,128)(2,1)} custom-call(bf16[8,3,128,1024]{3,2,1,0:T(8,128)(2,1)S(1)} %copy-done.2, bf16[1024,128]{1,0:T(8,128)(2,1)S(1)} %collective-permute-done.6.above_ref, bf16[1024,128]{1,0:T(8,128)(2,1)S(1)} %collective-permute-done.7.below_ref, f32[60,128]{1,0:T(8,128)S(1)} %get-tuple-element.45.weight_ref, ...), custom_call_target="tpu_custom_call" | custom-call | tf_op jit(solution)/shard_map/pallas_call | solution.py:358
  72.9 3.2 %collective-permute-done.9.refs_6_ = f32[1,32,32,128]{3,2,1,0:T(8,128)} collective-permute-done((f32[1,32,32,128]{3,2,1,0:T(8,128)}, f32[1,32,32,128]{3,2,1,0:T(8,128)}, u32[]{:S(2)}, u32[]{:S(2)}) %collective-permute-start.9) | collective-permute-done | bytes 524320 | tf_op jit(solution)/shard_map/ppermute | solution.py:664
  76.1 7.1 %all-to-all-start.1 = ((bf16[32,32,640]{2,1,0:T(8,128)(2,1)}), bf16[32,32,640]{2,1,0:T(8,128)(2,1)}, u32[]{:S(2)}, u32[]{:S(2)}) async-start(bf16[32,32,640]{2,1,0:T(8,128)(2,1)} %bitcast.8), calls=%async_computation.1 | async-start | bytes 2621440 | tf_op jit(solution)/shard_map/all_to_all | solution.py:737
  86.4 5.6 %shard_map.91 = (f32[4,32,32,128]{3,2,1,0:T(8,128)}, f32[4,32,32,128]{3,2,1,0:T(8,128)}, f32[4,32,32,128]{3,2,1,0:T(8,128)}) custom-call(s32[2]{0:T(128)S(1)} %pad_add_fusion.place_ref, f32[1,32,32,128]{3,2,1,0:T(8,128)S(1)} %get-tuple-element.34.refs_0_, f32[1,32,32,128]{3,2,1,0:T(8,128)S(1)} %copy-done.12, f32[1,32,32,128]{3,2,1,0:T(8,128)S(1)} %copy-done.14, ...), custom_call_target="tpu_custom_call" | custom-call | tf_op jit(solution)/shard_map/pallas_call | solution.py:559
  92.0 23.3 %all-to-all-done.1.coupled_ref = bf16[32,32,640]{2,1,0:T(8,128)(2,1)} async-done(((bf16[32,32,640]{2,1,0:T(8,128)(2,1)}), bf16[32,32,640]{2,1,0:T(8,128)(2,1)}, u32[]{:S(2)}, u32[]{:S(2)}) %all-to-all-start.1) | async-done | bytes 1310752 | tf_op jit(solution)/shard_map/all_to_all | solution.py:737
  115.3 6.3 %shard_map.92 = (f32[4,32,32,128]{3,2,1,0:T(8,128)S(1)}, bf16[32,32,512]{2,1,0:T(8,128)(2,1)S(1)}) custom-call(f32[4,32,32,128]{3,2,1,0:T(8,128)} %get-tuple-element.55.current_ref, f32[4,32,32,128]{3,2,1,0:T(8,128)} %get-tuple-element.56.base_ref, bf16[32,32,640]{2,1,0:T(8,128)(2,1)} %all-to-all-done.1.coupled_ref, ...), custom_call_target="tpu_custom_call" | custom-call | flops 1610612736 | bytes 11665408 | tf_op jit(solution)/shard_map/pallas_call | solution.py:541
  121.7 29.6 %all_to_all.36 = bf16[32,32,512]{2,1,0:T(8,128)(2,1)S(1)} all-to-all(bf16[32,32,512]{2,1,0:T(8,128)(2,1)S(1)} %get-tuple-element.60), channel_id=1, replica_groups=mesh['mode'=8,'slab'=4] {'mode','slab'}, dimensions={0} | all-to-all | bytes 2097152 | tf_op jit(solution)/shard_map/all_to_all | solution.py:743
  152.9 3.9 %collective-permute-start.12 = (bf16[1024,128]{1,0:T(8,128)(2,1)S(1)}, bf16[1024,128]{1,0:T(8,128)(2,1)S(1)}, u32[]{:S(2)}, u32[]{:S(2)}) collective-permute-start(bf16[1024,128]{1,0:T(8,128)(2,1)S(1)} %get-tuple-element.74), channel_id=1, source_target_pairs={{4,0},{8,4},{12,8},{16,12},{20,16},{24,20},{28,24},{1,28},{5,1},{9... | collective-permute-start | bytes 786440 | tf_op jit(solution)/shard_map/ppermute | solution.py:338
  156.7 5.4 %shard_map.94.inner_ref = f32[1024,512]{1,0:T(8,128)S(1)} custom-call(bf16[8,3,128,1024]{3,2,1,0:T(8,128)(2,1)S(1)} %bitcast.18, bf16[1024,512]{1,0:T(8,128)(2,1)S(1)} %bitcast.22, f32[60,128]{1,0:T(8,128)S(1)} %get-tuple-element.45.weight_ref), custom_call_target="tpu_custom_call" | custom-call | flops 3221225472 | bytes 6291456 | tf_op jit(solution)/shard_map/pallas_call | solution.py:344
  163.7 2.2 collective-permute-done.12.below_ref
  165.9 3.0 %shard_map.95 = bf16[1024,512]{1,0:T(8,128)(2,1)} custom-call(bf16[8,3,128,1024]{3,2,1,0:T(8,128)(2,1)S(1)} %bitcast.18, bf16[1024,128]{1,0:T(8,128)(2,1)S(1)} %collective-permute-done.11.above_ref, bf16[1024,128]{1,0:T(8,128)(2,1)S(1)} %collective-permute-done.12.below_ref, f32[60,128]{1,0:T(8,128)S(1)} %get-tuple-element.45.weight_ref, ...), custom_call_target="tpu_custom_call" | custom-call | tf_op jit(solution)/shard_map/pallas_call | solution.py:358
  168.9 3.1 %all-to-all-start.3 = ((bf16[32,32,512]{2,1,0:T(8,128)(2,1)}), bf16[32,32,512]{2,1,0:T(8,128)(2,1)S(1)}, u32[]{:S(2)}, u32[]{:S(2)}) async-start(bf16[32,32,512]{2,1,0:T(8,128)(2,1)} %bitcast.10), calls=%async_computation.3 | async-start | bytes 2097152 | tf_op jit(solution)/shard_map/all_to_all | solution.py:747
  172.0 2.7 %shard_map.93.base_ref = f32[4,32,32,128]{3,2,1,0:T(8,128)S(1)} custom-call(f32[4,32,32,128]{3,2,1,0:T(8,128)S(1)} %copy-done.7, f32[4,32,32,128]{3,2,1,0:T(8,128)} %get-tuple-element.59.right_side_ref, f32[5,128,128]{2,1,0:T(8,128)S(1)} %copy-done.10), custom_call_target="tpu_custom_call" | custom-call | bytes 9043968 | tf_op jit(solution)/shard_map/pallas_call | solution.py:541
  176.0 22.2 %all-to-all-done.3.coupled_ref = bf16[32,32,512]{2,1,0:T(8,128)(2,1)S(1)} async-done(((bf16[32,32,512]{2,1,0:T(8,128)(2,1)}), bf16[32,32,512]{2,1,0:T(8,128)(2,1)S(1)}, u32[]{:S(2)}, u32[]{:S(2)}) %all-to-all-start.3) | async-done | bytes 1048608 | tf_op jit(solution)/shard_map/all_to_all | solution.py:747
  198.2 4.0 %shard_map.96 = (f32[4,32,32,128]{3,2,1,0:T(8,128)S(1)}, bf16[1,32,32,128]{3,2,1,0:T(8,128)(2,1)S(1)}, bf16[1,32,32,128]{3,2,1,0:T(8,128)(2,1)S(1)}, bf16[1,32,3...) custom-call(s32[1]{0:T(128)} %bitcast.here_ref, f32[4,32,32,128]{3,2,1,0:T(8,128)} %copy-done.3, ...), custom_call_target="tpu_custom_call" | custom-call | bytes 4194304 | tf_op jit(solution)/shard_map/pallas_call | solution.py:618
  206.4 5.8 %shard_map.97 = bf16[4,32,32,128]{3,2,1,0:T(8,128)(2,1)} custom-call(f32[4,32,32,128]{3,2,1,0:T(8,128)} %copy-done.6, f32[4,32,32,128]{3,2,1,0:T(8,128)} %copy-done.21, bf16[256,256]{1,0:T(8,128)(2,1)} %copy-done.5, bf16[256,256]{1,0:T(8,128)(2,1)} %copy-done.15, f32[128,128]{1,0:T(8,128)} %copy-done.16), custom_call_target="tpu_custom_call" | custom-call | flops 1610612736 | bytes 9043968 | tf_op jit(solution)/shard_map/pallas_call | solution.py:541
  212.2 3.5 %all-to-all-start.4 = ((bf16[128,32,128]{2,1,0:T(8,128)(2,1)}), bf16[128,32,128]{2,1,0:T(8,128)(2,1)S(1)}, u32[]{:S(2)}, u32[]{:S(2)}) async-start(bf16[128,32,128]{2,1,0:T(8,128)(2,1)} %bitcast.26), calls=%async_computation.4 | async-start | bytes 2097152 | tf_op jit(solution)/shard_map/all_to_all | solution.py:698
  219.5 10.7 %all-to-all-done.4 = bf16[128,32,128]{2,1,0:T(8,128)(2,1)S(1)} async-done(((bf16[128,32,128]{2,1,0:T(8,128)(2,1)}), bf16[128,32,128]{2,1,0:T(8,128)(2,1)S(1)}, u32[]{:S(2)}, u32[]{:S(2)}) %all-to-all-start.4) | async-done | bytes 1048608 | tf_op jit(solution)/shard_map/all_to_all | solution.py:698
  230.2 2.2 fusion.10
  (94 shorter events, 24.7 us)
Async XLA Ops:
  4.0 47.9 %all-to-all-start = ((bf16[8,128,512]{2,1,0:T(8,128)(2,1)}), bf16[8,128,512]{2,1,0:T(8,128)(2,1)S(1)}, u32[]{:S(2)}, u32[]{:S(2)}) async-start(bf16[8,128,512]{2,1,0:T(8,128)(2,1)} %shard_map.86), calls=%async_computation | async-start | bytes 2097152 | tf_op jit(solution)/shard_map/all_to_all | solution.py:693
  11.3 9.5 %collective-permute-start.3 = (f32[1,4,32,128]{3,2,1,0:T(8,128)S(1)}, f32[1,4,32,128]{3,2,1,0:T(8,128)S(1)}, u32[]{:S(2)}, u32[]{:S(2)}) collective-permute-start(f32[1,4,32,128]{3,2,1,0:T(8,128)S(1)} %maximum_bitcast_fusion.refs_0_), channel_id=1, source_target_pairs={{0,1},{1,2},{2,3},{3,0},{4,5},{5,6},{6,7},{7,4},{8,9},{9,10},{10,1... | collective-permute-start | bytes 196616 | tf_op jit(solution)/shard_map/ppermute | solution.py:664
  11.3 10.7 %collective-permute-start.4 = (f32[1,4,32,128]{3,2,1,0:T(8,128)S(1)}, f32[1,4,32,128]{3,2,1,0:T(8,128)}, u32[]{:S(2)}, u32[]{:S(2)}) collective-permute-start(f32[1,4,32,128]{3,2,1,0:T(8,128)S(1)} %maximum_bitcast_fusion.refs_0_), channel_id=1, source_target_pairs={{0,2},{1,3},{2,0},{3,1},{4,6},{5,7},{6,4},{7,5},{8,10},{9,11},{10,... | collective-permute-start | bytes 196616 | tf_op jit(solution)/shard_map/ppermute | solution.py:664
  15.6 32.7 %collective-permute-start = (f32[1,32,32,128]{3,2,1,0:T(8,128)}, f32[1,32,32,128]{3,2,1,0:T(8,128)S(1)}, u32[]{:S(2)}, u32[]{:S(2)}) collective-permute-start(f32[1,32,32,128]{3,2,1,0:T(8,128)} %get-tuple-element.72), channel_id=1, source_target_pairs={{0,1},{1,2},{2,3},{3,0},{4,5},{5,6},{6,7},{7,4},{8,9},{9,10},{10,1... | collective-permute-start | bytes 1572872 | tf_op jit(solution)/shard_map/ppermute | solution.py:664
  15.9 32.4 %collective-permute-start.1 = (f32[1,32,32,128]{3,2,1,0:T(8,128)}, f32[1,32,32,128]{3,2,1,0:T(8,128)S(1)}, u32[]{:S(2)}, u32[]{:S(2)}) collective-permute-start(f32[1,32,32,128]{3,2,1,0:T(8,128)} %get-tuple-element.71), channel_id=1, source_target_pairs={{0,2},{1,3},{2,0},{3,1},{4,6},{5,7},{6,4},{7,5},{8,10},{9,11},{10,... | collective-permute-start | bytes 1572872 | tf_op jit(solution)/shard_map/ppermute | solution.py:664
  17.4 31.0 %collective-permute-start.2 = (f32[1,32,32,128]{3,2,1,0:T(8,128)}, f32[1,32,32,128]{3,2,1,0:T(8,128)}, u32[]{:S(2)}, u32[]{:S(2)}) collective-permute-start(f32[1,32,32,128]{3,2,1,0:T(8,128)} %get-tuple-element.70), channel_id=1, source_target_pairs={{0,3},{1,0},{2,1},{3,2},{4,7},{5,4},{6,5},{7,6},{8,11},{9,8},{10,9... | collective-permute-start | bytes 1572872 | tf_op jit(solution)/shard_map/ppermute | solution.py:664
  17.6 22.4 %copy-start.4 = (bf16[8,16,128,128]{3,2,1,0:T(8,128)(2,1)S(1)}, bf16[8,16,128,128]{3,2,1,0:T(8,128)(2,1)}, u32[]{:S(2)}) copy-start(bf16[8,16,128,128]{3,2,1,0:T(8,128)(2,1)} %coupling_ref) | copy-start | bytes 12582916
  17.6 22.4 %copy-start.19 = (s32[8,16]{1,0:T(8,128)S(1)}, s32[8,16]{1,0:T(8,128)}, u32[]{:S(2)}) copy-start(s32[8,16]{1,0:T(8,128)} %entry_ref.1) | copy-start | bytes 1540
  17.6 22.4 %copy-start.20 = (s32[8]{0:T(128)S(1)}, s32[8]{0:T(128)}, u32[]{:S(2)}) copy-start(s32[8]{0:T(128)} %count_ref.1) | copy-start | bytes 100
  20.8 94.5 %copy-start.15 = (bf16[256,256]{1,0:T(8,128)(2,1)}, bf16[256,256]{1,0:T(8,128)(2,1)S(1)}, u32[]{:S(2)}) copy-start(bf16[256,256]{1,0:T(8,128)(2,1)S(1)} %get-tuple-element.78.left_ref) | copy-start | bytes 393220
  20.8 145.1 %copy-start.5 = (bf16[256,256]{1,0:T(8,128)(2,1)}, bf16[256,256]{1,0:T(8,128)(2,1)S(1)}, u32[]{:S(2)}) copy-start(bf16[256,256]{1,0:T(8,128)(2,1)S(1)} %get-tuple-element.79.right_ref.refs_9_) | copy-start | bytes 393220
  21.5 18.5 %collective-permute-start.5 = (f32[1,4,32,128]{3,2,1,0:T(8,128)S(1)}, f32[1,4,32,128]{3,2,1,0:T(8,128)S(1)}, u32[]{:S(2)}, u32[]{:S(2)}) collective-permute-start(f32[1,4,32,128]{3,2,1,0:T(8,128)S(1)} %maximum_bitcast_fusion.refs_0_), channel_id=1, source_target_pairs={{0,3},{1,0},{2,1},{3,2},{4,7},{5,4},{6,5},{7,6},{8,11},{9,8},{10,9... | collective-permute-start | bytes 196616 | tf_op jit(solution)/shard_map/ppermute | solution.py:664
  22.0 23.9 %copy-start.18 = (f32[1,4,32,128]{3,2,1,0:T(8,128)S(1)}, f32[1,4,32,128]{3,2,1,0:T(8,128)}, u32[]{:S(2)}) copy-start(f32[1,4,32,128]{3,2,1,0:T(8,128)} %copy-done.17) | copy-start | bytes 196612
  48.3 17.4 %copy-start.11 = (f32[1,32,32,128]{3,2,1,0:T(8,128)}, f32[1,32,32,128]{3,2,1,0:T(8,128)S(1)}, u32[]{:S(2)}) copy-start(f32[1,32,32,128]{3,2,1,0:T(8,128)S(1)} %collective-permute-done.refs_1_) | copy-start | bytes 1572868
  48.3 17.4 %copy-start.13 = (f32[1,32,32,128]{3,2,1,0:T(8,128)}, f32[1,32,32,128]{3,2,1,0:T(8,128)S(1)}, u32[]{:S(2)}) copy-start(f32[1,32,32,128]{3,2,1,0:T(8,128)S(1)} %collective-permute-done.1.refs_2_) | copy-start | bytes 1572868
  48.3 24.6 %collective-permute-start.10 = (f32[1,32,32,128]{3,2,1,0:T(8,128)}, f32[1,32,32,128]{3,2,1,0:T(8,128)}, u32[]{:S(2)}, u32[]{:S(2)}) collective-permute-start(f32[1,32,32,128]{3,2,1,0:T(8,128)} %get-tuple-element.49), channel_id=1, source_target_pairs={{0,3},{1,0},{2,1},{3,2},{4,7},{5,4},{6,5},{7,6},{8,11},{9,8},{10,9... | collective-permute-start | bytes 1572872 | tf_op jit(solution)/shard_map/ppermute | solution.py:664
  50.3 22.6 %collective-permute-start.8 = (f32[1,32,32,128]{3,2,1,0:T(8,128)}, f32[1,32,32,128]{3,2,1,0:T(8,128)}, u32[]{:S(2)}, u32[]{:S(2)}) collective-permute-start(f32[1,32,32,128]{3,2,1,0:T(8,128)} %get-tuple-element.47), channel_id=1, source_target_pairs={{0,1},{1,2},{2,3},{3,0},{4,5},{5,6},{6,7},{7,4},{8,9},{9,10},{10,1... | collective-permute-start | bytes 1572872 | tf_op jit(solution)/shard_map/ppermute | solution.py:664
  50.3 25.8 %collective-permute-start.9 = (f32[1,32,32,128]{3,2,1,0:T(8,128)}, f32[1,32,32,128]{3,2,1,0:T(8,128)}, u32[]{:S(2)}, u32[]{:S(2)}) collective-permute-start(f32[1,32,32,128]{3,2,1,0:T(8,128)} %get-tuple-element.48), channel_id=1, source_target_pairs={{0,2},{1,3},{2,0},{3,1},{4,6},{5,7},{6,4},{7,5},{8,10},{9,11},{10,... | collective-permute-start | bytes 1572872 | tf_op jit(solution)/shard_map/ppermute | solution.py:664
  51.9 13.9 %collective-permute-start.6 = (bf16[1024,128]{1,0:T(8,128)(2,1)S(1)}, bf16[1024,128]{1,0:T(8,128)(2,1)S(1)}, u32[]{:S(2)}, u32[]{:S(2)}) collective-permute-start(bf16[1024,128]{1,0:T(8,128)(2,1)S(1)} %get-tuple-element.77), channel_id=1, source_target_pairs={{0,4},{4,8},{8,12},{12,16},{16,20},{20,24},{24,28},{28,1},{1,5},{5... | collective-permute-start | bytes 786440 | tf_op jit(solution)/shard_map/ppermute | solution.py:337
  53.9 13.9 %collective-permute-start.7 = (bf16[1024,128]{1,0:T(8,128)(2,1)S(1)}, bf16[1024,128]{1,0:T(8,128)(2,1)S(1)}, u32[]{:S(2)}, u32[]{:S(2)}) collective-permute-start(bf16[1024,128]{1,0:T(8,128)(2,1)S(1)} %get-tuple-element.76), channel_id=1, source_target_pairs={{4,0},{8,4},{12,8},{16,12},{20,16},{24,20},{28,24},{1,28},{5,1},{9... | collective-permute-start | bytes 786440 | tf_op jit(solution)/shard_map/ppermute | solution.py:338
  76.1 39.2 %all-to-all-start.1 = ((bf16[32,32,640]{2,1,0:T(8,128)(2,1)}), bf16[32,32,640]{2,1,0:T(8,128)(2,1)}, u32[]{:S(2)}, u32[]{:S(2)}) async-start(bf16[32,32,640]{2,1,0:T(8,128)(2,1)} %bitcast.8), calls=%async_computation.1 | async-start | bytes 2621440 | tf_op jit(solution)/shard_map/all_to_all | solution.py:737
  83.3 32.0 %copy-start.16 = (f32[128,128]{1,0:T(8,128)}, f32[128,128]{1,0:T(8,128)S(1)}, u32[]{:S(2)}) copy-start(f32[128,128]{1,0:T(8,128)S(1)} %subtract_divide_fusion.scale_ref) | copy-start | bytes 196612
  86.4 70.3 %slice-start = ((s8[6291456]{0:T(1024)(128)(4,1)}), s8[2097152]{0:T(1024)(128)(4,1)S(1)}, s32[]{:S(2)}) async-start(s8[6291456]{0:T(1024)(128)(4,1)} %bitcast.17), calls=%async_computation.5 | async-start | bytes 4194304
  115.3 41.4 %slice-start.1 = ((s8[6291456]{0:T(1024)(128)(4,1)}), s8[4194304]{0:T(1024)(128)(4,1)S(1)}, s32[]{:S(2)}) async-start(s8[6291456]{0:T(1024)(128)(4,1)} %bitcast.17), calls=%async_computation.6 | async-start | bytes 8388608
  121.7 40.4 %copy-start.6 = (f32[4,32,32,128]{3,2,1,0:T(8,128)}, f32[4,32,32,128]{3,2,1,0:T(8,128)S(1)}, u32[]{:S(2)}) copy-start(f32[4,32,32,128]{3,2,1,0:T(8,128)S(1)} %get-tuple-element.58.current_ref) | copy-start | bytes 6291460
  151.3 12.3 %collective-permute-start.11 = (bf16[1024,128]{1,0:T(8,128)(2,1)S(1)}, bf16[1024,128]{1,0:T(8,128)(2,1)S(1)}, u32[]{:S(2)}, u32[]{:S(2)}) collective-permute-start(bf16[1024,128]{1,0:T(8,128)(2,1)S(1)} %get-tuple-element.75), channel_id=1, source_target_pairs={{0,4},{4,8},{8,12},{12,16},{16,20},{20,24},{24,28},{28,1},{1,5},{5... | collective-permute-start | bytes 786440 | tf_op jit(solution)/shard_map/ppermute | solution.py:337
  152.9 13.0 %collective-permute-start.12 = (bf16[1024,128]{1,0:T(8,128)(2,1)S(1)}, bf16[1024,128]{1,0:T(8,128)(2,1)S(1)}, u32[]{:S(2)}, u32[]{:S(2)}) collective-permute-start(bf16[1024,128]{1,0:T(8,128)(2,1)S(1)} %get-tuple-element.74), channel_id=1, source_target_pairs={{4,0},{8,4},{12,8},{16,12},{20,16},{24,20},{28,24},{1,28},{5,1},{9... | collective-permute-start | bytes 786440 | tf_op jit(solution)/shard_map/ppermute | solution.py:338
  168.9 29.3 %all-to-all-start.3 = ((bf16[32,32,512]{2,1,0:T(8,128)(2,1)}), bf16[32,32,512]{2,1,0:T(8,128)(2,1)S(1)}, u32[]{:S(2)}, u32[]{:S(2)}) async-start(bf16[32,32,512]{2,1,0:T(8,128)(2,1)} %bitcast.10), calls=%async_computation.3 | async-start | bytes 2097152 | tf_op jit(solution)/shard_map/all_to_all | solution.py:747
  203.5 12.5 %collective-permute-start.13 = (bf16[1,32,32,128]{3,2,1,0:T(8,128)(2,1)S(1)}, bf16[1,32,32,128]{3,2,1,0:T(8,128)(2,1)S(1)}, u32[]{:S(2)}, u32[]{:S(2)}) collective-permute-start(bf16[1,32,32,128]{3,2,1,0:T(8,128)(2,1)S(1)} %get-tuple-element.63), channel_id=1, source_target_pairs={{0,1},{1,2},{2,3},{3,0},{4,5},{5,6},{6,7},{7,4},{8,9},{9,10},{10,1... | collective-permute-start | bytes 786440 | tf_op jit(solution)/shard_map/ppermute | solution.py:664
  203.5 12.6 %collective-permute-start.14 = (bf16[1,32,32,128]{3,2,1,0:T(8,128)(2,1)S(1)}, bf16[1,32,32,128]{3,2,1,0:T(8,128)(2,1)S(1)}, u32[]{:S(2)}, u32[]{:S(2)}) collective-permute-start(bf16[1,32,32,128]{3,2,1,0:T(8,128)(2,1)S(1)} %get-tuple-element.64), channel_id=1, source_target_pairs={{0,2},{1,3},{2,0},{3,1},{4,6},{5,7},{6,4},{7,5},{8,10},{9,11},{10,... | collective-permute-start | bytes 786440 | tf_op jit(solution)/shard_map/ppermute | solution.py:664
  205.0 11.7 %collective-permute-start.15 = (bf16[1,32,32,128]{3,2,1,0:T(8,128)(2,1)S(1)}, bf16[1,32,32,128]{3,2,1,0:T(8,128)(2,1)S(1)}, u32[]{:S(2)}, u32[]{:S(2)}) collective-permute-start(bf16[1,32,32,128]{3,2,1,0:T(8,128)(2,1)S(1)} %get-tuple-element.65), channel_id=1, source_target_pairs={{0,3},{1,0},{2,1},{3,2},{4,7},{5,4},{6,5},{7,6},{8,11},{9,8},{10,9... | collective-permute-start | bytes 786440 | tf_op jit(solution)/shard_map/ppermute | solution.py:664
  212.2 18.0 %all-to-all-start.4 = ((bf16[128,32,128]{2,1,0:T(8,128)(2,1)}), bf16[128,32,128]{2,1,0:T(8,128)(2,1)S(1)}, u32[]{:S(2)}, u32[]{:S(2)}) async-start(bf16[128,32,128]{2,1,0:T(8,128)(2,1)} %bitcast.26), calls=%async_computation.4 | async-start | bytes 2097152 | tf_op jit(solution)/shard_map/all_to_all | solution.py:698
  (14 other events, 35.9 us)

commit v10 on v9

--- a/solution.py
+++ b/solution.py
@@ -11,7 +11,7 @@
 RELAXATION = 0.6
 VMEM_BYTES = 60 << 20
 SHARED_VMEM_BYTES = 48 << 20
-COUPLING_VMEM_BYTES = 32 << 20
+SMALL_VMEM_BYTES = 9 << 20
 UNROLL = 4
 
 
@@ -54,53 +54,85 @@
     return lax.rem(here + count - shift, count)
 
 
-def weights_kernel(slabs, place_ref, *refs):
+def in_order(here, shift, count):
+    return lax.rem(here + count - shift, count)
+
+
+def strip_weights_kernel(slabs, height, place_ref, *refs):
     part_refs = refs[:slabs]
-    mean_ref, strip_weight_ref, coef_ref, full_ref = refs[slabs:]
-    _, nx, ny = mean_ref.shape
-    fields = coef_ref.shape[1] - 1
-    height = strip_weight_ref.shape[0] // (5 * fields)
+    out_ref, coef_ref = refs[slabs:]
+    _, nx, ny = coef_ref.shape
+    rows = nx // slabs
+    fields = out_ref.shape[0] // (5 * height)
     for shift, part_ref in enumerate(part_refs):
-        coef_ref[in_order(place_ref[0], shift, slabs)] = part_ref[0]
-    for which, weight in enumerate(stencil_weights(coef_ref[:, 0].reshape(nx, ny))):
-        mean_ref[which] = weight
+        start = in_order(place_ref[0], shift, slabs) * rows
+        coef_ref[:, pl.ds(pl.multiple_of(start, rows), rows), :] = part_ref[0]
+    col = lax.broadcasted_iota(jnp.int32, (1, ny), 1)
+    first = place_ref[1] * height
     for f in range(fields):
-        for which, weight in enumerate(stencil_weights(coef_ref[:, f + 1].reshape(nx, ny))):
-            full_ref[...] = weight
-            for r in range(height):
+        lines = []
+        for r in range(-1, height + 1):
+            at = jnp.clip(first + r, 0, nx - 1)
+            lines.append(coef_ref[f + 1, pl.ds(at, 1), :])
+        for r in range(height):
+            here = lines[r + 1]
+            up = 0.5 * (here + lines[r])
+            down = 0.5 * (here + lines[r + 2])
+            left = 0.5 * (here + jnp.where(col == 0, here, pltpu.roll(here, 1, 1)))
+            right = 0.5 * (here + jnp.where(col == ny - 1, here, pltpu.roll(here, ny - 1, 1)))
+            weights = (
+                up + down + left + right,
+                jnp.where(first + r == 0, 0.0, up),
+                jnp.where(first + r == nx - 1, 0.0, down),
+                jnp.where(col == 0, 0.0, left),
+                jnp.where(col == ny - 1, 0.0, right),
+            )
+            for which, weight in enumerate(weights):
                 at = (f * 5 + which) * height + r
-                strip_weight_ref[at : at + 1, :] = full_ref[
-                    pl.ds(place_ref[1] * height + r, 1), :
-                ]
-
-
-def all_weights(parts, place, height):
-    slab_count = len(parts)
-    _, coefs, rows, ny = parts[0].shape
-    nx = slab_count * rows
-    fields = coefs - 1
+                out_ref[at : at + 1, :] = weight
+
+
+def mean_weights_kernel(slabs, place_ref, *refs):
+    part_refs = refs[:slabs]
+    out_ref, coef_ref = refs[slabs:]
+    _, nx, ny = out_ref.shape
+    for shift, part_ref in enumerate(part_refs):
+        coef_ref[in_order(place_ref[0], shift, slabs)] = part_ref[0, 0]
+    for which, weight in enumerate(stencil_weights(coef_ref[...].reshape(nx, ny))):
+        out_ref[which] = weight
+
+
+def weights_of(kernel, parts, place, coefs, out, scratch):
+    _, entries, rows, ny = parts[0].shape
+    last = entries // coefs - 1
     return pl.pallas_call(
-        functools.partial(weights_kernel, slab_count),
+        kernel,
         grid_spec=pltpu.PrefetchScalarGridSpec(
             num_scalar_prefetch=1,
             grid=(1,),
-            in_specs=[pl.BlockSpec((1, coefs, rows, ny), lambda i, *_: (0, 0, 0, 0))]
-            * slab_count,
-            out_specs=[
-                pl.BlockSpec((5, nx, ny), lambda i, *_: (0, 0, 0)),
-                pl.BlockSpec((fields * 5 * height, ny), lambda i, *_: (0, 0)),
-            ],
-            scratch_shapes=[
-                pltpu.VMEM((slab_count, coefs, rows, ny), jnp.float32),
-                pltpu.VMEM((nx, ny), jnp.float32),
-            ],
+            in_specs=[pl.BlockSpec((1, coefs, rows, ny), lambda i, *_: (0, last, 0, 0))]
+            * len(parts),
+            out_specs=pl.BlockSpec(out, lambda i, *_: (0,) * len(out)),
+            scratch_shapes=[pltpu.VMEM(scratch, jnp.float32)],
         ),
-        out_shape=[
-            jax.ShapeDtypeStruct((5, nx, ny), jnp.float32),
-            jax.ShapeDtypeStruct((fields * 5 * height, ny), jnp.float32),
-        ],
-        compiler_params=pltpu.CompilerParams(vmem_limit_bytes=COUPLING_VMEM_BYTES),
+        out_shape=jax.ShapeDtypeStruct(out, jnp.float32),
+        compiler_params=pltpu.CompilerParams(vmem_limit_bytes=SMALL_VMEM_BYTES),
     )(place, *parts)
+
+
+def strip_weights_of(parts, place, coefs, height):
+    slabs = len(parts)
+    _, _, rows, ny = parts[0].shape
+    kernel = functools.partial(strip_weights_kernel, slabs, height)
+    out = ((coefs - 1) * 5 * height, ny)
+    return weights_of(kernel, parts, place, coefs, out, (coefs, slabs * rows, ny))
+
+
+def mean_weights_of(parts, place, coefs):
+    slabs = len(parts)
+    _, _, rows, ny = parts[0].shape
+    kernel = functools.partial(mean_weights_kernel, slabs)
+    return weights_of(kernel, parts, place, coefs, (5, slabs * rows, ny), (slabs, rows, ny))
 
 
 def split(value):
@@ -200,6 +232,7 @@
 
 def dense_coupling(coupling, coupling_list, pair_count, fields):
     blocks, entries, width, _ = coupling.shape
+    moved = 2 * width * width * (entries + fields * blocks) * coupling.dtype.itemsize
     return pl.pallas_call(
         functools.partial(dense_kernel, fields),
         grid_spec=pltpu.PrefetchScalarGridSpec(
@@ -211,7 +244,7 @@
             ),
         ),
         out_shape=jax.ShapeDtypeStruct((blocks, fields, width, blocks * width), coupling.dtype),
-        compiler_params=pltpu.CompilerParams(vmem_limit_bytes=COUPLING_VMEM_BYTES),
+        compiler_params=pltpu.CompilerParams(vmem_limit_bytes=SMALL_VMEM_BYTES + moved),
     )(coupling_list, pair_count, coupling)
 
 
@@ -340,7 +373,8 @@
     matrix_spec = pl.BlockSpec((unroll, fields, width, depth), lambda i: (i, 0, 0, 0))
     weight_spec = pl.BlockSpec(weights.shape, lambda i: (0, 0))
     sums_spec = pl.BlockSpec((unroll * width, cells), lambda i: (i, 0))
-    params = pltpu.CompilerParams(vmem_limit_bytes=COUPLING_VMEM_BYTES)
+    moved = 2 * unroll * fields * width * depth * matrix.dtype.itemsize
+    params = pltpu.CompilerParams(vmem_limit_bytes=2 * SMALL_VMEM_BYTES + moved)
     inner = pl.pallas_call(
         functools.partial(inner_kernel, height, cols),
         grid=(blocks // unroll,),
@@ -689,7 +723,6 @@
 
     strips = pack_strips(guess, mode_count)
     coefs = jnp.concatenate([mean_coef[None], field_coef], 0)[None]
-    strips, coefs = lax.optimization_barrier((strips, coefs))
     state = lax.all_to_all(strips, "mode", 0, 0, tiled=True)
     state = state.reshape(mode_count * modes, height * cols)
 
@@ -697,17 +730,17 @@
         flat = block.reshape(modes, rows, cols)
         return lax.all_to_all(flat, "slab", 0, 0, tiled=True)
 
-    coef_parts = moved_parts([coefs] * slab_count, "slab")
     guess_parts = parts_of(guess.reshape(slab_count, share, rows, cols), "slab")
+    guess_parts = [jnp.concatenate([part, coefs], axis=1) for part in guess_parts]
     guess_parts = moved_parts(guess_parts, "slab")
     right_parts = parts_of(right_side.reshape(slab_count, share, rows, cols), "slab")
-    guess_parts, right_parts = lax.optimization_barrier((guess_parts, right_parts))
+    state, guess_parts, right_parts = lax.optimization_barrier((state, guess_parts, right_parts))
     right_parts = moved_parts(right_parts, "slab")
 
     slab = lax.axis_index("slab")
     place = jnp.stack([slab, slab * mode_count + lax.axis_index("mode")])
-    coef_parts, coupling = lax.optimization_barrier((coef_parts, coupling))
-    mean_weights, strip_weights = all_weights(coef_parts, place, height)
+    strip_weights = strip_weights_of(guess_parts, place, fields + 1, height)
+    mean_weights = mean_weights_of(guess_parts, place, fields + 1)
     matrix = dense_coupling(coupling, coupling_list, pair_count, fields)
 
     row_high, row_low = split_table(sine_table(nx))

time: 233 us -> 224 us (0.961)
  waiting for transfers between devices: 83.8 us -> 74.1 us
  starting transfers between devices: 42.4 us -> 39.4 us
    ppermute x12 -> x9, waiting for transfers between devices: 21.8 us -> 14.9 us  [onwards(): lax.ppermute(part, axis, [(i, (i + shift) % count) for i in range(count)])]
    dynamic_slice x2, local copies, waits for them, and re-layouts: 5.59 us -> 1.57 us  [parts_of(): lax.dynamic_index_in_dim(block, lax.rem(here + shift, count), 0)]
    unnamed x52 -> x60, local copies, waits for them, and re-layouts: 12.6 us -> 15.9 us
    ppermute x12 -> x9, starting transfers between devices: 10.4 us -> 8.19 us  [onwards(): lax.ppermute(part, axis, [(i, (i + shift) % count) for i in range(count)])]
  transfers between devices with their start and end apart: 20 -> 17, of which waited for: 9 -> 9; matrix products, arithmetic and copies ran while one was open for 4% -> 4% of each run, Pallas kernels for 15% -> 16%
where the time goes in v10:
time: 224 us
  waiting for transfers between devices  74.1 us (33%)
  Pallas kernels  53 us (24%)
  starting transfers between devices  39.4 us (18%)
  blocking collectives  29.6 us (13%)
  local copies, waits for them, and re-layouts  18.9 us (8%)
  other arithmetic  7.53 us (3%)
    all_to_all x2, waiting for transfers between devices, local(): lax.all_to_all(sums, both, 0, 0, tiled=True).reshape(devices, share, -1)  44.8 us
    all_to_all x1, blocking collectives, local(): state = lax.all_to_all(state, both, 0, 0, tiled=True)  29.6 us
    unnamed x60, local copies, waits for them, and re-layouts  15.9 us
    ppermute x9, waiting for transfers between devices, onwards(): lax.ppermute(part, axis, [(i, (i + shift) % count) for i in range(count)])  14.9 us
    pallas_call x3, Pallas kernels, per_group(): pl.pallas_call(kernel, grid=(groups,), in_specs=in_specs, out_specs=out_s...  14.8 us
    pallas_call x2, Pallas kernels, coupled_sums(): pl.pallas_call(functools.partial(inner_kernel, height, cols), grid=(block...  12.1 us
    all_to_all x1, waiting for transfers between devices, to_slabs(): return lax.all_to_all(flat, 'slab', 0, 0, tiled=True)  10.6 us
    all_to_all x2, starting transfers between devices, local(): lax.all_to_all(sums, both, 0, 0, tiled=True).reshape(devices, share, -1)  9.58 us
  transfers between devices with their start and end apart: 17, of which 9 were waited for; matrix products, arithmetic and copies ran while one was open for 4% of the time, Pallas kernels for 16%

profile of v10, /device:TPU:0, one launch (start us, length us, event | category | flops | bytes accessed | tf_op | source)
XLA Modules:
  0.0 223.7 jit_solution(5933031614235848212)
XLA Ops:
  0.7 3.5 %shard_map.86 = bf16[8,128,512]{2,1,0:T(8,128)(2,1)} custom-call(f32[4096,128]{1,0:T(8,128)} %bitcast.24), custom_call_target="tpu_custom_call" | custom-call | tf_op jit(solution)/shard_map/pallas_call | solution.py:209
  4.1 7.3 %all-to-all-start = ((bf16[8,128,512]{2,1,0:T(8,128)(2,1)}), bf16[8,128,512]{2,1,0:T(8,128)(2,1)}, u32[]{:S(2)}, u32[]{:S(2)}) async-start(bf16[8,128,512]{2,1,0:T(8,128)(2,1)} %shard_map.86), calls=%async_computation | async-start | bytes 2097152 | tf_op jit(solution)/shard_map/all_to_all | solution.py:726
  16.0 2.2 copy-done.4
  18.1 3.0 %shard_map.87.matrix_ref = bf16[8,3,128,1024]{3,2,1,0:T(8,128)(2,1)S(1)} custom-call(s32[8,16]{1,0:T(8,128)S(1)} %copy-done.19, s32[8]{0:T(128)S(1)} %copy-done.20, bf16[8,16,128,128]{3,2,1,0:T(8,128)(2,1)S(1)} %copy-done.4), custom_call_target="tpu_custom_call" | custom-call | tf_op jit(solution)/shard_map/pallas_call | solution.py:236
  21.2 2.6 %copy-done = bf16[8,3,128,1024]{3,2,1,0:T(8,128)(2,1)} copy-done((bf16[8,3,128,1024]{3,2,1,0:T(8,128)(2,1)}, bf16[8,3,128,1024]{3,2,1,0:T(8,128)(2,1)S(1)}, u32[]{:S(2)}) %copy-start) | copy-done | bytes 6291480
  26.3 2.0 collective-permute-done.refs_1_
  29.5 11.1 %collective-permute-done.2.refs_3_ = f32[1,36,32,128]{3,2,1,0:T(8,128)} collective-permute-done((f32[1,36,32,128]{3,2,1,0:T(8,128)}, f32[1,36,32,128]{3,2,1,0:T(8,128)}, u32[]{:S(2)}, u32[]{:S(2)}) %collective-permute-start.2) | collective-permute-done | bytes 589856 | tf_op jit(solution)/shard_map/ppermute | solution.py:698
  44.0 2.1 collective-permute-start.3
  46.0 3.3 %collective-permute-start.4 = (bf16[1024,128]{1,0:T(8,128)(2,1)S(1)}, bf16[1024,128]{1,0:T(8,128)(2,1)S(1)}, u32[]{:S(2)}, u32[]{:S(2)}) collective-permute-start(bf16[1024,128]{1,0:T(8,128)(2,1)S(1)} %get-tuple-element.60), channel_id=1, source_target_pairs={{4,0},{8,4},{12,8},{16,12},{20,16},{24,20},{28,24},{1,28},{5,1},{9... | collective-permute-start | bytes 786440 | tf_op jit(solution)/shard_map/ppermute | solution.py:371
  50.9 2.8 %copy-done.1 = bf16[8,3,128,1024]{3,2,1,0:T(8,128)(2,1)S(1)} copy-done((bf16[8,3,128,1024]{3,2,1,0:T(8,128)(2,1)S(1)}, bf16[8,3,128,1024]{3,2,1,0:T(8,128)(2,1)}, u32[]{:S(2)}) %copy-start.1) | copy-done | bytes 6291480
  53.7 6.7 %shard_map.89.inner_ref = f32[1024,512]{1,0:T(8,128)S(1)} custom-call(bf16[8,3,128,1024]{3,2,1,0:T(8,128)(2,1)S(1)} %copy-done.1, bf16[1024,512]{1,0:T(8,128)(2,1)} %bitcast.3.state_ref, f32[60,128]{1,0:T(8,128)S(1)} %shard_map.88.weight_ref), custom_call_target="tpu_custom_call" | custom-call | flops 3221225472 | bytes 6291456 | tf_op jit(solution)/shard_map/pallas_call | solution.py:378
  60.5 4.2 %shard_map.90 = bf16[1024,640]{1,0:T(8,128)(2,1)S(1)} custom-call(bf16[8,3,128,1024]{3,2,1,0:T(8,128)(2,1)S(1)} %bitcast.18, bf16[1024,128]{1,0:T(8,128)(2,1)S(1)} %collective-permute-done.3.above_ref, bf16[1024,128]{1,0:T(8,128)(2,1)S(1)} %collective-permute-done.4.below_ref, f32[60,128]{1,0:T(8,128)S(1)} %shard_map.88.weight_ref, ...), custom_call_target="tpu_custom_call" | custom-call | tf_op jit(solution)/shard_map/pallas_call | solution.py:392
  67.2 6.5 %all-to-all-start.1 = ((bf16[32,32,640]{2,1,0:T(8,128)(2,1)}), bf16[32,32,640]{2,1,0:T(8,128)(2,1)}, u32[]{:S(2)}, u32[]{:S(2)}) async-start(bf16[32,32,640]{2,1,0:T(8,128)(2,1)} %bitcast.21), calls=%async_computation.1 | async-start | bytes 2621440 | tf_op jit(solution)/shard_map/all_to_all | solution.py:770
  75.5 5.4 %shard_map.92 = (f32[4,32,32,128]{3,2,1,0:T(8,128)}, f32[4,32,32,128]{3,2,1,0:T(8,128)}, f32[4,32,32,128]{3,2,1,0:T(8,128)}) custom-call(s32[2]{0:T(128)S(1)} %pad_add_fusion.place_ref, f32[1,36,32,128]{3,2,1,0:T(8,128)S(1)} %get-tuple-element.26.refs_0_, f32[1,36,32,128]{3,2,1,0:T(8,128)S(1)} %collective-permute-done.refs_1_, ...), custom_call_target="tpu_custom_call" | custom-call | tf_op jit(solution)/shard_map/pallas_call | solution.py:593
  81.7 24.2 %all-to-all-done.1.coupled_ref = bf16[32,32,640]{2,1,0:T(8,128)(2,1)} async-done(((bf16[32,32,640]{2,1,0:T(8,128)(2,1)}), bf16[32,32,640]{2,1,0:T(8,128)(2,1)}, u32[]{:S(2)}, u32[]{:S(2)}) %all-to-all-start.1) | async-done | bytes 1310752 | tf_op jit(solution)/shard_map/all_to_all | solution.py:770
  106.8 6.3 %shard_map.93 = (f32[4,32,32,128]{3,2,1,0:T(8,128)S(1)}, bf16[32,32,512]{2,1,0:T(8,128)(2,1)S(1)}) custom-call(f32[4,32,32,128]{3,2,1,0:T(8,128)} %get-tuple-element.39.current_ref, f32[4,32,32,128]{3,2,1,0:T(8,128)} %get-tuple-element.40.base_ref, bf16[32,32,640]{2,1,0:T(8,128)(2,1)} %all-to-all-done.1.coupled_ref, ...), custom_call_target="tpu_custom_call" | custom-call | flops 1610612736 | bytes 11665408 | tf_op jit(solution)/shard_map/pallas_call | solution.py:575
  113.1 29.6 %all_to_all.36 = bf16[32,32,512]{2,1,0:T(8,128)(2,1)S(1)} all-to-all(bf16[32,32,512]{2,1,0:T(8,128)(2,1)S(1)} %get-tuple-element.44), channel_id=1, replica_groups=mesh['mode'=8,'slab'=4] {'mode','slab'}, dimensions={0} | all-to-all | bytes 2097152 | tf_op jit(solution)/shard_map/all_to_all | solution.py:776
  144.3 3.9 %collective-permute-start.9 = (bf16[1024,128]{1,0:T(8,128)(2,1)S(1)}, bf16[1024,128]{1,0:T(8,128)(2,1)S(1)}, u32[]{:S(2)}, u32[]{:S(2)}) collective-permute-start(bf16[1024,128]{1,0:T(8,128)(2,1)S(1)} %get-tuple-element.58), channel_id=1, source_target_pairs={{4,0},{8,4},{12,8},{16,12},{20,16},{24,20},{28,24},{1,28},{5,1},{9... | collective-permute-start | bytes 786440 | tf_op jit(solution)/shard_map/ppermute | solution.py:371
  148.2 5.4 %shard_map.95.inner_ref = f32[1024,512]{1,0:T(8,128)S(1)} custom-call(bf16[8,3,128,1024]{3,2,1,0:T(8,128)(2,1)S(1)} %bitcast.20, bf16[1024,512]{1,0:T(8,128)(2,1)S(1)} %bitcast.23, f32[60,128]{1,0:T(8,128)S(1)} %shard_map.88.weight_ref), custom_call_target="tpu_custom_call" | custom-call | flops 3221225472 | bytes 6291456 | tf_op jit(solution)/shard_map/pallas_call | solution.py:378
  153.6 1.5 collective-permute-done.8.above_ref
  155.1 2.2 collective-permute-done.9.below_ref
  157.3 3.0 %shard_map.96 = bf16[1024,512]{1,0:T(8,128)(2,1)} custom-call(bf16[8,3,128,1024]{3,2,1,0:T(8,128)(2,1)S(1)} %bitcast.20, bf16[1024,128]{1,0:T(8,128)(2,1)S(1)} %collective-permute-done.8.above_ref, bf16[1024,128]{1,0:T(8,128)(2,1)S(1)} %collective-permute-done.9.below_ref, f32[60,128]{1,0:T(8,128)S(1)} %shard_map.88.weight_ref, ...), custom_call_target="tpu_custom_call" | custom-call | tf_op jit(solution)/shard_map/pallas_call | solution.py:392
  160.3 3.0 %all-to-all-start.3 = ((bf16[32,32,512]{2,1,0:T(8,128)(2,1)}), bf16[32,32,512]{2,1,0:T(8,128)(2,1)S(1)}, u32[]{:S(2)}, u32[]{:S(2)}) async-start(bf16[32,32,512]{2,1,0:T(8,128)(2,1)} %bitcast.10), calls=%async_computation.3 | async-start | bytes 2097152 | tf_op jit(solution)/shard_map/all_to_all | solution.py:780
  163.4 1.6 copy-done.9
  165.0 2.7 %shard_map.94.base_ref = f32[4,32,32,128]{3,2,1,0:T(8,128)S(1)} custom-call(f32[4,32,32,128]{3,2,1,0:T(8,128)S(1)} %copy-done.9, f32[4,32,32,128]{3,2,1,0:T(8,128)} %get-tuple-element.43.right_side_ref, f32[5,128,128]{2,1,0:T(8,128)S(1)} %copy-done.6), custom_call_target="tpu_custom_call" | custom-call | bytes 9043968 | tf_op jit(solution)/shard_map/pallas_call | solution.py:575
  169.0 20.6 %all-to-all-done.3.coupled_ref = bf16[32,32,512]{2,1,0:T(8,128)(2,1)S(1)} async-done(((bf16[32,32,512]{2,1,0:T(8,128)(2,1)}), bf16[32,32,512]{2,1,0:T(8,128)(2,1)S(1)}, u32[]{:S(2)}, u32[]{:S(2)}) %all-to-all-start.3) | async-done | bytes 1048608 | tf_op jit(solution)/shard_map/all_to_all | solution.py:780
  189.6 4.0 %shard_map.97 = (f32[4,32,32,128]{3,2,1,0:T(8,128)S(1)}, bf16[1,32,32,128]{3,2,1,0:T(8,128)(2,1)S(1)}, bf16[1,32,32,128]{3,2,1,0:T(8,128)(2,1)S(1)}, bf16[1,32,3...) custom-call(s32[1]{0:T(128)} %bitcast.here_ref, f32[4,32,32,128]{3,2,1,0:T(8,128)} %copy-done.2, ...), custom_call_target="tpu_custom_call" | custom-call | bytes 4194304 | tf_op jit(solution)/shard_map/pallas_call | solution.py:652
  197.8 5.8 %shard_map.98 = bf16[4,32,32,128]{3,2,1,0:T(8,128)(2,1)} custom-call(f32[4,32,32,128]{3,2,1,0:T(8,128)} %copy-done.8, f32[4,32,32,128]{3,2,1,0:T(8,128)} %copy-done.21, bf16[256,256]{1,0:T(8,128)(2,1)} %copy-done.7, bf16[256,256]{1,0:T(8,128)(2,1)} %get-tuple-element.62.left_ref, f32[128,128]{1,0:T(8,128)} %copy-done.18), custom_call_target="tpu_custom_call" | custom-call | flops 1610612736 | bytes 9043968 | tf_op jit(solution)/shard_map/pallas_call | solution.py:575
  203.6 3.5 %all-to-all-start.4 = ((bf16[128,32,128]{2,1,0:T(8,128)(2,1)}), bf16[128,32,128]{2,1,0:T(8,128)(2,1)S(1)}, u32[]{:S(2)}, u32[]{:S(2)}) async-start(bf16[128,32,128]{2,1,0:T(8,128)(2,1)} %bitcast.27), calls=%async_computation.4 | async-start | bytes 2097152 | tf_op jit(solution)/shard_map/all_to_all | solution.py:731
  209.1 1.8 fusion.11
  210.9 10.6 %all-to-all-done.4 = bf16[128,32,128]{2,1,0:T(8,128)(2,1)S(1)} async-done(((bf16[128,32,128]{2,1,0:T(8,128)(2,1)}), bf16[128,32,128]{2,1,0:T(8,128)(2,1)S(1)}, u32[]{:S(2)}, u32[]{:S(2)}) %all-to-all-start.4) | async-done | bytes 1048608 | tf_op jit(solution)/shard_map/all_to_all | solution.py:731
  221.5 2.2 fusion.10
  (99 shorter events, 27.9 us)
Async XLA Ops:
  0.6 10.8 %copy-start.24 = (f32[3,32,128]{2,1,0:T(8,128)S(1)}, f32[3,32,128]{2,1,0:T(8,128)}, u32[]{:S(2)}) copy-start(f32[3,32,128]{2,1,0:T(8,128)} %param.10) | copy-start | bytes 147460
  0.6 10.8 %copy-start.25 = (f32[32,128]{1,0:T(8,128)S(1)}, f32[32,128]{1,0:T(8,128)}, u32[]{:S(2)}) copy-start(f32[32,128]{1,0:T(8,128)} %param.9) | copy-start | bytes 49156
  0.6 10.8 %copy-start.22 = (f32[128,32,128]{2,1,0:T(8,128)S(1)}, f32[128,32,128]{2,1,0:T(8,128)}, u32[]{:S(2)}) copy-start(f32[128,32,128]{2,1,0:T(8,128)} %param.7) | copy-start | bytes 6291460
  4.1 36.5 %all-to-all-start = ((bf16[8,128,512]{2,1,0:T(8,128)(2,1)}), bf16[8,128,512]{2,1,0:T(8,128)(2,1)}, u32[]{:S(2)}, u32[]{:S(2)}) async-start(bf16[8,128,512]{2,1,0:T(8,128)(2,1)} %shard_map.86), calls=%async_computation | async-start | bytes 2097152 | tf_op jit(solution)/shard_map/all_to_all | solution.py:726
  11.6 4.3 %copy-start.19 = (s32[8,16]{1,0:T(8,128)S(1)}, s32[8,16]{1,0:T(8,128)}, u32[]{:S(2)}) copy-start(s32[8,16]{1,0:T(8,128)} %entry_ref.1) | copy-start | bytes 1540
  11.6 4.3 %copy-start.20 = (s32[8]{0:T(128)S(1)}, s32[8]{0:T(128)}, u32[]{:S(2)}) copy-start(s32[8]{0:T(128)} %count_ref.1) | copy-start | bytes 100
  13.0 15.3 %collective-permute-start = (f32[1,36,32,128]{3,2,1,0:T(8,128)}, f32[1,36,32,128]{3,2,1,0:T(8,128)S(1)}, u32[]{:S(2)}, u32[]{:S(2)}) collective-permute-start(f32[1,36,32,128]{3,2,1,0:T(8,128)} %get-tuple-element.65), channel_id=1, source_target_pairs={{0,1},{1,2},{2,3},{3,0},{4,5},{5,6},{6,7},{7,4},{8,9},{9,10},{10,1... | collective-permute-start | bytes 1769480 | tf_op jit(solution)/shard_map/ppermute | solution.py:698
  13.0 16.5 %collective-permute-start.1 = (f32[1,36,32,128]{3,2,1,0:T(8,128)}, f32[1,36,32,128]{3,2,1,0:T(8,128)}, u32[]{:S(2)}, u32[]{:S(2)}) collective-permute-start(f32[1,36,32,128]{3,2,1,0:T(8,128)} %get-tuple-element.66), channel_id=1, source_target_pairs={{0,2},{1,3},{2,0},{3,1},{4,6},{5,7},{6,4},{7,5},{8,10},{9,11},{10,... | collective-permute-start | bytes 1769480 | tf_op jit(solution)/shard_map/ppermute | solution.py:698
  14.5 26.1 %collective-permute-start.2 = (f32[1,36,32,128]{3,2,1,0:T(8,128)}, f32[1,36,32,128]{3,2,1,0:T(8,128)}, u32[]{:S(2)}, u32[]{:S(2)}) collective-permute-start(f32[1,36,32,128]{3,2,1,0:T(8,128)} %get-tuple-element.64), channel_id=1, source_target_pairs={{0,3},{1,0},{2,1},{3,2},{4,7},{5,4},{6,5},{7,6},{8,11},{9,8},{10,9... | collective-permute-start | bytes 1769480 | tf_op jit(solution)/shard_map/ppermute | solution.py:698
  18.1 6.8 %copy-start.23 = (f32[128,32,128]{2,1,0:T(8,128)S(1)}, f32[128,32,128]{2,1,0:T(8,128)}, u32[]{:S(2)}) copy-start(f32[128,32,128]{2,1,0:T(8,128)} %param.8) | copy-start | bytes 6291460
  24.9 132.4 %copy-start.7 = (bf16[256,256]{1,0:T(8,128)(2,1)}, bf16[256,256]{1,0:T(8,128)(2,1)S(1)}, u32[]{:S(2)}) copy-start(bf16[256,256]{1,0:T(8,128)(2,1)S(1)} %get-tuple-element.63.right_ref.refs_9_) | copy-start | bytes 393220
  24.9 35.5 %slice-start = ((s8[6291456]{0:T(1024)(128)(4,1)}), s8[2097152]{0:T(1024)(128)(4,1)S(1)}, s32[]{:S(2)}) async-start(s8[6291456]{0:T(1024)(128)(4,1)} %bitcast.17), calls=%async_computation.5 | async-start | bytes 4194304
  40.6 24.2 %collective-permute-start.5 = (f32[1,32,32,128]{3,2,1,0:T(8,128)}, f32[1,32,32,128]{3,2,1,0:T(8,128)S(1)}, u32[]{:S(2)}, u32[]{:S(2)}) collective-permute-start(f32[1,32,32,128]{3,2,1,0:T(8,128)} %get-tuple-element.32), channel_id=1, source_target_pairs={{0,1},{1,2},{2,3},{3,0},{4,5},{5,6},{6,7},{7,4},{8,9},{9,10},{10,1... | collective-permute-start | bytes 1572872 | tf_op jit(solution)/shard_map/ppermute | solution.py:698
  41.4 24.2 %collective-permute-start.6 = (f32[1,32,32,128]{3,2,1,0:T(8,128)}, f32[1,32,32,128]{3,2,1,0:T(8,128)S(1)}, u32[]{:S(2)}, u32[]{:S(2)}) collective-permute-start(f32[1,32,32,128]{3,2,1,0:T(8,128)} %get-tuple-element.33), channel_id=1, source_target_pairs={{0,2},{1,3},{2,0},{3,1},{4,6},{5,7},{6,4},{7,5},{8,10},{9,11},{10,... | collective-permute-start | bytes 1572872 | tf_op jit(solution)/shard_map/ppermute | solution.py:698
  42.9 23.5 %collective-permute-start.7 = (f32[1,32,32,128]{3,2,1,0:T(8,128)}, f32[1,32,32,128]{3,2,1,0:T(8,128)S(1)}, u32[]{:S(2)}, u32[]{:S(2)}) collective-permute-start(f32[1,32,32,128]{3,2,1,0:T(8,128)} %get-tuple-element.34), channel_id=1, source_target_pairs={{0,3},{1,0},{2,1},{3,2},{4,7},{5,4},{6,5},{7,6},{8,11},{9,8},{10,9... | collective-permute-start | bytes 1572872 | tf_op jit(solution)/shard_map/ppermute | solution.py:698
  44.0 16.5 %collective-permute-start.3 = (bf16[1024,128]{1,0:T(8,128)(2,1)S(1)}, bf16[1024,128]{1,0:T(8,128)(2,1)S(1)}, u32[]{:S(2)}, u32[]{:S(2)}) collective-permute-start(bf16[1024,128]{1,0:T(8,128)(2,1)S(1)} %get-tuple-element.61), channel_id=1, source_target_pairs={{0,4},{4,8},{8,12},{12,16},{16,20},{20,24},{24,28},{28,1},{1,5},{5... | collective-permute-start | bytes 786440 | tf_op jit(solution)/shard_map/ppermute | solution.py:370
  46.0 14.4 %collective-permute-start.4 = (bf16[1024,128]{1,0:T(8,128)(2,1)S(1)}, bf16[1024,128]{1,0:T(8,128)(2,1)S(1)}, u32[]{:S(2)}, u32[]{:S(2)}) collective-permute-start(bf16[1024,128]{1,0:T(8,128)(2,1)S(1)} %get-tuple-element.60), channel_id=1, source_target_pairs={{4,0},{8,4},{12,8},{16,12},{20,16},{24,20},{28,24},{1,28},{5,1},{9... | collective-permute-start | bytes 786440 | tf_op jit(solution)/shard_map/ppermute | solution.py:371
  50.9 2.8 %copy-start.1 = (bf16[8,3,128,1024]{3,2,1,0:T(8,128)(2,1)S(1)}, bf16[8,3,128,1024]{3,2,1,0:T(8,128)(2,1)}, u32[]{:S(2)}) copy-start(bf16[8,3,128,1024]{3,2,1,0:T(8,128)(2,1)} %copy-done) | copy-start | bytes 18874372
  53.7 6.8 %slice-start.1 = ((s8[6291456]{0:T(1024)(128)(4,1)}), s8[4194304]{0:T(1024)(128)(4,1)S(1)}, s32[]{:S(2)}) async-start(s8[6291456]{0:T(1024)(128)(4,1)} %bitcast.17), calls=%async_computation.6 | async-start | bytes 8388608
  67.2 38.7 %all-to-all-start.1 = ((bf16[32,32,640]{2,1,0:T(8,128)(2,1)}), bf16[32,32,640]{2,1,0:T(8,128)(2,1)}, u32[]{:S(2)}, u32[]{:S(2)}) async-start(bf16[32,32,640]{2,1,0:T(8,128)(2,1)} %bitcast.21), calls=%async_computation.1 | async-start | bytes 2621440 | tf_op jit(solution)/shard_map/all_to_all | solution.py:770
  73.9 31.9 %copy-start.18 = (f32[128,128]{1,0:T(8,128)}, f32[128,128]{1,0:T(8,128)S(1)}, u32[]{:S(2)}) copy-start(f32[128,128]{1,0:T(8,128)S(1)} %subtract_divide_fusion.scale_ref) | copy-start | bytes 196612
  75.5 72.7 %slice-start.2 = ((s8[6291456]{0:T(1024)(128)(4,1)}), s8[2097152]{0:T(1024)(128)(4,1)S(1)}, s32[]{:S(2)}) async-start(s8[6291456]{0:T(1024)(128)(4,1)} %bitcast.19), calls=%async_computation.7 | async-start | bytes 4194304
  106.8 41.4 %slice-start.3 = ((s8[6291456]{0:T(1024)(128)(4,1)}), s8[4194304]{0:T(1024)(128)(4,1)S(1)}, s32[]{:S(2)}) async-start(s8[6291456]{0:T(1024)(128)(4,1)} %bitcast.19), calls=%async_computation.8 | async-start | bytes 8388608
  113.1 40.5 %copy-start.8 = (f32[4,32,32,128]{3,2,1,0:T(8,128)}, f32[4,32,32,128]{3,2,1,0:T(8,128)S(1)}, u32[]{:S(2)}) copy-start(f32[4,32,32,128]{3,2,1,0:T(8,128)S(1)} %get-tuple-element.42.current_ref) | copy-start | bytes 6291460
  142.8 12.3 %collective-permute-start.8 = (bf16[1024,128]{1,0:T(8,128)(2,1)S(1)}, bf16[1024,128]{1,0:T(8,128)(2,1)S(1)}, u32[]{:S(2)}, u32[]{:S(2)}) collective-permute-start(bf16[1024,128]{1,0:T(8,128)(2,1)S(1)} %get-tuple-element.59), channel_id=1, source_target_pairs={{0,4},{4,8},{8,12},{12,16},{16,20},{20,24},{24,28},{28,1},{1,5},{5... | collective-permute-start | bytes 786440 | tf_op jit(solution)/shard_map/ppermute | solution.py:370
  144.3 13.0 %collective-permute-start.9 = (bf16[1024,128]{1,0:T(8,128)(2,1)S(1)}, bf16[1024,128]{1,0:T(8,128)(2,1)S(1)}, u32[]{:S(2)}, u32[]{:S(2)}) collective-permute-start(bf16[1024,128]{1,0:T(8,128)(2,1)S(1)} %get-tuple-element.58), channel_id=1, source_target_pairs={{4,0},{8,4},{12,8},{16,12},{20,16},{24,20},{28,24},{1,28},{5,1},{9... | collective-permute-start | bytes 786440 | tf_op jit(solution)/shard_map/ppermute | solution.py:371
  160.3 3.1 %copy-start.6 = (f32[5,128,128]{2,1,0:T(8,128)S(1)}, f32[5,128,128]{2,1,0:T(8,128)}, u32[]{:S(2)}) copy-start(f32[5,128,128]{2,1,0:T(8,128)} %copy-done.5) | copy-start | bytes 983044
  160.3 29.3 %all-to-all-start.3 = ((bf16[32,32,512]{2,1,0:T(8,128)(2,1)}), bf16[32,32,512]{2,1,0:T(8,128)(2,1)S(1)}, u32[]{:S(2)}, u32[]{:S(2)}) async-start(bf16[32,32,512]{2,1,0:T(8,128)(2,1)} %bitcast.10), calls=%async_computation.3 | async-start | bytes 2097152 | tf_op jit(solution)/shard_map/all_to_all | solution.py:780
  194.9 12.4 %collective-permute-start.10 = (bf16[1,32,32,128]{3,2,1,0:T(8,128)(2,1)S(1)}, bf16[1,32,32,128]{3,2,1,0:T(8,128)(2,1)S(1)}, u32[]{:S(2)}, u32[]{:S(2)}) collective-permute-start(bf16[1,32,32,128]{3,2,1,0:T(8,128)(2,1)S(1)} %get-tuple-element.47), channel_id=1, source_target_pairs={{0,1},{1,2},{2,3},{3,0},{4,5},{5,6},{6,7},{7,4},{8,9},{9,10},{10,1... | collective-permute-start | bytes 786440 | tf_op jit(solution)/shard_map/ppermute | solution.py:698
  194.9 12.5 %collective-permute-start.11 = (bf16[1,32,32,128]{3,2,1,0:T(8,128)(2,1)S(1)}, bf16[1,32,32,128]{3,2,1,0:T(8,128)(2,1)S(1)}, u32[]{:S(2)}, u32[]{:S(2)}) collective-permute-start(bf16[1,32,32,128]{3,2,1,0:T(8,128)(2,1)S(1)} %get-tuple-element.48), channel_id=1, source_target_pairs={{0,2},{1,3},{2,0},{3,1},{4,6},{5,7},{6,4},{7,5},{8,10},{9,11},{10,... | collective-permute-start | bytes 786440 | tf_op jit(solution)/shard_map/ppermute | solution.py:698
  196.4 11.7 %collective-permute-start.12 = (bf16[1,32,32,128]{3,2,1,0:T(8,128)(2,1)S(1)}, bf16[1,32,32,128]{3,2,1,0:T(8,128)(2,1)S(1)}, u32[]{:S(2)}, u32[]{:S(2)}) collective-permute-start(bf16[1,32,32,128]{3,2,1,0:T(8,128)(2,1)S(1)} %get-tuple-element.49), channel_id=1, source_target_pairs={{0,3},{1,0},{2,1},{3,2},{4,7},{5,4},{6,5},{7,6},{8,11},{9,8},{10,9... | collective-permute-start | bytes 786440 | tf_op jit(solution)/shard_map/ppermute | solution.py:698
  203.6 18.0 %all-to-all-start.4 = ((bf16[128,32,128]{2,1,0:T(8,128)(2,1)}), bf16[128,32,128]{2,1,0:T(8,128)(2,1)S(1)}, u32[]{:S(2)}, u32[]{:S(2)}) async-start(bf16[128,32,128]{2,1,0:T(8,128)(2,1)} %bitcast.27), calls=%async_computation.4 | async-start | bytes 2097152 | tf_op jit(solution)/shard_map/all_to_all | solution.py:731
  (15 other events, 21.7 us)

commit v11 on v10

--- a/solution.py
+++ b/solution.py
@@ -58,22 +58,25 @@
     return lax.rem(here + count - shift, count)
 
 
-def strip_weights_kernel(slabs, height, place_ref, *refs):
-    part_refs = refs[:slabs]
-    out_ref, coef_ref = refs[slabs:]
-    _, nx, ny = coef_ref.shape
-    rows = nx // slabs
+MARGIN = 8
+
+
+def strip_weights_kernel(slabs, height, place_ref, own_ref, low_ref, high_ref, out_ref, coef_ref):
+    _, rows, ny = own_ref.shape
+    nx = slabs * rows
     fields = out_ref.shape[0] // (5 * height)
-    for shift, part_ref in enumerate(part_refs):
-        start = in_order(place_ref[0], shift, slabs) * rows
-        coef_ref[:, pl.ds(pl.multiple_of(start, rows), rows), :] = part_ref[0]
+    for f in range(1, fields + 1):
+        coef_ref[f, MARGIN - 1 : MARGIN, :] = low_ref[f : f + 1, :]
+        coef_ref[f, MARGIN : MARGIN + rows, :] = own_ref[f]
+        coef_ref[f, MARGIN + rows : MARGIN + rows + 1, :] = high_ref[f : f + 1, :]
+    offset = MARGIN - place_ref[0] * rows
     col = lax.broadcasted_iota(jnp.int32, (1, ny), 1)
     first = place_ref[1] * height
     for f in range(fields):
         lines = []
         for r in range(-1, height + 1):
             at = jnp.clip(first + r, 0, nx - 1)
-            lines.append(coef_ref[f + 1, pl.ds(at, 1), :])
+            lines.append(coef_ref[f + 1, pl.ds(at + offset, 1), :])
         for r in range(height):
             here = lines[r + 1]
             up = 0.5 * (here + lines[r])
@@ -102,37 +105,41 @@
         out_ref[which] = weight
 
 
-def weights_of(kernel, parts, place, coefs, out, scratch):
-    _, entries, rows, ny = parts[0].shape
-    last = entries // coefs - 1
+def strip_weights_of(own, low, high, place, slabs, height):
+    coefs, rows, ny = own.shape
+    out = ((coefs - 1) * 5 * height, ny)
+    edge = pl.BlockSpec((coefs, ny), lambda i, *_: (0, 0))
     return pl.pallas_call(
-        kernel,
+        functools.partial(strip_weights_kernel, slabs, height),
         grid_spec=pltpu.PrefetchScalarGridSpec(
             num_scalar_prefetch=1,
             grid=(1,),
-            in_specs=[pl.BlockSpec((1, coefs, rows, ny), lambda i, *_: (0, last, 0, 0))]
-            * len(parts),
-            out_specs=pl.BlockSpec(out, lambda i, *_: (0,) * len(out)),
-            scratch_shapes=[pltpu.VMEM(scratch, jnp.float32)],
+            in_specs=[pl.BlockSpec((coefs, rows, ny), lambda i, *_: (0, 0, 0)), edge, edge],
+            out_specs=pl.BlockSpec(out, lambda i, *_: (0, 0)),
+            scratch_shapes=[pltpu.VMEM((coefs, rows + 2 * MARGIN, ny), jnp.float32)],
+        ),
+        out_shape=jax.ShapeDtypeStruct(out, jnp.float32),
+        compiler_params=pltpu.CompilerParams(vmem_limit_bytes=SMALL_VMEM_BYTES),
+    )(place, own, low, high)
+
+
+def mean_weights_of(parts, place, coefs):
+    slabs = len(parts)
+    _, entries, rows, ny = parts[0].shape
+    last = entries // coefs - 1
+    out = (5, slabs * rows, ny)
+    return pl.pallas_call(
+        functools.partial(mean_weights_kernel, slabs),
+        grid_spec=pltpu.PrefetchScalarGridSpec(
+            num_scalar_prefetch=1,
+            grid=(1,),
+            in_specs=[pl.BlockSpec((1, coefs, rows, ny), lambda i, *_: (0, last, 0, 0))] * slabs,
+            out_specs=pl.BlockSpec(out, lambda i, *_: (0, 0, 0)),
+            scratch_shapes=[pltpu.VMEM((slabs, rows, ny), jnp.float32)],
         ),
         out_shape=jax.ShapeDtypeStruct(out, jnp.float32),
         compiler_params=pltpu.CompilerParams(vmem_limit_bytes=SMALL_VMEM_BYTES),
     )(place, *parts)
-
-
-def strip_weights_of(parts, place, coefs, height):
-    slabs = len(parts)
-    _, _, rows, ny = parts[0].shape
-    kernel = functools.partial(strip_weights_kernel, slabs, height)
-    out = ((coefs - 1) * 5 * height, ny)
-    return weights_of(kernel, parts, place, coefs, out, (coefs, slabs * rows, ny))
-
-
-def mean_weights_of(parts, place, coefs):
-    slabs = len(parts)
-    _, _, rows, ny = parts[0].shape
-    kernel = functools.partial(mean_weights_kernel, slabs)
-    return weights_of(kernel, parts, place, coefs, (5, slabs * rows, ny), (slabs, rows, ny))
 
 
 def split(value):
@@ -232,7 +239,6 @@
 
 def dense_coupling(coupling, coupling_list, pair_count, fields):
     blocks, entries, width, _ = coupling.shape
-    moved = 2 * width * width * (entries + fields * blocks) * coupling.dtype.itemsize
     return pl.pallas_call(
         functools.partial(dense_kernel, fields),
         grid_spec=pltpu.PrefetchScalarGridSpec(
@@ -244,7 +250,7 @@
             ),
         ),
         out_shape=jax.ShapeDtypeStruct((blocks, fields, width, blocks * width), coupling.dtype),
-        compiler_params=pltpu.CompilerParams(vmem_limit_bytes=SMALL_VMEM_BYTES + moved),
+        compiler_params=pltpu.CompilerParams(vmem_limit_bytes=VMEM_BYTES),
     )(coupling_list, pair_count, coupling)
 
 
@@ -356,7 +362,7 @@
                 out_ref[modes, at : at + cols] = packed.astype(jnp.bfloat16)
 
 
-def coupled_sums(matrix, state, weights, right, first, scale, both):
+def coupled_sums(matrix, state, borders, weights, right, first, scale, both):
     blocks, fields, width, depth = matrix.shape
     cells = state.shape[1]
     height = weights.shape[0] // (5 * fields)
@@ -367,8 +373,8 @@
         (t % mode_count) * slab_count + t // mode_count for t in range(mode_count * slab_count)
     ]
     onward = list(zip(place, place[1:] + place[:1]))
-    above = lax.ppermute(state[:, -cols:], both, onward)
-    below = lax.ppermute(state[:, :cols], both, [(b, a) for a, b in onward])
+    above = lax.ppermute(borders[1], both, onward)
+    below = lax.ppermute(borders[0], both, [(b, a) for a, b in onward])
     unroll = math.gcd(blocks, UNROLL)
     matrix_spec = pl.BlockSpec((unroll, fields, width, depth), lambda i: (i, 0, 0, 0))
     weight_spec = pl.BlockSpec(weights.shape, lambda i: (0, 0))
@@ -679,7 +685,6 @@
         slabs,
         (),
         solve_flops(resid, tables),
-        VMEM_BYTES,
     )
 
 
@@ -723,23 +728,29 @@
 
     strips = pack_strips(guess, mode_count)
     coefs = jnp.concatenate([mean_coef[None], field_coef], 0)[None]
+    strips, coefs = lax.optimization_barrier((strips, coefs))
     state = lax.all_to_all(strips, "mode", 0, 0, tiled=True)
     state = state.reshape(mode_count * modes, height * cols)
 
     def to_slabs(block):
         flat = block.reshape(modes, rows, cols)
         return lax.all_to_all(flat, "slab", 0, 0, tiled=True)
+
+    borders = (state[:, :cols], state[:, -cols:])
+
+    slab = lax.axis_index("slab")
+    place = jnp.stack([slab, slab * mode_count + lax.axis_index("mode")])
+    forward = [(i, i + 1) for i in range(slab_count - 1)]
+    low = lax.ppermute(coefs[0, :, -1], "slab", forward)
+    high = lax.ppermute(coefs[0, :, 0], "slab", [(b, a) for a, b in forward])
+    strip_weights = strip_weights_of(coefs[0], low, high, place, slab_count, height)
 
     guess_parts = parts_of(guess.reshape(slab_count, share, rows, cols), "slab")
     guess_parts = [jnp.concatenate([part, coefs], axis=1) for part in guess_parts]
     guess_parts = moved_parts(guess_parts, "slab")
     right_parts = parts_of(right_side.reshape(slab_count, share, rows, cols), "slab")
-    state, guess_parts, right_parts = lax.optimization_barrier((state, guess_parts, right_parts))
+    guess_parts, right_parts, _ = lax.optimization_barrier((guess_parts, right_parts, borders))
     right_parts = moved_parts(right_parts, "slab")
-
-    slab = lax.axis_index("slab")
-    place = jnp.stack([slab, slab * mode_count + lax.axis_index("mode")])
-    strip_weights = strip_weights_of(guess_parts, place, fields + 1, height)
     mean_weights = mean_weights_of(guess_parts, place, fields + 1)
     matrix = dense_coupling(coupling, coupling_list, pair_count, fields)
 
@@ -765,8 +776,10 @@
 
     first_scale, sum_scale, solution_scale = code_scales(nx, cols, coupling.shape[1], modes)
 
-    sums = coupled_sums(matrix, state, strip_weights, tables[0], True, first_scale, both)
-    sums, right_parts = lax.optimization_barrier((sums, right_parts))
+    sums = coupled_sums(
+        matrix, state, borders, strip_weights, tables[0], True, first_scale, both
+    )
+    sums, *right_parts[1::2] = lax.optimization_barrier((sums, *right_parts[1::2]))
     sums = lax.all_to_all(sums, both, 0, 0, tiled=True).reshape(devices, share, -1)
     current, right_side, base = first_mean_part(
         place, guess_parts, right_parts, mean_weights, tables[0]
@@ -776,7 +789,10 @@
     state = lax.all_to_all(state, both, 0, 0, tiled=True)
 
     base = mean_part(current, right_side, mean_weights)
-    sums = coupled_sums(matrix, state, strip_weights, tables[0], False, sum_scale, both)
+    borders = (state[:, :cols], state[:, -cols:])
+    sums = coupled_sums(
+        matrix, state, borders, strip_weights, tables[0], False, sum_scale, both
+    )
     sums = lax.all_to_all(sums, both, 0, 0, tiled=True).reshape(devices, share, -1)
     resid, parts = last_residual(base, sums, mode_count, slab_count, sum_scale)
     moved = collect(moved_parts(parts, "slab"), "slab").reshape(modes, rows, cols)

time: 224 us -> 231 us (1.031)
  waiting for transfers between devices: 74.1 us -> 78 us
  local copies, waits for them, and re-layouts: 18.9 us -> 15 us
  Pallas kernels: 53 us -> 56.4 us
  blocking collectives: 29.6 us -> 32 us
    all_to_all x2, waiting for transfers between devices: 44.8 us -> 20.6 us  [local(): lax.all_to_all(sums, both, 0, 0, tiled=True).reshape(devices, share, -1)]
    all_to_all x1, waiting for transfers between devices: 0.01 us -> 15.7 us  [local(): state = lax.all_to_all(strips, 'mode', 0, 0, tiled=True)]
    ppermute x9, waiting for transfers between devices: 14.9 us -> 28.9 us  [onwards(): lax.ppermute(part, axis, [(i, (i + shift) % count) for i in range(count)])]
    unnamed x60 -> x40, local copies, waits for them, and re-layouts: 15.9 us -> 9.73 us
    pallas_call x1, Pallas kernels: 3.04 us -> 8.85 us  [dense_coupling(): pl.pallas_call(functools.partial(dense_kernel, fields), grid_spec=pltpu.P...]
    ppermute x4 -> x6, starting transfers between devices: 10.8 us -> 13.4 us  [the longest x2 7.19 us: coupled_sums(): below = lax.ppermute(borders[0], both, [(b, a) for a, b in onward])]
    all_to_all x1, blocking collectives: 29.6 us -> 32 us  [local(): state = lax.all_to_all(state, both, 0, 0, tiled=True)]
  transfers between devices with their start and end apart: 17 -> 19, of which waited for: 9 -> 9; matrix products, arithmetic and copies ran while one was open for 4% -> 4% of each run, Pallas kernels for 16% -> 17%
where the time goes in v11:
time: 231 us
  waiting for transfers between devices  78 us (34%)
  Pallas kernels  56.4 us (24%)
  starting transfers between devices  41.2 us (18%)
  blocking collectives  32 us (14%)
  local copies, waits for them, and re-layouts  15 us (6%)
  other arithmetic  6.78 us (3%)
    all_to_all x1, blocking collectives, local(): state = lax.all_to_all(state, both, 0, 0, tiled=True)  32 us
    ppermute x9, waiting for transfers between devices, onwards(): lax.ppermute(part, axis, [(i, (i + shift) % count) for i in range(count)])  28.9 us
    all_to_all x2, waiting for transfers between devices, local(): lax.all_to_all(sums, both, 0, 0, tiled=True).reshape(devices, share, -1)  20.6 us
    all_to_all x1, waiting for transfers between devices, local(): state = lax.all_to_all(strips, 'mode', 0, 0, tiled=True)  15.7 us
    pallas_call x3, Pallas kernels, per_group(): pl.pallas_call(kernel, grid=(groups,), in_specs=in_specs, out_specs=out_s...  13.5 us
    pallas_call x2, Pallas kernels, coupled_sums(): pl.pallas_call(functools.partial(inner_kernel, height, cols), grid=(block...  12.1 us
    unnamed x40, local copies, waits for them, and re-layouts  9.73 us
    ppermute x9, starting transfers between devices, onwards(): lax.ppermute(part, axis, [(i, (i + shift) % count) for i in range(count)])  9.61 us
  transfers between devices with their start and end apart: 19, of which 9 were waited for; matrix products, arithmetic and copies ran while one was open for 4% of the time, Pallas kernels for 17%

profile of v11, /device:TPU:0, one launch (start us, length us, event | category | flops | bytes accessed | tf_op | source)
XLA Modules:
  0.0 230.5 jit_solution(3611581053176429649)
XLA Ops:
  0.6 3.3 %shard_map.86 = bf16[8,128,512]{2,1,0:T(8,128)(2,1)} custom-call(f32[4096,128]{1,0:T(8,128)} %bitcast.25), custom_call_target="tpu_custom_call" | custom-call | tf_op jit(solution)/shard_map/pallas_call | solution.py:216
  4.0 7.3 %all-to-all-start = ((bf16[8,128,512]{2,1,0:T(8,128)(2,1)}), bf16[8,128,512]{2,1,0:T(8,128)(2,1)}, u32[]{:S(2)}, u32[]{:S(2)}) async-start(bf16[8,128,512]{2,1,0:T(8,128)(2,1)} %shard_map.86), calls=%async_computation | async-start | bytes 2097152 | tf_op jit(solution)/shard_map/all_to_all | solution.py:732
  11.3 1.7 constant_dynamic-slice_fusion.4
  21.5 15.7 %all-to-all-done = bf16[8,128,512]{2,1,0:T(8,128)(2,1)} async-done(((bf16[8,128,512]{2,1,0:T(8,128)(2,1)}), bf16[8,128,512]{2,1,0:T(8,128)(2,1)}, u32[]{:S(2)}, u32[]{:S(2)}) %all-to-all-start) | async-done | bytes 1048608 | tf_op jit(solution)/shard_map/all_to_all | solution.py:732
  37.1 1.9 fusion.18
  39.0 2.7 %collective-permute-done.2.refs_3_ = f32[1,36,32,128]{3,2,1,0:T(8,128)S(1)} collective-permute-done((f32[1,36,32,128]{3,2,1,0:T(8,128)S(1)}, f32[1,36,32,128]{3,2,1,0:T(8,128)S(1)}, u32[]{:S(2)}, u32[]{:S(2)}) %collective-permute-start.2) | collective-permute-done | bytes 589856 | tf_op jit(solution)/shard_map/ppermute | solution.py:703
  43.7 8.9 %shard_map.87.matrix_ref = bf16[8,3,128,1024]{3,2,1,0:T(8,128)(2,1)} custom-call(s32[8,16]{1,0:T(8,128)} %entry_ref.1, s32[8]{0:T(128)} %count_ref.1, bf16[8,16,128,128]{3,2,1,0:T(8,128)(2,1)} %coupling_ref.1), custom_call_target="tpu_custom_call" | custom-call | tf_op jit(solution)/shard_map/pallas_call | solution.py:242
  53.3 2.1 collective-permute-start.3
  55.3 3.3 %collective-permute-start.4 = (bf16[1024,128]{1,0:T(8,128)(2,1)}, bf16[1024,128]{1,0:T(8,128)(2,1)S(1)}, u32[]{:S(2)}, u32[]{:S(2)}) collective-permute-start(bf16[1024,128]{1,0:T(8,128)(2,1)} %get-tuple-element.59), channel_id=1, source_target_pairs={{4,0},{8,4},{12,8},{16,12},{20,16},{24,20},{28,24},{1,28},{5,1},{9... | collective-permute-start | bytes 786440 | tf_op jit(solution)/shard_map/ppermute | solution.py:377
  58.7 2.8 %copy-done = bf16[8,3,128,1024]{3,2,1,0:T(8,128)(2,1)S(1)} copy-done((bf16[8,3,128,1024]{3,2,1,0:T(8,128)(2,1)S(1)}, bf16[8,3,128,1024]{3,2,1,0:T(8,128)(2,1)}, u32[]{:S(2)}) %copy-start) | copy-done | bytes 6291480
  61.4 6.7 %shard_map.89.inner_ref = f32[1024,512]{1,0:T(8,128)S(1)} custom-call(bf16[8,3,128,1024]{3,2,1,0:T(8,128)(2,1)S(1)} %copy-done, bf16[1024,512]{1,0:T(8,128)(2,1)} %bitcast.7.state_ref, f32[60,128]{1,0:T(8,128)S(1)} %shard_map.88.weight_ref), custom_call_target="tpu_custom_call" | custom-call | flops 3221225472 | bytes 6291456 | tf_op jit(solution)/shard_map/pallas_call | solution.py:384
  68.5 5.1 %shard_map.90 = bf16[1024,640]{1,0:T(8,128)(2,1)} custom-call(bf16[8,3,128,1024]{3,2,1,0:T(8,128)(2,1)S(1)} %copy-done.1, bf16[1024,128]{1,0:T(8,128)(2,1)S(1)} %collective-permute-done.3.above_ref, bf16[1024,128]{1,0:T(8,128)(2,1)S(1)} %collective-permute-done.4.below_ref, f32[60,128]{1,0:T(8,128)S(1)} %shard_map.88.weight_ref, ...), custom_call_target="tpu_custom_call" | custom-call | tf_op jit(solution)/shard_map/pallas_call | solution.py:398
  74.3 4.4 %all-to-all-start.1 = ((bf16[32,32,640]{2,1,0:T(8,128)(2,1)}), bf16[32,32,640]{2,1,0:T(8,128)(2,1)}, u32[]{:S(2)}, u32[]{:S(2)}) async-start(bf16[32,32,640]{2,1,0:T(8,128)(2,1)} %bitcast.11), calls=%async_computation.1 | async-start | bytes 2621440 | tf_op jit(solution)/shard_map/all_to_all | solution.py:783
  78.8 1.8 collective-permute-start.9
  81.4 23.6 %collective-permute-done.9.refs_6_ = f32[1,32,32,128]{3,2,1,0:T(8,128)S(1)} collective-permute-done((f32[1,32,32,128]{3,2,1,0:T(8,128)}, f32[1,32,32,128]{3,2,1,0:T(8,128)S(1)}, u32[]{:S(2)}, u32[]{:S(2)}) %collective-permute-start.9) | collective-permute-done | bytes 524320 | tf_op jit(solution)/shard_map/ppermute | solution.py:703
  108.2 5.2 %shard_map.92 = (f32[4,32,32,128]{3,2,1,0:T(8,128)}, f32[4,32,32,128]{3,2,1,0:T(8,128)}, f32[4,32,32,128]{3,2,1,0:T(8,128)}) custom-call(s32[2]{0:T(128)S(1)} %pad_add_fusion.place_ref, f32[1,36,32,128]{3,2,1,0:T(8,128)S(1)} %get-tuple-element.27.refs_0_, f32[1,36,32,128]{3,2,1,0:T(8,128)S(1)} %copy-done.4, f32[1,36,32,128]{3,2,1,0:T(8,128)S(1)} %copy-done.6, ...), custom_call_target="tpu_custom_call" | custom-call | tf_op jit(solution)/shard_map/pallas_call | solution.py:599
  113.4 6.3 %shard_map.93 = (f32[4,32,32,128]{3,2,1,0:T(8,128)S(1)}, bf16[32,32,512]{2,1,0:T(8,128)(2,1)S(1)}) custom-call(f32[4,32,32,128]{3,2,1,0:T(8,128)} %get-tuple-element.37.current_ref, f32[4,32,32,128]{3,2,1,0:T(8,128)} %get-tuple-element.38.base_ref, bf16[32,32,640]{2,1,0:T(8,128)(2,1)} %all-to-all-done.1.coupled_ref, ...), custom_call_target="tpu_custom_call" | custom-call | flops 1610612736 | bytes 11665408 | tf_op jit(solution)/shard_map/pallas_call | solution.py:581
  119.8 32.0 %all_to_all.36 = bf16[32,32,512]{2,1,0:T(8,128)(2,1)S(1)} all-to-all(bf16[32,32,512]{2,1,0:T(8,128)(2,1)S(1)} %get-tuple-element.42), channel_id=1, replica_groups=mesh['mode'=8,'slab'=4] {'mode','slab'}, dimensions={0} | all-to-all | bytes 2097152 | tf_op jit(solution)/shard_map/all_to_all | solution.py:789
  153.4 3.9 %collective-permute-start.11 = (bf16[1024,128]{1,0:T(8,128)(2,1)S(1)}, bf16[1024,128]{1,0:T(8,128)(2,1)S(1)}, u32[]{:S(2)}, u32[]{:S(2)}) collective-permute-start(bf16[1024,128]{1,0:T(8,128)(2,1)S(1)} %get-tuple-element.56), channel_id=1, source_target_pairs={{4,0},{8,4},{12,8},{16,12},{20,16},{24,20},{28,24},{1,28},{5,1},{9... | collective-permute-start | bytes 786440 | tf_op jit(solution)/shard_map/ppermute | solution.py:377
  157.3 5.4 %shard_map.95.inner_ref = f32[1024,512]{1,0:T(8,128)S(1)} custom-call(bf16[8,3,128,1024]{3,2,1,0:T(8,128)(2,1)S(1)} %bitcast.21, bf16[1024,512]{1,0:T(8,128)(2,1)S(1)} %bitcast.23, f32[60,128]{1,0:T(8,128)S(1)} %shard_map.88.weight_ref), custom_call_target="tpu_custom_call" | custom-call | flops 3221225472 | bytes 6291456 | tf_op jit(solution)/shard_map/pallas_call | solution.py:384
  164.2 2.2 collective-permute-done.11.below_ref
  166.4 3.0 %shard_map.96 = bf16[1024,512]{1,0:T(8,128)(2,1)} custom-call(bf16[8,3,128,1024]{3,2,1,0:T(8,128)(2,1)S(1)} %bitcast.21, bf16[1024,128]{1,0:T(8,128)(2,1)S(1)} %collective-permute-done.10.above_ref, bf16[1024,128]{1,0:T(8,128)(2,1)S(1)} %collective-permute-done.11.below_ref, f32[60,128]{1,0:T(8,128)S(1)} %shard_map.88.weight_ref, ...), custom_call_target="tpu_custom_call" | custom-call | tf_op jit(solution)/shard_map/pallas_call | solution.py:398
  169.4 3.0 %all-to-all-start.3 = ((bf16[32,32,512]{2,1,0:T(8,128)(2,1)}), bf16[32,32,512]{2,1,0:T(8,128)(2,1)S(1)}, u32[]{:S(2)}, u32[]{:S(2)}) async-start(bf16[32,32,512]{2,1,0:T(8,128)(2,1)} %bitcast.13), calls=%async_computation.3 | async-start | bytes 2097152 | tf_op jit(solution)/shard_map/all_to_all | solution.py:796
  174.0 2.7 %shard_map.94.base_ref = f32[4,32,32,128]{3,2,1,0:T(8,128)S(1)} custom-call(f32[4,32,32,128]{3,2,1,0:T(8,128)S(1)} %copy-done.10, f32[4,32,32,128]{3,2,1,0:T(8,128)} %get-tuple-element.41.right_side_ref, f32[5,128,128]{2,1,0:T(8,128)S(1)} %shard_map.91.refs_8_.weight_ref), custom_call_target="tpu_custom_call" | custom-call | bytes 9043968 | tf_op jit(solution)/shard_map/pallas_call | solution.py:581
  178.1 20.6 %all-to-all-done.3.coupled_ref = bf16[32,32,512]{2,1,0:T(8,128)(2,1)S(1)} async-done(((bf16[32,32,512]{2,1,0:T(8,128)(2,1)}), bf16[32,32,512]{2,1,0:T(8,128)(2,1)S(1)}, u32[]{:S(2)}, u32[]{:S(2)}) %all-to-all-start.3) | async-done | bytes 1048608 | tf_op jit(solution)/shard_map/all_to_all | solution.py:796
  198.7 4.1 %shard_map.97 = (f32[4,32,32,128]{3,2,1,0:T(8,128)S(1)}, bf16[1,32,32,128]{3,2,1,0:T(8,128)(2,1)S(1)}, bf16[1,32,32,128]{3,2,1,0:T(8,128)(2,1)S(1)}, bf16[1,32,3...) custom-call(s32[1]{0:T(128)} %bitcast.here_ref, f32[4,32,32,128]{3,2,1,0:T(8,128)} %copy-done.2, ...), custom_call_target="tpu_custom_call" | custom-call | bytes 4194304 | tf_op jit(solution)/shard_map/pallas_call | solution.py:658
  205.8 4.5 %shard_map.98 = bf16[4,32,32,128]{3,2,1,0:T(8,128)(2,1)} custom-call(f32[4,32,32,128]{3,2,1,0:T(8,128)S(1)} %copy-done.11, f32[4,32,32,128]{3,2,1,0:T(8,128)S(1)} %get-tuple-element.43.resid_ref, bf16[256,256]{1,0:T(8,128)(2,1)S(1)} %get-tuple-element.61.right_ref.refs_9_, bf16[256,256]{1,0:T(8,128)(2,1)S(1)} %get-tuple-element.60.left_ref, ...), custom_call_target="tpu_custom_call" | custom-call | flops 1610612736 | bytes 9043968 | tf_op jit(solution)/shard_map/pallas_call | solution.py:581
  210.3 3.5 %all-to-all-start.4 = ((bf16[128,32,128]{2,1,0:T(8,128)(2,1)}), bf16[128,32,128]{2,1,0:T(8,128)(2,1)S(1)}, u32[]{:S(2)}, u32[]{:S(2)}) async-start(bf16[128,32,128]{2,1,0:T(8,128)(2,1)} %bitcast.14), calls=%async_computation.4 | async-start | bytes 2097152 | tf_op jit(solution)/shard_map/all_to_all | solution.py:737
  214.1 2.5 %collective-permute-done.14 = bf16[1,32,32,128]{3,2,1,0:T(8,128)(2,1)S(1)} collective-permute-done((bf16[1,32,32,128]{3,2,1,0:T(8,128)(2,1)S(1)}, bf16[1,32,32,128]{3,2,1,0:T(8,128)(2,1)S(1)}, u32[]{:S(2)}, u32[]{:S(2)}) %collective-permute-start.14) | collective-permute-done | bytes 262176 | tf_op jit(solution)/shard_map/ppermute | solution.py:703
  217.7 1.8 fusion.11
  219.5 8.8 %all-to-all-done.4 = bf16[128,32,128]{2,1,0:T(8,128)(2,1)S(1)} async-done(((bf16[128,32,128]{2,1,0:T(8,128)(2,1)}), bf16[128,32,128]{2,1,0:T(8,128)(2,1)S(1)}, u32[]{:S(2)}, u32[]{:S(2)}) %all-to-all-start.4) | async-done | bytes 1048608 | tf_op jit(solution)/shard_map/all_to_all | solution.py:737
  228.3 2.2 fusion.10
  (83 shorter events, 26.5 us)
Async XLA Ops:
  0.6 3.3 %copy-start.17 = (f32[32,128]{1,0:T(8,128)S(1)}, f32[32,128]{1,0:T(8,128)}, u32[]{:S(2)}) copy-start(f32[32,128]{1,0:T(8,128)} %param.9) | copy-start | bytes 49156
  0.6 3.3 %copy-start.16 = (f32[3,32,128]{2,1,0:T(8,128)S(1)}, f32[3,32,128]{2,1,0:T(8,128)}, u32[]{:S(2)}) copy-start(f32[3,32,128]{2,1,0:T(8,128)} %param.10) | copy-start | bytes 147460
  4.0 33.2 %all-to-all-start = ((bf16[8,128,512]{2,1,0:T(8,128)(2,1)}), bf16[8,128,512]{2,1,0:T(8,128)(2,1)}, u32[]{:S(2)}, u32[]{:S(2)}) async-start(bf16[8,128,512]{2,1,0:T(8,128)(2,1)} %shard_map.86), calls=%async_computation | async-start | bytes 2097152 | tf_op jit(solution)/shard_map/all_to_all | solution.py:732
  13.0 6.8 %copy-start.15 = (f32[128,32,128]{2,1,0:T(8,128)S(1)}, f32[128,32,128]{2,1,0:T(8,128)}, u32[]{:S(2)}) copy-start(f32[128,32,128]{2,1,0:T(8,128)} %param.8) | copy-start | bytes 6291460
  14.2 24.8 %collective-permute-start = (f32[1,36,32,128]{3,2,1,0:T(8,128)}, f32[1,36,32,128]{3,2,1,0:T(8,128)S(1)}, u32[]{:S(2)}, u32[]{:S(2)}) collective-permute-start(f32[1,36,32,128]{3,2,1,0:T(8,128)} %get-tuple-element.65), channel_id=1, source_target_pairs={{0,1},{1,2},{2,3},{3,0},{4,5},{5,6},{6,7},{7,4},{8,9},{9,10},{10,1... | collective-permute-start | bytes 1769480 | tf_op jit(solution)/shard_map/ppermute | solution.py:703
  14.2 24.8 %collective-permute-start.1 = (f32[1,36,32,128]{3,2,1,0:T(8,128)}, f32[1,36,32,128]{3,2,1,0:T(8,128)S(1)}, u32[]{:S(2)}, u32[]{:S(2)}) collective-permute-start(f32[1,36,32,128]{3,2,1,0:T(8,128)} %get-tuple-element.66), channel_id=1, source_target_pairs={{0,2},{1,3},{2,0},{3,1},{4,6},{5,7},{6,4},{7,5},{8,10},{9,11},{10,... | collective-permute-start | bytes 1769480 | tf_op jit(solution)/shard_map/ppermute | solution.py:703
  15.7 26.0 %collective-permute-start.2 = (f32[1,36,32,128]{3,2,1,0:T(8,128)S(1)}, f32[1,36,32,128]{3,2,1,0:T(8,128)S(1)}, u32[]{:S(2)}, u32[]{:S(2)}) collective-permute-start(f32[1,36,32,128]{3,2,1,0:T(8,128)S(1)} %get-tuple-element.64), channel_id=1, source_target_pairs={{0,3},{1,0},{2,1},{3,2},{4,7},{5,4},{6,5},{7,6},{8,11},{9,8},{10,9... | collective-permute-start | bytes 1769480 | tf_op jit(solution)/shard_map/ppermute | solution.py:703
  17.2 35.4 %collective-permute-start.5 = (f32[4,128]{1,0:T(4,128)S(1)}, f32[4,128]{1,0:T(4,128)S(1)}, u32[]{:S(2)}, u32[]{:S(2)}) collective-permute-start(f32[4,128]{1,0:T(4,128)S(1)} %bitcast.30), channel_id=1, source_target_pairs={{0,1},{1,2},{2,3},{4,5},{5,6},{6,7},{8,9},{9,10},{10,11},{12,13},{... | collective-permute-start | bytes 6152 | tf_op jit(solution)/shard_map/ppermute | solution.py:744
  18.5 34.1 %collective-permute-start.6 = (f32[4,128]{1,0:T(4,128)S(1)}, f32[4,128]{1,0:T(4,128)S(1)}, u32[]{:S(2)}, u32[]{:S(2)}) collective-permute-start(f32[4,128]{1,0:T(4,128)S(1)} %bitcast.29), channel_id=1, source_target_pairs={{1,0},{2,1},{3,2},{5,4},{6,5},{7,6},{9,8},{10,9},{11,10},{13,12},{... | collective-permute-start | bytes 6152 | tf_op jit(solution)/shard_map/ppermute | solution.py:745
  39.0 41.7 %copy-start.3 = (f32[1,36,32,128]{3,2,1,0:T(8,128)}, f32[1,36,32,128]{3,2,1,0:T(8,128)S(1)}, u32[]{:S(2)}) copy-start(f32[1,36,32,128]{3,2,1,0:T(8,128)S(1)} %collective-permute-done.refs_1_) | copy-start | bytes 1769476
  39.0 41.7 %copy-start.5 = (f32[1,36,32,128]{3,2,1,0:T(8,128)}, f32[1,36,32,128]{3,2,1,0:T(8,128)S(1)}, u32[]{:S(2)}) copy-start(f32[1,36,32,128]{3,2,1,0:T(8,128)S(1)} %collective-permute-done.1.refs_2_) | copy-start | bytes 1769476
  41.7 39.0 %copy-start.7 = (f32[1,36,32,128]{3,2,1,0:T(8,128)}, f32[1,36,32,128]{3,2,1,0:T(8,128)S(1)}, u32[]{:S(2)}) copy-start(f32[1,36,32,128]{3,2,1,0:T(8,128)S(1)} %collective-permute-done.2.refs_3_) | copy-start | bytes 1769476
  41.7 31.8 %collective-permute-start.7 = (f32[1,32,32,128]{3,2,1,0:T(8,128)}, f32[1,32,32,128]{3,2,1,0:T(8,128)S(1)}, u32[]{:S(2)}, u32[]{:S(2)}) collective-permute-start(f32[1,32,32,128]{3,2,1,0:T(8,128)} %get-tuple-element.32), channel_id=1, source_target_pairs={{0,1},{1,2},{2,3},{3,0},{4,5},{5,6},{6,7},{7,4},{8,9},{9,10},{10,1... | collective-permute-start | bytes 1572872 | tf_op jit(solution)/shard_map/ppermute | solution.py:703
  42.5 31.8 %collective-permute-start.8 = (f32[1,32,32,128]{3,2,1,0:T(8,128)}, f32[1,32,32,128]{3,2,1,0:T(8,128)}, u32[]{:S(2)}, u32[]{:S(2)}) collective-permute-start(f32[1,32,32,128]{3,2,1,0:T(8,128)} %get-tuple-element.33), channel_id=1, source_target_pairs={{0,3},{1,0},{2,1},{3,2},{4,7},{5,4},{6,5},{7,6},{8,11},{9,8},{10,9... | collective-permute-start | bytes 1572872 | tf_op jit(solution)/shard_map/ppermute | solution.py:703
  53.3 14.9 %collective-permute-start.3 = (bf16[1024,128]{1,0:T(8,128)(2,1)}, bf16[1024,128]{1,0:T(8,128)(2,1)S(1)}, u32[]{:S(2)}, u32[]{:S(2)}) collective-permute-start(bf16[1024,128]{1,0:T(8,128)(2,1)} %get-tuple-element.58), channel_id=1, source_target_pairs={{0,4},{4,8},{8,12},{12,16},{16,20},{20,24},{24,28},{28,1},{1,5},{5... | collective-permute-start | bytes 786440 | tf_op jit(solution)/shard_map/ppermute | solution.py:376
  55.3 13.1 %collective-permute-start.4 = (bf16[1024,128]{1,0:T(8,128)(2,1)}, bf16[1024,128]{1,0:T(8,128)(2,1)S(1)}, u32[]{:S(2)}, u32[]{:S(2)}) collective-permute-start(bf16[1024,128]{1,0:T(8,128)(2,1)} %get-tuple-element.59), channel_id=1, source_target_pairs={{4,0},{8,4},{12,8},{16,12},{20,16},{24,20},{28,24},{1,28},{5,1},{9... | collective-permute-start | bytes 786440 | tf_op jit(solution)/shard_map/ppermute | solution.py:377
  61.4 7.0 %copy-start.1 = (bf16[8,3,128,1024]{3,2,1,0:T(8,128)(2,1)S(1)}, bf16[8,3,128,1024]{3,2,1,0:T(8,128)(2,1)}, u32[]{:S(2)}) copy-start(bf16[8,3,128,1024]{3,2,1,0:T(8,128)(2,1)} %shard_map.87.matrix_ref) | copy-start | bytes 18874372
  74.3 39.1 %all-to-all-start.1 = ((bf16[32,32,640]{2,1,0:T(8,128)(2,1)}), bf16[32,32,640]{2,1,0:T(8,128)(2,1)}, u32[]{:S(2)}, u32[]{:S(2)}) async-start(bf16[32,32,640]{2,1,0:T(8,128)(2,1)} %bitcast.11), calls=%async_computation.1 | async-start | bytes 2621440 | tf_op jit(solution)/shard_map/all_to_all | solution.py:783
  78.8 26.3 %copy-start.12 = (f32[1,32,32,128]{3,2,1,0:T(8,128)S(1)}, f32[1,32,32,128]{3,2,1,0:T(8,128)}, u32[]{:S(2)}) copy-start(f32[1,32,32,128]{3,2,1,0:T(8,128)} %get-tuple-element.31.refs_4_) | copy-start | bytes 1572868
  78.8 26.3 %copy-start.14 = (f32[1,32,32,128]{3,2,1,0:T(8,128)S(1)}, f32[1,32,32,128]{3,2,1,0:T(8,128)}, u32[]{:S(2)}) copy-start(f32[1,32,32,128]{3,2,1,0:T(8,128)} %copy-done.13) | copy-start | bytes 1572868
  78.8 26.2 %collective-permute-start.9 = (f32[1,32,32,128]{3,2,1,0:T(8,128)}, f32[1,32,32,128]{3,2,1,0:T(8,128)S(1)}, u32[]{:S(2)}, u32[]{:S(2)}) collective-permute-start(f32[1,32,32,128]{3,2,1,0:T(8,128)} %get-tuple-element.35), channel_id=1, source_target_pairs={{0,2},{1,3},{2,0},{3,1},{4,6},{5,7},{6,4},{7,5},{8,10},{9,11},{10,... | collective-permute-start | bytes 1572872 | tf_op jit(solution)/shard_map/ppermute | solution.py:703
  108.2 49.0 %slice-start = ((s8[6291456]{0:T(1024)(128)(4,1)}), s8[2097152]{0:T(1024)(128)(4,1)S(1)}, s32[]{:S(2)}) async-start(s8[6291456]{0:T(1024)(128)(4,1)} %bitcast.20), calls=%async_computation.5 | async-start | bytes 4194304
  113.4 43.8 %slice-start.1 = ((s8[6291456]{0:T(1024)(128)(4,1)}), s8[4194304]{0:T(1024)(128)(4,1)S(1)}, s32[]{:S(2)}) async-start(s8[6291456]{0:T(1024)(128)(4,1)} %bitcast.20), calls=%async_computation.6 | async-start | bytes 8388608
  119.8 42.9 %copy-start.9 = (f32[4,32,32,128]{3,2,1,0:T(8,128)}, f32[4,32,32,128]{3,2,1,0:T(8,128)S(1)}, u32[]{:S(2)}) copy-start(f32[4,32,32,128]{3,2,1,0:T(8,128)S(1)} %get-tuple-element.40.current_ref) | copy-start | bytes 6291460
  151.9 12.3 %collective-permute-start.10 = (bf16[1024,128]{1,0:T(8,128)(2,1)S(1)}, bf16[1024,128]{1,0:T(8,128)(2,1)S(1)}, u32[]{:S(2)}, u32[]{:S(2)}) collective-permute-start(bf16[1024,128]{1,0:T(8,128)(2,1)S(1)} %get-tuple-element.57), channel_id=1, source_target_pairs={{0,4},{4,8},{8,12},{12,16},{16,20},{20,24},{24,28},{28,1},{1,5},{5... | collective-permute-start | bytes 786440 | tf_op jit(solution)/shard_map/ppermute | solution.py:376
  153.4 13.0 %collective-permute-start.11 = (bf16[1024,128]{1,0:T(8,128)(2,1)S(1)}, bf16[1024,128]{1,0:T(8,128)(2,1)S(1)}, u32[]{:S(2)}, u32[]{:S(2)}) collective-permute-start(bf16[1024,128]{1,0:T(8,128)(2,1)S(1)} %get-tuple-element.56), channel_id=1, source_target_pairs={{4,0},{8,4},{12,8},{16,12},{20,16},{24,20},{28,24},{1,28},{5,1},{9... | collective-permute-start | bytes 786440 | tf_op jit(solution)/shard_map/ppermute | solution.py:377
  169.4 29.3 %all-to-all-start.3 = ((bf16[32,32,512]{2,1,0:T(8,128)(2,1)}), bf16[32,32,512]{2,1,0:T(8,128)(2,1)S(1)}, u32[]{:S(2)}, u32[]{:S(2)}) async-start(bf16[32,32,512]{2,1,0:T(8,128)(2,1)} %bitcast.13), calls=%async_computation.3 | async-start | bytes 2097152 | tf_op jit(solution)/shard_map/all_to_all | solution.py:796
  198.7 7.1 %copy-start.11 = (f32[4,32,32,128]{3,2,1,0:T(8,128)S(1)}, f32[4,32,32,128]{3,2,1,0:T(8,128)}, u32[]{:S(2)}) copy-start(f32[4,32,32,128]{3,2,1,0:T(8,128)} %copy-done.9) | copy-start | bytes 6291460
  202.8 11.2 %collective-permute-start.12 = (bf16[1,32,32,128]{3,2,1,0:T(8,128)(2,1)S(1)}, bf16[1,32,32,128]{3,2,1,0:T(8,128)(2,1)S(1)}, u32[]{:S(2)}, u32[]{:S(2)}) collective-permute-start(bf16[1,32,32,128]{3,2,1,0:T(8,128)(2,1)S(1)} %get-tuple-element.45), channel_id=1, source_target_pairs={{0,1},{1,2},{2,3},{3,0},{4,5},{5,6},{6,7},{7,4},{8,9},{9,10},{10,1... | collective-permute-start | bytes 786440 | tf_op jit(solution)/shard_map/ppermute | solution.py:703
  202.9 11.2 %collective-permute-start.13 = (bf16[1,32,32,128]{3,2,1,0:T(8,128)(2,1)S(1)}, bf16[1,32,32,128]{3,2,1,0:T(8,128)(2,1)S(1)}, u32[]{:S(2)}, u32[]{:S(2)}) collective-permute-start(bf16[1,32,32,128]{3,2,1,0:T(8,128)(2,1)S(1)} %get-tuple-element.46), channel_id=1, source_target_pairs={{0,2},{1,3},{2,0},{3,1},{4,6},{5,7},{6,4},{7,5},{8,10},{9,11},{10,... | collective-permute-start | bytes 786440 | tf_op jit(solution)/shard_map/ppermute | solution.py:703
  204.4 12.3 %collective-permute-start.14 = (bf16[1,32,32,128]{3,2,1,0:T(8,128)(2,1)S(1)}, bf16[1,32,32,128]{3,2,1,0:T(8,128)(2,1)S(1)}, u32[]{:S(2)}, u32[]{:S(2)}) collective-permute-start(bf16[1,32,32,128]{3,2,1,0:T(8,128)(2,1)S(1)} %get-tuple-element.47), channel_id=1, source_target_pairs={{0,3},{1,0},{2,1},{3,2},{4,7},{5,4},{6,5},{7,6},{8,11},{9,8},{10,9... | collective-permute-start | bytes 786440 | tf_op jit(solution)/shard_map/ppermute | solution.py:703
  210.3 18.0 %all-to-all-start.4 = ((bf16[128,32,128]{2,1,0:T(8,128)(2,1)}), bf16[128,32,128]{2,1,0:T(8,128)(2,1)S(1)}, u32[]{:S(2)}, u32[]{:S(2)}) async-start(bf16[128,32,128]{2,1,0:T(8,128)(2,1)} %bitcast.14), calls=%async_computation.4 | async-start | bytes 2097152 | tf_op jit(solution)/shard_map/all_to_all | solution.py:737
  (7 other events, 9.7 us)

commit v12 on v11

--- a/solution.py
+++ b/solution.py
@@ -609,7 +609,7 @@
             out_specs=[slab] * 3,
         ),
         out_shape=[shape] * 3,
-        compiler_params=pltpu.CompilerParams(vmem_limit_bytes=SHARED_VMEM_BYTES),
+        compiler_params=pltpu.CompilerParams(vmem_limit_bytes=3 * SMALL_VMEM_BYTES),
     )(place, *current_parts, *right_side_parts, weights, right)
 
 
@@ -736,7 +736,7 @@
         flat = block.reshape(modes, rows, cols)
         return lax.all_to_all(flat, "slab", 0, 0, tiled=True)
 
-    borders = (state[:, :cols], state[:, -cols:])
+    matrix = dense_coupling(coupling, coupling_list, pair_count, fields)
 
     slab = lax.axis_index("slab")
     place = jnp.stack([slab, slab * mode_count + lax.axis_index("mode")])
@@ -744,6 +744,9 @@
     low = lax.ppermute(coefs[0, :, -1], "slab", forward)
     high = lax.ppermute(coefs[0, :, 0], "slab", [(b, a) for a, b in forward])
     strip_weights = strip_weights_of(coefs[0], low, high, place, slab_count, height)
+
+    state, matrix, strip_weights = lax.optimization_barrier((state, matrix, strip_weights))
+    borders = (state[:, :cols], state[:, -cols:])
 
     guess_parts = parts_of(guess.reshape(slab_count, share, rows, cols), "slab")
     guess_parts = [jnp.concatenate([part, coefs], axis=1) for part in guess_parts]
@@ -752,7 +755,6 @@
     guess_parts, right_parts, _ = lax.optimization_barrier((guess_parts, right_parts, borders))
     right_parts = moved_parts(right_parts, "slab")
     mean_weights = mean_weights_of(guess_parts, place, fields + 1)
-    matrix = dense_coupling(coupling, coupling_list, pair_count, fields)
 
     row_high, row_low = split_table(sine_table(nx))
     col_high, col_low = split_table(sine_table(cols))
@@ -779,7 +781,7 @@
     sums = coupled_sums(
         matrix, state, borders, strip_weights, tables[0], True, first_scale, both
     )
-    sums, *right_parts[1::2] = lax.optimization_barrier((sums, *right_parts[1::2]))
+    sums, right_parts = lax.optimization_barrier((sums, right_parts))
     sums = lax.all_to_all(sums, both, 0, 0, tiled=True).reshape(devices, share, -1)
     current, right_side, base = first_mean_part(
         place, guess_parts, right_parts, mean_weights, tables[0]

time: 231 us -> 226 us (0.978)
  waiting for transfers between devices: 78 us -> 65 us
  local copies, waits for them, and re-layouts: 15 us -> 22 us
  starting transfers between devices: 41.2 us -> 46.7 us
  Pallas kernels: 56.4 us -> 53.8 us
  blocking collectives: 32 us -> 29.6 us
    ppermute x9, waiting for transfers between devices: 28.9 us -> 6.21 us  [onwards(): lax.ppermute(part, axis, [(i, (i + shift) % count) for i in range(count)])]
    all_to_all x2, waiting for transfers between devices: 20.6 us -> 41.2 us  [local(): lax.all_to_all(sums, both, 0, 0, tiled=True).reshape(devices, share, -1)]
    all_to_all x1, waiting for transfers between devices: 15.7 us -> 5.06 us  [local(): state = lax.all_to_all(strips, 'mode', 0, 0, tiled=True)]
    unnamed x40 -> x52, local copies, waits for them, and re-layouts: 9.73 us -> 16 us
    all_to_all x2, starting transfers between devices: 7.45 us -> 11.4 us  [local(): lax.all_to_all(sums, both, 0, 0, tiled=True).reshape(devices, share, -1)]
    all_to_all x1, blocking collectives: 32 us -> 29.6 us  [local(): state = lax.all_to_all(state, both, 0, 0, tiled=True)]
    pallas_call x1, Pallas kernels: 5.19 us -> 2.79 us  [first_mean_part(): pl.pallas_call(functools.partial(first_mean_kernel, slabs), grid_spec=plt...]
  transfers between devices with their start and end apart: 19 -> 19, of which waited for: 9 -> 8; matrix products, arithmetic and copies ran while one was open for 4% -> 5% of each run, Pallas kernels for 17% -> 16%
where the time goes in v12:
time: 226 us; the launch traced here: 225 us
  waiting for transfers between devices  65 us (29%)
  Pallas kernels  53.8 us (24%)
  starting transfers between devices  46.7 us (21%)
  blocking collectives  29.6 us (13%)
  local copies, waits for them, and re-layouts  22 us (10%)
  other arithmetic  6.86 us (3%)
    all_to_all x2, waiting for transfers between devices, local(): lax.all_to_all(sums, both, 0, 0, tiled=True).reshape(devices, share, -1)  41.2 us
    all_to_all x1, blocking collectives, local(): state = lax.all_to_all(state, both, 0, 0, tiled=True)  29.6 us
    unnamed x52, local copies, waits for them, and re-layouts  16 us
    pallas_call x3, Pallas kernels, per_group(): pl.pallas_call(kernel, grid=(groups,), in_specs=in_specs, out_specs=out_s...  13.5 us
    pallas_call x2, Pallas kernels, coupled_sums(): pl.pallas_call(functools.partial(inner_kernel, height, cols), grid=(block...  12.1 us
    all_to_all x2, starting transfers between devices, local(): lax.all_to_all(sums, both, 0, 0, tiled=True).reshape(devices, share, -1)  11.4 us
    ppermute x9, starting transfers between devices, onwards(): lax.ppermute(part, axis, [(i, (i + shift) % count) for i in range(count)])  11.1 us
    all_to_all x1, waiting for transfers between devices, to_slabs(): return lax.all_to_all(flat, 'slab', 0, 0, tiled=True)  8.83 us
  transfers between devices with their start and end apart: 19, of which 8 were waited for; matrix products, arithmetic and copies ran while one was open for 5% of the time, Pallas kernels for 16%

profile of v12, /device:TPU:0, one launch (start us, length us, event | category | flops | bytes accessed | tf_op | source)
XLA Modules:
  0.0 225.1 jit_solution(5134045312420328350)
XLA Ops:
  0.6 3.3 %shard_map.86 = bf16[8,128,512]{2,1,0:T(8,128)(2,1)} custom-call(f32[4096,128]{1,0:T(8,128)} %bitcast.25), custom_call_target="tpu_custom_call" | custom-call | tf_op jit(solution)/shard_map/pallas_call | solution.py:216
  4.0 7.3 %all-to-all-start = ((bf16[8,128,512]{2,1,0:T(8,128)(2,1)}), bf16[8,128,512]{2,1,0:T(8,128)(2,1)}, u32[]{:S(2)}, u32[]{:S(2)}) async-start(bf16[8,128,512]{2,1,0:T(8,128)(2,1)} %shard_map.86), calls=%async_computation | async-start | bytes 2097152 | tf_op jit(solution)/shard_map/all_to_all | solution.py:732
  11.3 1.7 constant_dynamic-slice_fusion.4
  19.9 2.9 %constant_dynamic-slice_fusion = (f32[1,32,32,128]{3,2,1,0:T(8,128)}, f32[1,32,32,128]{3,2,1,0:T(8,128)}, f32[1,32,32,128]{3,2,1,0:T(8,128)}, f32[1,32,32,128]{3,2,1,0:T(8,128)}) fusion(f32[4,32,32,128]{3,2,1,0:T(8,128)} %bitcast.27, s32[]{:T(128)S(6)} %select_n.40, s32[]{:T(128)S(6)} %select_n.39, s32[]{:T(128)S(6)} %select_n.38, s32[]{:T(128)S(6)} %select_n.37), kind=kLoop, calls=%fused_computation.39 | loop fusion | bytes 4194320 | tf_op jit(solution)/shard_map/jit(dynamic_index_in_dim)/dynamic_slice | solution.py:710
  22.8 8.6 %shard_map.87.matrix_ref = bf16[8,3,128,1024]{3,2,1,0:T(8,128)(2,1)} custom-call(s32[8,16]{1,0:T(8,128)} %entry_ref.1, s32[8]{0:T(128)} %count_ref.1, bf16[8,16,128,128]{3,2,1,0:T(8,128)(2,1)} %coupling_ref.1), custom_call_target="tpu_custom_call" | custom-call | tf_op jit(solution)/shard_map/pallas_call | solution.py:242
  32.1 5.1 %all-to-all-done = bf16[8,128,512]{2,1,0:T(8,128)(2,1)} async-done(((bf16[8,128,512]{2,1,0:T(8,128)(2,1)}), bf16[8,128,512]{2,1,0:T(8,128)(2,1)}, u32[]{:S(2)}, u32[]{:S(2)}) %all-to-all-start) | async-done | bytes 1048608 | tf_op jit(solution)/shard_map/all_to_all | solution.py:732
  38.3 3.6 %collective-permute-done.2.refs_3_ = f32[1,36,32,128]{3,2,1,0:T(8,128)S(1)} collective-permute-done((f32[1,36,32,128]{3,2,1,0:T(8,128)}, f32[1,36,32,128]{3,2,1,0:T(8,128)S(1)}, u32[]{:S(2)}, u32[]{:S(2)}) %collective-permute-start.2) | collective-permute-done | bytes 589856 | tf_op jit(solution)/shard_map/ppermute | solution.py:703
  41.9 2.6 %collective-permute-start.7 = (f32[1,32,32,128]{3,2,1,0:T(8,128)}, f32[1,32,32,128]{3,2,1,0:T(8,128)S(1)}, u32[]{:S(2)}, u32[]{:S(2)}) collective-permute-start(f32[1,32,32,128]{3,2,1,0:T(8,128)} %get-tuple-element.40), channel_id=1, source_target_pairs={{0,1},{1,2},{2,3},{3,0},{4,5},{5,6},{6,7},{7,4},{8,9},{9,10},{10,1... | collective-permute-start | bytes 1572872 | tf_op jit(solution)/shard_map/ppermute | solution.py:703
  47.4 2.1 collective-permute-start.5
  49.5 3.3 %collective-permute-start.6 = (bf16[1024,128]{1,0:T(8,128)(2,1)S(1)}, bf16[1024,128]{1,0:T(8,128)(2,1)S(1)}, u32[]{:S(2)}, u32[]{:S(2)}) collective-permute-start(bf16[1024,128]{1,0:T(8,128)(2,1)S(1)} %get-tuple-element.69), channel_id=1, source_target_pairs={{4,0},{8,4},{12,8},{16,12},{20,16},{24,20},{28,24},{1,28},{5,1},{9... | collective-permute-start | bytes 786440 | tf_op jit(solution)/shard_map/ppermute | solution.py:377
  52.8 2.8 %copy-done = bf16[8,3,128,1024]{3,2,1,0:T(8,128)(2,1)S(1)} copy-done((bf16[8,3,128,1024]{3,2,1,0:T(8,128)(2,1)S(1)}, bf16[8,3,128,1024]{3,2,1,0:T(8,128)(2,1)}, u32[]{:S(2)}) %copy-start) | copy-done | bytes 6291480
  55.6 6.7 %shard_map.89.inner_ref = f32[1024,512]{1,0:T(8,128)S(1)} custom-call(bf16[8,3,128,1024]{3,2,1,0:T(8,128)(2,1)S(1)} %copy-done, bf16[1024,512]{1,0:T(8,128)(2,1)} %bitcast.7.state_ref, f32[60,128]{1,0:T(8,128)S(1)} %shard_map.88.weight_ref), custom_call_target="tpu_custom_call" | custom-call | flops 3221225472 | bytes 6291456 | tf_op jit(solution)/shard_map/pallas_call | solution.py:384
  62.4 5.1 %shard_map.90 = bf16[1024,640]{1,0:T(8,128)(2,1)} custom-call(bf16[8,3,128,1024]{3,2,1,0:T(8,128)(2,1)S(1)} %copy-done.1, bf16[1024,128]{1,0:T(8,128)(2,1)S(1)} %collective-permute-done.5.above_ref, bf16[1024,128]{1,0:T(8,128)(2,1)S(1)} %collective-permute-done.6.below_ref, f32[60,128]{1,0:T(8,128)S(1)} %shard_map.88.weight_ref, ...), custom_call_target="tpu_custom_call" | custom-call | tf_op jit(solution)/shard_map/pallas_call | solution.py:398
  69.9 8.4 %all-to-all-start.1 = ((bf16[32,32,640]{2,1,0:T(8,128)(2,1)}), bf16[32,32,640]{2,1,0:T(8,128)(2,1)}, u32[]{:S(2)}, u32[]{:S(2)}) async-start(bf16[32,32,640]{2,1,0:T(8,128)(2,1)} %bitcast.11), calls=%async_computation.1 | async-start | bytes 2621440 | tf_op jit(solution)/shard_map/all_to_all | solution.py:785
  83.0 2.8 %shard_map.92 = (f32[4,32,32,128]{3,2,1,0:T(8,128)S(1)}, f32[4,32,32,128]{3,2,1,0:T(8,128)S(1)}, f32[4,32,32,128]{3,2,1,0:T(8,128)S(1)}) custom-call(s32[2]{0:T(128)S(1)} %pad_add_fusion.place_ref, f32[1,36,32,128]{3,2,1,0:T(8,128)S(1)} %get-tuple-element.33.refs_0_, f32[1,36,32,128]{3,2,1,0:T(8,128)S(1)} %copy-done.4, f32[1,36,32,128]{3,2,1,0:T(8,128)S(1)} %copy-done.6, ...), custom_call_target="tpu_custom_call" | custom-call | tf_op jit(solution)/shard_map/pallas_call | solution.py:599
  89.8 20.6 %all-to-all-done.1.coupled_ref = bf16[32,32,640]{2,1,0:T(8,128)(2,1)} async-done(((bf16[32,32,640]{2,1,0:T(8,128)(2,1)}), bf16[32,32,640]{2,1,0:T(8,128)(2,1)}, u32[]{:S(2)}, u32[]{:S(2)}) %all-to-all-start.1) | async-done | bytes 1310752 | tf_op jit(solution)/shard_map/all_to_all | solution.py:785
  110.4 6.3 %shard_map.93 = (f32[4,32,32,128]{3,2,1,0:T(8,128)S(1)}, bf16[32,32,512]{2,1,0:T(8,128)(2,1)S(1)}) custom-call(f32[4,32,32,128]{3,2,1,0:T(8,128)} %copy-done.20, f32[4,32,32,128]{3,2,1,0:T(8,128)} %copy-done.21, bf16[32,32,640]{2,1,0:T(8,128)(2,1)} %all-to-all-done.1.coupled_ref, bf16[256,256]{1,0:T(8,128)(2,1)S(1)} %get-tuple-element.71.right_ref.refs_9_, ...), custom_call_target="tpu_custom_call" | custom-call | flops 1610612736 | bytes 11665408 | tf_op jit(solution)/shard_map/pallas_call | solution.py:581
  116.8 29.6 %all_to_all.36 = bf16[32,32,512]{2,1,0:T(8,128)(2,1)S(1)} all-to-all(bf16[32,32,512]{2,1,0:T(8,128)(2,1)S(1)} %get-tuple-element.52), channel_id=1, replica_groups=mesh['mode'=8,'slab'=4] {'mode','slab'}, dimensions={0} | all-to-all | bytes 2097152 | tf_op jit(solution)/shard_map/all_to_all | solution.py:791
  147.9 3.9 %collective-permute-start.11 = (bf16[1024,128]{1,0:T(8,128)(2,1)S(1)}, bf16[1024,128]{1,0:T(8,128)(2,1)S(1)}, u32[]{:S(2)}, u32[]{:S(2)}) collective-permute-start(bf16[1024,128]{1,0:T(8,128)(2,1)S(1)} %get-tuple-element.66), channel_id=1, source_target_pairs={{4,0},{8,4},{12,8},{16,12},{20,16},{24,20},{28,24},{1,28},{5,1},{9... | collective-permute-start | bytes 786440 | tf_op jit(solution)/shard_map/ppermute | solution.py:377
  151.8 5.4 %shard_map.95.inner_ref = f32[1024,512]{1,0:T(8,128)S(1)} custom-call(bf16[8,3,128,1024]{3,2,1,0:T(8,128)(2,1)S(1)} %bitcast.21, bf16[1024,512]{1,0:T(8,128)(2,1)S(1)} %bitcast.23, f32[60,128]{1,0:T(8,128)S(1)} %shard_map.88.weight_ref), custom_call_target="tpu_custom_call" | custom-call | flops 3221225472 | bytes 6291456 | tf_op jit(solution)/shard_map/pallas_call | solution.py:384
  158.8 2.2 collective-permute-done.11.below_ref
  161.0 3.0 %shard_map.96 = bf16[1024,512]{1,0:T(8,128)(2,1)} custom-call(bf16[8,3,128,1024]{3,2,1,0:T(8,128)(2,1)S(1)} %bitcast.21, bf16[1024,128]{1,0:T(8,128)(2,1)S(1)} %collective-permute-done.10.above_ref, bf16[1024,128]{1,0:T(8,128)(2,1)S(1)} %collective-permute-done.11.below_ref, f32[60,128]{1,0:T(8,128)S(1)} %shard_map.88.weight_ref, ...), custom_call_target="tpu_custom_call" | custom-call | tf_op jit(solution)/shard_map/pallas_call | solution.py:398
  163.9 3.0 %all-to-all-start.3 = ((bf16[32,32,512]{2,1,0:T(8,128)(2,1)}), bf16[32,32,512]{2,1,0:T(8,128)(2,1)S(1)}, u32[]{:S(2)}, u32[]{:S(2)}) async-start(bf16[32,32,512]{2,1,0:T(8,128)(2,1)} %bitcast.13), calls=%async_computation.3 | async-start | bytes 2097152 | tf_op jit(solution)/shard_map/all_to_all | solution.py:798
  168.6 2.7 %shard_map.94.base_ref = f32[4,32,32,128]{3,2,1,0:T(8,128)S(1)} custom-call(f32[4,32,32,128]{3,2,1,0:T(8,128)S(1)} %copy-done.10, f32[4,32,32,128]{3,2,1,0:T(8,128)} %copy-done.12, f32[5,128,128]{2,1,0:T(8,128)S(1)} %shard_map.91.refs_8_.weight_ref), custom_call_target="tpu_custom_call" | custom-call | bytes 9043968 | tf_op jit(solution)/shard_map/pallas_call | solution.py:581
  172.6 20.6 %all-to-all-done.3.coupled_ref = bf16[32,32,512]{2,1,0:T(8,128)(2,1)S(1)} async-done(((bf16[32,32,512]{2,1,0:T(8,128)(2,1)}), bf16[32,32,512]{2,1,0:T(8,128)(2,1)S(1)}, u32[]{:S(2)}, u32[]{:S(2)}) %all-to-all-start.3) | async-done | bytes 1048608 | tf_op jit(solution)/shard_map/all_to_all | solution.py:798
  193.2 4.1 %shard_map.97 = (f32[4,32,32,128]{3,2,1,0:T(8,128)S(1)}, bf16[1,32,32,128]{3,2,1,0:T(8,128)(2,1)S(1)}, bf16[1,32,32,128]{3,2,1,0:T(8,128)(2,1)S(1)}, bf16[1,32,3...) custom-call(s32[1]{0:T(128)} %bitcast.here_ref, f32[4,32,32,128]{3,2,1,0:T(8,128)} %copy-done.2, ...), custom_call_target="tpu_custom_call" | custom-call | bytes 4194304 | tf_op jit(solution)/shard_map/pallas_call | solution.py:658
  200.3 4.5 %shard_map.98 = bf16[4,32,32,128]{3,2,1,0:T(8,128)(2,1)} custom-call(f32[4,32,32,128]{3,2,1,0:T(8,128)S(1)} %copy-done.11, f32[4,32,32,128]{3,2,1,0:T(8,128)S(1)} %get-tuple-element.53.resid_ref, bf16[256,256]{1,0:T(8,128)(2,1)S(1)} %get-tuple-element.71.right_ref.refs_9_, bf16[256,256]{1,0:T(8,128)(2,1)S(1)} %get-tuple-element.70.left_ref, ...), custom_call_target="tpu_custom_call" | custom-call | flops 1610612736 | bytes 9043968 | tf_op jit(solution)/shard_map/pallas_call | solution.py:581
  204.8 3.5 %all-to-all-start.4 = ((bf16[128,32,128]{2,1,0:T(8,128)(2,1)}), bf16[128,32,128]{2,1,0:T(8,128)(2,1)S(1)}, u32[]{:S(2)}, u32[]{:S(2)}) async-start(bf16[128,32,128]{2,1,0:T(8,128)(2,1)} %bitcast.14), calls=%async_computation.4 | async-start | bytes 2097152 | tf_op jit(solution)/shard_map/all_to_all | solution.py:737
  208.7 2.5 %collective-permute-done.14 = bf16[1,32,32,128]{3,2,1,0:T(8,128)(2,1)S(1)} collective-permute-done((bf16[1,32,32,128]{3,2,1,0:T(8,128)(2,1)S(1)}, bf16[1,32,32,128]{3,2,1,0:T(8,128)(2,1)S(1)}, u32[]{:S(2)}, u32[]{:S(2)}) %collective-permute-start.14) | collective-permute-done | bytes 262176 | tf_op jit(solution)/shard_map/ppermute | solution.py:703
  212.2 1.8 fusion.11
  214.0 8.8 %all-to-all-done.4 = bf16[128,32,128]{2,1,0:T(8,128)(2,1)S(1)} async-done(((bf16[128,32,128]{2,1,0:T(8,128)(2,1)}), bf16[128,32,128]{2,1,0:T(8,128)(2,1)S(1)}, u32[]{:S(2)}, u32[]{:S(2)}) %all-to-all-start.4) | async-done | bytes 1048608 | tf_op jit(solution)/shard_map/all_to_all | solution.py:737
  222.8 2.2 fusion.10
  (95 shorter events, 33.0 us)
Async XLA Ops:
  0.6 3.3 %copy-start.23 = (f32[32,128]{1,0:T(8,128)S(1)}, f32[32,128]{1,0:T(8,128)}, u32[]{:S(2)}) copy-start(f32[32,128]{1,0:T(8,128)} %param.9) | copy-start | bytes 49156
  0.6 3.3 %copy-start.22 = (f32[3,32,128]{2,1,0:T(8,128)S(1)}, f32[3,32,128]{2,1,0:T(8,128)}, u32[]{:S(2)}) copy-start(f32[3,32,128]{2,1,0:T(8,128)} %param.10) | copy-start | bytes 147460
  4.0 33.2 %all-to-all-start = ((bf16[8,128,512]{2,1,0:T(8,128)(2,1)}), bf16[8,128,512]{2,1,0:T(8,128)(2,1)}, u32[]{:S(2)}, u32[]{:S(2)}) async-start(bf16[8,128,512]{2,1,0:T(8,128)(2,1)} %shard_map.86), calls=%async_computation | async-start | bytes 2097152 | tf_op jit(solution)/shard_map/all_to_all | solution.py:732
  14.3 23.9 %collective-permute-start = (f32[1,36,32,128]{3,2,1,0:T(8,128)}, f32[1,36,32,128]{3,2,1,0:T(8,128)S(1)}, u32[]{:S(2)}, u32[]{:S(2)}) collective-permute-start(f32[1,36,32,128]{3,2,1,0:T(8,128)} %get-tuple-element.75), channel_id=1, source_target_pairs={{0,1},{1,2},{2,3},{3,0},{4,5},{5,6},{6,7},{7,4},{8,9},{9,10},{10,1... | collective-permute-start | bytes 1769480 | tf_op jit(solution)/shard_map/ppermute | solution.py:703
  14.3 23.9 %collective-permute-start.1 = (f32[1,36,32,128]{3,2,1,0:T(8,128)}, f32[1,36,32,128]{3,2,1,0:T(8,128)S(1)}, u32[]{:S(2)}, u32[]{:S(2)}) collective-permute-start(f32[1,36,32,128]{3,2,1,0:T(8,128)} %get-tuple-element.76), channel_id=1, source_target_pairs={{0,2},{1,3},{2,0},{3,1},{4,6},{5,7},{6,4},{7,5},{8,10},{9,11},{10,... | collective-permute-start | bytes 1769480 | tf_op jit(solution)/shard_map/ppermute | solution.py:703
  15.8 26.1 %collective-permute-start.2 = (f32[1,36,32,128]{3,2,1,0:T(8,128)}, f32[1,36,32,128]{3,2,1,0:T(8,128)S(1)}, u32[]{:S(2)}, u32[]{:S(2)}) collective-permute-start(f32[1,36,32,128]{3,2,1,0:T(8,128)} %get-tuple-element.74), channel_id=1, source_target_pairs={{0,3},{1,0},{2,1},{3,2},{4,7},{5,4},{6,5},{7,6},{8,11},{9,8},{10,9... | collective-permute-start | bytes 1769480 | tf_op jit(solution)/shard_map/ppermute | solution.py:703
  17.3 14.2 %collective-permute-start.3 = (f32[4,128]{1,0:T(4,128)S(1)}, f32[4,128]{1,0:T(4,128)S(1)}, u32[]{:S(2)}, u32[]{:S(2)}) collective-permute-start(f32[4,128]{1,0:T(4,128)S(1)} %bitcast.30), channel_id=1, source_target_pairs={{0,1},{1,2},{2,3},{4,5},{5,6},{6,7},{8,9},{9,10},{10,11},{12,13},{... | collective-permute-start | bytes 6152 | tf_op jit(solution)/shard_map/ppermute | solution.py:744
  18.5 12.9 %collective-permute-start.4 = (f32[4,128]{1,0:T(4,128)S(1)}, f32[4,128]{1,0:T(4,128)S(1)}, u32[]{:S(2)}, u32[]{:S(2)}) collective-permute-start(f32[4,128]{1,0:T(4,128)S(1)} %bitcast.29), channel_id=1, source_target_pairs={{1,0},{2,1},{3,2},{5,4},{6,5},{7,6},{9,8},{10,9},{11,10},{13,12},{... | collective-permute-start | bytes 6152 | tf_op jit(solution)/shard_map/ppermute | solution.py:745
  38.2 40.3 %copy-start.3 = (f32[1,36,32,128]{3,2,1,0:T(8,128)}, f32[1,36,32,128]{3,2,1,0:T(8,128)S(1)}, u32[]{:S(2)}) copy-start(f32[1,36,32,128]{3,2,1,0:T(8,128)S(1)} %collective-permute-done.refs_1_) | copy-start | bytes 1769476
  38.2 40.2 %copy-start.5 = (f32[1,36,32,128]{3,2,1,0:T(8,128)}, f32[1,36,32,128]{3,2,1,0:T(8,128)S(1)}, u32[]{:S(2)}) copy-start(f32[1,36,32,128]{3,2,1,0:T(8,128)S(1)} %collective-permute-done.1.refs_2_) | copy-start | bytes 1769476
  41.9 36.6 %copy-start.7 = (f32[1,36,32,128]{3,2,1,0:T(8,128)}, f32[1,36,32,128]{3,2,1,0:T(8,128)S(1)}, u32[]{:S(2)}) copy-start(f32[1,36,32,128]{3,2,1,0:T(8,128)S(1)} %collective-permute-done.2.refs_3_) | copy-start | bytes 1769476
  41.9 25.6 %collective-permute-start.7 = (f32[1,32,32,128]{3,2,1,0:T(8,128)}, f32[1,32,32,128]{3,2,1,0:T(8,128)S(1)}, u32[]{:S(2)}, u32[]{:S(2)}) collective-permute-start(f32[1,32,32,128]{3,2,1,0:T(8,128)} %get-tuple-element.40), channel_id=1, source_target_pairs={{0,1},{1,2},{2,3},{3,0},{4,5},{5,6},{6,7},{7,4},{8,9},{9,10},{10,1... | collective-permute-start | bytes 1572872 | tf_op jit(solution)/shard_map/ppermute | solution.py:703
  44.5 23.8 %collective-permute-start.8 = (f32[1,32,32,128]{3,2,1,0:T(8,128)}, f32[1,32,32,128]{3,2,1,0:T(8,128)S(1)}, u32[]{:S(2)}, u32[]{:S(2)}) collective-permute-start(f32[1,32,32,128]{3,2,1,0:T(8,128)} %get-tuple-element.41), channel_id=1, source_target_pairs={{0,2},{1,3},{2,0},{3,1},{4,6},{5,7},{6,4},{7,5},{8,10},{9,11},{10,... | collective-permute-start | bytes 1572872 | tf_op jit(solution)/shard_map/ppermute | solution.py:703
  45.7 23.4 %collective-permute-start.9 = (f32[1,32,32,128]{3,2,1,0:T(8,128)}, f32[1,32,32,128]{3,2,1,0:T(8,128)S(1)}, u32[]{:S(2)}, u32[]{:S(2)}) collective-permute-start(f32[1,32,32,128]{3,2,1,0:T(8,128)} %get-tuple-element.42), channel_id=1, source_target_pairs={{0,3},{1,0},{2,1},{3,2},{4,7},{5,4},{6,5},{7,6},{8,11},{9,8},{10,9... | collective-permute-start | bytes 1572872 | tf_op jit(solution)/shard_map/ppermute | solution.py:703
  47.4 14.9 %collective-permute-start.5 = (bf16[1024,128]{1,0:T(8,128)(2,1)S(1)}, bf16[1024,128]{1,0:T(8,128)(2,1)S(1)}, u32[]{:S(2)}, u32[]{:S(2)}) collective-permute-start(bf16[1024,128]{1,0:T(8,128)(2,1)S(1)} %get-tuple-element.68), channel_id=1, source_target_pairs={{0,4},{4,8},{8,12},{12,16},{16,20},{20,24},{24,28},{28,1},{1,5},{5... | collective-permute-start | bytes 786440 | tf_op jit(solution)/shard_map/ppermute | solution.py:376
  49.5 12.9 %collective-permute-start.6 = (bf16[1024,128]{1,0:T(8,128)(2,1)S(1)}, bf16[1024,128]{1,0:T(8,128)(2,1)S(1)}, u32[]{:S(2)}, u32[]{:S(2)}) collective-permute-start(bf16[1024,128]{1,0:T(8,128)(2,1)S(1)} %get-tuple-element.69), channel_id=1, source_target_pairs={{4,0},{8,4},{12,8},{16,12},{20,16},{24,20},{28,24},{1,28},{5,1},{9... | collective-permute-start | bytes 786440 | tf_op jit(solution)/shard_map/ppermute | solution.py:377
  52.8 2.8 %copy-start = (bf16[8,3,128,1024]{3,2,1,0:T(8,128)(2,1)S(1)}, bf16[8,3,128,1024]{3,2,1,0:T(8,128)(2,1)}, u32[]{:S(2)}) copy-start(bf16[8,3,128,1024]{3,2,1,0:T(8,128)(2,1)} %shard_map.87.matrix_ref) | copy-start | bytes 18874372
  55.6 6.8 %copy-start.1 = (bf16[8,3,128,1024]{3,2,1,0:T(8,128)(2,1)S(1)}, bf16[8,3,128,1024]{3,2,1,0:T(8,128)(2,1)}, u32[]{:S(2)}) copy-start(bf16[8,3,128,1024]{3,2,1,0:T(8,128)(2,1)} %shard_map.87.matrix_ref) | copy-start | bytes 18874372
  69.9 40.5 %all-to-all-start.1 = ((bf16[32,32,640]{2,1,0:T(8,128)(2,1)}), bf16[32,32,640]{2,1,0:T(8,128)(2,1)}, u32[]{:S(2)}, u32[]{:S(2)}) async-start(bf16[32,32,640]{2,1,0:T(8,128)(2,1)} %bitcast.11), calls=%async_computation.1 | async-start | bytes 2621440 | tf_op jit(solution)/shard_map/all_to_all | solution.py:785
  78.3 1.5 copy-start.19
  83.0 68.8 %slice-start = ((s8[6291456]{0:T(1024)(128)(4,1)}), s8[2097152]{0:T(1024)(128)(4,1)S(1)}, s32[]{:S(2)}) async-start(s8[6291456]{0:T(1024)(128)(4,1)} %bitcast.20), calls=%async_computation.5 | async-start | bytes 4194304
  110.4 41.4 %slice-start.1 = ((s8[6291456]{0:T(1024)(128)(4,1)}), s8[4194304]{0:T(1024)(128)(4,1)S(1)}, s32[]{:S(2)}) async-start(s8[6291456]{0:T(1024)(128)(4,1)} %bitcast.20), calls=%async_computation.6 | async-start | bytes 8388608
  116.7 40.5 %copy-start.9 = (f32[4,32,32,128]{3,2,1,0:T(8,128)}, f32[4,32,32,128]{3,2,1,0:T(8,128)S(1)}, u32[]{:S(2)}) copy-start(f32[4,32,32,128]{3,2,1,0:T(8,128)S(1)} %get-tuple-element.50.current_ref) | copy-start | bytes 6291460
  146.4 12.3 %collective-permute-start.10 = (bf16[1024,128]{1,0:T(8,128)(2,1)S(1)}, bf16[1024,128]{1,0:T(8,128)(2,1)S(1)}, u32[]{:S(2)}, u32[]{:S(2)}) collective-permute-start(bf16[1024,128]{1,0:T(8,128)(2,1)S(1)} %get-tuple-element.67), channel_id=1, source_target_pairs={{0,4},{4,8},{8,12},{12,16},{16,20},{20,24},{24,28},{28,1},{1,5},{5... | collective-permute-start | bytes 786440 | tf_op jit(solution)/shard_map/ppermute | solution.py:376
  147.9 13.0 %collective-permute-start.11 = (bf16[1024,128]{1,0:T(8,128)(2,1)S(1)}, bf16[1024,128]{1,0:T(8,128)(2,1)S(1)}, u32[]{:S(2)}, u32[]{:S(2)}) collective-permute-start(bf16[1024,128]{1,0:T(8,128)(2,1)S(1)} %get-tuple-element.66), channel_id=1, source_target_pairs={{4,0},{8,4},{12,8},{16,12},{20,16},{24,20},{28,24},{1,28},{5,1},{9... | collective-permute-start | bytes 786440 | tf_op jit(solution)/shard_map/ppermute | solution.py:377
  163.9 29.3 %all-to-all-start.3 = ((bf16[32,32,512]{2,1,0:T(8,128)(2,1)}), bf16[32,32,512]{2,1,0:T(8,128)(2,1)S(1)}, u32[]{:S(2)}, u32[]{:S(2)}) async-start(bf16[32,32,512]{2,1,0:T(8,128)(2,1)} %bitcast.13), calls=%async_computation.3 | async-start | bytes 2097152 | tf_op jit(solution)/shard_map/all_to_all | solution.py:798
  167.0 1.6 copy-start.10
  193.2 7.1 %copy-start.11 = (f32[4,32,32,128]{3,2,1,0:T(8,128)S(1)}, f32[4,32,32,128]{3,2,1,0:T(8,128)}, u32[]{:S(2)}) copy-start(f32[4,32,32,128]{3,2,1,0:T(8,128)} %copy-done.9) | copy-start | bytes 6291460
  197.3 11.2 %collective-permute-start.12 = (bf16[1,32,32,128]{3,2,1,0:T(8,128)(2,1)S(1)}, bf16[1,32,32,128]{3,2,1,0:T(8,128)(2,1)S(1)}, u32[]{:S(2)}, u32[]{:S(2)}) collective-permute-start(bf16[1,32,32,128]{3,2,1,0:T(8,128)(2,1)S(1)} %get-tuple-element.55), channel_id=1, source_target_pairs={{0,1},{1,2},{2,3},{3,0},{4,5},{5,6},{6,7},{7,4},{8,9},{9,10},{10,1... | collective-permute-start | bytes 786440 | tf_op jit(solution)/shard_map/ppermute | solution.py:703
  197.4 11.2 %collective-permute-start.13 = (bf16[1,32,32,128]{3,2,1,0:T(8,128)(2,1)S(1)}, bf16[1,32,32,128]{3,2,1,0:T(8,128)(2,1)S(1)}, u32[]{:S(2)}, u32[]{:S(2)}) collective-permute-start(bf16[1,32,32,128]{3,2,1,0:T(8,128)(2,1)S(1)} %get-tuple-element.56), channel_id=1, source_target_pairs={{0,2},{1,3},{2,0},{3,1},{4,6},{5,7},{6,4},{7,5},{8,10},{9,11},{10,... | collective-permute-start | bytes 786440 | tf_op jit(solution)/shard_map/ppermute | solution.py:703
  198.9 12.3 %collective-permute-start.14 = (bf16[1,32,32,128]{3,2,1,0:T(8,128)(2,1)S(1)}, bf16[1,32,32,128]{3,2,1,0:T(8,128)(2,1)S(1)}, u32[]{:S(2)}, u32[]{:S(2)}) collective-permute-start(bf16[1,32,32,128]{3,2,1,0:T(8,128)(2,1)S(1)} %get-tuple-element.57), channel_id=1, source_target_pairs={{0,3},{1,0},{2,1},{3,2},{4,7},{5,4},{6,5},{7,6},{8,11},{9,8},{10,9... | collective-permute-start | bytes 786440 | tf_op jit(solution)/shard_map/ppermute | solution.py:703
  204.8 18.0 %all-to-all-start.4 = ((bf16[128,32,128]{2,1,0:T(8,128)(2,1)}), bf16[128,32,128]{2,1,0:T(8,128)(2,1)S(1)}, u32[]{:S(2)}, u32[]{:S(2)}) async-start(bf16[128,32,128]{2,1,0:T(8,128)(2,1)} %bitcast.14), calls=%async_computation.4 | async-start | bytes 2097152 | tf_op jit(solution)/shard_map/all_to_all | solution.py:737
  (13 other events, 14.5 us)

commit v13 on v12

--- a/solution.py
+++ b/solution.py
@@ -239,6 +239,7 @@
 
 def dense_coupling(coupling, coupling_list, pair_count, fields):
     blocks, entries, width, _ = coupling.shape
+    moved = 2 * width * width * (entries + fields * blocks) * coupling.dtype.itemsize
     return pl.pallas_call(
         functools.partial(dense_kernel, fields),
         grid_spec=pltpu.PrefetchScalarGridSpec(
@@ -250,7 +251,7 @@
             ),
         ),
         out_shape=jax.ShapeDtypeStruct((blocks, fields, width, blocks * width), coupling.dtype),
-        compiler_params=pltpu.CompilerParams(vmem_limit_bytes=VMEM_BYTES),
+        compiler_params=pltpu.CompilerParams(vmem_limit_bytes=SMALL_VMEM_BYTES + moved),
     )(coupling_list, pair_count, coupling)
 
 
@@ -609,7 +610,7 @@
             out_specs=[slab] * 3,
         ),
         out_shape=[shape] * 3,
-        compiler_params=pltpu.CompilerParams(vmem_limit_bytes=3 * SMALL_VMEM_BYTES),
+        compiler_params=pltpu.CompilerParams(vmem_limit_bytes=SHARED_VMEM_BYTES),
     )(place, *current_parts, *right_side_parts, weights, right)
 
 

time: 226 us -> 226 us (level)
  waiting for transfers between devices: 65 us -> 70.4 us
  Pallas kernels: 53.8 us -> 49.6 us
    pallas_call x1, Pallas kernels: 8.6 us -> 2.98 us  [dense_coupling(): pl.pallas_call(functools.partial(dense_kernel, fields), grid_spec=pltpu.P...]
    all_to_all x1, waiting for transfers between devices: 5.06 us -> 7.82 us  [local(): state = lax.all_to_all(strips, 'mode', 0, 0, tiled=True)]
    all_to_all x2, waiting for transfers between devices: 41.2 us -> 43.8 us  [local(): lax.all_to_all(sums, both, 0, 0, tiled=True).reshape(devices, share, -1)]
    unnamed x52 -> x54, local copies, waits for them, and re-layouts: 16 us -> 14.7 us
  transfers between devices with their start and end apart: 19 -> 19, of which waited for: 8 -> 8; matrix products, arithmetic and copies ran while one was open for 5% -> 5% of each run, Pallas kernels for 16% -> 15%
where the time goes in v13:
time: 226 us; the launch traced here: 225 us
  waiting for transfers between devices  70.4 us (31%)
  Pallas kernels  49.6 us (22%)
  starting transfers between devices  46.6 us (21%)
  blocking collectives  29.6 us (13%)
  local copies, waits for them, and re-layouts  20.8 us (9%)
  other arithmetic  6.86 us (3%)
    all_to_all x2, waiting for transfers between devices, local(): lax.all_to_all(sums, both, 0, 0, tiled=True).reshape(devices, share, -1)  43.8 us
    all_to_all x1, blocking collectives, local(): state = lax.all_to_all(state, both, 0, 0, tiled=True)  29.6 us
    unnamed x54, local copies, waits for them, and re-layouts  14.7 us
    pallas_call x3, Pallas kernels, per_group(): pl.pallas_call(kernel, grid=(groups,), in_specs=in_specs, out_specs=out_s...  13.5 us
    pallas_call x2, Pallas kernels, coupled_sums(): pl.pallas_call(functools.partial(inner_kernel, height, cols), grid=(block...  12.1 us
    all_to_all x2, starting transfers between devices, local(): lax.all_to_all(sums, both, 0, 0, tiled=True).reshape(devices, share, -1)  11.4 us
    ppermute x9, starting transfers between devices, onwards(): lax.ppermute(part, axis, [(i, (i + shift) % count) for i in range(count)])  11.1 us
    all_to_all x1, waiting for transfers between devices, to_slabs(): return lax.all_to_all(flat, 'slab', 0, 0, tiled=True)  8.83 us
  transfers between devices with their start and end apart: 19, of which 8 were waited for; matrix products, arithmetic and copies ran while one was open for 5% of the time, Pallas kernels for 15%

profile of v13, /device:TPU:0, one launch (start us, length us, event | category | flops | bytes accessed | tf_op | source)
XLA Modules:
  0.0 225.1 jit_solution(1425509163444885962)
XLA Ops:
  0.6 3.3 %shard_map.86 = bf16[8,128,512]{2,1,0:T(8,128)(2,1)} custom-call(f32[4096,128]{1,0:T(8,128)} %bitcast.25), custom_call_target="tpu_custom_call" | custom-call | tf_op jit(solution)/shard_map/pallas_call | solution.py:216
  4.0 7.3 %all-to-all-start = ((bf16[8,128,512]{2,1,0:T(8,128)(2,1)}), bf16[8,128,512]{2,1,0:T(8,128)(2,1)}, u32[]{:S(2)}, u32[]{:S(2)}) async-start(bf16[8,128,512]{2,1,0:T(8,128)(2,1)} %shard_map.86), calls=%async_computation | async-start | bytes 2097152 | tf_op jit(solution)/shard_map/all_to_all | solution.py:733
  19.9 3.0 %constant_dynamic-slice_fusion = (f32[1,32,32,128]{3,2,1,0:T(8,128)}, f32[1,32,32,128]{3,2,1,0:T(8,128)}, f32[1,32,32,128]{3,2,1,0:T(8,128)}, f32[1,32,32,128]{3,2,1,0:T(8,128)}) fusion(f32[4,32,32,128]{3,2,1,0:T(8,128)} %bitcast.27, s32[]{:T(128)S(6)} %select_n.40, s32[]{:T(128)S(6)} %select_n.39, s32[]{:T(128)S(6)} %select_n.38, s32[]{:T(128)S(6)} %select_n.37), kind=kLoop, calls=%fused_computation.39 | loop fusion | bytes 4194320 | tf_op jit(solution)/shard_map/jit(dynamic_index_in_dim)/dynamic_slice | solution.py:711
  23.0 3.0 %shard_map.87.matrix_ref = bf16[8,3,128,1024]{3,2,1,0:T(8,128)(2,1)S(1)} custom-call(s32[8,16]{1,0:T(8,128)S(1)} %copy-done.21, s32[8]{0:T(128)S(1)} %copy-done.22, bf16[8,16,128,128]{3,2,1,0:T(8,128)(2,1)S(1)} %copy-done.4), custom_call_target="tpu_custom_call" | custom-call | tf_op jit(solution)/shard_map/pallas_call | solution.py:243
  26.0 2.6 %copy-done = bf16[8,3,128,1024]{3,2,1,0:T(8,128)(2,1)} copy-done((bf16[8,3,128,1024]{3,2,1,0:T(8,128)(2,1)}, bf16[8,3,128,1024]{3,2,1,0:T(8,128)(2,1)S(1)}, u32[]{:S(2)}) %copy-start) | copy-done | bytes 6291480
  29.3 7.8 %all-to-all-done = bf16[8,128,512]{2,1,0:T(8,128)(2,1)} async-done(((bf16[8,128,512]{2,1,0:T(8,128)(2,1)}), bf16[8,128,512]{2,1,0:T(8,128)(2,1)}, u32[]{:S(2)}, u32[]{:S(2)}) %all-to-all-start) | async-done | bytes 1048608 | tf_op jit(solution)/shard_map/all_to_all | solution.py:733
  38.3 3.7 %collective-permute-done.2.refs_3_ = f32[1,36,32,128]{3,2,1,0:T(8,128)S(1)} collective-permute-done((f32[1,36,32,128]{3,2,1,0:T(8,128)}, f32[1,36,32,128]{3,2,1,0:T(8,128)S(1)}, u32[]{:S(2)}, u32[]{:S(2)}) %collective-permute-start.2) | collective-permute-done | bytes 589856 | tf_op jit(solution)/shard_map/ppermute | solution.py:704
  41.9 2.6 %collective-permute-start.7 = (f32[1,32,32,128]{3,2,1,0:T(8,128)}, f32[1,32,32,128]{3,2,1,0:T(8,128)S(1)}, u32[]{:S(2)}, u32[]{:S(2)}) collective-permute-start(f32[1,32,32,128]{3,2,1,0:T(8,128)} %get-tuple-element.40), channel_id=1, source_target_pairs={{0,1},{1,2},{2,3},{3,0},{4,5},{5,6},{6,7},{7,4},{8,9},{9,10},{10,1... | collective-permute-start | bytes 1572872 | tf_op jit(solution)/shard_map/ppermute | solution.py:704
  47.4 2.1 collective-permute-start.5
  49.5 3.3 %collective-permute-start.6 = (bf16[1024,128]{1,0:T(8,128)(2,1)S(1)}, bf16[1024,128]{1,0:T(8,128)(2,1)S(1)}, u32[]{:S(2)}, u32[]{:S(2)}) collective-permute-start(bf16[1024,128]{1,0:T(8,128)(2,1)S(1)} %get-tuple-element.69), channel_id=1, source_target_pairs={{4,0},{8,4},{12,8},{16,12},{20,16},{24,20},{28,24},{1,28},{5,1},{9... | collective-permute-start | bytes 786440 | tf_op jit(solution)/shard_map/ppermute | solution.py:378
  52.8 2.8 %copy-done.1 = bf16[8,3,128,1024]{3,2,1,0:T(8,128)(2,1)S(1)} copy-done((bf16[8,3,128,1024]{3,2,1,0:T(8,128)(2,1)S(1)}, bf16[8,3,128,1024]{3,2,1,0:T(8,128)(2,1)}, u32[]{:S(2)}) %copy-start.1) | copy-done | bytes 6291480
  55.6 6.7 %shard_map.89.inner_ref = f32[1024,512]{1,0:T(8,128)S(1)} custom-call(bf16[8,3,128,1024]{3,2,1,0:T(8,128)(2,1)S(1)} %copy-done.1, bf16[1024,512]{1,0:T(8,128)(2,1)} %bitcast.7.state_ref, f32[60,128]{1,0:T(8,128)S(1)} %shard_map.88.weight_ref), custom_call_target="tpu_custom_call" | custom-call | flops 3221225472 | bytes 6291456 | tf_op jit(solution)/shard_map/pallas_call | solution.py:385
  62.4 5.1 %shard_map.90 = bf16[1024,640]{1,0:T(8,128)(2,1)} custom-call(bf16[8,3,128,1024]{3,2,1,0:T(8,128)(2,1)S(1)} %copy-done.2, bf16[1024,128]{1,0:T(8,128)(2,1)S(1)} %collective-permute-done.5.above_ref, bf16[1024,128]{1,0:T(8,128)(2,1)S(1)} %collective-permute-done.6.below_ref, f32[60,128]{1,0:T(8,128)S(1)} %shard_map.88.weight_ref, ...), custom_call_target="tpu_custom_call" | custom-call | tf_op jit(solution)/shard_map/pallas_call | solution.py:399
  70.0 8.3 %all-to-all-start.1 = ((bf16[32,32,640]{2,1,0:T(8,128)(2,1)}), bf16[32,32,640]{2,1,0:T(8,128)(2,1)}, u32[]{:S(2)}, u32[]{:S(2)}) async-start(bf16[32,32,640]{2,1,0:T(8,128)(2,1)} %bitcast.11), calls=%async_computation.1 | async-start | bytes 2621440 | tf_op jit(solution)/shard_map/all_to_all | solution.py:786
  83.0 4.2 %shard_map.92 = (f32[4,32,32,128]{3,2,1,0:T(8,128)}, f32[4,32,32,128]{3,2,1,0:T(8,128)}, f32[4,32,32,128]{3,2,1,0:T(8,128)}) custom-call(s32[2]{0:T(128)S(1)} %pad_add_fusion.place_ref, f32[1,36,32,128]{3,2,1,0:T(8,128)S(1)} %get-tuple-element.33.refs_0_, f32[1,36,32,128]{3,2,1,0:T(8,128)S(1)} %copy-done.6, f32[1,36,32,128]{3,2,1,0:T(8,128)S(1)} %copy-done.8, ...), custom_call_target="tpu_custom_call" | custom-call | tf_op jit(solution)/shard_map/pallas_call | solution.py:600
  87.2 23.2 %all-to-all-done.1.coupled_ref = bf16[32,32,640]{2,1,0:T(8,128)(2,1)} async-done(((bf16[32,32,640]{2,1,0:T(8,128)(2,1)}), bf16[32,32,640]{2,1,0:T(8,128)(2,1)}, u32[]{:S(2)}, u32[]{:S(2)}) %all-to-all-start.1) | async-done | bytes 1310752 | tf_op jit(solution)/shard_map/all_to_all | solution.py:786
  110.4 6.3 %shard_map.93 = (f32[4,32,32,128]{3,2,1,0:T(8,128)S(1)}, bf16[32,32,512]{2,1,0:T(8,128)(2,1)S(1)}) custom-call(f32[4,32,32,128]{3,2,1,0:T(8,128)} %get-tuple-element.47.current_ref, f32[4,32,32,128]{3,2,1,0:T(8,128)} %get-tuple-element.48.base_ref, bf16[32,32,640]{2,1,0:T(8,128)(2,1)} %all-to-all-done.1.coupled_ref, ...), custom_call_target="tpu_custom_call" | custom-call | flops 1610612736 | bytes 11665408 | tf_op jit(solution)/shard_map/pallas_call | solution.py:582
  116.8 29.6 %all_to_all.36 = bf16[32,32,512]{2,1,0:T(8,128)(2,1)S(1)} all-to-all(bf16[32,32,512]{2,1,0:T(8,128)(2,1)S(1)} %get-tuple-element.52), channel_id=1, replica_groups=mesh['mode'=8,'slab'=4] {'mode','slab'}, dimensions={0} | all-to-all | bytes 2097152 | tf_op jit(solution)/shard_map/all_to_all | solution.py:792
  148.0 3.9 %collective-permute-start.11 = (bf16[1024,128]{1,0:T(8,128)(2,1)S(1)}, bf16[1024,128]{1,0:T(8,128)(2,1)S(1)}, u32[]{:S(2)}, u32[]{:S(2)}) collective-permute-start(bf16[1024,128]{1,0:T(8,128)(2,1)S(1)} %get-tuple-element.66), channel_id=1, source_target_pairs={{4,0},{8,4},{12,8},{16,12},{20,16},{24,20},{28,24},{1,28},{5,1},{9... | collective-permute-start | bytes 786440 | tf_op jit(solution)/shard_map/ppermute | solution.py:378
  151.8 5.4 %shard_map.95.inner_ref = f32[1024,512]{1,0:T(8,128)S(1)} custom-call(bf16[8,3,128,1024]{3,2,1,0:T(8,128)(2,1)S(1)} %bitcast.21, bf16[1024,512]{1,0:T(8,128)(2,1)S(1)} %bitcast.23, f32[60,128]{1,0:T(8,128)S(1)} %shard_map.88.weight_ref), custom_call_target="tpu_custom_call" | custom-call | flops 3221225472 | bytes 6291456 | tf_op jit(solution)/shard_map/pallas_call | solution.py:385
  158.8 2.2 collective-permute-done.11.below_ref
  161.0 3.0 %shard_map.96 = bf16[1024,512]{1,0:T(8,128)(2,1)} custom-call(bf16[8,3,128,1024]{3,2,1,0:T(8,128)(2,1)S(1)} %bitcast.21, bf16[1024,128]{1,0:T(8,128)(2,1)S(1)} %collective-permute-done.10.above_ref, bf16[1024,128]{1,0:T(8,128)(2,1)S(1)} %collective-permute-done.11.below_ref, f32[60,128]{1,0:T(8,128)S(1)} %shard_map.88.weight_ref, ...), custom_call_target="tpu_custom_call" | custom-call | tf_op jit(solution)/shard_map/pallas_call | solution.py:399
  164.0 3.0 %all-to-all-start.3 = ((bf16[32,32,512]{2,1,0:T(8,128)(2,1)}), bf16[32,32,512]{2,1,0:T(8,128)(2,1)S(1)}, u32[]{:S(2)}, u32[]{:S(2)}) async-start(bf16[32,32,512]{2,1,0:T(8,128)(2,1)} %bitcast.13), calls=%async_computation.3 | async-start | bytes 2097152 | tf_op jit(solution)/shard_map/all_to_all | solution.py:799
  168.6 2.7 %shard_map.94.base_ref = f32[4,32,32,128]{3,2,1,0:T(8,128)S(1)} custom-call(f32[4,32,32,128]{3,2,1,0:T(8,128)S(1)} %copy-done.12, f32[4,32,32,128]{3,2,1,0:T(8,128)} %get-tuple-element.51.right_side_ref, f32[5,128,128]{2,1,0:T(8,128)S(1)} %shard_map.91.refs_8_.weight_ref), custom_call_target="tpu_custom_call" | custom-call | bytes 9043968 | tf_op jit(solution)/shard_map/pallas_call | solution.py:582
  172.6 20.6 %all-to-all-done.3.coupled_ref = bf16[32,32,512]{2,1,0:T(8,128)(2,1)S(1)} async-done(((bf16[32,32,512]{2,1,0:T(8,128)(2,1)}), bf16[32,32,512]{2,1,0:T(8,128)(2,1)S(1)}, u32[]{:S(2)}, u32[]{:S(2)}) %all-to-all-start.3) | async-done | bytes 1048608 | tf_op jit(solution)/shard_map/all_to_all | solution.py:799
  193.2 4.1 %shard_map.97 = (f32[4,32,32,128]{3,2,1,0:T(8,128)S(1)}, bf16[1,32,32,128]{3,2,1,0:T(8,128)(2,1)S(1)}, bf16[1,32,32,128]{3,2,1,0:T(8,128)(2,1)S(1)}, bf16[1,32,3...) custom-call(s32[1]{0:T(128)} %bitcast.here_ref, f32[4,32,32,128]{3,2,1,0:T(8,128)} %copy-done.3, ...), custom_call_target="tpu_custom_call" | custom-call | bytes 4194304 | tf_op jit(solution)/shard_map/pallas_call | solution.py:659
  200.3 4.5 %shard_map.98 = bf16[4,32,32,128]{3,2,1,0:T(8,128)(2,1)} custom-call(f32[4,32,32,128]{3,2,1,0:T(8,128)S(1)} %copy-done.13, f32[4,32,32,128]{3,2,1,0:T(8,128)S(1)} %get-tuple-element.53.resid_ref, bf16[256,256]{1,0:T(8,128)(2,1)S(1)} %get-tuple-element.71.right_ref.refs_9_, bf16[256,256]{1,0:T(8,128)(2,1)S(1)} %get-tuple-element.70.left_ref, ...), custom_call_target="tpu_custom_call" | custom-call | flops 1610612736 | bytes 9043968 | tf_op jit(solution)/shard_map/pallas_call | solution.py:582
  204.8 3.5 %all-to-all-start.4 = ((bf16[128,32,128]{2,1,0:T(8,128)(2,1)}), bf16[128,32,128]{2,1,0:T(8,128)(2,1)S(1)}, u32[]{:S(2)}, u32[]{:S(2)}) async-start(bf16[128,32,128]{2,1,0:T(8,128)(2,1)} %bitcast.14), calls=%async_computation.4 | async-start | bytes 2097152 | tf_op jit(solution)/shard_map/all_to_all | solution.py:738
  208.7 2.5 %collective-permute-done.14 = bf16[1,32,32,128]{3,2,1,0:T(8,128)(2,1)S(1)} collective-permute-done((bf16[1,32,32,128]{3,2,1,0:T(8,128)(2,1)S(1)}, bf16[1,32,32,128]{3,2,1,0:T(8,128)(2,1)S(1)}, u32[]{:S(2)}, u32[]{:S(2)}) %collective-permute-start.14) | collective-permute-done | bytes 262176 | tf_op jit(solution)/shard_map/ppermute | solution.py:704
  212.2 1.8 fusion.11
  214.0 8.8 %all-to-all-done.4 = bf16[128,32,128]{2,1,0:T(8,128)(2,1)S(1)} async-done(((bf16[128,32,128]{2,1,0:T(8,128)(2,1)}), bf16[128,32,128]{2,1,0:T(8,128)(2,1)S(1)}, u32[]{:S(2)}, u32[]{:S(2)}) %all-to-all-start.4) | async-done | bytes 1048608 | tf_op jit(solution)/shard_map/all_to_all | solution.py:738
  222.9 2.2 fusion.10
  (97 shorter events, 30.7 us)
Async XLA Ops:
  0.6 3.3 %copy-start.24 = (f32[32,128]{1,0:T(8,128)S(1)}, f32[32,128]{1,0:T(8,128)}, u32[]{:S(2)}) copy-start(f32[32,128]{1,0:T(8,128)} %param.9) | copy-start | bytes 49156
  0.6 3.3 %copy-start.23 = (f32[3,32,128]{2,1,0:T(8,128)S(1)}, f32[3,32,128]{2,1,0:T(8,128)}, u32[]{:S(2)}) copy-start(f32[3,32,128]{2,1,0:T(8,128)} %param.10) | copy-start | bytes 147460
  4.0 33.2 %all-to-all-start = ((bf16[8,128,512]{2,1,0:T(8,128)(2,1)}), bf16[8,128,512]{2,1,0:T(8,128)(2,1)}, u32[]{:S(2)}, u32[]{:S(2)}) async-start(bf16[8,128,512]{2,1,0:T(8,128)(2,1)} %shard_map.86), calls=%async_computation | async-start | bytes 2097152 | tf_op jit(solution)/shard_map/all_to_all | solution.py:733
  14.3 23.9 %collective-permute-start = (f32[1,36,32,128]{3,2,1,0:T(8,128)}, f32[1,36,32,128]{3,2,1,0:T(8,128)S(1)}, u32[]{:S(2)}, u32[]{:S(2)}) collective-permute-start(f32[1,36,32,128]{3,2,1,0:T(8,128)} %get-tuple-element.75), channel_id=1, source_target_pairs={{0,1},{1,2},{2,3},{3,0},{4,5},{5,6},{6,7},{7,4},{8,9},{9,10},{10,1... | collective-permute-start | bytes 1769480 | tf_op jit(solution)/shard_map/ppermute | solution.py:704
  14.3 23.9 %collective-permute-start.1 = (f32[1,36,32,128]{3,2,1,0:T(8,128)}, f32[1,36,32,128]{3,2,1,0:T(8,128)S(1)}, u32[]{:S(2)}, u32[]{:S(2)}) collective-permute-start(f32[1,36,32,128]{3,2,1,0:T(8,128)} %get-tuple-element.76), channel_id=1, source_target_pairs={{0,2},{1,3},{2,0},{3,1},{4,6},{5,7},{6,4},{7,5},{8,10},{9,11},{10,... | collective-permute-start | bytes 1769480 | tf_op jit(solution)/shard_map/ppermute | solution.py:704
  15.8 26.1 %collective-permute-start.2 = (f32[1,36,32,128]{3,2,1,0:T(8,128)}, f32[1,36,32,128]{3,2,1,0:T(8,128)S(1)}, u32[]{:S(2)}, u32[]{:S(2)}) collective-permute-start(f32[1,36,32,128]{3,2,1,0:T(8,128)} %get-tuple-element.74), channel_id=1, source_target_pairs={{0,3},{1,0},{2,1},{3,2},{4,7},{5,4},{6,5},{7,6},{8,11},{9,8},{10,9... | collective-permute-start | bytes 1769480 | tf_op jit(solution)/shard_map/ppermute | solution.py:704
  17.3 11.4 %collective-permute-start.3 = (f32[4,128]{1,0:T(4,128)S(1)}, f32[4,128]{1,0:T(4,128)S(1)}, u32[]{:S(2)}, u32[]{:S(2)}) collective-permute-start(f32[4,128]{1,0:T(4,128)S(1)} %bitcast.30), channel_id=1, source_target_pairs={{0,1},{1,2},{2,3},{4,5},{5,6},{6,7},{8,9},{9,10},{10,11},{12,13},{... | collective-permute-start | bytes 6152 | tf_op jit(solution)/shard_map/ppermute | solution.py:745
  18.5 10.1 %collective-permute-start.4 = (f32[4,128]{1,0:T(4,128)S(1)}, f32[4,128]{1,0:T(4,128)S(1)}, u32[]{:S(2)}, u32[]{:S(2)}) collective-permute-start(f32[4,128]{1,0:T(4,128)S(1)} %bitcast.29), channel_id=1, source_target_pairs={{1,0},{2,1},{3,2},{5,4},{6,5},{7,6},{9,8},{10,9},{11,10},{13,12},{... | collective-permute-start | bytes 6152 | tf_op jit(solution)/shard_map/ppermute | solution.py:746
  19.9 3.2 %copy-start.4 = (bf16[8,16,128,128]{3,2,1,0:T(8,128)(2,1)S(1)}, bf16[8,16,128,128]{3,2,1,0:T(8,128)(2,1)}, u32[]{:S(2)}) copy-start(bf16[8,16,128,128]{3,2,1,0:T(8,128)(2,1)} %coupling_ref.1) | copy-start | bytes 12582916
  19.9 3.1 %copy-start.21 = (s32[8,16]{1,0:T(8,128)S(1)}, s32[8,16]{1,0:T(8,128)}, u32[]{:S(2)}) copy-start(s32[8,16]{1,0:T(8,128)} %entry_ref.1) | copy-start | bytes 1540
  19.9 3.1 %copy-start.22 = (s32[8]{0:T(128)S(1)}, s32[8]{0:T(128)}, u32[]{:S(2)}) copy-start(s32[8]{0:T(128)} %count_ref.1) | copy-start | bytes 100
  38.2 40.3 %copy-start.5 = (f32[1,36,32,128]{3,2,1,0:T(8,128)}, f32[1,36,32,128]{3,2,1,0:T(8,128)S(1)}, u32[]{:S(2)}) copy-start(f32[1,36,32,128]{3,2,1,0:T(8,128)S(1)} %collective-permute-done.refs_1_) | copy-start | bytes 1769476
  38.2 40.3 %copy-start.7 = (f32[1,36,32,128]{3,2,1,0:T(8,128)}, f32[1,36,32,128]{3,2,1,0:T(8,128)S(1)}, u32[]{:S(2)}) copy-start(f32[1,36,32,128]{3,2,1,0:T(8,128)S(1)} %collective-permute-done.1.refs_2_) | copy-start | bytes 1769476
  41.9 36.6 %copy-start.9 = (f32[1,36,32,128]{3,2,1,0:T(8,128)}, f32[1,36,32,128]{3,2,1,0:T(8,128)S(1)}, u32[]{:S(2)}) copy-start(f32[1,36,32,128]{3,2,1,0:T(8,128)S(1)} %collective-permute-done.2.refs_3_) | copy-start | bytes 1769476
  41.9 25.6 %collective-permute-start.7 = (f32[1,32,32,128]{3,2,1,0:T(8,128)}, f32[1,32,32,128]{3,2,1,0:T(8,128)S(1)}, u32[]{:S(2)}, u32[]{:S(2)}) collective-permute-start(f32[1,32,32,128]{3,2,1,0:T(8,128)} %get-tuple-element.40), channel_id=1, source_target_pairs={{0,1},{1,2},{2,3},{3,0},{4,5},{5,6},{6,7},{7,4},{8,9},{9,10},{10,1... | collective-permute-start | bytes 1572872 | tf_op jit(solution)/shard_map/ppermute | solution.py:704
  44.5 23.8 %collective-permute-start.8 = (f32[1,32,32,128]{3,2,1,0:T(8,128)}, f32[1,32,32,128]{3,2,1,0:T(8,128)S(1)}, u32[]{:S(2)}, u32[]{:S(2)}) collective-permute-start(f32[1,32,32,128]{3,2,1,0:T(8,128)} %get-tuple-element.41), channel_id=1, source_target_pairs={{0,2},{1,3},{2,0},{3,1},{4,6},{5,7},{6,4},{7,5},{8,10},{9,11},{10,... | collective-permute-start | bytes 1572872 | tf_op jit(solution)/shard_map/ppermute | solution.py:704
  45.7 23.4 %collective-permute-start.9 = (f32[1,32,32,128]{3,2,1,0:T(8,128)}, f32[1,32,32,128]{3,2,1,0:T(8,128)S(1)}, u32[]{:S(2)}, u32[]{:S(2)}) collective-permute-start(f32[1,32,32,128]{3,2,1,0:T(8,128)} %get-tuple-element.42), channel_id=1, source_target_pairs={{0,3},{1,0},{2,1},{3,2},{4,7},{5,4},{6,5},{7,6},{8,11},{9,8},{10,9... | collective-permute-start | bytes 1572872 | tf_op jit(solution)/shard_map/ppermute | solution.py:704
  47.4 14.9 %collective-permute-start.5 = (bf16[1024,128]{1,0:T(8,128)(2,1)S(1)}, bf16[1024,128]{1,0:T(8,128)(2,1)S(1)}, u32[]{:S(2)}, u32[]{:S(2)}) collective-permute-start(bf16[1024,128]{1,0:T(8,128)(2,1)S(1)} %get-tuple-element.68), channel_id=1, source_target_pairs={{0,4},{4,8},{8,12},{12,16},{16,20},{20,24},{24,28},{28,1},{1,5},{5... | collective-permute-start | bytes 786440 | tf_op jit(solution)/shard_map/ppermute | solution.py:377
  49.5 12.9 %collective-permute-start.6 = (bf16[1024,128]{1,0:T(8,128)(2,1)S(1)}, bf16[1024,128]{1,0:T(8,128)(2,1)S(1)}, u32[]{:S(2)}, u32[]{:S(2)}) collective-permute-start(bf16[1024,128]{1,0:T(8,128)(2,1)S(1)} %get-tuple-element.69), channel_id=1, source_target_pairs={{4,0},{8,4},{12,8},{16,12},{20,16},{24,20},{28,24},{1,28},{5,1},{9... | collective-permute-start | bytes 786440 | tf_op jit(solution)/shard_map/ppermute | solution.py:378
  55.6 6.8 %copy-start.2 = (bf16[8,3,128,1024]{3,2,1,0:T(8,128)(2,1)S(1)}, bf16[8,3,128,1024]{3,2,1,0:T(8,128)(2,1)}, u32[]{:S(2)}) copy-start(bf16[8,3,128,1024]{3,2,1,0:T(8,128)(2,1)} %copy-done) | copy-start | bytes 18874372
  70.0 40.5 %all-to-all-start.1 = ((bf16[32,32,640]{2,1,0:T(8,128)(2,1)}), bf16[32,32,640]{2,1,0:T(8,128)(2,1)}, u32[]{:S(2)}, u32[]{:S(2)}) async-start(bf16[32,32,640]{2,1,0:T(8,128)(2,1)} %bitcast.11), calls=%async_computation.1 | async-start | bytes 2621440 | tf_op jit(solution)/shard_map/all_to_all | solution.py:786
  83.0 68.8 %slice-start = ((s8[6291456]{0:T(1024)(128)(4,1)}), s8[2097152]{0:T(1024)(128)(4,1)S(1)}, s32[]{:S(2)}) async-start(s8[6291456]{0:T(1024)(128)(4,1)} %bitcast.20), calls=%async_computation.5 | async-start | bytes 4194304
  110.4 41.4 %slice-start.1 = ((s8[6291456]{0:T(1024)(128)(4,1)}), s8[4194304]{0:T(1024)(128)(4,1)S(1)}, s32[]{:S(2)}) async-start(s8[6291456]{0:T(1024)(128)(4,1)} %bitcast.20), calls=%async_computation.6 | async-start | bytes 8388608
  116.8 40.5 %copy-start.11 = (f32[4,32,32,128]{3,2,1,0:T(8,128)}, f32[4,32,32,128]{3,2,1,0:T(8,128)S(1)}, u32[]{:S(2)}) copy-start(f32[4,32,32,128]{3,2,1,0:T(8,128)S(1)} %get-tuple-element.50.current_ref) | copy-start | bytes 6291460
  146.4 12.3 %collective-permute-start.10 = (bf16[1024,128]{1,0:T(8,128)(2,1)S(1)}, bf16[1024,128]{1,0:T(8,128)(2,1)S(1)}, u32[]{:S(2)}, u32[]{:S(2)}) collective-permute-start(bf16[1024,128]{1,0:T(8,128)(2,1)S(1)} %get-tuple-element.67), channel_id=1, source_target_pairs={{0,4},{4,8},{8,12},{12,16},{16,20},{20,24},{24,28},{28,1},{1,5},{5... | collective-permute-start | bytes 786440 | tf_op jit(solution)/shard_map/ppermute | solution.py:377
  148.0 13.0 %collective-permute-start.11 = (bf16[1024,128]{1,0:T(8,128)(2,1)S(1)}, bf16[1024,128]{1,0:T(8,128)(2,1)S(1)}, u32[]{:S(2)}, u32[]{:S(2)}) collective-permute-start(bf16[1024,128]{1,0:T(8,128)(2,1)S(1)} %get-tuple-element.66), channel_id=1, source_target_pairs={{4,0},{8,4},{12,8},{16,12},{20,16},{24,20},{28,24},{1,28},{5,1},{9... | collective-permute-start | bytes 786440 | tf_op jit(solution)/shard_map/ppermute | solution.py:378
  164.0 29.3 %all-to-all-start.3 = ((bf16[32,32,512]{2,1,0:T(8,128)(2,1)}), bf16[32,32,512]{2,1,0:T(8,128)(2,1)S(1)}, u32[]{:S(2)}, u32[]{:S(2)}) async-start(bf16[32,32,512]{2,1,0:T(8,128)(2,1)} %bitcast.13), calls=%async_computation.3 | async-start | bytes 2097152 | tf_op jit(solution)/shard_map/all_to_all | solution.py:799
  193.2 7.1 %copy-start.13 = (f32[4,32,32,128]{3,2,1,0:T(8,128)S(1)}, f32[4,32,32,128]{3,2,1,0:T(8,128)}, u32[]{:S(2)}) copy-start(f32[4,32,32,128]{3,2,1,0:T(8,128)} %copy-done.11) | copy-start | bytes 6291460
  197.4 11.2 %collective-permute-start.12 = (bf16[1,32,32,128]{3,2,1,0:T(8,128)(2,1)S(1)}, bf16[1,32,32,128]{3,2,1,0:T(8,128)(2,1)S(1)}, u32[]{:S(2)}, u32[]{:S(2)}) collective-permute-start(bf16[1,32,32,128]{3,2,1,0:T(8,128)(2,1)S(1)} %get-tuple-element.55), channel_id=1, source_target_pairs={{0,1},{1,2},{2,3},{3,0},{4,5},{5,6},{6,7},{7,4},{8,9},{9,10},{10,1... | collective-permute-start | bytes 786440 | tf_op jit(solution)/shard_map/ppermute | solution.py:704
  197.4 11.2 %collective-permute-start.13 = (bf16[1,32,32,128]{3,2,1,0:T(8,128)(2,1)S(1)}, bf16[1,32,32,128]{3,2,1,0:T(8,128)(2,1)S(1)}, u32[]{:S(2)}, u32[]{:S(2)}) collective-permute-start(bf16[1,32,32,128]{3,2,1,0:T(8,128)(2,1)S(1)} %get-tuple-element.56), channel_id=1, source_target_pairs={{0,2},{1,3},{2,0},{3,1},{4,6},{5,7},{6,4},{7,5},{8,10},{9,11},{10,... | collective-permute-start | bytes 786440 | tf_op jit(solution)/shard_map/ppermute | solution.py:704
  199.0 12.3 %collective-permute-start.14 = (bf16[1,32,32,128]{3,2,1,0:T(8,128)(2,1)S(1)}, bf16[1,32,32,128]{3,2,1,0:T(8,128)(2,1)S(1)}, u32[]{:S(2)}, u32[]{:S(2)}) collective-permute-start(bf16[1,32,32,128]{3,2,1,0:T(8,128)(2,1)S(1)} %get-tuple-element.57), channel_id=1, source_target_pairs={{0,3},{1,0},{2,1},{3,2},{4,7},{5,4},{6,5},{7,6},{8,11},{9,8},{10,9... | collective-permute-start | bytes 786440 | tf_op jit(solution)/shard_map/ppermute | solution.py:704
  204.8 18.0 %all-to-all-start.4 = ((bf16[128,32,128]{2,1,0:T(8,128)(2,1)}), bf16[128,32,128]{2,1,0:T(8,128)(2,1)S(1)}, u32[]{:S(2)}, u32[]{:S(2)}) async-start(bf16[128,32,128]{2,1,0:T(8,128)(2,1)} %bitcast.14), calls=%async_computation.4 | async-start | bytes 2097152 | tf_op jit(solution)/shard_map/all_to_all | solution.py:738
  (14 other events, 19.1 us)

commit v14 on v10

--- a/solution.py
+++ b/solution.py
@@ -679,7 +679,6 @@
         slabs,
         (),
         solve_flops(resid, tables),
-        VMEM_BYTES,
     )
 
 

time: 224 us -> 224 us (level)
  waiting for transfers between devices: 74.1 us -> 71.5 us
    dynamic_update_slice x4, local copies, waits for them, and re-layouts: 0.16 us -> 3.01 us  [collect(): out = lax.dynamic_update_slice_in_dim(out, part, source, 0)]
    all_to_all x1, waiting for transfers between devices: 10.6 us -> 7.83 us  [to_slabs(): return lax.all_to_all(flat, 'slab', 0, 0, tiled=True)]
    unnamed x60 -> x62, local copies, waits for them, and re-layouts: 15.9 us -> 15.3 us
  transfers between devices with their start and end apart: 17 -> 17, of which waited for: 9 -> 9; matrix products, arithmetic and copies ran while one was open for 4% -> 5% of each run, Pallas kernels for 16% -> 16%
where the time goes in v14:
time: 224 us; the launch traced here: 223 us
  waiting for transfers between devices  71.5 us (32%)
  Pallas kernels  52.5 us (23%)
  starting transfers between devices  39.5 us (18%)
  blocking collectives  29.6 us (13%)
  local copies, waits for them, and re-layouts  21.1 us (9%)
  other arithmetic  7.52 us (3%)
    all_to_all x2, waiting for transfers between devices, local(): lax.all_to_all(sums, both, 0, 0, tiled=True).reshape(devices, share, -1)  44.8 us
    all_to_all x1, blocking collectives, local(): state = lax.all_to_all(state, both, 0, 0, tiled=True)  29.6 us
    unnamed x62, local copies, waits for them, and re-layouts  15.3 us
    ppermute x9, waiting for transfers between devices, onwards(): lax.ppermute(part, axis, [(i, (i + shift) % count) for i in range(count)])  15.1 us
    pallas_call x3, Pallas kernels, per_group(): pl.pallas_call(kernel, grid=(groups,), in_specs=in_specs, out_specs=out_s...  13.5 us
    pallas_call x2, Pallas kernels, coupled_sums(): pl.pallas_call(functools.partial(inner_kernel, height, cols), grid=(block...  12.1 us
    all_to_all x2, starting transfers between devices, local(): lax.all_to_all(sums, both, 0, 0, tiled=True).reshape(devices, share, -1)  9.56 us
    ppermute x9, starting transfers between devices, onwards(): lax.ppermute(part, axis, [(i, (i + shift) % count) for i in range(count)])  8.19 us
  transfers between devices with their start and end apart: 17, of which 9 were waited for; matrix products, arithmetic and copies ran while one was open for 5% of the time, Pallas kernels for 16%

profile of v14, /device:TPU:0, one launch (start us, length us, event | category | flops | bytes accessed | tf_op | source)
XLA Modules:
  0.0 222.8 jit_solution(757016922271859087)
XLA Ops:
  0.7 3.5 %shard_map.86 = bf16[8,128,512]{2,1,0:T(8,128)(2,1)} custom-call(f32[4096,128]{1,0:T(8,128)} %bitcast.24), custom_call_target="tpu_custom_call" | custom-call | tf_op jit(solution)/shard_map/pallas_call | solution.py:209
  4.1 7.3 %all-to-all-start = ((bf16[8,128,512]{2,1,0:T(8,128)(2,1)}), bf16[8,128,512]{2,1,0:T(8,128)(2,1)}, u32[]{:S(2)}, u32[]{:S(2)}) async-start(bf16[8,128,512]{2,1,0:T(8,128)(2,1)} %shard_map.86), calls=%async_computation | async-start | bytes 2097152 | tf_op jit(solution)/shard_map/all_to_all | solution.py:725
  15.9 2.2 copy-done.4
  18.1 3.1 %shard_map.87.matrix_ref = bf16[8,3,128,1024]{3,2,1,0:T(8,128)(2,1)S(1)} custom-call(s32[8,16]{1,0:T(8,128)S(1)} %copy-done.21, s32[8]{0:T(128)S(1)} %copy-done.22, bf16[8,16,128,128]{3,2,1,0:T(8,128)(2,1)S(1)} %copy-done.4), custom_call_target="tpu_custom_call" | custom-call | tf_op jit(solution)/shard_map/pallas_call | solution.py:236
  21.2 2.6 %copy-done = bf16[8,3,128,1024]{3,2,1,0:T(8,128)(2,1)} copy-done((bf16[8,3,128,1024]{3,2,1,0:T(8,128)(2,1)}, bf16[8,3,128,1024]{3,2,1,0:T(8,128)(2,1)S(1)}, u32[]{:S(2)}) %copy-start) | copy-done | bytes 6291480
  26.3 2.0 collective-permute-done.refs_1_
  29.5 11.1 %collective-permute-done.2.refs_3_ = f32[1,36,32,128]{3,2,1,0:T(8,128)} collective-permute-done((f32[1,36,32,128]{3,2,1,0:T(8,128)}, f32[1,36,32,128]{3,2,1,0:T(8,128)}, u32[]{:S(2)}, u32[]{:S(2)}) %collective-permute-start.2) | collective-permute-done | bytes 589856 | tf_op jit(solution)/shard_map/ppermute | solution.py:697
  44.0 2.1 collective-permute-start.3
  46.0 3.3 %collective-permute-start.4 = (bf16[1024,128]{1,0:T(8,128)(2,1)S(1)}, bf16[1024,128]{1,0:T(8,128)(2,1)S(1)}, u32[]{:S(2)}, u32[]{:S(2)}) collective-permute-start(bf16[1024,128]{1,0:T(8,128)(2,1)S(1)} %get-tuple-element.60), channel_id=1, source_target_pairs={{4,0},{8,4},{12,8},{16,12},{20,16},{24,20},{28,24},{1,28},{5,1},{9... | collective-permute-start | bytes 786440 | tf_op jit(solution)/shard_map/ppermute | solution.py:371
  50.9 2.8 %copy-done.1 = bf16[8,3,128,1024]{3,2,1,0:T(8,128)(2,1)S(1)} copy-done((bf16[8,3,128,1024]{3,2,1,0:T(8,128)(2,1)S(1)}, bf16[8,3,128,1024]{3,2,1,0:T(8,128)(2,1)}, u32[]{:S(2)}) %copy-start.1) | copy-done | bytes 6291480
  53.7 6.7 %shard_map.89.inner_ref = f32[1024,512]{1,0:T(8,128)S(1)} custom-call(bf16[8,3,128,1024]{3,2,1,0:T(8,128)(2,1)S(1)} %copy-done.1, bf16[1024,512]{1,0:T(8,128)(2,1)} %bitcast.3.state_ref, f32[60,128]{1,0:T(8,128)S(1)} %shard_map.88.weight_ref), custom_call_target="tpu_custom_call" | custom-call | flops 3221225472 | bytes 6291456 | tf_op jit(solution)/shard_map/pallas_call | solution.py:378
  60.5 4.2 %shard_map.90 = bf16[1024,640]{1,0:T(8,128)(2,1)S(1)} custom-call(bf16[8,3,128,1024]{3,2,1,0:T(8,128)(2,1)S(1)} %bitcast.18, bf16[1024,128]{1,0:T(8,128)(2,1)S(1)} %collective-permute-done.3.above_ref, bf16[1024,128]{1,0:T(8,128)(2,1)S(1)} %collective-permute-done.4.below_ref, f32[60,128]{1,0:T(8,128)S(1)} %shard_map.88.weight_ref, ...), custom_call_target="tpu_custom_call" | custom-call | tf_op jit(solution)/shard_map/pallas_call | solution.py:392
  67.2 6.5 %all-to-all-start.1 = ((bf16[32,32,640]{2,1,0:T(8,128)(2,1)}), bf16[32,32,640]{2,1,0:T(8,128)(2,1)}, u32[]{:S(2)}, u32[]{:S(2)}) async-start(bf16[32,32,640]{2,1,0:T(8,128)(2,1)} %bitcast.21), calls=%async_computation.1 | async-start | bytes 2621440 | tf_op jit(solution)/shard_map/all_to_all | solution.py:769
  75.5 5.4 %shard_map.92 = (f32[4,32,32,128]{3,2,1,0:T(8,128)}, f32[4,32,32,128]{3,2,1,0:T(8,128)}, f32[4,32,32,128]{3,2,1,0:T(8,128)}) custom-call(s32[2]{0:T(128)S(1)} %pad_add_fusion.place_ref, f32[1,36,32,128]{3,2,1,0:T(8,128)S(1)} %get-tuple-element.26.refs_0_, f32[1,36,32,128]{3,2,1,0:T(8,128)S(1)} %collective-permute-done.refs_1_, ...), custom_call_target="tpu_custom_call" | custom-call | tf_op jit(solution)/shard_map/pallas_call | solution.py:593
  81.6 24.2 %all-to-all-done.1.coupled_ref = bf16[32,32,640]{2,1,0:T(8,128)(2,1)} async-done(((bf16[32,32,640]{2,1,0:T(8,128)(2,1)}), bf16[32,32,640]{2,1,0:T(8,128)(2,1)}, u32[]{:S(2)}, u32[]{:S(2)}) %all-to-all-start.1) | async-done | bytes 1310752 | tf_op jit(solution)/shard_map/all_to_all | solution.py:769
  106.8 6.3 %shard_map.93 = (f32[4,32,32,128]{3,2,1,0:T(8,128)S(1)}, bf16[32,32,512]{2,1,0:T(8,128)(2,1)S(1)}) custom-call(f32[4,32,32,128]{3,2,1,0:T(8,128)} %get-tuple-element.39.current_ref, f32[4,32,32,128]{3,2,1,0:T(8,128)} %get-tuple-element.40.base_ref, bf16[32,32,640]{2,1,0:T(8,128)(2,1)} %all-to-all-done.1.coupled_ref, ...), custom_call_target="tpu_custom_call" | custom-call | flops 1610612736 | bytes 11665408 | tf_op jit(solution)/shard_map/pallas_call | solution.py:575
  113.1 29.6 %all_to_all.36 = bf16[32,32,512]{2,1,0:T(8,128)(2,1)S(1)} all-to-all(bf16[32,32,512]{2,1,0:T(8,128)(2,1)S(1)} %get-tuple-element.44), channel_id=1, replica_groups=mesh['mode'=8,'slab'=4] {'mode','slab'}, dimensions={0} | all-to-all | bytes 2097152 | tf_op jit(solution)/shard_map/all_to_all | solution.py:775
  144.3 3.9 %collective-permute-start.9 = (bf16[1024,128]{1,0:T(8,128)(2,1)S(1)}, bf16[1024,128]{1,0:T(8,128)(2,1)S(1)}, u32[]{:S(2)}, u32[]{:S(2)}) collective-permute-start(bf16[1024,128]{1,0:T(8,128)(2,1)S(1)} %get-tuple-element.58), channel_id=1, source_target_pairs={{4,0},{8,4},{12,8},{16,12},{20,16},{24,20},{28,24},{1,28},{5,1},{9... | collective-permute-start | bytes 786440 | tf_op jit(solution)/shard_map/ppermute | solution.py:371
  148.2 5.4 %shard_map.95.inner_ref = f32[1024,512]{1,0:T(8,128)S(1)} custom-call(bf16[8,3,128,1024]{3,2,1,0:T(8,128)(2,1)S(1)} %bitcast.20, bf16[1024,512]{1,0:T(8,128)(2,1)S(1)} %bitcast.23, f32[60,128]{1,0:T(8,128)S(1)} %shard_map.88.weight_ref), custom_call_target="tpu_custom_call" | custom-call | flops 3221225472 | bytes 6291456 | tf_op jit(solution)/shard_map/pallas_call | solution.py:378
  153.6 1.5 collective-permute-done.8.above_ref
  155.1 2.2 collective-permute-done.9.below_ref
  157.3 3.0 %shard_map.96 = bf16[1024,512]{1,0:T(8,128)(2,1)} custom-call(bf16[8,3,128,1024]{3,2,1,0:T(8,128)(2,1)S(1)} %bitcast.20, bf16[1024,128]{1,0:T(8,128)(2,1)S(1)} %collective-permute-done.8.above_ref, bf16[1024,128]{1,0:T(8,128)(2,1)S(1)} %collective-permute-done.9.below_ref, f32[60,128]{1,0:T(8,128)S(1)} %shard_map.88.weight_ref, ...), custom_call_target="tpu_custom_call" | custom-call | tf_op jit(solution)/shard_map/pallas_call | solution.py:392
  160.3 3.0 %all-to-all-start.3 = ((bf16[32,32,512]{2,1,0:T(8,128)(2,1)}), bf16[32,32,512]{2,1,0:T(8,128)(2,1)S(1)}, u32[]{:S(2)}, u32[]{:S(2)}) async-start(bf16[32,32,512]{2,1,0:T(8,128)(2,1)} %bitcast.10), calls=%async_computation.3 | async-start | bytes 2097152 | tf_op jit(solution)/shard_map/all_to_all | solution.py:779
  163.3 1.6 copy-done.8
  164.9 2.7 %shard_map.94.base_ref = f32[4,32,32,128]{3,2,1,0:T(8,128)S(1)} custom-call(f32[4,32,32,128]{3,2,1,0:T(8,128)S(1)} %copy-done.8, f32[4,32,32,128]{3,2,1,0:T(8,128)} %get-tuple-element.43.right_side_ref, f32[5,128,128]{2,1,0:T(8,128)S(1)} %copy-done.6), custom_call_target="tpu_custom_call" | custom-call | bytes 9043968 | tf_op jit(solution)/shard_map/pallas_call | solution.py:575
  169.0 20.6 %all-to-all-done.3.coupled_ref = bf16[32,32,512]{2,1,0:T(8,128)(2,1)S(1)} async-done(((bf16[32,32,512]{2,1,0:T(8,128)(2,1)}), bf16[32,32,512]{2,1,0:T(8,128)(2,1)S(1)}, u32[]{:S(2)}, u32[]{:S(2)}) %all-to-all-start.3) | async-done | bytes 1048608 | tf_op jit(solution)/shard_map/all_to_all | solution.py:779
  189.6 4.7 %shard_map.97 = (f32[4,32,32,128]{3,2,1,0:T(8,128)S(1)}, bf16[1,32,32,128]{3,2,1,0:T(8,128)(2,1)S(1)}, bf16[1,32,32,128]{3,2,1,0:T(8,128)(2,1)}, bf16[1,32,32,12...) custom-call(s32[1]{0:T(128)} %bitcast.here_ref, f32[4,32,32,128]{3,2,1,0:T(8,128)} %copy-done.2, ...), custom_call_target="tpu_custom_call" | custom-call | bytes 4194304 | tf_op jit(solution)/shard_map/pallas_call | solution.py:652
  197.9 4.5 %shard_map.98 = bf16[4,32,32,128]{3,2,1,0:T(8,128)(2,1)} custom-call(f32[4,32,32,128]{3,2,1,0:T(8,128)S(1)} %copy-done.9, f32[4,32,32,128]{3,2,1,0:T(8,128)S(1)} %get-tuple-element.45.resid_ref, bf16[256,256]{1,0:T(8,128)(2,1)S(1)} %get-tuple-element.63.right_ref.refs_9_, bf16[256,256]{1,0:T(8,128)(2,1)S(1)} %copy-done.20, ...), custom_call_target="tpu_custom_call" | custom-call | flops 1610612736 | bytes 9043968 | tf_op jit(solution)/shard_map/pallas_call | solution.py:575
  202.4 3.6 %all-to-all-start.4 = ((bf16[128,32,128]{2,1,0:T(8,128)(2,1)}), bf16[128,32,128]{2,1,0:T(8,128)(2,1)S(1)}, u32[]{:S(2)}, u32[]{:S(2)}) async-start(bf16[128,32,128]{2,1,0:T(8,128)(2,1)} %bitcast.11), calls=%async_computation.4 | async-start | bytes 2097152 | tf_op jit(solution)/shard_map/all_to_all | solution.py:730
  211.0 1.8 fusion.11
  212.8 7.8 %all-to-all-done.4 = bf16[128,32,128]{2,1,0:T(8,128)(2,1)S(1)} async-done(((bf16[128,32,128]{2,1,0:T(8,128)(2,1)}), bf16[128,32,128]{2,1,0:T(8,128)(2,1)S(1)}, u32[]{:S(2)}, u32[]{:S(2)}) %all-to-all-start.4) | async-done | bytes 1048608 | tf_op jit(solution)/shard_map/all_to_all | solution.py:730
  220.6 2.2 fusion.10
  (101 shorter events, 30.2 us)
Async XLA Ops:
  0.6 10.8 %copy-start.25 = (f32[3,32,128]{2,1,0:T(8,128)S(1)}, f32[3,32,128]{2,1,0:T(8,128)}, u32[]{:S(2)}) copy-start(f32[3,32,128]{2,1,0:T(8,128)} %param.10) | copy-start | bytes 147460
  0.6 10.8 %copy-start.26 = (f32[32,128]{1,0:T(8,128)S(1)}, f32[32,128]{1,0:T(8,128)}, u32[]{:S(2)}) copy-start(f32[32,128]{1,0:T(8,128)} %param.9) | copy-start | bytes 49156
  0.6 10.8 %copy-start.23 = (f32[128,32,128]{2,1,0:T(8,128)S(1)}, f32[128,32,128]{2,1,0:T(8,128)}, u32[]{:S(2)}) copy-start(f32[128,32,128]{2,1,0:T(8,128)} %param.7) | copy-start | bytes 6291460
  4.1 36.5 %all-to-all-start = ((bf16[8,128,512]{2,1,0:T(8,128)(2,1)}), bf16[8,128,512]{2,1,0:T(8,128)(2,1)}, u32[]{:S(2)}, u32[]{:S(2)}) async-start(bf16[8,128,512]{2,1,0:T(8,128)(2,1)} %shard_map.86), calls=%async_computation | async-start | bytes 2097152 | tf_op jit(solution)/shard_map/all_to_all | solution.py:725
  11.6 4.3 %copy-start.21 = (s32[8,16]{1,0:T(8,128)S(1)}, s32[8,16]{1,0:T(8,128)}, u32[]{:S(2)}) copy-start(s32[8,16]{1,0:T(8,128)} %entry_ref.1) | copy-start | bytes 1540
  11.6 4.3 %copy-start.22 = (s32[8]{0:T(128)S(1)}, s32[8]{0:T(128)}, u32[]{:S(2)}) copy-start(s32[8]{0:T(128)} %count_ref.1) | copy-start | bytes 100
  13.0 15.3 %collective-permute-start = (f32[1,36,32,128]{3,2,1,0:T(8,128)}, f32[1,36,32,128]{3,2,1,0:T(8,128)S(1)}, u32[]{:S(2)}, u32[]{:S(2)}) collective-permute-start(f32[1,36,32,128]{3,2,1,0:T(8,128)} %get-tuple-element.65), channel_id=1, source_target_pairs={{0,1},{1,2},{2,3},{3,0},{4,5},{5,6},{6,7},{7,4},{8,9},{9,10},{10,1... | collective-permute-start | bytes 1769480 | tf_op jit(solution)/shard_map/ppermute | solution.py:697
  13.0 16.5 %collective-permute-start.1 = (f32[1,36,32,128]{3,2,1,0:T(8,128)}, f32[1,36,32,128]{3,2,1,0:T(8,128)}, u32[]{:S(2)}, u32[]{:S(2)}) collective-permute-start(f32[1,36,32,128]{3,2,1,0:T(8,128)} %get-tuple-element.66), channel_id=1, source_target_pairs={{0,2},{1,3},{2,0},{3,1},{4,6},{5,7},{6,4},{7,5},{8,10},{9,11},{10,... | collective-permute-start | bytes 1769480 | tf_op jit(solution)/shard_map/ppermute | solution.py:697
  14.5 26.1 %collective-permute-start.2 = (f32[1,36,32,128]{3,2,1,0:T(8,128)}, f32[1,36,32,128]{3,2,1,0:T(8,128)}, u32[]{:S(2)}, u32[]{:S(2)}) collective-permute-start(f32[1,36,32,128]{3,2,1,0:T(8,128)} %get-tuple-element.64), channel_id=1, source_target_pairs={{0,3},{1,0},{2,1},{3,2},{4,7},{5,4},{6,5},{7,6},{8,11},{9,8},{10,9... | collective-permute-start | bytes 1769480 | tf_op jit(solution)/shard_map/ppermute | solution.py:697
  18.1 6.8 %copy-start.24 = (f32[128,32,128]{2,1,0:T(8,128)S(1)}, f32[128,32,128]{2,1,0:T(8,128)}, u32[]{:S(2)}) copy-start(f32[128,32,128]{2,1,0:T(8,128)} %param.8) | copy-start | bytes 6291460
  24.9 35.5 %slice-start = ((s8[6291456]{0:T(1024)(128)(4,1)}), s8[2097152]{0:T(1024)(128)(4,1)S(1)}, s32[]{:S(2)}) async-start(s8[6291456]{0:T(1024)(128)(4,1)} %bitcast.17), calls=%async_computation.5 | async-start | bytes 4194304
  40.6 24.2 %collective-permute-start.5 = (f32[1,32,32,128]{3,2,1,0:T(8,128)}, f32[1,32,32,128]{3,2,1,0:T(8,128)S(1)}, u32[]{:S(2)}, u32[]{:S(2)}) collective-permute-start(f32[1,32,32,128]{3,2,1,0:T(8,128)} %get-tuple-element.32), channel_id=1, source_target_pairs={{0,1},{1,2},{2,3},{3,0},{4,5},{5,6},{6,7},{7,4},{8,9},{9,10},{10,1... | collective-permute-start | bytes 1572872 | tf_op jit(solution)/shard_map/ppermute | solution.py:697
  41.4 24.2 %collective-permute-start.6 = (f32[1,32,32,128]{3,2,1,0:T(8,128)}, f32[1,32,32,128]{3,2,1,0:T(8,128)S(1)}, u32[]{:S(2)}, u32[]{:S(2)}) collective-permute-start(f32[1,32,32,128]{3,2,1,0:T(8,128)} %get-tuple-element.33), channel_id=1, source_target_pairs={{0,2},{1,3},{2,0},{3,1},{4,6},{5,7},{6,4},{7,5},{8,10},{9,11},{10,... | collective-permute-start | bytes 1572872 | tf_op jit(solution)/shard_map/ppermute | solution.py:697
  42.9 23.5 %collective-permute-start.7 = (f32[1,32,32,128]{3,2,1,0:T(8,128)}, f32[1,32,32,128]{3,2,1,0:T(8,128)S(1)}, u32[]{:S(2)}, u32[]{:S(2)}) collective-permute-start(f32[1,32,32,128]{3,2,1,0:T(8,128)} %get-tuple-element.34), channel_id=1, source_target_pairs={{0,3},{1,0},{2,1},{3,2},{4,7},{5,4},{6,5},{7,6},{8,11},{9,8},{10,9... | collective-permute-start | bytes 1572872 | tf_op jit(solution)/shard_map/ppermute | solution.py:697
  44.0 16.5 %collective-permute-start.3 = (bf16[1024,128]{1,0:T(8,128)(2,1)S(1)}, bf16[1024,128]{1,0:T(8,128)(2,1)S(1)}, u32[]{:S(2)}, u32[]{:S(2)}) collective-permute-start(bf16[1024,128]{1,0:T(8,128)(2,1)S(1)} %get-tuple-element.61), channel_id=1, source_target_pairs={{0,4},{4,8},{8,12},{12,16},{16,20},{20,24},{24,28},{28,1},{1,5},{5... | collective-permute-start | bytes 786440 | tf_op jit(solution)/shard_map/ppermute | solution.py:370
  46.0 14.4 %collective-permute-start.4 = (bf16[1024,128]{1,0:T(8,128)(2,1)S(1)}, bf16[1024,128]{1,0:T(8,128)(2,1)S(1)}, u32[]{:S(2)}, u32[]{:S(2)}) collective-permute-start(bf16[1024,128]{1,0:T(8,128)(2,1)S(1)} %get-tuple-element.60), channel_id=1, source_target_pairs={{4,0},{8,4},{12,8},{16,12},{20,16},{24,20},{28,24},{1,28},{5,1},{9... | collective-permute-start | bytes 786440 | tf_op jit(solution)/shard_map/ppermute | solution.py:371
  53.7 6.8 %slice-start.1 = ((s8[6291456]{0:T(1024)(128)(4,1)}), s8[4194304]{0:T(1024)(128)(4,1)S(1)}, s32[]{:S(2)}) async-start(s8[6291456]{0:T(1024)(128)(4,1)} %bitcast.17), calls=%async_computation.6 | async-start | bytes 8388608
  67.2 38.7 %all-to-all-start.1 = ((bf16[32,32,640]{2,1,0:T(8,128)(2,1)}), bf16[32,32,640]{2,1,0:T(8,128)(2,1)}, u32[]{:S(2)}, u32[]{:S(2)}) async-start(bf16[32,32,640]{2,1,0:T(8,128)(2,1)} %bitcast.21), calls=%async_computation.1 | async-start | bytes 2621440 | tf_op jit(solution)/shard_map/all_to_all | solution.py:769
  75.5 72.7 %slice-start.2 = ((s8[6291456]{0:T(1024)(128)(4,1)}), s8[2097152]{0:T(1024)(128)(4,1)S(1)}, s32[]{:S(2)}) async-start(s8[6291456]{0:T(1024)(128)(4,1)} %bitcast.19), calls=%async_computation.7 | async-start | bytes 4194304
  106.8 41.4 %slice-start.3 = ((s8[6291456]{0:T(1024)(128)(4,1)}), s8[4194304]{0:T(1024)(128)(4,1)S(1)}, s32[]{:S(2)}) async-start(s8[6291456]{0:T(1024)(128)(4,1)} %bitcast.19), calls=%async_computation.8 | async-start | bytes 8388608
  113.1 40.5 %copy-start.7 = (f32[4,32,32,128]{3,2,1,0:T(8,128)}, f32[4,32,32,128]{3,2,1,0:T(8,128)S(1)}, u32[]{:S(2)}) copy-start(f32[4,32,32,128]{3,2,1,0:T(8,128)S(1)} %get-tuple-element.42.current_ref) | copy-start | bytes 6291460
  142.8 12.3 %collective-permute-start.8 = (bf16[1024,128]{1,0:T(8,128)(2,1)S(1)}, bf16[1024,128]{1,0:T(8,128)(2,1)S(1)}, u32[]{:S(2)}, u32[]{:S(2)}) collective-permute-start(bf16[1024,128]{1,0:T(8,128)(2,1)S(1)} %get-tuple-element.59), channel_id=1, source_target_pairs={{0,4},{4,8},{8,12},{12,16},{16,20},{20,24},{24,28},{28,1},{1,5},{5... | collective-permute-start | bytes 786440 | tf_op jit(solution)/shard_map/ppermute | solution.py:370
  144.3 13.0 %collective-permute-start.9 = (bf16[1024,128]{1,0:T(8,128)(2,1)S(1)}, bf16[1024,128]{1,0:T(8,128)(2,1)S(1)}, u32[]{:S(2)}, u32[]{:S(2)}) collective-permute-start(bf16[1024,128]{1,0:T(8,128)(2,1)S(1)} %get-tuple-element.58), channel_id=1, source_target_pairs={{4,0},{8,4},{12,8},{16,12},{20,16},{24,20},{28,24},{1,28},{5,1},{9... | collective-permute-start | bytes 786440 | tf_op jit(solution)/shard_map/ppermute | solution.py:371
  160.3 3.0 %copy-start.6 = (f32[5,128,128]{2,1,0:T(8,128)S(1)}, f32[5,128,128]{2,1,0:T(8,128)}, u32[]{:S(2)}) copy-start(f32[5,128,128]{2,1,0:T(8,128)} %copy-done.5) | copy-start | bytes 983044
  160.3 29.3 %all-to-all-start.3 = ((bf16[32,32,512]{2,1,0:T(8,128)(2,1)}), bf16[32,32,512]{2,1,0:T(8,128)(2,1)S(1)}, u32[]{:S(2)}, u32[]{:S(2)}) async-start(bf16[32,32,512]{2,1,0:T(8,128)(2,1)} %bitcast.10), calls=%async_computation.3 | async-start | bytes 2097152 | tf_op jit(solution)/shard_map/all_to_all | solution.py:779
  169.0 28.9 %copy-start.9 = (f32[4,32,32,128]{3,2,1,0:T(8,128)S(1)}, f32[4,32,32,128]{3,2,1,0:T(8,128)}, u32[]{:S(2)}) copy-start(f32[4,32,32,128]{3,2,1,0:T(8,128)} %copy-done.7) | copy-start | bytes 6291460
  169.0 28.9 %copy-start.20 = (bf16[256,256]{1,0:T(8,128)(2,1)S(1)}, bf16[256,256]{1,0:T(8,128)(2,1)}, u32[]{:S(2)}) copy-start(bf16[256,256]{1,0:T(8,128)(2,1)} %get-tuple-element.62.left_ref) | copy-start | bytes 393220
  195.0 11.3 %collective-permute-start.10 = (bf16[1,32,32,128]{3,2,1,0:T(8,128)(2,1)}, bf16[1,32,32,128]{3,2,1,0:T(8,128)(2,1)}, u32[]{:S(2)}, u32[]{:S(2)}) collective-permute-start(bf16[1,32,32,128]{3,2,1,0:T(8,128)(2,1)} %get-tuple-element.47), channel_id=1, source_target_pairs={{0,1},{1,2},{2,3},{3,0},{4,5},{5,6},{6,7},{7,4},{8,9},{9,10},{10,1... | collective-permute-start | bytes 786440 | tf_op jit(solution)/shard_map/ppermute | solution.py:697
  195.0 12.3 %collective-permute-start.11 = (bf16[1,32,32,128]{3,2,1,0:T(8,128)(2,1)}, bf16[1,32,32,128]{3,2,1,0:T(8,128)(2,1)}, u32[]{:S(2)}, u32[]{:S(2)}) collective-permute-start(bf16[1,32,32,128]{3,2,1,0:T(8,128)(2,1)} %get-tuple-element.48), channel_id=1, source_target_pairs={{0,2},{1,3},{2,0},{3,1},{4,6},{5,7},{6,4},{7,5},{8,10},{9,11},{10,... | collective-permute-start | bytes 786440 | tf_op jit(solution)/shard_map/ppermute | solution.py:697
  196.5 12.6 %collective-permute-start.12 = (bf16[1,32,32,128]{3,2,1,0:T(8,128)(2,1)}, bf16[1,32,32,128]{3,2,1,0:T(8,128)(2,1)}, u32[]{:S(2)}, u32[]{:S(2)}) collective-permute-start(bf16[1,32,32,128]{3,2,1,0:T(8,128)(2,1)} %get-tuple-element.49), channel_id=1, source_target_pairs={{0,3},{1,0},{2,1},{3,2},{4,7},{5,4},{6,5},{7,6},{8,11},{9,8},{10,9... | collective-permute-start | bytes 786440 | tf_op jit(solution)/shard_map/ppermute | solution.py:697
  202.4 3.8 %copy-start.18 = (bf16[1,32,32,128]{3,2,1,0:T(8,128)(2,1)S(1)}, bf16[1,32,32,128]{3,2,1,0:T(8,128)(2,1)}, u32[]{:S(2)}) copy-start(bf16[1,32,32,128]{3,2,1,0:T(8,128)(2,1)} %copy-done.17) | copy-start | bytes 786436
  202.4 18.2 %all-to-all-start.4 = ((bf16[128,32,128]{2,1,0:T(8,128)(2,1)}), bf16[128,32,128]{2,1,0:T(8,128)(2,1)S(1)}, u32[]{:S(2)}, u32[]{:S(2)}) async-start(bf16[128,32,128]{2,1,0:T(8,128)(2,1)} %bitcast.11), calls=%async_computation.4 | async-start | bytes 2097152 | tf_op jit(solution)/shard_map/all_to_all | solution.py:730
  (16 other events, 23.8 us)

commit v15 on v14

--- a/solution.py
+++ b/solution.py
@@ -11,6 +11,7 @@
 RELAXATION = 0.6
 VMEM_BYTES = 60 << 20
 SHARED_VMEM_BYTES = 48 << 20
+STEP_VMEM_BYTES = 40 << 20
 SMALL_VMEM_BYTES = 9 << 20
 UNROLL = 4
 
@@ -166,8 +167,11 @@
 def decode(code, power):
     code = code.astype(jnp.float32)
     size = jnp.abs(code)
-    value = jnp.exp(jnp.log(size) * (1.0 / power))
-    value = jnp.where(size > 0.0, value, 0.0)
+    if power == 4:
+        value = jnp.sqrt(jnp.sqrt(size))
+    else:
+        value = jnp.exp(jnp.log(size) * (1.0 / power))
+        value = jnp.where(size > 0.0, value, 0.0)
     return jnp.where(code < 0.0, -value, value)
 
 
@@ -603,7 +607,7 @@
             out_specs=[slab] * 3,
         ),
         out_shape=[shape] * 3,
-        compiler_params=pltpu.CompilerParams(vmem_limit_bytes=SHARED_VMEM_BYTES),
+        compiler_params=pltpu.CompilerParams(vmem_limit_bytes=VMEM_BYTES),
     )(place, *current_parts, *right_side_parts, weights, right)
 
 
@@ -641,6 +645,7 @@
         [slabs, strips_of(state)],
         [pltpu.VMEM((nx * GROUP, ny), jnp.float32)],
         solve_flops(base, tables),
+        STEP_VMEM_BYTES,
     )
 
 

time: 224 us -> 224 us (level)
  local copies, waits for them, and re-layouts: 21.1 us -> 18.5 us
    dynamic_update_slice x4, local copies, waits for them, and re-layouts: 3.01 us -> 0.16 us  [collect(): out = lax.dynamic_update_slice_in_dim(out, part, source, 0)]
    unnamed x62 -> x56, local copies, waits for them, and re-layouts: 15.3 us -> 15.5 us
  transfers between devices with their start and end apart: 17 -> 17, of which waited for: 9 -> 9; matrix products, arithmetic and copies ran while one was open for 5% -> 4% of each run, Pallas kernels for 16% -> 16%
where the time goes in v15:
time: 224 us; the launch traced here: 223 us
  waiting for transfers between devices  73.7 us (33%)
  Pallas kernels  52 us (23%)
  starting transfers between devices  40.1 us (18%)
  blocking collectives  29.6 us (13%)
  local copies, waits for them, and re-layouts  18.5 us (8%)
  other arithmetic  8.01 us (4%)
    all_to_all x2, waiting for transfers between devices, local(): lax.all_to_all(sums, both, 0, 0, tiled=True).reshape(devices, share, -1)  44.2 us
    all_to_all x1, blocking collectives, local(): state = lax.all_to_all(state, both, 0, 0, tiled=True)  29.6 us
    ppermute x9, waiting for transfers between devices, onwards(): lax.ppermute(part, axis, [(i, (i + shift) % count) for i in range(count)])  16.9 us
    unnamed x56, local copies, waits for them, and re-layouts  15.5 us
    pallas_call x3, Pallas kernels, per_group(): pl.pallas_call(kernel, grid=(groups,), in_specs=in_specs, out_specs=out_s...  13 us
    pallas_call x2, Pallas kernels, coupled_sums(): pl.pallas_call(functools.partial(inner_kernel, height, cols), grid=(block...  12.1 us
    all_to_all x2, starting transfers between devices, local(): lax.all_to_all(sums, both, 0, 0, tiled=True).reshape(devices, share, -1)  10.3 us
    all_to_all x1, waiting for transfers between devices, to_slabs(): return lax.all_to_all(flat, 'slab', 0, 0, tiled=True)  8.83 us
  transfers between devices with their start and end apart: 17, of which 9 were waited for; matrix products, arithmetic and copies ran while one was open for 4% of the time, Pallas kernels for 16%

profile of v15, /device:TPU:0, one launch (start us, length us, event | category | flops | bytes accessed | tf_op | source)
XLA Modules:
  0.0 223.0 jit_solution(9138799041315557394)
XLA Ops:
  0.7 3.5 %shard_map.86 = bf16[8,128,512]{2,1,0:T(8,128)(2,1)} custom-call(f32[4096,128]{1,0:T(8,128)} %bitcast.24), custom_call_target="tpu_custom_call" | custom-call | tf_op jit(solution)/shard_map/pallas_call | solution.py:213
  4.1 7.3 %all-to-all-start = ((bf16[8,128,512]{2,1,0:T(8,128)(2,1)}), bf16[8,128,512]{2,1,0:T(8,128)(2,1)}, u32[]{:S(2)}, u32[]{:S(2)}) async-start(bf16[8,128,512]{2,1,0:T(8,128)(2,1)} %shard_map.86), calls=%async_computation | async-start | bytes 2097152 | tf_op jit(solution)/shard_map/all_to_all | solution.py:730
  16.0 2.2 copy-done.6
  18.2 3.0 %shard_map.87.matrix_ref = bf16[8,3,128,1024]{3,2,1,0:T(8,128)(2,1)S(1)} custom-call(s32[8,16]{1,0:T(8,128)S(1)} %copy-done.16, s32[8]{0:T(128)S(1)} %copy-done.17, bf16[8,16,128,128]{3,2,1,0:T(8,128)(2,1)S(1)} %copy-done.6), custom_call_target="tpu_custom_call" | custom-call | tf_op jit(solution)/shard_map/pallas_call | solution.py:240
  21.1 2.6 %copy-done = bf16[8,3,128,1024]{3,2,1,0:T(8,128)(2,1)} copy-done((bf16[8,3,128,1024]{3,2,1,0:T(8,128)(2,1)}, bf16[8,3,128,1024]{3,2,1,0:T(8,128)(2,1)S(1)}, u32[]{:S(2)}) %copy-start) | copy-done | bytes 6291480
  26.2 2.1 collective-permute-done.refs_1_
  29.5 11.1 %collective-permute-done.2.refs_3_ = f32[1,36,32,128]{3,2,1,0:T(8,128)} collective-permute-done((f32[1,36,32,128]{3,2,1,0:T(8,128)}, f32[1,36,32,128]{3,2,1,0:T(8,128)}, u32[]{:S(2)}, u32[]{:S(2)}) %collective-permute-start.2) | collective-permute-done | bytes 589856 | tf_op jit(solution)/shard_map/ppermute | solution.py:702
  44.0 2.1 collective-permute-start.3
  46.0 3.3 %collective-permute-start.4 = (bf16[1024,128]{1,0:T(8,128)(2,1)S(1)}, bf16[1024,128]{1,0:T(8,128)(2,1)S(1)}, u32[]{:S(2)}, u32[]{:S(2)}) collective-permute-start(bf16[1024,128]{1,0:T(8,128)(2,1)S(1)} %get-tuple-element.60), channel_id=1, source_target_pairs={{4,0},{8,4},{12,8},{16,12},{20,16},{24,20},{28,24},{1,28},{5,1},{9... | collective-permute-start | bytes 786440 | tf_op jit(solution)/shard_map/ppermute | solution.py:375
  50.9 2.8 %copy-done.1 = bf16[8,3,128,1024]{3,2,1,0:T(8,128)(2,1)S(1)} copy-done((bf16[8,3,128,1024]{3,2,1,0:T(8,128)(2,1)S(1)}, bf16[8,3,128,1024]{3,2,1,0:T(8,128)(2,1)}, u32[]{:S(2)}) %copy-start.1) | copy-done | bytes 6291480
  53.7 6.7 %shard_map.89.inner_ref = f32[1024,512]{1,0:T(8,128)S(1)} custom-call(bf16[8,3,128,1024]{3,2,1,0:T(8,128)(2,1)S(1)} %copy-done.1, bf16[1024,512]{1,0:T(8,128)(2,1)} %bitcast.3.state_ref, f32[60,128]{1,0:T(8,128)S(1)} %shard_map.88.weight_ref), custom_call_target="tpu_custom_call" | custom-call | flops 3221225472 | bytes 6291456 | tf_op jit(solution)/shard_map/pallas_call | solution.py:382
  60.5 4.2 %shard_map.90 = bf16[1024,640]{1,0:T(8,128)(2,1)S(1)} custom-call(bf16[8,3,128,1024]{3,2,1,0:T(8,128)(2,1)S(1)} %bitcast.18, bf16[1024,128]{1,0:T(8,128)(2,1)S(1)} %collective-permute-done.3.above_ref, bf16[1024,128]{1,0:T(8,128)(2,1)S(1)} %collective-permute-done.4.below_ref, f32[60,128]{1,0:T(8,128)S(1)} %shard_map.88.weight_ref, ...), custom_call_target="tpu_custom_call" | custom-call | tf_op jit(solution)/shard_map/pallas_call | solution.py:396
  65.8 7.2 %all-to-all-start.1 = ((bf16[32,32,640]{2,1,0:T(8,128)(2,1)}), bf16[32,32,640]{2,1,0:T(8,128)(2,1)}, u32[]{:S(2)}, u32[]{:S(2)}) async-start(bf16[32,32,640]{2,1,0:T(8,128)(2,1)} %bitcast.21), calls=%async_computation.1 | async-start | bytes 2621440 | tf_op jit(solution)/shard_map/all_to_all | solution.py:774
  75.5 6.1 %shard_map.92 = (f32[4,32,32,128]{3,2,1,0:T(8,128)}, f32[4,32,32,128]{3,2,1,0:T(8,128)}, f32[4,32,32,128]{3,2,1,0:T(8,128)}) custom-call(s32[2]{0:T(128)} %copy-done.15, f32[1,36,32,128]{3,2,1,0:T(8,128)} %copy-done.2, f32[1,36,32,128]{3,2,1,0:T(8,128)} %copy-done.4, f32[1,36,32,128]{3,2,1,0:T(8,128)} %collective-permute-done.1.refs_2_, ...), custom_call_target="tpu_custom_call" | custom-call | tf_op jit(solution)/shard_map/pallas_call | solution.py:597
  81.6 23.6 %all-to-all-done.1.coupled_ref = bf16[32,32,640]{2,1,0:T(8,128)(2,1)} async-done(((bf16[32,32,640]{2,1,0:T(8,128)(2,1)}), bf16[32,32,640]{2,1,0:T(8,128)(2,1)}, u32[]{:S(2)}, u32[]{:S(2)}) %all-to-all-start.1) | async-done | bytes 1310752 | tf_op jit(solution)/shard_map/all_to_all | solution.py:774
  105.2 1.6 copy-done.18
  108.4 5.8 %shard_map.93 = (f32[4,32,32,128]{3,2,1,0:T(8,128)S(1)}, bf16[32,32,512]{2,1,0:T(8,128)(2,1)S(1)}) custom-call(f32[4,32,32,128]{3,2,1,0:T(8,128)S(1)} %copy-done.18, f32[4,32,32,128]{3,2,1,0:T(8,128)S(1)} %copy-done.19, bf16[32,32,640]{2,1,0:T(8,128)(2,1)} %all-to-all-done.1.coupled_ref, bf16[256,256]{1,0:T(8,128)(2,1)S(1)} %copy-done.10, ...), custom_call_target="tpu_custom_call" | custom-call | flops 1610612736 | bytes 11665408 | tf_op jit(solution)/shard_map/pallas_call | solution.py:579
  114.2 29.6 %all_to_all.36 = bf16[32,32,512]{2,1,0:T(8,128)(2,1)S(1)} all-to-all(bf16[32,32,512]{2,1,0:T(8,128)(2,1)S(1)} %get-tuple-element.44), channel_id=1, replica_groups=mesh['mode'=8,'slab'=4] {'mode','slab'}, dimensions={0} | all-to-all | bytes 2097152 | tf_op jit(solution)/shard_map/all_to_all | solution.py:780
  145.4 3.9 %collective-permute-start.9 = (bf16[1024,128]{1,0:T(8,128)(2,1)S(1)}, bf16[1024,128]{1,0:T(8,128)(2,1)S(1)}, u32[]{:S(2)}, u32[]{:S(2)}) collective-permute-start(bf16[1024,128]{1,0:T(8,128)(2,1)S(1)} %get-tuple-element.58), channel_id=1, source_target_pairs={{4,0},{8,4},{12,8},{16,12},{20,16},{24,20},{28,24},{1,28},{5,1},{9... | collective-permute-start | bytes 786440 | tf_op jit(solution)/shard_map/ppermute | solution.py:375
  149.3 5.4 %shard_map.95.inner_ref = f32[1024,512]{1,0:T(8,128)S(1)} custom-call(bf16[8,3,128,1024]{3,2,1,0:T(8,128)(2,1)S(1)} %bitcast.20, bf16[1024,512]{1,0:T(8,128)(2,1)S(1)} %bitcast.23, f32[60,128]{1,0:T(8,128)S(1)} %shard_map.88.weight_ref), custom_call_target="tpu_custom_call" | custom-call | flops 3221225472 | bytes 6291456 | tf_op jit(solution)/shard_map/pallas_call | solution.py:382
  156.2 2.2 collective-permute-done.9.below_ref
  158.4 3.0 %shard_map.96 = bf16[1024,512]{1,0:T(8,128)(2,1)} custom-call(bf16[8,3,128,1024]{3,2,1,0:T(8,128)(2,1)S(1)} %bitcast.20, bf16[1024,128]{1,0:T(8,128)(2,1)S(1)} %collective-permute-done.8.above_ref, bf16[1024,128]{1,0:T(8,128)(2,1)S(1)} %collective-permute-done.9.below_ref, f32[60,128]{1,0:T(8,128)S(1)} %shard_map.88.weight_ref, ...), custom_call_target="tpu_custom_call" | custom-call | tf_op jit(solution)/shard_map/pallas_call | solution.py:396
  161.4 3.0 %all-to-all-start.3 = ((bf16[32,32,512]{2,1,0:T(8,128)(2,1)}), bf16[32,32,512]{2,1,0:T(8,128)(2,1)S(1)}, u32[]{:S(2)}, u32[]{:S(2)}) async-start(bf16[32,32,512]{2,1,0:T(8,128)(2,1)} %bitcast.10), calls=%async_computation.3 | async-start | bytes 2097152 | tf_op jit(solution)/shard_map/all_to_all | solution.py:784
  166.1 2.7 %shard_map.94.base_ref = f32[4,32,32,128]{3,2,1,0:T(8,128)S(1)} custom-call(f32[4,32,32,128]{3,2,1,0:T(8,128)S(1)} %copy-done.12, f32[4,32,32,128]{3,2,1,0:T(8,128)} %get-tuple-element.43.right_side_ref, f32[5,128,128]{2,1,0:T(8,128)S(1)} %copy-done.8), custom_call_target="tpu_custom_call" | custom-call | bytes 9043968 | tf_op jit(solution)/shard_map/pallas_call | solution.py:579
  170.1 20.6 %all-to-all-done.3.coupled_ref = bf16[32,32,512]{2,1,0:T(8,128)(2,1)S(1)} async-done(((bf16[32,32,512]{2,1,0:T(8,128)(2,1)}), bf16[32,32,512]{2,1,0:T(8,128)(2,1)S(1)}, u32[]{:S(2)}, u32[]{:S(2)}) %all-to-all-start.3) | async-done | bytes 1048608 | tf_op jit(solution)/shard_map/all_to_all | solution.py:784
  190.7 4.1 %shard_map.97 = (f32[4,32,32,128]{3,2,1,0:T(8,128)S(1)}, bf16[1,32,32,128]{3,2,1,0:T(8,128)(2,1)S(1)}, bf16[1,32,32,128]{3,2,1,0:T(8,128)(2,1)S(1)}, bf16[1,32,3...) custom-call(s32[1]{0:T(128)} %bitcast.here_ref, f32[4,32,32,128]{3,2,1,0:T(8,128)} %copy-done.3, ...), custom_call_target="tpu_custom_call" | custom-call | bytes 4194304 | tf_op jit(solution)/shard_map/pallas_call | solution.py:657
  197.8 4.5 %shard_map.98 = bf16[4,32,32,128]{3,2,1,0:T(8,128)(2,1)} custom-call(f32[4,32,32,128]{3,2,1,0:T(8,128)S(1)} %copy-done.13, f32[4,32,32,128]{3,2,1,0:T(8,128)S(1)} %get-tuple-element.45.resid_ref, bf16[256,256]{1,0:T(8,128)(2,1)S(1)} %copy-done.10, bf16[256,256]{1,0:T(8,128)(2,1)S(1)} %copy-done.14, f32[128,128]{1,0:T(8,128)S(1)} %subtract_divide_fusion.scale_ref), custom_call_target="tpu_custom_call" | custom-call | flops 1610612736 | bytes 9043968 | tf_op jit(solution)/shard_map/pallas_call | solution.py:579
  202.3 3.5 %all-to-all-start.4 = ((bf16[128,32,128]{2,1,0:T(8,128)(2,1)}), bf16[128,32,128]{2,1,0:T(8,128)(2,1)S(1)}, u32[]{:S(2)}, u32[]{:S(2)}) async-start(bf16[128,32,128]{2,1,0:T(8,128)(2,1)} %bitcast.11), calls=%async_computation.4 | async-start | bytes 2097152 | tf_op jit(solution)/shard_map/all_to_all | solution.py:735
  206.1 2.5 %collective-permute-done.12 = bf16[1,32,32,128]{3,2,1,0:T(8,128)(2,1)S(1)} collective-permute-done((bf16[1,32,32,128]{3,2,1,0:T(8,128)(2,1)S(1)}, bf16[1,32,32,128]{3,2,1,0:T(8,128)(2,1)S(1)}, u32[]{:S(2)}, u32[]{:S(2)}) %collective-permute-start.12) | collective-permute-done | bytes 262176 | tf_op jit(solution)/shard_map/ppermute | solution.py:702
  209.7 1.8 fusion.8
  211.5 8.8 %all-to-all-done.4 = bf16[128,32,128]{2,1,0:T(8,128)(2,1)S(1)} async-done(((bf16[128,32,128]{2,1,0:T(8,128)(2,1)}), bf16[128,32,128]{2,1,0:T(8,128)(2,1)S(1)}, u32[]{:S(2)}, u32[]{:S(2)}) %all-to-all-start.4) | async-done | bytes 1048608 | tf_op jit(solution)/shard_map/all_to_all | solution.py:735
  220.3 2.7 %fusion.7 = f32[128,32,128]{2,1,0:T(8,128)} fusion(bf16[128,32,128]{2,1,0:T(8,128)(2,1)S(1)} %all-to-all-done.4), kind=kLoop, calls=%fused_computation.13 | loop fusion | flops 3145728 | bytes 3145728 | tf_op jit(solution)/shard_map/mul | solution.py:789
  (95 shorter events, 28.4 us)
Async XLA Ops:
  0.6 10.8 %copy-start.22 = (f32[3,32,128]{2,1,0:T(8,128)S(1)}, f32[3,32,128]{2,1,0:T(8,128)}, u32[]{:S(2)}) copy-start(f32[3,32,128]{2,1,0:T(8,128)} %param.10) | copy-start | bytes 147460
  0.6 10.8 %copy-start.23 = (f32[32,128]{1,0:T(8,128)S(1)}, f32[32,128]{1,0:T(8,128)}, u32[]{:S(2)}) copy-start(f32[32,128]{1,0:T(8,128)} %param.9) | copy-start | bytes 49156
  0.6 10.8 %copy-start.20 = (f32[128,32,128]{2,1,0:T(8,128)S(1)}, f32[128,32,128]{2,1,0:T(8,128)}, u32[]{:S(2)}) copy-start(f32[128,32,128]{2,1,0:T(8,128)} %param.7) | copy-start | bytes 6291460
  4.1 36.5 %all-to-all-start = ((bf16[8,128,512]{2,1,0:T(8,128)(2,1)}), bf16[8,128,512]{2,1,0:T(8,128)(2,1)}, u32[]{:S(2)}, u32[]{:S(2)}) async-start(bf16[8,128,512]{2,1,0:T(8,128)(2,1)} %shard_map.86), calls=%async_computation | async-start | bytes 2097152 | tf_op jit(solution)/shard_map/all_to_all | solution.py:730
  13.0 60.2 %copy-start.2 = (f32[1,36,32,128]{3,2,1,0:T(8,128)}, f32[1,36,32,128]{3,2,1,0:T(8,128)S(1)}, u32[]{:S(2)}) copy-start(f32[1,36,32,128]{3,2,1,0:T(8,128)S(1)} %get-tuple-element.26.refs_0_) | copy-start | bytes 1769476
  13.0 15.3 %collective-permute-start = (f32[1,36,32,128]{3,2,1,0:T(8,128)}, f32[1,36,32,128]{3,2,1,0:T(8,128)S(1)}, u32[]{:S(2)}, u32[]{:S(2)}) collective-permute-start(f32[1,36,32,128]{3,2,1,0:T(8,128)} %get-tuple-element.65), channel_id=1, source_target_pairs={{0,1},{1,2},{2,3},{3,0},{4,5},{5,6},{6,7},{7,4},{8,9},{9,10},{10,1... | collective-permute-start | bytes 1769480 | tf_op jit(solution)/shard_map/ppermute | solution.py:702
  13.0 16.5 %collective-permute-start.1 = (f32[1,36,32,128]{3,2,1,0:T(8,128)}, f32[1,36,32,128]{3,2,1,0:T(8,128)}, u32[]{:S(2)}, u32[]{:S(2)}) collective-permute-start(f32[1,36,32,128]{3,2,1,0:T(8,128)} %get-tuple-element.66), channel_id=1, source_target_pairs={{0,2},{1,3},{2,0},{3,1},{4,6},{5,7},{6,4},{7,5},{8,10},{9,11},{10,... | collective-permute-start | bytes 1769480 | tf_op jit(solution)/shard_map/ppermute | solution.py:702
  14.5 26.1 %collective-permute-start.2 = (f32[1,36,32,128]{3,2,1,0:T(8,128)}, f32[1,36,32,128]{3,2,1,0:T(8,128)}, u32[]{:S(2)}, u32[]{:S(2)}) collective-permute-start(f32[1,36,32,128]{3,2,1,0:T(8,128)} %get-tuple-element.64), channel_id=1, source_target_pairs={{0,3},{1,0},{2,1},{3,2},{4,7},{5,4},{6,5},{7,6},{8,11},{9,8},{10,9... | collective-permute-start | bytes 1769480 | tf_op jit(solution)/shard_map/ppermute | solution.py:702
  23.9 49.4 %copy-start.15 = (s32[2]{0:T(128)}, s32[2]{0:T(128)S(1)}, u32[]{:S(2)}) copy-start(s32[2]{0:T(128)S(1)} %pad_add_fusion.place_ref) | copy-start | bytes 28
  24.9 35.6 %copy-start.9 = (bf16[256,256]{1,0:T(8,128)(2,1)}, bf16[256,256]{1,0:T(8,128)(2,1)S(1)}, u32[]{:S(2)}) copy-start(bf16[256,256]{1,0:T(8,128)(2,1)S(1)} %get-tuple-element.63.right_ref.refs_9_) | copy-start | bytes 393220
  24.9 35.6 %slice-start = ((s8[6291456]{0:T(1024)(128)(4,1)}), s8[2097152]{0:T(1024)(128)(4,1)S(1)}, s32[]{:S(2)}) async-start(s8[6291456]{0:T(1024)(128)(4,1)} %bitcast.17), calls=%async_computation.5 | async-start | bytes 4194304
  28.3 45.0 %copy-start.4 = (f32[1,36,32,128]{3,2,1,0:T(8,128)}, f32[1,36,32,128]{3,2,1,0:T(8,128)S(1)}, u32[]{:S(2)}) copy-start(f32[1,36,32,128]{3,2,1,0:T(8,128)S(1)} %collective-permute-done.refs_1_) | copy-start | bytes 1769476
  40.6 24.2 %collective-permute-start.5 = (f32[1,32,32,128]{3,2,1,0:T(8,128)}, f32[1,32,32,128]{3,2,1,0:T(8,128)}, u32[]{:S(2)}, u32[]{:S(2)}) collective-permute-start(f32[1,32,32,128]{3,2,1,0:T(8,128)} %get-tuple-element.32), channel_id=1, source_target_pairs={{0,1},{1,2},{2,3},{3,0},{4,5},{5,6},{6,7},{7,4},{8,9},{9,10},{10,1... | collective-permute-start | bytes 1572872 | tf_op jit(solution)/shard_map/ppermute | solution.py:702
  41.4 23.4 %collective-permute-start.6 = (f32[1,32,32,128]{3,2,1,0:T(8,128)}, f32[1,32,32,128]{3,2,1,0:T(8,128)}, u32[]{:S(2)}, u32[]{:S(2)}) collective-permute-start(f32[1,32,32,128]{3,2,1,0:T(8,128)} %get-tuple-element.33), channel_id=1, source_target_pairs={{0,2},{1,3},{2,0},{3,1},{4,6},{5,7},{6,4},{7,5},{8,10},{9,11},{10,... | collective-permute-start | bytes 1572872 | tf_op jit(solution)/shard_map/ppermute | solution.py:702
  42.9 21.9 %collective-permute-start.7 = (f32[1,32,32,128]{3,2,1,0:T(8,128)}, f32[1,32,32,128]{3,2,1,0:T(8,128)}, u32[]{:S(2)}, u32[]{:S(2)}) collective-permute-start(f32[1,32,32,128]{3,2,1,0:T(8,128)} %get-tuple-element.34), channel_id=1, source_target_pairs={{0,3},{1,0},{2,1},{3,2},{4,7},{5,4},{6,5},{7,6},{8,11},{9,8},{10,9... | collective-permute-start | bytes 1572872 | tf_op jit(solution)/shard_map/ppermute | solution.py:702
  44.0 16.5 %collective-permute-start.3 = (bf16[1024,128]{1,0:T(8,128)(2,1)S(1)}, bf16[1024,128]{1,0:T(8,128)(2,1)S(1)}, u32[]{:S(2)}, u32[]{:S(2)}) collective-permute-start(bf16[1024,128]{1,0:T(8,128)(2,1)S(1)} %get-tuple-element.61), channel_id=1, source_target_pairs={{0,4},{4,8},{8,12},{12,16},{16,20},{20,24},{24,28},{28,1},{1,5},{5... | collective-permute-start | bytes 786440 | tf_op jit(solution)/shard_map/ppermute | solution.py:374
  46.0 14.4 %collective-permute-start.4 = (bf16[1024,128]{1,0:T(8,128)(2,1)S(1)}, bf16[1024,128]{1,0:T(8,128)(2,1)S(1)}, u32[]{:S(2)}, u32[]{:S(2)}) collective-permute-start(bf16[1024,128]{1,0:T(8,128)(2,1)S(1)} %get-tuple-element.60), channel_id=1, source_target_pairs={{4,0},{8,4},{12,8},{16,12},{20,16},{24,20},{28,24},{1,28},{5,1},{9... | collective-permute-start | bytes 786440 | tf_op jit(solution)/shard_map/ppermute | solution.py:375
  53.7 6.8 %slice-start.1 = ((s8[6291456]{0:T(1024)(128)(4,1)}), s8[4194304]{0:T(1024)(128)(4,1)S(1)}, s32[]{:S(2)}) async-start(s8[6291456]{0:T(1024)(128)(4,1)} %bitcast.17), calls=%async_computation.6 | async-start | bytes 8388608
  65.8 39.4 %all-to-all-start.1 = ((bf16[32,32,640]{2,1,0:T(8,128)(2,1)}), bf16[32,32,640]{2,1,0:T(8,128)(2,1)}, u32[]{:S(2)}, u32[]{:S(2)}) async-start(bf16[32,32,640]{2,1,0:T(8,128)(2,1)} %bitcast.21), calls=%async_computation.1 | async-start | bytes 2621440 | tf_op jit(solution)/shard_map/all_to_all | solution.py:774
  75.5 29.7 %copy-start.10 = (bf16[256,256]{1,0:T(8,128)(2,1)S(1)}, bf16[256,256]{1,0:T(8,128)(2,1)}, u32[]{:S(2)}) copy-start(bf16[256,256]{1,0:T(8,128)(2,1)} %copy-done.9) | copy-start | bytes 393220
  75.5 29.7 %copy-start.14 = (bf16[256,256]{1,0:T(8,128)(2,1)S(1)}, bf16[256,256]{1,0:T(8,128)(2,1)}, u32[]{:S(2)}) copy-start(bf16[256,256]{1,0:T(8,128)(2,1)} %get-tuple-element.62.left_ref) | copy-start | bytes 393220
  75.5 73.8 %slice-start.2 = ((s8[6291456]{0:T(1024)(128)(4,1)}), s8[2097152]{0:T(1024)(128)(4,1)S(1)}, s32[]{:S(2)}) async-start(s8[6291456]{0:T(1024)(128)(4,1)} %bitcast.19), calls=%async_computation.7 | async-start | bytes 4194304
  108.4 40.9 %slice-start.3 = ((s8[6291456]{0:T(1024)(128)(4,1)}), s8[4194304]{0:T(1024)(128)(4,1)S(1)}, s32[]{:S(2)}) async-start(s8[6291456]{0:T(1024)(128)(4,1)} %bitcast.19), calls=%async_computation.8 | async-start | bytes 8388608
  114.2 40.5 %copy-start.11 = (f32[4,32,32,128]{3,2,1,0:T(8,128)}, f32[4,32,32,128]{3,2,1,0:T(8,128)S(1)}, u32[]{:S(2)}) copy-start(f32[4,32,32,128]{3,2,1,0:T(8,128)S(1)} %get-tuple-element.42.current_ref) | copy-start | bytes 6291460
  143.9 12.3 %collective-permute-start.8 = (bf16[1024,128]{1,0:T(8,128)(2,1)S(1)}, bf16[1024,128]{1,0:T(8,128)(2,1)S(1)}, u32[]{:S(2)}, u32[]{:S(2)}) collective-permute-start(bf16[1024,128]{1,0:T(8,128)(2,1)S(1)} %get-tuple-element.59), channel_id=1, source_target_pairs={{0,4},{4,8},{8,12},{12,16},{16,20},{20,24},{24,28},{28,1},{1,5},{5... | collective-permute-start | bytes 786440 | tf_op jit(solution)/shard_map/ppermute | solution.py:374
  145.4 13.0 %collective-permute-start.9 = (bf16[1024,128]{1,0:T(8,128)(2,1)S(1)}, bf16[1024,128]{1,0:T(8,128)(2,1)S(1)}, u32[]{:S(2)}, u32[]{:S(2)}) collective-permute-start(bf16[1024,128]{1,0:T(8,128)(2,1)S(1)} %get-tuple-element.58), channel_id=1, source_target_pairs={{4,0},{8,4},{12,8},{16,12},{20,16},{24,20},{28,24},{1,28},{5,1},{9... | collective-permute-start | bytes 786440 | tf_op jit(solution)/shard_map/ppermute | solution.py:375
  161.4 29.3 %all-to-all-start.3 = ((bf16[32,32,512]{2,1,0:T(8,128)(2,1)}), bf16[32,32,512]{2,1,0:T(8,128)(2,1)S(1)}, u32[]{:S(2)}, u32[]{:S(2)}) async-start(bf16[32,32,512]{2,1,0:T(8,128)(2,1)} %bitcast.10), calls=%async_computation.3 | async-start | bytes 2097152 | tf_op jit(solution)/shard_map/all_to_all | solution.py:784
  190.7 7.1 %copy-start.13 = (f32[4,32,32,128]{3,2,1,0:T(8,128)S(1)}, f32[4,32,32,128]{3,2,1,0:T(8,128)}, u32[]{:S(2)}) copy-start(f32[4,32,32,128]{3,2,1,0:T(8,128)} %copy-done.11) | copy-start | bytes 6291460
  194.8 11.2 %collective-permute-start.10 = (bf16[1,32,32,128]{3,2,1,0:T(8,128)(2,1)S(1)}, bf16[1,32,32,128]{3,2,1,0:T(8,128)(2,1)S(1)}, u32[]{:S(2)}, u32[]{:S(2)}) collective-permute-start(bf16[1,32,32,128]{3,2,1,0:T(8,128)(2,1)S(1)} %get-tuple-element.47), channel_id=1, source_target_pairs={{0,1},{1,2},{2,3},{3,0},{4,5},{5,6},{6,7},{7,4},{8,9},{9,10},{10,1... | collective-permute-start | bytes 786440 | tf_op jit(solution)/shard_map/ppermute | solution.py:702
  194.9 11.2 %collective-permute-start.11 = (bf16[1,32,32,128]{3,2,1,0:T(8,128)(2,1)S(1)}, bf16[1,32,32,128]{3,2,1,0:T(8,128)(2,1)S(1)}, u32[]{:S(2)}, u32[]{:S(2)}) collective-permute-start(bf16[1,32,32,128]{3,2,1,0:T(8,128)(2,1)S(1)} %get-tuple-element.48), channel_id=1, source_target_pairs={{0,2},{1,3},{2,0},{3,1},{4,6},{5,7},{6,4},{7,5},{8,10},{9,11},{10,... | collective-permute-start | bytes 786440 | tf_op jit(solution)/shard_map/ppermute | solution.py:702
  196.4 12.3 %collective-permute-start.12 = (bf16[1,32,32,128]{3,2,1,0:T(8,128)(2,1)S(1)}, bf16[1,32,32,128]{3,2,1,0:T(8,128)(2,1)S(1)}, u32[]{:S(2)}, u32[]{:S(2)}) collective-permute-start(bf16[1,32,32,128]{3,2,1,0:T(8,128)(2,1)S(1)} %get-tuple-element.49), channel_id=1, source_target_pairs={{0,3},{1,0},{2,1},{3,2},{4,7},{5,4},{6,5},{7,6},{8,11},{9,8},{10,9... | collective-permute-start | bytes 786440 | tf_op jit(solution)/shard_map/ppermute | solution.py:702
  202.3 18.0 %all-to-all-start.4 = ((bf16[128,32,128]{2,1,0:T(8,128)(2,1)}), bf16[128,32,128]{2,1,0:T(8,128)(2,1)S(1)}, u32[]{:S(2)}, u32[]{:S(2)}) async-start(bf16[128,32,128]{2,1,0:T(8,128)(2,1)} %bitcast.11), calls=%async_computation.4 | async-start | bytes 2097152 | tf_op jit(solution)/shard_map/all_to_all | solution.py:735
  (13 other events, 34.0 us)

commit v16 on v14

--- a/solution.py
+++ b/solution.py
@@ -603,7 +603,7 @@
             out_specs=[slab] * 3,
         ),
         out_shape=[shape] * 3,
-        compiler_params=pltpu.CompilerParams(vmem_limit_bytes=SHARED_VMEM_BYTES),
+        compiler_params=pltpu.CompilerParams(vmem_limit_bytes=VMEM_BYTES),
     )(place, *current_parts, *right_side_parts, weights, right)
 
 

time: 224 us -> 221 us (0.987)
  local copies, waits for them, and re-layouts: 21.1 us -> 15.3 us
    unnamed x62 -> x52, local copies, waits for them, and re-layouts: 15.3 us -> 12.4 us
    dynamic_update_slice x4, local copies, waits for them, and re-layouts: 3.01 us -> 0.16 us  [collect(): out = lax.dynamic_update_slice_in_dim(out, part, source, 0)]
  transfers between devices with their start and end apart: 17 -> 17, of which waited for: 9 -> 9; matrix products, arithmetic and copies ran while one was open for 5% -> 4% of each run, Pallas kernels for 16% -> 16%
where the time goes in v16:
time: 221 us; the launch traced here: 220 us
  waiting for transfers between devices  73.5 us (33%)
  Pallas kernels  52.7 us (24%)
  starting transfers between devices  40.1 us (18%)
  blocking collectives  29.6 us (13%)
  local copies, waits for them, and re-layouts  15.3 us (7%)
  other arithmetic  7.52 us (3%)
    all_to_all x2, waiting for transfers between devices, local(): lax.all_to_all(sums, both, 0, 0, tiled=True).reshape(devices, share, -1)  44.2 us
    all_to_all x1, blocking collectives, local(): state = lax.all_to_all(state, both, 0, 0, tiled=True)  29.6 us
    ppermute x9, waiting for transfers between devices, onwards(): lax.ppermute(part, axis, [(i, (i + shift) % count) for i in range(count)])  16.8 us
    pallas_call x3, Pallas kernels, per_group(): pl.pallas_call(kernel, grid=(groups,), in_specs=in_specs, out_specs=out_s...  13.5 us
    unnamed x52, local copies, waits for them, and re-layouts  12.4 us
    pallas_call x2, Pallas kernels, coupled_sums(): pl.pallas_call(functools.partial(inner_kernel, height, cols), grid=(block...  12.1 us
    all_to_all x2, starting transfers between devices, local(): lax.all_to_all(sums, both, 0, 0, tiled=True).reshape(devices, share, -1)  10.3 us
    all_to_all x1, waiting for transfers between devices, to_slabs(): return lax.all_to_all(flat, 'slab', 0, 0, tiled=True)  8.83 us
  transfers between devices with their start and end apart: 17, of which 9 were waited for; matrix products, arithmetic and copies ran while one was open for 4% of the time, Pallas kernels for 16%

profile of v16, /device:TPU:0, one launch (start us, length us, event | category | flops | bytes accessed | tf_op | source)
XLA Modules:
  0.0 219.9 jit_solution(6450568775551124545)
XLA Ops:
  0.7 3.5 %shard_map.86 = bf16[8,128,512]{2,1,0:T(8,128)(2,1)} custom-call(f32[4096,128]{1,0:T(8,128)} %bitcast.24), custom_call_target="tpu_custom_call" | custom-call | tf_op jit(solution)/shard_map/pallas_call | solution.py:209
  4.1 7.3 %all-to-all-start = ((bf16[8,128,512]{2,1,0:T(8,128)(2,1)}), bf16[8,128,512]{2,1,0:T(8,128)(2,1)}, u32[]{:S(2)}, u32[]{:S(2)}) async-start(bf16[8,128,512]{2,1,0:T(8,128)(2,1)} %shard_map.86), calls=%async_computation | async-start | bytes 2097152 | tf_op jit(solution)/shard_map/all_to_all | solution.py:725
  16.0 2.2 copy-done.6
  18.1 3.1 %shard_map.87.matrix_ref = bf16[8,3,128,1024]{3,2,1,0:T(8,128)(2,1)S(1)} custom-call(s32[8,16]{1,0:T(8,128)S(1)} %copy-done.16, s32[8]{0:T(128)S(1)} %copy-done.17, bf16[8,16,128,128]{3,2,1,0:T(8,128)(2,1)S(1)} %copy-done.6), custom_call_target="tpu_custom_call" | custom-call | tf_op jit(solution)/shard_map/pallas_call | solution.py:236
  21.3 2.7 %copy-done = bf16[8,3,128,1024]{3,2,1,0:T(8,128)(2,1)} copy-done((bf16[8,3,128,1024]{3,2,1,0:T(8,128)(2,1)}, bf16[8,3,128,1024]{3,2,1,0:T(8,128)(2,1)S(1)}, u32[]{:S(2)}) %copy-start) | copy-done | bytes 6291480
  26.4 1.9 collective-permute-done.refs_1_
  29.5 11.1 %collective-permute-done.2.refs_3_ = f32[1,36,32,128]{3,2,1,0:T(8,128)} collective-permute-done((f32[1,36,32,128]{3,2,1,0:T(8,128)}, f32[1,36,32,128]{3,2,1,0:T(8,128)}, u32[]{:S(2)}, u32[]{:S(2)}) %collective-permute-start.2) | collective-permute-done | bytes 589856 | tf_op jit(solution)/shard_map/ppermute | solution.py:697
  44.0 2.1 collective-permute-start.3
  46.0 3.3 %collective-permute-start.4 = (bf16[1024,128]{1,0:T(8,128)(2,1)S(1)}, bf16[1024,128]{1,0:T(8,128)(2,1)S(1)}, u32[]{:S(2)}, u32[]{:S(2)}) collective-permute-start(bf16[1024,128]{1,0:T(8,128)(2,1)S(1)} %get-tuple-element.60), channel_id=1, source_target_pairs={{4,0},{8,4},{12,8},{16,12},{20,16},{24,20},{28,24},{1,28},{5,1},{9... | collective-permute-start | bytes 786440 | tf_op jit(solution)/shard_map/ppermute | solution.py:371
  50.9 2.8 %copy-done.1 = bf16[8,3,128,1024]{3,2,1,0:T(8,128)(2,1)S(1)} copy-done((bf16[8,3,128,1024]{3,2,1,0:T(8,128)(2,1)S(1)}, bf16[8,3,128,1024]{3,2,1,0:T(8,128)(2,1)}, u32[]{:S(2)}) %copy-start.1) | copy-done | bytes 6291480
  53.7 6.7 %shard_map.89.inner_ref = f32[1024,512]{1,0:T(8,128)S(1)} custom-call(bf16[8,3,128,1024]{3,2,1,0:T(8,128)(2,1)S(1)} %copy-done.1, bf16[1024,512]{1,0:T(8,128)(2,1)} %bitcast.3.state_ref, f32[60,128]{1,0:T(8,128)S(1)} %shard_map.88.weight_ref), custom_call_target="tpu_custom_call" | custom-call | flops 3221225472 | bytes 6291456 | tf_op jit(solution)/shard_map/pallas_call | solution.py:378
  60.5 4.2 %shard_map.90 = bf16[1024,640]{1,0:T(8,128)(2,1)S(1)} custom-call(bf16[8,3,128,1024]{3,2,1,0:T(8,128)(2,1)S(1)} %bitcast.18, bf16[1024,128]{1,0:T(8,128)(2,1)S(1)} %collective-permute-done.3.above_ref, bf16[1024,128]{1,0:T(8,128)(2,1)S(1)} %collective-permute-done.4.below_ref, f32[60,128]{1,0:T(8,128)S(1)} %shard_map.88.weight_ref, ...), custom_call_target="tpu_custom_call" | custom-call | tf_op jit(solution)/shard_map/pallas_call | solution.py:392
  65.8 7.2 %all-to-all-start.1 = ((bf16[32,32,640]{2,1,0:T(8,128)(2,1)}), bf16[32,32,640]{2,1,0:T(8,128)(2,1)}, u32[]{:S(2)}, u32[]{:S(2)}) async-start(bf16[32,32,640]{2,1,0:T(8,128)(2,1)} %bitcast.21), calls=%async_computation.1 | async-start | bytes 2621440 | tf_op jit(solution)/shard_map/all_to_all | solution.py:769
  75.5 6.1 %shard_map.92 = (f32[4,32,32,128]{3,2,1,0:T(8,128)}, f32[4,32,32,128]{3,2,1,0:T(8,128)}, f32[4,32,32,128]{3,2,1,0:T(8,128)}) custom-call(s32[2]{0:T(128)} %copy-done.15, f32[1,36,32,128]{3,2,1,0:T(8,128)} %copy-done.2, f32[1,36,32,128]{3,2,1,0:T(8,128)} %copy-done.4, f32[1,36,32,128]{3,2,1,0:T(8,128)} %collective-permute-done.1.refs_2_, ...), custom_call_target="tpu_custom_call" | custom-call | tf_op jit(solution)/shard_map/pallas_call | solution.py:593
  81.6 23.6 %all-to-all-done.1.coupled_ref = bf16[32,32,640]{2,1,0:T(8,128)(2,1)} async-done(((bf16[32,32,640]{2,1,0:T(8,128)(2,1)}), bf16[32,32,640]{2,1,0:T(8,128)(2,1)}, u32[]{:S(2)}, u32[]{:S(2)}) %all-to-all-start.1) | async-done | bytes 1310752 | tf_op jit(solution)/shard_map/all_to_all | solution.py:769
  105.2 6.3 %shard_map.93 = (f32[4,32,32,128]{3,2,1,0:T(8,128)S(1)}, bf16[32,32,512]{2,1,0:T(8,128)(2,1)S(1)}) custom-call(f32[4,32,32,128]{3,2,1,0:T(8,128)} %get-tuple-element.39.current_ref, f32[4,32,32,128]{3,2,1,0:T(8,128)} %get-tuple-element.40.base_ref, bf16[32,32,640]{2,1,0:T(8,128)(2,1)} %all-to-all-done.1.coupled_ref, bf16[256,256]{1,0:T(8,128)(2,1)S(1)} %copy-done.10, ...), custom_call_target="tpu_custom_call" | custom-call | flops 1610612736 | bytes 11665408 | tf_op jit(solution)/shard_map/pallas_call | solution.py:575
  111.6 29.6 %all_to_all.36 = bf16[32,32,512]{2,1,0:T(8,128)(2,1)S(1)} all-to-all(bf16[32,32,512]{2,1,0:T(8,128)(2,1)S(1)} %get-tuple-element.44), channel_id=1, replica_groups=mesh['mode'=8,'slab'=4] {'mode','slab'}, dimensions={0} | all-to-all | bytes 2097152 | tf_op jit(solution)/shard_map/all_to_all | solution.py:775
  142.7 3.9 %collective-permute-start.9 = (bf16[1024,128]{1,0:T(8,128)(2,1)S(1)}, bf16[1024,128]{1,0:T(8,128)(2,1)S(1)}, u32[]{:S(2)}, u32[]{:S(2)}) collective-permute-start(bf16[1024,128]{1,0:T(8,128)(2,1)S(1)} %get-tuple-element.58), channel_id=1, source_target_pairs={{4,0},{8,4},{12,8},{16,12},{20,16},{24,20},{28,24},{1,28},{5,1},{9... | collective-permute-start | bytes 786440 | tf_op jit(solution)/shard_map/ppermute | solution.py:371
  146.6 5.4 %shard_map.95.inner_ref = f32[1024,512]{1,0:T(8,128)S(1)} custom-call(bf16[8,3,128,1024]{3,2,1,0:T(8,128)(2,1)S(1)} %bitcast.20, bf16[1024,512]{1,0:T(8,128)(2,1)S(1)} %bitcast.23, f32[60,128]{1,0:T(8,128)S(1)} %shard_map.88.weight_ref), custom_call_target="tpu_custom_call" | custom-call | flops 3221225472 | bytes 6291456 | tf_op jit(solution)/shard_map/pallas_call | solution.py:378
  153.5 2.2 %collective-permute-done.9.below_ref = bf16[1024,128]{1,0:T(8,128)(2,1)S(1)} collective-permute-done((bf16[1024,128]{1,0:T(8,128)(2,1)S(1)}, bf16[1024,128]{1,0:T(8,128)(2,1)S(1)}, u32[]{:S(2)}, u32[]{:S(2)}) %collective-permute-start.9) | collective-permute-done | bytes 262176 | tf_op jit(solution)/shard_map/ppermute | solution.py:371
  155.8 3.0 %shard_map.96 = bf16[1024,512]{1,0:T(8,128)(2,1)} custom-call(bf16[8,3,128,1024]{3,2,1,0:T(8,128)(2,1)S(1)} %bitcast.20, bf16[1024,128]{1,0:T(8,128)(2,1)S(1)} %collective-permute-done.8.above_ref, bf16[1024,128]{1,0:T(8,128)(2,1)S(1)} %collective-permute-done.9.below_ref, f32[60,128]{1,0:T(8,128)S(1)} %shard_map.88.weight_ref, ...), custom_call_target="tpu_custom_call" | custom-call | tf_op jit(solution)/shard_map/pallas_call | solution.py:392
  158.8 3.0 %all-to-all-start.3 = ((bf16[32,32,512]{2,1,0:T(8,128)(2,1)}), bf16[32,32,512]{2,1,0:T(8,128)(2,1)S(1)}, u32[]{:S(2)}, u32[]{:S(2)}) async-start(bf16[32,32,512]{2,1,0:T(8,128)(2,1)} %bitcast.10), calls=%async_computation.3 | async-start | bytes 2097152 | tf_op jit(solution)/shard_map/all_to_all | solution.py:779
  161.8 1.6 copy-done.12
  163.4 2.7 %shard_map.94.base_ref = f32[4,32,32,128]{3,2,1,0:T(8,128)S(1)} custom-call(f32[4,32,32,128]{3,2,1,0:T(8,128)S(1)} %copy-done.12, f32[4,32,32,128]{3,2,1,0:T(8,128)} %get-tuple-element.43.right_side_ref, f32[5,128,128]{2,1,0:T(8,128)S(1)} %copy-done.8), custom_call_target="tpu_custom_call" | custom-call | bytes 9043968 | tf_op jit(solution)/shard_map/pallas_call | solution.py:575
  167.4 20.6 %all-to-all-done.3.coupled_ref = bf16[32,32,512]{2,1,0:T(8,128)(2,1)S(1)} async-done(((bf16[32,32,512]{2,1,0:T(8,128)(2,1)}), bf16[32,32,512]{2,1,0:T(8,128)(2,1)S(1)}, u32[]{:S(2)}, u32[]{:S(2)}) %all-to-all-start.3) | async-done | bytes 1048608 | tf_op jit(solution)/shard_map/all_to_all | solution.py:779
  188.0 4.1 %shard_map.97 = (f32[4,32,32,128]{3,2,1,0:T(8,128)S(1)}, bf16[1,32,32,128]{3,2,1,0:T(8,128)(2,1)S(1)}, bf16[1,32,32,128]{3,2,1,0:T(8,128)(2,1)S(1)}, bf16[1,32,3...) custom-call(s32[1]{0:T(128)} %bitcast.here_ref, f32[4,32,32,128]{3,2,1,0:T(8,128)} %copy-done.3, ...), custom_call_target="tpu_custom_call" | custom-call | bytes 4194304 | tf_op jit(solution)/shard_map/pallas_call | solution.py:652
  195.1 4.5 %shard_map.98 = bf16[4,32,32,128]{3,2,1,0:T(8,128)(2,1)} custom-call(f32[4,32,32,128]{3,2,1,0:T(8,128)S(1)} %copy-done.13, f32[4,32,32,128]{3,2,1,0:T(8,128)S(1)} %get-tuple-element.45.resid_ref, bf16[256,256]{1,0:T(8,128)(2,1)S(1)} %copy-done.10, bf16[256,256]{1,0:T(8,128)(2,1)S(1)} %copy-done.14, f32[128,128]{1,0:T(8,128)S(1)} %subtract_divide_fusion.scale_ref), custom_call_target="tpu_custom_call" | custom-call | flops 1610612736 | bytes 9043968 | tf_op jit(solution)/shard_map/pallas_call | solution.py:575
  199.6 3.5 %all-to-all-start.4 = ((bf16[128,32,128]{2,1,0:T(8,128)(2,1)}), bf16[128,32,128]{2,1,0:T(8,128)(2,1)S(1)}, u32[]{:S(2)}, u32[]{:S(2)}) async-start(bf16[128,32,128]{2,1,0:T(8,128)(2,1)} %bitcast.11), calls=%async_computation.4 | async-start | bytes 2097152 | tf_op jit(solution)/shard_map/all_to_all | solution.py:730
  203.5 2.5 %collective-permute-done.12 = bf16[1,32,32,128]{3,2,1,0:T(8,128)(2,1)S(1)} collective-permute-done((bf16[1,32,32,128]{3,2,1,0:T(8,128)(2,1)S(1)}, bf16[1,32,32,128]{3,2,1,0:T(8,128)(2,1)S(1)}, u32[]{:S(2)}, u32[]{:S(2)}) %collective-permute-start.12) | collective-permute-done | bytes 262176 | tf_op jit(solution)/shard_map/ppermute | solution.py:697
  207.0 1.8 fusion.11
  208.8 8.8 %all-to-all-done.4 = bf16[128,32,128]{2,1,0:T(8,128)(2,1)S(1)} async-done(((bf16[128,32,128]{2,1,0:T(8,128)(2,1)}), bf16[128,32,128]{2,1,0:T(8,128)(2,1)S(1)}, u32[]{:S(2)}, u32[]{:S(2)}) %all-to-all-start.4) | async-done | bytes 1048608 | tf_op jit(solution)/shard_map/all_to_all | solution.py:730
  217.7 2.2 %fusion.10 = f32[128,32,128]{2,1,0:T(8,128)} fusion(bf16[128,32,128]{2,1,0:T(8,128)(2,1)S(1)} %all-to-all-done.4), kind=kLoop, calls=%fused_computation.16 | loop fusion | flops 4718592 | bytes 3145728 | tf_op jit(solution)/shard_map/mul | solution.py:784
  (91 shorter events, 25.2 us)
Async XLA Ops:
  0.6 10.8 %copy-start.20 = (f32[3,32,128]{2,1,0:T(8,128)S(1)}, f32[3,32,128]{2,1,0:T(8,128)}, u32[]{:S(2)}) copy-start(f32[3,32,128]{2,1,0:T(8,128)} %param.10) | copy-start | bytes 147460
  0.6 10.8 %copy-start.21 = (f32[32,128]{1,0:T(8,128)S(1)}, f32[32,128]{1,0:T(8,128)}, u32[]{:S(2)}) copy-start(f32[32,128]{1,0:T(8,128)} %param.9) | copy-start | bytes 49156
  0.6 10.8 %copy-start.18 = (f32[128,32,128]{2,1,0:T(8,128)S(1)}, f32[128,32,128]{2,1,0:T(8,128)}, u32[]{:S(2)}) copy-start(f32[128,32,128]{2,1,0:T(8,128)} %param.7) | copy-start | bytes 6291460
  4.1 36.5 %all-to-all-start = ((bf16[8,128,512]{2,1,0:T(8,128)(2,1)}), bf16[8,128,512]{2,1,0:T(8,128)(2,1)}, u32[]{:S(2)}, u32[]{:S(2)}) async-start(bf16[8,128,512]{2,1,0:T(8,128)(2,1)} %shard_map.86), calls=%async_computation | async-start | bytes 2097152 | tf_op jit(solution)/shard_map/all_to_all | solution.py:725
  13.0 60.2 %copy-start.2 = (f32[1,36,32,128]{3,2,1,0:T(8,128)}, f32[1,36,32,128]{3,2,1,0:T(8,128)S(1)}, u32[]{:S(2)}) copy-start(f32[1,36,32,128]{3,2,1,0:T(8,128)S(1)} %get-tuple-element.26.refs_0_) | copy-start | bytes 1769476
  13.0 15.3 %collective-permute-start = (f32[1,36,32,128]{3,2,1,0:T(8,128)}, f32[1,36,32,128]{3,2,1,0:T(8,128)S(1)}, u32[]{:S(2)}, u32[]{:S(2)}) collective-permute-start(f32[1,36,32,128]{3,2,1,0:T(8,128)} %get-tuple-element.65), channel_id=1, source_target_pairs={{0,1},{1,2},{2,3},{3,0},{4,5},{5,6},{6,7},{7,4},{8,9},{9,10},{10,1... | collective-permute-start | bytes 1769480 | tf_op jit(solution)/shard_map/ppermute | solution.py:697
  13.0 16.5 %collective-permute-start.1 = (f32[1,36,32,128]{3,2,1,0:T(8,128)}, f32[1,36,32,128]{3,2,1,0:T(8,128)}, u32[]{:S(2)}, u32[]{:S(2)}) collective-permute-start(f32[1,36,32,128]{3,2,1,0:T(8,128)} %get-tuple-element.66), channel_id=1, source_target_pairs={{0,2},{1,3},{2,0},{3,1},{4,6},{5,7},{6,4},{7,5},{8,10},{9,11},{10,... | collective-permute-start | bytes 1769480 | tf_op jit(solution)/shard_map/ppermute | solution.py:697
  14.5 26.1 %collective-permute-start.2 = (f32[1,36,32,128]{3,2,1,0:T(8,128)}, f32[1,36,32,128]{3,2,1,0:T(8,128)}, u32[]{:S(2)}, u32[]{:S(2)}) collective-permute-start(f32[1,36,32,128]{3,2,1,0:T(8,128)} %get-tuple-element.64), channel_id=1, source_target_pairs={{0,3},{1,0},{2,1},{3,2},{4,7},{5,4},{6,5},{7,6},{8,11},{9,8},{10,9... | collective-permute-start | bytes 1769480 | tf_op jit(solution)/shard_map/ppermute | solution.py:697
  18.1 6.9 %copy-start.19 = (f32[128,32,128]{2,1,0:T(8,128)S(1)}, f32[128,32,128]{2,1,0:T(8,128)}, u32[]{:S(2)}) copy-start(f32[128,32,128]{2,1,0:T(8,128)} %param.8) | copy-start | bytes 6291460
  24.0 49.2 %copy-start.15 = (s32[2]{0:T(128)}, s32[2]{0:T(128)S(1)}, u32[]{:S(2)}) copy-start(s32[2]{0:T(128)S(1)} %pad_add_fusion.place_ref) | copy-start | bytes 28
  25.0 35.5 %copy-start.9 = (bf16[256,256]{1,0:T(8,128)(2,1)}, bf16[256,256]{1,0:T(8,128)(2,1)S(1)}, u32[]{:S(2)}) copy-start(bf16[256,256]{1,0:T(8,128)(2,1)S(1)} %get-tuple-element.63.right_ref.refs_9_) | copy-start | bytes 393220
  25.0 35.5 %slice-start = ((s8[6291456]{0:T(1024)(128)(4,1)}), s8[2097152]{0:T(1024)(128)(4,1)S(1)}, s32[]{:S(2)}) async-start(s8[6291456]{0:T(1024)(128)(4,1)} %bitcast.17), calls=%async_computation.5 | async-start | bytes 4194304
  28.3 45.0 %copy-start.4 = (f32[1,36,32,128]{3,2,1,0:T(8,128)}, f32[1,36,32,128]{3,2,1,0:T(8,128)S(1)}, u32[]{:S(2)}) copy-start(f32[1,36,32,128]{3,2,1,0:T(8,128)S(1)} %collective-permute-done.refs_1_) | copy-start | bytes 1769476
  40.6 24.2 %collective-permute-start.5 = (f32[1,32,32,128]{3,2,1,0:T(8,128)}, f32[1,32,32,128]{3,2,1,0:T(8,128)}, u32[]{:S(2)}, u32[]{:S(2)}) collective-permute-start(f32[1,32,32,128]{3,2,1,0:T(8,128)} %get-tuple-element.32), channel_id=1, source_target_pairs={{0,1},{1,2},{2,3},{3,0},{4,5},{5,6},{6,7},{7,4},{8,9},{9,10},{10,1... | collective-permute-start | bytes 1572872 | tf_op jit(solution)/shard_map/ppermute | solution.py:697
  41.4 23.4 %collective-permute-start.6 = (f32[1,32,32,128]{3,2,1,0:T(8,128)}, f32[1,32,32,128]{3,2,1,0:T(8,128)}, u32[]{:S(2)}, u32[]{:S(2)}) collective-permute-start(f32[1,32,32,128]{3,2,1,0:T(8,128)} %get-tuple-element.33), channel_id=1, source_target_pairs={{0,2},{1,3},{2,0},{3,1},{4,6},{5,7},{6,4},{7,5},{8,10},{9,11},{10,... | collective-permute-start | bytes 1572872 | tf_op jit(solution)/shard_map/ppermute | solution.py:697
  42.9 21.9 %collective-permute-start.7 = (f32[1,32,32,128]{3,2,1,0:T(8,128)}, f32[1,32,32,128]{3,2,1,0:T(8,128)}, u32[]{:S(2)}, u32[]{:S(2)}) collective-permute-start(f32[1,32,32,128]{3,2,1,0:T(8,128)} %get-tuple-element.34), channel_id=1, source_target_pairs={{0,3},{1,0},{2,1},{3,2},{4,7},{5,4},{6,5},{7,6},{8,11},{9,8},{10,9... | collective-permute-start | bytes 1572872 | tf_op jit(solution)/shard_map/ppermute | solution.py:697
  44.0 16.5 %collective-permute-start.3 = (bf16[1024,128]{1,0:T(8,128)(2,1)S(1)}, bf16[1024,128]{1,0:T(8,128)(2,1)S(1)}, u32[]{:S(2)}, u32[]{:S(2)}) collective-permute-start(bf16[1024,128]{1,0:T(8,128)(2,1)S(1)} %get-tuple-element.61), channel_id=1, source_target_pairs={{0,4},{4,8},{8,12},{12,16},{16,20},{20,24},{24,28},{28,1},{1,5},{5... | collective-permute-start | bytes 786440 | tf_op jit(solution)/shard_map/ppermute | solution.py:370
  46.0 14.4 %collective-permute-start.4 = (bf16[1024,128]{1,0:T(8,128)(2,1)S(1)}, bf16[1024,128]{1,0:T(8,128)(2,1)S(1)}, u32[]{:S(2)}, u32[]{:S(2)}) collective-permute-start(bf16[1024,128]{1,0:T(8,128)(2,1)S(1)} %get-tuple-element.60), channel_id=1, source_target_pairs={{4,0},{8,4},{12,8},{16,12},{20,16},{24,20},{28,24},{1,28},{5,1},{9... | collective-permute-start | bytes 786440 | tf_op jit(solution)/shard_map/ppermute | solution.py:371
  65.8 39.4 %all-to-all-start.1 = ((bf16[32,32,640]{2,1,0:T(8,128)(2,1)}), bf16[32,32,640]{2,1,0:T(8,128)(2,1)}, u32[]{:S(2)}, u32[]{:S(2)}) async-start(bf16[32,32,640]{2,1,0:T(8,128)(2,1)} %bitcast.21), calls=%async_computation.1 | async-start | bytes 2621440 | tf_op jit(solution)/shard_map/all_to_all | solution.py:769
  75.5 29.7 %copy-start.10 = (bf16[256,256]{1,0:T(8,128)(2,1)S(1)}, bf16[256,256]{1,0:T(8,128)(2,1)}, u32[]{:S(2)}) copy-start(bf16[256,256]{1,0:T(8,128)(2,1)} %copy-done.9) | copy-start | bytes 393220
  75.5 29.7 %copy-start.14 = (bf16[256,256]{1,0:T(8,128)(2,1)S(1)}, bf16[256,256]{1,0:T(8,128)(2,1)}, u32[]{:S(2)}) copy-start(bf16[256,256]{1,0:T(8,128)(2,1)} %get-tuple-element.62.left_ref) | copy-start | bytes 393220
  75.5 71.1 %slice-start.2 = ((s8[6291456]{0:T(1024)(128)(4,1)}), s8[2097152]{0:T(1024)(128)(4,1)S(1)}, s32[]{:S(2)}) async-start(s8[6291456]{0:T(1024)(128)(4,1)} %bitcast.19), calls=%async_computation.7 | async-start | bytes 4194304
  105.2 41.4 %slice-start.3 = ((s8[6291456]{0:T(1024)(128)(4,1)}), s8[4194304]{0:T(1024)(128)(4,1)S(1)}, s32[]{:S(2)}) async-start(s8[6291456]{0:T(1024)(128)(4,1)} %bitcast.19), calls=%async_computation.8 | async-start | bytes 8388608
  111.5 40.5 %copy-start.11 = (f32[4,32,32,128]{3,2,1,0:T(8,128)}, f32[4,32,32,128]{3,2,1,0:T(8,128)S(1)}, u32[]{:S(2)}) copy-start(f32[4,32,32,128]{3,2,1,0:T(8,128)S(1)} %get-tuple-element.42.current_ref) | copy-start | bytes 6291460
  141.2 12.3 %collective-permute-start.8 = (bf16[1024,128]{1,0:T(8,128)(2,1)S(1)}, bf16[1024,128]{1,0:T(8,128)(2,1)S(1)}, u32[]{:S(2)}, u32[]{:S(2)}) collective-permute-start(bf16[1024,128]{1,0:T(8,128)(2,1)S(1)} %get-tuple-element.59), channel_id=1, source_target_pairs={{0,4},{4,8},{8,12},{12,16},{16,20},{20,24},{24,28},{28,1},{1,5},{5... | collective-permute-start | bytes 786440 | tf_op jit(solution)/shard_map/ppermute | solution.py:370
  142.7 13.0 %collective-permute-start.9 = (bf16[1024,128]{1,0:T(8,128)(2,1)S(1)}, bf16[1024,128]{1,0:T(8,128)(2,1)S(1)}, u32[]{:S(2)}, u32[]{:S(2)}) collective-permute-start(bf16[1024,128]{1,0:T(8,128)(2,1)S(1)} %get-tuple-element.58), channel_id=1, source_target_pairs={{4,0},{8,4},{12,8},{16,12},{20,16},{24,20},{28,24},{1,28},{5,1},{9... | collective-permute-start | bytes 786440 | tf_op jit(solution)/shard_map/ppermute | solution.py:371
  158.8 29.3 %all-to-all-start.3 = ((bf16[32,32,512]{2,1,0:T(8,128)(2,1)}), bf16[32,32,512]{2,1,0:T(8,128)(2,1)S(1)}, u32[]{:S(2)}, u32[]{:S(2)}) async-start(bf16[32,32,512]{2,1,0:T(8,128)(2,1)} %bitcast.10), calls=%async_computation.3 | async-start | bytes 2097152 | tf_op jit(solution)/shard_map/all_to_all | solution.py:779
  188.0 7.1 %copy-start.13 = (f32[4,32,32,128]{3,2,1,0:T(8,128)S(1)}, f32[4,32,32,128]{3,2,1,0:T(8,128)}, u32[]{:S(2)}) copy-start(f32[4,32,32,128]{3,2,1,0:T(8,128)} %copy-done.11) | copy-start | bytes 6291460
  192.1 11.2 %collective-permute-start.10 = (bf16[1,32,32,128]{3,2,1,0:T(8,128)(2,1)S(1)}, bf16[1,32,32,128]{3,2,1,0:T(8,128)(2,1)S(1)}, u32[]{:S(2)}, u32[]{:S(2)}) collective-permute-start(bf16[1,32,32,128]{3,2,1,0:T(8,128)(2,1)S(1)} %get-tuple-element.47), channel_id=1, source_target_pairs={{0,1},{1,2},{2,3},{3,0},{4,5},{5,6},{6,7},{7,4},{8,9},{9,10},{10,1... | collective-permute-start | bytes 786440 | tf_op jit(solution)/shard_map/ppermute | solution.py:697
  192.2 11.2 %collective-permute-start.11 = (bf16[1,32,32,128]{3,2,1,0:T(8,128)(2,1)S(1)}, bf16[1,32,32,128]{3,2,1,0:T(8,128)(2,1)S(1)}, u32[]{:S(2)}, u32[]{:S(2)}) collective-permute-start(bf16[1,32,32,128]{3,2,1,0:T(8,128)(2,1)S(1)} %get-tuple-element.48), channel_id=1, source_target_pairs={{0,2},{1,3},{2,0},{3,1},{4,6},{5,7},{6,4},{7,5},{8,10},{9,11},{10,... | collective-permute-start | bytes 786440 | tf_op jit(solution)/shard_map/ppermute | solution.py:697
  193.7 12.3 %collective-permute-start.12 = (bf16[1,32,32,128]{3,2,1,0:T(8,128)(2,1)S(1)}, bf16[1,32,32,128]{3,2,1,0:T(8,128)(2,1)S(1)}, u32[]{:S(2)}, u32[]{:S(2)}) collective-permute-start(bf16[1,32,32,128]{3,2,1,0:T(8,128)(2,1)S(1)} %get-tuple-element.49), channel_id=1, source_target_pairs={{0,3},{1,0},{2,1},{3,2},{4,7},{5,4},{6,5},{7,6},{8,11},{9,8},{10,9... | collective-permute-start | bytes 786440 | tf_op jit(solution)/shard_map/ppermute | solution.py:697
  199.6 18.0 %all-to-all-start.4 = ((bf16[128,32,128]{2,1,0:T(8,128)(2,1)}), bf16[128,32,128]{2,1,0:T(8,128)(2,1)S(1)}, u32[]{:S(2)}, u32[]{:S(2)}) async-start(bf16[128,32,128]{2,1,0:T(8,128)(2,1)} %bitcast.11), calls=%async_computation.4 | async-start | bytes 2097152 | tf_op jit(solution)/shard_map/all_to_all | solution.py:730
  (11 other events, 30.8 us)

commit v17 on v13

--- a/solution.py
+++ b/solution.py
@@ -610,7 +610,7 @@
             out_specs=[slab] * 3,
         ),
         out_shape=[shape] * 3,
-        compiler_params=pltpu.CompilerParams(vmem_limit_bytes=SHARED_VMEM_BYTES),
+        compiler_params=pltpu.CompilerParams(vmem_limit_bytes=VMEM_BYTES),
     )(place, *current_parts, *right_side_parts, weights, right)
 
 
@@ -746,14 +746,14 @@
     high = lax.ppermute(coefs[0, :, 0], "slab", [(b, a) for a, b in forward])
     strip_weights = strip_weights_of(coefs[0], low, high, place, slab_count, height)
 
-    state, matrix, strip_weights = lax.optimization_barrier((state, matrix, strip_weights))
-    borders = (state[:, :cols], state[:, -cols:])
-
     guess_parts = parts_of(guess.reshape(slab_count, share, rows, cols), "slab")
     guess_parts = [jnp.concatenate([part, coefs], axis=1) for part in guess_parts]
     guess_parts = moved_parts(guess_parts, "slab")
     right_parts = parts_of(right_side.reshape(slab_count, share, rows, cols), "slab")
-    guess_parts, right_parts, _ = lax.optimization_barrier((guess_parts, right_parts, borders))
+    state, guess_parts, right_parts, strip_weights = lax.optimization_barrier(
+        (state, guess_parts, right_parts, strip_weights)
+    )
+    borders = (state[:, :cols], state[:, -cols:])
     right_parts = moved_parts(right_parts, "slab")
     mean_weights = mean_weights_of(guess_parts, place, fields + 1)
 

time: 226 us -> 222 us (0.982)
  local copies, waits for them, and re-layouts: 20.8 us -> 14 us
    ppermute x9, waiting for transfers between devices: 6.21 us -> 14.7 us  [onwards(): lax.ppermute(part, axis, [(i, (i + shift) % count) for i in range(count)])]
    all_to_all x1, waiting for transfers between devices: 7.82 us -> 0.01 us  [local(): state = lax.all_to_all(strips, 'mode', 0, 0, tiled=True)]
    unnamed x54 -> x50, local copies, waits for them, and re-layouts: 14.7 us -> 9.38 us
  transfers between devices with their start and end apart: 19 -> 19, of which waited for: 8 -> 9; matrix products, arithmetic and copies ran while one was open for 5% -> 4% of each run, Pallas kernels for 15% -> 16%
where the time goes in v17:
time: 222 us
  waiting for transfers between devices  72.3 us (33%)
  Pallas kernels  51.4 us (23%)
  starting transfers between devices  45.8 us (21%)
  blocking collectives  29.6 us (13%)
  local copies, waits for them, and re-layouts  14 us (6%)
  other arithmetic  7.45 us (3%)
    all_to_all x2, waiting for transfers between devices, local(): lax.all_to_all(sums, both, 0, 0, tiled=True).reshape(devices, share, -1)  45 us
    all_to_all x1, blocking collectives, local(): state = lax.all_to_all(state, both, 0, 0, tiled=True)  29.6 us
    ppermute x9, waiting for transfers between devices, onwards(): lax.ppermute(part, axis, [(i, (i + shift) % count) for i in range(count)])  14.7 us
    pallas_call x3, Pallas kernels, per_group(): pl.pallas_call(kernel, grid=(groups,), in_specs=in_specs, out_specs=out_s...  13.5 us
    pallas_call x2, Pallas kernels, coupled_sums(): pl.pallas_call(functools.partial(inner_kernel, height, cols), grid=(block...  12.1 us
    all_to_all x2, starting transfers between devices, local(): lax.all_to_all(sums, both, 0, 0, tiled=True).reshape(devices, share, -1)  11.5 us
    ppermute x9, starting transfers between devices, onwards(): lax.ppermute(part, axis, [(i, (i + shift) % count) for i in range(count)])  10.1 us
    unnamed x50, local copies, waits for them, and re-layouts  9.38 us
  transfers between devices with their start and end apart: 19, of which 9 were waited for; matrix products, arithmetic and copies ran while one was open for 4% of the time, Pallas kernels for 16%

profile of v17, /device:TPU:0, one launch (start us, length us, event | category | flops | bytes accessed | tf_op | source)
XLA Modules:
  0.0 221.7 jit_solution(16131368119235004446)
XLA Ops:
  0.7 3.5 %shard_map.86 = bf16[8,128,512]{2,1,0:T(8,128)(2,1)} custom-call(f32[4096,128]{1,0:T(8,128)} %bitcast.25), custom_call_target="tpu_custom_call" | custom-call | tf_op jit(solution)/shard_map/pallas_call | solution.py:216
  4.1 7.3 %all-to-all-start = ((bf16[8,128,512]{2,1,0:T(8,128)(2,1)}), bf16[8,128,512]{2,1,0:T(8,128)(2,1)}, u32[]{:S(2)}, u32[]{:S(2)}) async-start(bf16[8,128,512]{2,1,0:T(8,128)(2,1)} %shard_map.86), calls=%async_computation | async-start | bytes 2097152 | tf_op jit(solution)/shard_map/all_to_all | solution.py:733
  19.5 3.0 %constant_dynamic-slice_fusion = (f32[1,32,32,128]{3,2,1,0:T(8,128)}, f32[1,32,32,128]{3,2,1,0:T(8,128)}, f32[1,32,32,128]{3,2,1,0:T(8,128)}, f32[1,32,32,128]{3,2,1,0:T(8,128)}) fusion(f32[4,32,32,128]{3,2,1,0:T(8,128)} %bitcast.27, s32[]{:T(128)S(6)} %select_n.40, s32[]{:T(128)S(6)} %select_n.39, s32[]{:T(128)S(6)} %select_n.38, s32[]{:T(128)S(6)} %select_n.37), kind=kLoop, calls=%fused_computation.39 | loop fusion | bytes 4194320 | tf_op jit(solution)/shard_map/jit(dynamic_index_in_dim)/dynamic_slice | solution.py:711
  22.8 2.8 %shard_map.88.matrix_ref = bf16[8,3,128,1024]{3,2,1,0:T(8,128)(2,1)S(1)} custom-call(s32[8,16]{1,0:T(8,128)S(1)} %copy-done.18, s32[8]{0:T(128)S(1)} %copy-done.19, bf16[8,16,128,128]{3,2,1,0:T(8,128)(2,1)S(1)} %copy-done.5), custom_call_target="tpu_custom_call" | custom-call | tf_op jit(solution)/shard_map/pallas_call | solution.py:243
  25.6 2.7 %copy-done = bf16[8,3,128,1024]{3,2,1,0:T(8,128)(2,1)} copy-done((bf16[8,3,128,1024]{3,2,1,0:T(8,128)(2,1)}, bf16[8,3,128,1024]{3,2,1,0:T(8,128)(2,1)S(1)}, u32[]{:S(2)}) %copy-start) | copy-done | bytes 6291480
  29.3 11.1 %collective-permute-done.2.refs_3_ = f32[1,36,32,128]{3,2,1,0:T(8,128)S(1)} collective-permute-done((f32[1,36,32,128]{3,2,1,0:T(8,128)S(1)}, f32[1,36,32,128]{3,2,1,0:T(8,128)S(1)}, u32[]{:S(2)}, u32[]{:S(2)}) %collective-permute-start.2) | collective-permute-done | bytes 589856 | tf_op jit(solution)/shard_map/ppermute | solution.py:704
  40.4 1.6 collective-permute-start.7
  45.7 2.1 collective-permute-start.5
  47.7 3.3 %collective-permute-start.6 = (bf16[1024,128]{1,0:T(8,128)(2,1)S(1)}, bf16[1024,128]{1,0:T(8,128)(2,1)S(1)}, u32[]{:S(2)}, u32[]{:S(2)}) collective-permute-start(bf16[1024,128]{1,0:T(8,128)(2,1)S(1)} %get-tuple-element.66), channel_id=1, source_target_pairs={{4,0},{8,4},{12,8},{16,12},{20,16},{24,20},{28,24},{1,28},{5,1},{9... | collective-permute-start | bytes 786440 | tf_op jit(solution)/shard_map/ppermute | solution.py:378
  51.1 2.8 %copy-done.1 = bf16[8,3,128,1024]{3,2,1,0:T(8,128)(2,1)S(1)} copy-done((bf16[8,3,128,1024]{3,2,1,0:T(8,128)(2,1)S(1)}, bf16[8,3,128,1024]{3,2,1,0:T(8,128)(2,1)}, u32[]{:S(2)}) %copy-start.1) | copy-done | bytes 6291480
  53.9 6.7 %shard_map.89.inner_ref = f32[1024,512]{1,0:T(8,128)S(1)} custom-call(bf16[8,3,128,1024]{3,2,1,0:T(8,128)(2,1)S(1)} %copy-done.1, bf16[1024,512]{1,0:T(8,128)(2,1)} %bitcast.5.state_ref, f32[60,128]{1,0:T(8,128)S(1)} %shard_map.87.weight_ref), custom_call_target="tpu_custom_call" | custom-call | flops 3221225472 | bytes 6291456 | tf_op jit(solution)/shard_map/pallas_call | solution.py:385
  60.6 5.1 %shard_map.90 = bf16[1024,640]{1,0:T(8,128)(2,1)} custom-call(bf16[8,3,128,1024]{3,2,1,0:T(8,128)(2,1)S(1)} %copy-done.2, bf16[1024,128]{1,0:T(8,128)(2,1)S(1)} %collective-permute-done.5.above_ref, bf16[1024,128]{1,0:T(8,128)(2,1)S(1)} %collective-permute-done.6.below_ref, f32[60,128]{1,0:T(8,128)S(1)} %shard_map.87.weight_ref, ...), custom_call_target="tpu_custom_call" | custom-call | tf_op jit(solution)/shard_map/pallas_call | solution.py:399
  66.4 8.4 %all-to-all-start.1 = ((bf16[32,32,640]{2,1,0:T(8,128)(2,1)}), bf16[32,32,640]{2,1,0:T(8,128)(2,1)}, u32[]{:S(2)}, u32[]{:S(2)}) async-start(bf16[32,32,640]{2,1,0:T(8,128)(2,1)} %bitcast.11), calls=%async_computation.1 | async-start | bytes 2621440 | tf_op jit(solution)/shard_map/all_to_all | solution.py:786
  76.5 6.1 %shard_map.92 = (f32[4,32,32,128]{3,2,1,0:T(8,128)}, f32[4,32,32,128]{3,2,1,0:T(8,128)}, f32[4,32,32,128]{3,2,1,0:T(8,128)}) custom-call(s32[2]{0:T(128)} %copy-done.17, f32[1,36,32,128]{3,2,1,0:T(8,128)} %copy-done.4, f32[1,36,32,128]{3,2,1,0:T(8,128)} %copy-done.8, f32[1,36,32,128]{3,2,1,0:T(8,128)} %copy-done.9, f32[1,36,32,128]{3,2,1,0:T(8,128)} %copy-done.10, ...), custom_call_target="tpu_custom_call" | custom-call | tf_op jit(solution)/shard_map/pallas_call | solution.py:600
  82.6 24.4 %all-to-all-done.1.coupled_ref = bf16[32,32,640]{2,1,0:T(8,128)(2,1)} async-done(((bf16[32,32,640]{2,1,0:T(8,128)(2,1)}), bf16[32,32,640]{2,1,0:T(8,128)(2,1)}, u32[]{:S(2)}, u32[]{:S(2)}) %all-to-all-start.1) | async-done | bytes 1310752 | tf_op jit(solution)/shard_map/all_to_all | solution.py:786
  107.0 6.3 %shard_map.93 = (f32[4,32,32,128]{3,2,1,0:T(8,128)S(1)}, bf16[32,32,512]{2,1,0:T(8,128)(2,1)S(1)}) custom-call(f32[4,32,32,128]{3,2,1,0:T(8,128)} %get-tuple-element.45.current_ref, f32[4,32,32,128]{3,2,1,0:T(8,128)} %get-tuple-element.46.base_ref, bf16[32,32,640]{2,1,0:T(8,128)(2,1)} %all-to-all-done.1.coupled_ref, bf16[256,256]{1,0:T(8,128)(2,1)S(1)} %copy-done.12, ...), custom_call_target="tpu_custom_call" | custom-call | flops 1610612736 | bytes 11665408 | tf_op jit(solution)/shard_map/pallas_call | solution.py:582
  113.4 29.6 %all_to_all.36 = bf16[32,32,512]{2,1,0:T(8,128)(2,1)S(1)} all-to-all(bf16[32,32,512]{2,1,0:T(8,128)(2,1)S(1)} %get-tuple-element.50), channel_id=1, replica_groups=mesh['mode'=8,'slab'=4] {'mode','slab'}, dimensions={0} | all-to-all | bytes 2097152 | tf_op jit(solution)/shard_map/all_to_all | solution.py:792
  144.5 3.9 %collective-permute-start.11 = (bf16[1024,128]{1,0:T(8,128)(2,1)S(1)}, bf16[1024,128]{1,0:T(8,128)(2,1)S(1)}, u32[]{:S(2)}, u32[]{:S(2)}) collective-permute-start(bf16[1024,128]{1,0:T(8,128)(2,1)S(1)} %get-tuple-element.64), channel_id=1, source_target_pairs={{4,0},{8,4},{12,8},{16,12},{20,16},{24,20},{28,24},{1,28},{5,1},{9... | collective-permute-start | bytes 786440 | tf_op jit(solution)/shard_map/ppermute | solution.py:378
  148.4 5.4 %shard_map.95.inner_ref = f32[1024,512]{1,0:T(8,128)S(1)} custom-call(bf16[8,3,128,1024]{3,2,1,0:T(8,128)(2,1)S(1)} %bitcast.21, bf16[1024,512]{1,0:T(8,128)(2,1)S(1)} %bitcast.23, f32[60,128]{1,0:T(8,128)S(1)} %shard_map.87.weight_ref), custom_call_target="tpu_custom_call" | custom-call | flops 3221225472 | bytes 6291456 | tf_op jit(solution)/shard_map/pallas_call | solution.py:385
  155.3 2.2 collective-permute-done.11.below_ref
  157.6 3.0 %shard_map.96 = bf16[1024,512]{1,0:T(8,128)(2,1)} custom-call(bf16[8,3,128,1024]{3,2,1,0:T(8,128)(2,1)S(1)} %bitcast.21, bf16[1024,128]{1,0:T(8,128)(2,1)S(1)} %collective-permute-done.10.above_ref, bf16[1024,128]{1,0:T(8,128)(2,1)S(1)} %collective-permute-done.11.below_ref, f32[60,128]{1,0:T(8,128)S(1)} %shard_map.87.weight_ref, ...), custom_call_target="tpu_custom_call" | custom-call | tf_op jit(solution)/shard_map/pallas_call | solution.py:399
  160.6 3.0 %all-to-all-start.3 = ((bf16[32,32,512]{2,1,0:T(8,128)(2,1)}), bf16[32,32,512]{2,1,0:T(8,128)(2,1)S(1)}, u32[]{:S(2)}, u32[]{:S(2)}) async-start(bf16[32,32,512]{2,1,0:T(8,128)(2,1)} %bitcast.13), calls=%async_computation.3 | async-start | bytes 2097152 | tf_op jit(solution)/shard_map/all_to_all | solution.py:799
  163.6 1.6 copy-done.14
  165.2 2.7 %shard_map.94.base_ref = f32[4,32,32,128]{3,2,1,0:T(8,128)S(1)} custom-call(f32[4,32,32,128]{3,2,1,0:T(8,128)S(1)} %copy-done.14, f32[4,32,32,128]{3,2,1,0:T(8,128)} %get-tuple-element.49.right_side_ref, f32[5,128,128]{2,1,0:T(8,128)S(1)} %copy-done.7), custom_call_target="tpu_custom_call" | custom-call | bytes 9043968 | tf_op jit(solution)/shard_map/pallas_call | solution.py:582
  169.2 20.6 %all-to-all-done.3.coupled_ref = bf16[32,32,512]{2,1,0:T(8,128)(2,1)S(1)} async-done(((bf16[32,32,512]{2,1,0:T(8,128)(2,1)}), bf16[32,32,512]{2,1,0:T(8,128)(2,1)S(1)}, u32[]{:S(2)}, u32[]{:S(2)}) %all-to-all-start.3) | async-done | bytes 1048608 | tf_op jit(solution)/shard_map/all_to_all | solution.py:799
  189.8 4.1 %shard_map.97 = (f32[4,32,32,128]{3,2,1,0:T(8,128)S(1)}, bf16[1,32,32,128]{3,2,1,0:T(8,128)(2,1)S(1)}, bf16[1,32,32,128]{3,2,1,0:T(8,128)(2,1)S(1)}, bf16[1,32,3...) custom-call(s32[1]{0:T(128)} %bitcast.here_ref, f32[4,32,32,128]{3,2,1,0:T(8,128)} %copy-done.3, ...), custom_call_target="tpu_custom_call" | custom-call | bytes 4194304 | tf_op jit(solution)/shard_map/pallas_call | solution.py:659
  196.9 4.5 %shard_map.98 = bf16[4,32,32,128]{3,2,1,0:T(8,128)(2,1)} custom-call(f32[4,32,32,128]{3,2,1,0:T(8,128)S(1)} %copy-done.15, f32[4,32,32,128]{3,2,1,0:T(8,128)S(1)} %get-tuple-element.51.resid_ref, bf16[256,256]{1,0:T(8,128)(2,1)S(1)} %copy-done.12, bf16[256,256]{1,0:T(8,128)(2,1)S(1)} %copy-done.16, f32[128,128]{1,0:T(8,128)S(1)} %subtract_divide_fusion.scale_ref), custom_call_target="tpu_custom_call" | custom-call | flops 1610612736 | bytes 9043968 | tf_op jit(solution)/shard_map/pallas_call | solution.py:582
  201.4 3.5 %all-to-all-start.4 = ((bf16[128,32,128]{2,1,0:T(8,128)(2,1)}), bf16[128,32,128]{2,1,0:T(8,128)(2,1)S(1)}, u32[]{:S(2)}, u32[]{:S(2)}) async-start(bf16[128,32,128]{2,1,0:T(8,128)(2,1)} %bitcast.14), calls=%async_computation.4 | async-start | bytes 2097152 | tf_op jit(solution)/shard_map/all_to_all | solution.py:738
  205.3 2.5 %collective-permute-done.14 = bf16[1,32,32,128]{3,2,1,0:T(8,128)(2,1)S(1)} collective-permute-done((bf16[1,32,32,128]{3,2,1,0:T(8,128)(2,1)S(1)}, bf16[1,32,32,128]{3,2,1,0:T(8,128)(2,1)S(1)}, u32[]{:S(2)}, u32[]{:S(2)}) %collective-permute-start.14) | collective-permute-done | bytes 262176 | tf_op jit(solution)/shard_map/ppermute | solution.py:704
  208.8 1.8 fusion.11
  210.6 8.8 %all-to-all-done.4 = bf16[128,32,128]{2,1,0:T(8,128)(2,1)S(1)} async-done(((bf16[128,32,128]{2,1,0:T(8,128)(2,1)}), bf16[128,32,128]{2,1,0:T(8,128)(2,1)S(1)}, u32[]{:S(2)}, u32[]{:S(2)}) %all-to-all-start.4) | async-done | bytes 1048608 | tf_op jit(solution)/shard_map/all_to_all | solution.py:738
  219.5 2.2 fusion.10
  (93 shorter events, 24.0 us)
Async XLA Ops:
  0.6 10.8 %copy-start.20 = (f32[128,32,128]{2,1,0:T(8,128)S(1)}, f32[128,32,128]{2,1,0:T(8,128)}, u32[]{:S(2)}) copy-start(f32[128,32,128]{2,1,0:T(8,128)} %param.7) | copy-start | bytes 6291460
  4.1 36.3 %all-to-all-start = ((bf16[8,128,512]{2,1,0:T(8,128)(2,1)}), bf16[8,128,512]{2,1,0:T(8,128)(2,1)}, u32[]{:S(2)}, u32[]{:S(2)}) async-start(bf16[8,128,512]{2,1,0:T(8,128)(2,1)} %shard_map.86), calls=%async_computation | async-start | bytes 2097152 | tf_op jit(solution)/shard_map/all_to_all | solution.py:733
  12.9 62.1 %copy-start.4 = (f32[1,36,32,128]{3,2,1,0:T(8,128)}, f32[1,36,32,128]{3,2,1,0:T(8,128)S(1)}, u32[]{:S(2)}) copy-start(f32[1,36,32,128]{3,2,1,0:T(8,128)S(1)} %get-tuple-element.31.refs_0_) | copy-start | bytes 1769476
  12.9 16.0 %collective-permute-start = (f32[1,36,32,128]{3,2,1,0:T(8,128)}, f32[1,36,32,128]{3,2,1,0:T(8,128)S(1)}, u32[]{:S(2)}, u32[]{:S(2)}) collective-permute-start(f32[1,36,32,128]{3,2,1,0:T(8,128)} %get-tuple-element.73), channel_id=1, source_target_pairs={{0,1},{1,2},{2,3},{3,0},{4,5},{5,6},{6,7},{7,4},{8,9},{9,10},{10,1... | collective-permute-start | bytes 1769480 | tf_op jit(solution)/shard_map/ppermute | solution.py:704
  12.9 16.4 %collective-permute-start.1 = (f32[1,36,32,128]{3,2,1,0:T(8,128)}, f32[1,36,32,128]{3,2,1,0:T(8,128)S(1)}, u32[]{:S(2)}, u32[]{:S(2)}) collective-permute-start(f32[1,36,32,128]{3,2,1,0:T(8,128)} %get-tuple-element.74), channel_id=1, source_target_pairs={{0,2},{1,3},{2,0},{3,1},{4,6},{5,7},{6,4},{7,5},{8,10},{9,11},{10,... | collective-permute-start | bytes 1769480 | tf_op jit(solution)/shard_map/ppermute | solution.py:704
  14.4 26.0 %collective-permute-start.2 = (f32[1,36,32,128]{3,2,1,0:T(8,128)S(1)}, f32[1,36,32,128]{3,2,1,0:T(8,128)S(1)}, u32[]{:S(2)}, u32[]{:S(2)}) collective-permute-start(f32[1,36,32,128]{3,2,1,0:T(8,128)S(1)} %get-tuple-element.72), channel_id=1, source_target_pairs={{0,3},{1,0},{2,1},{3,2},{4,7},{5,4},{6,5},{7,6},{8,11},{9,8},{10,9... | collective-permute-start | bytes 1769480 | tf_op jit(solution)/shard_map/ppermute | solution.py:704
  15.9 12.4 %collective-permute-start.3 = (f32[4,128]{1,0:T(4,128)S(1)}, f32[4,128]{1,0:T(4,128)S(1)}, u32[]{:S(2)}, u32[]{:S(2)}) collective-permute-start(f32[4,128]{1,0:T(4,128)S(1)} %bitcast.30), channel_id=1, source_target_pairs={{0,1},{1,2},{2,3},{4,5},{5,6},{6,7},{8,9},{9,10},{10,11},{12,13},{... | collective-permute-start | bytes 6152 | tf_op jit(solution)/shard_map/ppermute | solution.py:745
  17.1 11.1 %collective-permute-start.4 = (f32[4,128]{1,0:T(4,128)S(1)}, f32[4,128]{1,0:T(4,128)S(1)}, u32[]{:S(2)}, u32[]{:S(2)}) collective-permute-start(f32[4,128]{1,0:T(4,128)S(1)} %bitcast.29), channel_id=1, source_target_pairs={{1,0},{2,1},{3,2},{5,4},{6,5},{7,6},{9,8},{10,9},{11,10},{13,12},{... | collective-permute-start | bytes 6152 | tf_op jit(solution)/shard_map/ppermute | solution.py:746
  19.4 41.2 %copy-start.11 = (bf16[256,256]{1,0:T(8,128)(2,1)}, bf16[256,256]{1,0:T(8,128)(2,1)S(1)}, u32[]{:S(2)}) copy-start(bf16[256,256]{1,0:T(8,128)(2,1)S(1)} %get-tuple-element.69.right_ref.refs_9_) | copy-start | bytes 393220
  22.8 52.2 %copy-start.17 = (s32[2]{0:T(128)}, s32[2]{0:T(128)S(1)}, u32[]{:S(2)}) copy-start(s32[2]{0:T(128)S(1)} %pad_add_fusion.place_ref) | copy-start | bytes 28
  28.9 46.1 %copy-start.8 = (f32[1,36,32,128]{3,2,1,0:T(8,128)}, f32[1,36,32,128]{3,2,1,0:T(8,128)S(1)}, u32[]{:S(2)}) copy-start(f32[1,36,32,128]{3,2,1,0:T(8,128)S(1)} %collective-permute-done.refs_1_) | copy-start | bytes 1769476
  29.3 45.8 %copy-start.9 = (f32[1,36,32,128]{3,2,1,0:T(8,128)}, f32[1,36,32,128]{3,2,1,0:T(8,128)S(1)}, u32[]{:S(2)}) copy-start(f32[1,36,32,128]{3,2,1,0:T(8,128)S(1)} %collective-permute-done.1.refs_2_) | copy-start | bytes 1769476
  40.4 34.7 %copy-start.10 = (f32[1,36,32,128]{3,2,1,0:T(8,128)}, f32[1,36,32,128]{3,2,1,0:T(8,128)S(1)}, u32[]{:S(2)}) copy-start(f32[1,36,32,128]{3,2,1,0:T(8,128)S(1)} %collective-permute-done.2.refs_3_) | copy-start | bytes 1769476
  40.4 25.3 %collective-permute-start.7 = (f32[1,32,32,128]{3,2,1,0:T(8,128)}, f32[1,32,32,128]{3,2,1,0:T(8,128)}, u32[]{:S(2)}, u32[]{:S(2)}) collective-permute-start(f32[1,32,32,128]{3,2,1,0:T(8,128)} %get-tuple-element.38), channel_id=1, source_target_pairs={{0,1},{1,2},{2,3},{3,0},{4,5},{5,6},{6,7},{7,4},{8,9},{9,10},{10,1... | collective-permute-start | bytes 1572872 | tf_op jit(solution)/shard_map/ppermute | solution.py:704
  42.0 23.8 %collective-permute-start.8 = (f32[1,32,32,128]{3,2,1,0:T(8,128)}, f32[1,32,32,128]{3,2,1,0:T(8,128)}, u32[]{:S(2)}, u32[]{:S(2)}) collective-permute-start(f32[1,32,32,128]{3,2,1,0:T(8,128)} %get-tuple-element.39), channel_id=1, source_target_pairs={{0,2},{1,3},{2,0},{3,1},{4,6},{5,7},{6,4},{7,5},{8,10},{9,11},{10,... | collective-permute-start | bytes 1572872 | tf_op jit(solution)/shard_map/ppermute | solution.py:704
  43.2 23.2 %collective-permute-start.9 = (f32[1,32,32,128]{3,2,1,0:T(8,128)}, f32[1,32,32,128]{3,2,1,0:T(8,128)}, u32[]{:S(2)}, u32[]{:S(2)}) collective-permute-start(f32[1,32,32,128]{3,2,1,0:T(8,128)} %get-tuple-element.40), channel_id=1, source_target_pairs={{0,3},{1,0},{2,1},{3,2},{4,7},{5,4},{6,5},{7,6},{8,11},{9,8},{10,9... | collective-permute-start | bytes 1572872 | tf_op jit(solution)/shard_map/ppermute | solution.py:704
  45.7 14.9 %collective-permute-start.5 = (bf16[1024,128]{1,0:T(8,128)(2,1)S(1)}, bf16[1024,128]{1,0:T(8,128)(2,1)S(1)}, u32[]{:S(2)}, u32[]{:S(2)}) collective-permute-start(bf16[1024,128]{1,0:T(8,128)(2,1)S(1)} %get-tuple-element.67), channel_id=1, source_target_pairs={{0,4},{4,8},{8,12},{12,16},{16,20},{20,24},{24,28},{28,1},{1,5},{5... | collective-permute-start | bytes 786440 | tf_op jit(solution)/shard_map/ppermute | solution.py:377
  47.7 12.9 %collective-permute-start.6 = (bf16[1024,128]{1,0:T(8,128)(2,1)S(1)}, bf16[1024,128]{1,0:T(8,128)(2,1)S(1)}, u32[]{:S(2)}, u32[]{:S(2)}) collective-permute-start(bf16[1024,128]{1,0:T(8,128)(2,1)S(1)} %get-tuple-element.66), channel_id=1, source_target_pairs={{4,0},{8,4},{12,8},{16,12},{20,16},{24,20},{28,24},{1,28},{5,1},{9... | collective-permute-start | bytes 786440 | tf_op jit(solution)/shard_map/ppermute | solution.py:378
  66.4 40.6 %all-to-all-start.1 = ((bf16[32,32,640]{2,1,0:T(8,128)(2,1)}), bf16[32,32,640]{2,1,0:T(8,128)(2,1)}, u32[]{:S(2)}, u32[]{:S(2)}) async-start(bf16[32,32,640]{2,1,0:T(8,128)(2,1)} %bitcast.11), calls=%async_computation.1 | async-start | bytes 2621440 | tf_op jit(solution)/shard_map/all_to_all | solution.py:786
  76.5 30.5 %copy-start.12 = (bf16[256,256]{1,0:T(8,128)(2,1)S(1)}, bf16[256,256]{1,0:T(8,128)(2,1)}, u32[]{:S(2)}) copy-start(bf16[256,256]{1,0:T(8,128)(2,1)} %copy-done.11) | copy-start | bytes 393220
  76.5 30.5 %copy-start.16 = (bf16[256,256]{1,0:T(8,128)(2,1)S(1)}, bf16[256,256]{1,0:T(8,128)(2,1)}, u32[]{:S(2)}) copy-start(bf16[256,256]{1,0:T(8,128)(2,1)} %get-tuple-element.68.left_ref) | copy-start | bytes 393220
  76.5 71.9 %slice-start = ((s8[6291456]{0:T(1024)(128)(4,1)}), s8[2097152]{0:T(1024)(128)(4,1)S(1)}, s32[]{:S(2)}) async-start(s8[6291456]{0:T(1024)(128)(4,1)} %bitcast.20), calls=%async_computation.5 | async-start | bytes 4194304
  107.0 41.4 %slice-start.1 = ((s8[6291456]{0:T(1024)(128)(4,1)}), s8[4194304]{0:T(1024)(128)(4,1)S(1)}, s32[]{:S(2)}) async-start(s8[6291456]{0:T(1024)(128)(4,1)} %bitcast.20), calls=%async_computation.6 | async-start | bytes 8388608
  113.3 40.5 %copy-start.13 = (f32[4,32,32,128]{3,2,1,0:T(8,128)}, f32[4,32,32,128]{3,2,1,0:T(8,128)S(1)}, u32[]{:S(2)}) copy-start(f32[4,32,32,128]{3,2,1,0:T(8,128)S(1)} %get-tuple-element.48.current_ref) | copy-start | bytes 6291460
  143.0 12.3 %collective-permute-start.10 = (bf16[1024,128]{1,0:T(8,128)(2,1)S(1)}, bf16[1024,128]{1,0:T(8,128)(2,1)S(1)}, u32[]{:S(2)}, u32[]{:S(2)}) collective-permute-start(bf16[1024,128]{1,0:T(8,128)(2,1)S(1)} %get-tuple-element.65), channel_id=1, source_target_pairs={{0,4},{4,8},{8,12},{12,16},{16,20},{20,24},{24,28},{28,1},{1,5},{5... | collective-permute-start | bytes 786440 | tf_op jit(solution)/shard_map/ppermute | solution.py:377
  144.5 13.0 %collective-permute-start.11 = (bf16[1024,128]{1,0:T(8,128)(2,1)S(1)}, bf16[1024,128]{1,0:T(8,128)(2,1)S(1)}, u32[]{:S(2)}, u32[]{:S(2)}) collective-permute-start(bf16[1024,128]{1,0:T(8,128)(2,1)S(1)} %get-tuple-element.64), channel_id=1, source_target_pairs={{4,0},{8,4},{12,8},{16,12},{20,16},{24,20},{28,24},{1,28},{5,1},{9... | collective-permute-start | bytes 786440 | tf_op jit(solution)/shard_map/ppermute | solution.py:378
  160.6 29.3 %all-to-all-start.3 = ((bf16[32,32,512]{2,1,0:T(8,128)(2,1)}), bf16[32,32,512]{2,1,0:T(8,128)(2,1)S(1)}, u32[]{:S(2)}, u32[]{:S(2)}) async-start(bf16[32,32,512]{2,1,0:T(8,128)(2,1)} %bitcast.13), calls=%async_computation.3 | async-start | bytes 2097152 | tf_op jit(solution)/shard_map/all_to_all | solution.py:799
  189.8 7.1 %copy-start.15 = (f32[4,32,32,128]{3,2,1,0:T(8,128)S(1)}, f32[4,32,32,128]{3,2,1,0:T(8,128)}, u32[]{:S(2)}) copy-start(f32[4,32,32,128]{3,2,1,0:T(8,128)} %copy-done.13) | copy-start | bytes 6291460
  193.9 11.2 %collective-permute-start.12 = (bf16[1,32,32,128]{3,2,1,0:T(8,128)(2,1)S(1)}, bf16[1,32,32,128]{3,2,1,0:T(8,128)(2,1)S(1)}, u32[]{:S(2)}, u32[]{:S(2)}) collective-permute-start(bf16[1,32,32,128]{3,2,1,0:T(8,128)(2,1)S(1)} %get-tuple-element.53), channel_id=1, source_target_pairs={{0,1},{1,2},{2,3},{3,0},{4,5},{5,6},{6,7},{7,4},{8,9},{9,10},{10,1... | collective-permute-start | bytes 786440 | tf_op jit(solution)/shard_map/ppermute | solution.py:704
  194.0 11.2 %collective-permute-start.13 = (bf16[1,32,32,128]{3,2,1,0:T(8,128)(2,1)S(1)}, bf16[1,32,32,128]{3,2,1,0:T(8,128)(2,1)S(1)}, u32[]{:S(2)}, u32[]{:S(2)}) collective-permute-start(bf16[1,32,32,128]{3,2,1,0:T(8,128)(2,1)S(1)} %get-tuple-element.54), channel_id=1, source_target_pairs={{0,2},{1,3},{2,0},{3,1},{4,6},{5,7},{6,4},{7,5},{8,10},{9,11},{10,... | collective-permute-start | bytes 786440 | tf_op jit(solution)/shard_map/ppermute | solution.py:704
  195.5 12.3 %collective-permute-start.14 = (bf16[1,32,32,128]{3,2,1,0:T(8,128)(2,1)S(1)}, bf16[1,32,32,128]{3,2,1,0:T(8,128)(2,1)S(1)}, u32[]{:S(2)}, u32[]{:S(2)}) collective-permute-start(bf16[1,32,32,128]{3,2,1,0:T(8,128)(2,1)S(1)} %get-tuple-element.55), channel_id=1, source_target_pairs={{0,3},{1,0},{2,1},{3,2},{4,7},{5,4},{6,5},{7,6},{8,11},{9,8},{10,9... | collective-permute-start | bytes 786440 | tf_op jit(solution)/shard_map/ppermute | solution.py:704
  201.4 18.0 %all-to-all-start.4 = ((bf16[128,32,128]{2,1,0:T(8,128)(2,1)}), bf16[128,32,128]{2,1,0:T(8,128)(2,1)S(1)}, u32[]{:S(2)}, u32[]{:S(2)}) async-start(bf16[128,32,128]{2,1,0:T(8,128)(2,1)} %bitcast.14), calls=%async_computation.4 | async-start | bytes 2097152 | tf_op jit(solution)/shard_map/all_to_all | solution.py:738
  (12 other events, 36.0 us)

commit v18 on v16

--- a/solution.py
+++ b/solution.py
@@ -12,7 +12,7 @@
 VMEM_BYTES = 60 << 20
 SHARED_VMEM_BYTES = 48 << 20
 SMALL_VMEM_BYTES = 9 << 20
-UNROLL = 4
+UNROLL = 2
 
 
 def sine_table(length):

time: 221 us -> 221 us (level)
  transfers between devices with their start and end apart: 17 -> 17, of which waited for: 9 -> 9; matrix products, arithmetic and copies ran while one was open for 4% -> 4% of each run, Pallas kernels for 16% -> 17%
where the time goes in v18:
time: 221 us; the launch traced here: 220 us
  waiting for transfers between devices  73.1 us (33%)
  Pallas kernels  54.5 us (25%)
  starting transfers between devices  39 us (18%)
  blocking collectives  29.6 us (13%)
  local copies, waits for them, and re-layouts  15.3 us (7%)
  other arithmetic  7.52 us (3%)
    all_to_all x2, waiting for transfers between devices, local(): lax.all_to_all(sums, both, 0, 0, tiled=True).reshape(devices, share, -1)  44 us
    all_to_all x1, blocking collectives, local(): state = lax.all_to_all(state, both, 0, 0, tiled=True)  29.6 us
    ppermute x9, waiting for transfers between devices, onwards(): lax.ppermute(part, axis, [(i, (i + shift) % count) for i in range(count)])  17.2 us
    pallas_call x2, Pallas kernels, coupled_sums(): pl.pallas_call(functools.partial(inner_kernel, height, cols), grid=(block...  13.5 us
    pallas_call x3, Pallas kernels, per_group(): pl.pallas_call(kernel, grid=(groups,), in_specs=in_specs, out_specs=out_s...  13.5 us
    unnamed x52, local copies, waits for them, and re-layouts  12.4 us
    all_to_all x2, starting transfers between devices, local(): lax.all_to_all(sums, both, 0, 0, tiled=True).reshape(devices, share, -1)  9.18 us
    all_to_all x1, waiting for transfers between devices, to_slabs(): return lax.all_to_all(flat, 'slab', 0, 0, tiled=True)  8.83 us
  transfers between devices with their start and end apart: 17, of which 9 were waited for; matrix products, arithmetic and copies ran while one was open for 4% of the time, Pallas kernels for 17%

profile of v18, /device:TPU:0, one launch (start us, length us, event | category | flops | bytes accessed | tf_op | source)
XLA Modules:
  0.0 220.2 jit_solution(4377253628921056003)
XLA Ops:
  0.7 3.5 %shard_map.86 = bf16[8,128,512]{2,1,0:T(8,128)(2,1)} custom-call(f32[4096,128]{1,0:T(8,128)} %bitcast.24), custom_call_target="tpu_custom_call" | custom-call | tf_op jit(solution)/shard_map/pallas_call | solution.py:209
  4.1 7.3 %all-to-all-start = ((bf16[8,128,512]{2,1,0:T(8,128)(2,1)}), bf16[8,128,512]{2,1,0:T(8,128)(2,1)}, u32[]{:S(2)}, u32[]{:S(2)}) async-start(bf16[8,128,512]{2,1,0:T(8,128)(2,1)} %shard_map.86), calls=%async_computation | async-start | bytes 2097152 | tf_op jit(solution)/shard_map/all_to_all | solution.py:725
  16.0 2.2 copy-done.6
  18.1 2.7 %shard_map.87.matrix_ref = bf16[8,3,128,1024]{3,2,1,0:T(8,128)(2,1)S(1)} custom-call(s32[8,16]{1,0:T(8,128)S(1)} %copy-done.16, s32[8]{0:T(128)S(1)} %copy-done.17, bf16[8,16,128,128]{3,2,1,0:T(8,128)(2,1)S(1)} %copy-done.6), custom_call_target="tpu_custom_call" | custom-call | tf_op jit(solution)/shard_map/pallas_call | solution.py:236
  20.8 2.7 %copy-done = bf16[8,3,128,1024]{3,2,1,0:T(8,128)(2,1)} copy-done((bf16[8,3,128,1024]{3,2,1,0:T(8,128)(2,1)}, bf16[8,3,128,1024]{3,2,1,0:T(8,128)(2,1)S(1)}, u32[]{:S(2)}) %copy-start) | copy-done | bytes 6291480
  25.9 2.4 %collective-permute-done.refs_1_ = f32[1,36,32,128]{3,2,1,0:T(8,128)S(1)} collective-permute-done((f32[1,36,32,128]{3,2,1,0:T(8,128)}, f32[1,36,32,128]{3,2,1,0:T(8,128)S(1)}, u32[]{:S(2)}, u32[]{:S(2)}) %collective-permute-start) | collective-permute-done | bytes 589856 | tf_op jit(solution)/shard_map/ppermute | solution.py:697
  29.5 11.1 %collective-permute-done.2.refs_3_ = f32[1,36,32,128]{3,2,1,0:T(8,128)} collective-permute-done((f32[1,36,32,128]{3,2,1,0:T(8,128)}, f32[1,36,32,128]{3,2,1,0:T(8,128)}, u32[]{:S(2)}, u32[]{:S(2)}) %collective-permute-start.2) | collective-permute-done | bytes 589856 | tf_op jit(solution)/shard_map/ppermute | solution.py:697
  44.0 2.1 collective-permute-start.3
  46.0 3.3 %collective-permute-start.4 = (bf16[1024,128]{1,0:T(8,128)(2,1)S(1)}, bf16[1024,128]{1,0:T(8,128)(2,1)S(1)}, u32[]{:S(2)}, u32[]{:S(2)}) collective-permute-start(bf16[1024,128]{1,0:T(8,128)(2,1)S(1)} %get-tuple-element.60), channel_id=1, source_target_pairs={{4,0},{8,4},{12,8},{16,12},{20,16},{24,20},{28,24},{1,28},{5,1},{9... | collective-permute-start | bytes 786440 | tf_op jit(solution)/shard_map/ppermute | solution.py:371
  50.9 2.8 %copy-done.1 = bf16[8,3,128,1024]{3,2,1,0:T(8,128)(2,1)S(1)} copy-done((bf16[8,3,128,1024]{3,2,1,0:T(8,128)(2,1)S(1)}, bf16[8,3,128,1024]{3,2,1,0:T(8,128)(2,1)}, u32[]{:S(2)}) %copy-start.1) | copy-done | bytes 6291480
  53.7 7.5 %shard_map.89.inner_ref = f32[1024,512]{1,0:T(8,128)S(1)} custom-call(bf16[8,3,128,1024]{3,2,1,0:T(8,128)(2,1)S(1)} %copy-done.1, bf16[1024,512]{1,0:T(8,128)(2,1)} %bitcast.3.state_ref, f32[60,128]{1,0:T(8,128)S(1)} %shard_map.88.weight_ref), custom_call_target="tpu_custom_call" | custom-call | flops 3221225472 | bytes 6291456 | tf_op jit(solution)/shard_map/pallas_call | solution.py:378
  61.2 4.8 %shard_map.90 = bf16[1024,640]{1,0:T(8,128)(2,1)S(1)} custom-call(bf16[8,3,128,1024]{3,2,1,0:T(8,128)(2,1)S(1)} %bitcast.18, bf16[1024,128]{1,0:T(8,128)(2,1)S(1)} %collective-permute-done.3.above_ref, bf16[1024,128]{1,0:T(8,128)(2,1)S(1)} %collective-permute-done.4.below_ref, f32[60,128]{1,0:T(8,128)S(1)} %shard_map.88.weight_ref, ...), custom_call_target="tpu_custom_call" | custom-call | tf_op jit(solution)/shard_map/pallas_call | solution.py:392
  67.1 6.0 %all-to-all-start.1 = ((bf16[32,32,640]{2,1,0:T(8,128)(2,1)}), bf16[32,32,640]{2,1,0:T(8,128)(2,1)}, u32[]{:S(2)}, u32[]{:S(2)}) async-start(bf16[32,32,640]{2,1,0:T(8,128)(2,1)} %bitcast.21), calls=%async_computation.1 | async-start | bytes 2621440 | tf_op jit(solution)/shard_map/all_to_all | solution.py:769
  75.5 6.1 %shard_map.92 = (f32[4,32,32,128]{3,2,1,0:T(8,128)}, f32[4,32,32,128]{3,2,1,0:T(8,128)}, f32[4,32,32,128]{3,2,1,0:T(8,128)}) custom-call(s32[2]{0:T(128)} %copy-done.15, f32[1,36,32,128]{3,2,1,0:T(8,128)} %copy-done.2, f32[1,36,32,128]{3,2,1,0:T(8,128)} %copy-done.4, f32[1,36,32,128]{3,2,1,0:T(8,128)} %collective-permute-done.1.refs_2_, ...), custom_call_target="tpu_custom_call" | custom-call | tf_op jit(solution)/shard_map/pallas_call | solution.py:593
  81.6 23.6 %all-to-all-done.1.coupled_ref = bf16[32,32,640]{2,1,0:T(8,128)(2,1)} async-done(((bf16[32,32,640]{2,1,0:T(8,128)(2,1)}), bf16[32,32,640]{2,1,0:T(8,128)(2,1)}, u32[]{:S(2)}, u32[]{:S(2)}) %all-to-all-start.1) | async-done | bytes 1310752 | tf_op jit(solution)/shard_map/all_to_all | solution.py:769
  105.2 6.3 %shard_map.93 = (f32[4,32,32,128]{3,2,1,0:T(8,128)S(1)}, bf16[32,32,512]{2,1,0:T(8,128)(2,1)S(1)}) custom-call(f32[4,32,32,128]{3,2,1,0:T(8,128)} %get-tuple-element.39.current_ref, f32[4,32,32,128]{3,2,1,0:T(8,128)} %get-tuple-element.40.base_ref, bf16[32,32,640]{2,1,0:T(8,128)(2,1)} %all-to-all-done.1.coupled_ref, bf16[256,256]{1,0:T(8,128)(2,1)S(1)} %copy-done.10, ...), custom_call_target="tpu_custom_call" | custom-call | flops 1610612736 | bytes 11665408 | tf_op jit(solution)/shard_map/pallas_call | solution.py:575
  111.6 29.6 %all_to_all.36 = bf16[32,32,512]{2,1,0:T(8,128)(2,1)S(1)} all-to-all(bf16[32,32,512]{2,1,0:T(8,128)(2,1)S(1)} %get-tuple-element.44), channel_id=1, replica_groups=mesh['mode'=8,'slab'=4] {'mode','slab'}, dimensions={0} | all-to-all | bytes 2097152 | tf_op jit(solution)/shard_map/all_to_all | solution.py:775
  142.7 3.9 %collective-permute-start.9 = (bf16[1024,128]{1,0:T(8,128)(2,1)S(1)}, bf16[1024,128]{1,0:T(8,128)(2,1)S(1)}, u32[]{:S(2)}, u32[]{:S(2)}) collective-permute-start(bf16[1024,128]{1,0:T(8,128)(2,1)S(1)} %get-tuple-element.58), channel_id=1, source_target_pairs={{4,0},{8,4},{12,8},{16,12},{20,16},{24,20},{28,24},{1,28},{5,1},{9... | collective-permute-start | bytes 786440 | tf_op jit(solution)/shard_map/ppermute | solution.py:371
  146.6 6.1 %shard_map.95.inner_ref = f32[1024,512]{1,0:T(8,128)S(1)} custom-call(bf16[8,3,128,1024]{3,2,1,0:T(8,128)(2,1)S(1)} %bitcast.20, bf16[1024,512]{1,0:T(8,128)(2,1)S(1)} %bitcast.23, f32[60,128]{1,0:T(8,128)S(1)} %shard_map.88.weight_ref), custom_call_target="tpu_custom_call" | custom-call | flops 3221225472 | bytes 6291456 | tf_op jit(solution)/shard_map/pallas_call | solution.py:378
  153.5 2.2 collective-permute-done.9.below_ref
  155.7 3.3 %shard_map.96 = bf16[1024,512]{1,0:T(8,128)(2,1)} custom-call(bf16[8,3,128,1024]{3,2,1,0:T(8,128)(2,1)S(1)} %bitcast.20, bf16[1024,128]{1,0:T(8,128)(2,1)S(1)} %collective-permute-done.8.above_ref, bf16[1024,128]{1,0:T(8,128)(2,1)S(1)} %collective-permute-done.9.below_ref, f32[60,128]{1,0:T(8,128)S(1)} %shard_map.88.weight_ref, ...), custom_call_target="tpu_custom_call" | custom-call | tf_op jit(solution)/shard_map/pallas_call | solution.py:392
  159.1 3.2 %all-to-all-start.3 = ((bf16[32,32,512]{2,1,0:T(8,128)(2,1)}), bf16[32,32,512]{2,1,0:T(8,128)(2,1)S(1)}, u32[]{:S(2)}, u32[]{:S(2)}) async-start(bf16[32,32,512]{2,1,0:T(8,128)(2,1)} %bitcast.10), calls=%async_computation.3 | async-start | bytes 2097152 | tf_op jit(solution)/shard_map/all_to_all | solution.py:779
  162.3 1.6 copy-done.12
  163.9 2.7 %shard_map.94.base_ref = f32[4,32,32,128]{3,2,1,0:T(8,128)S(1)} custom-call(f32[4,32,32,128]{3,2,1,0:T(8,128)S(1)} %copy-done.12, f32[4,32,32,128]{3,2,1,0:T(8,128)} %get-tuple-element.43.right_side_ref, f32[5,128,128]{2,1,0:T(8,128)S(1)} %copy-done.8), custom_call_target="tpu_custom_call" | custom-call | bytes 9043968 | tf_op jit(solution)/shard_map/pallas_call | solution.py:575
  167.9 20.4 %all-to-all-done.3.coupled_ref = bf16[32,32,512]{2,1,0:T(8,128)(2,1)S(1)} async-done(((bf16[32,32,512]{2,1,0:T(8,128)(2,1)}), bf16[32,32,512]{2,1,0:T(8,128)(2,1)S(1)}, u32[]{:S(2)}, u32[]{:S(2)}) %all-to-all-start.3) | async-done | bytes 1048608 | tf_op jit(solution)/shard_map/all_to_all | solution.py:779
  188.3 4.1 %shard_map.97 = (f32[4,32,32,128]{3,2,1,0:T(8,128)S(1)}, bf16[1,32,32,128]{3,2,1,0:T(8,128)(2,1)S(1)}, bf16[1,32,32,128]{3,2,1,0:T(8,128)(2,1)S(1)}, bf16[1,32,3...) custom-call(s32[1]{0:T(128)} %bitcast.here_ref, f32[4,32,32,128]{3,2,1,0:T(8,128)} %copy-done.3, ...), custom_call_target="tpu_custom_call" | custom-call | bytes 4194304 | tf_op jit(solution)/shard_map/pallas_call | solution.py:652
  195.4 4.5 %shard_map.98 = bf16[4,32,32,128]{3,2,1,0:T(8,128)(2,1)} custom-call(f32[4,32,32,128]{3,2,1,0:T(8,128)S(1)} %copy-done.13, f32[4,32,32,128]{3,2,1,0:T(8,128)S(1)} %get-tuple-element.45.resid_ref, bf16[256,256]{1,0:T(8,128)(2,1)S(1)} %copy-done.10, bf16[256,256]{1,0:T(8,128)(2,1)S(1)} %copy-done.14, f32[128,128]{1,0:T(8,128)S(1)} %subtract_divide_fusion.scale_ref), custom_call_target="tpu_custom_call" | custom-call | flops 1610612736 | bytes 9043968 | tf_op jit(solution)/shard_map/pallas_call | solution.py:575
  199.9 3.5 %all-to-all-start.4 = ((bf16[128,32,128]{2,1,0:T(8,128)(2,1)}), bf16[128,32,128]{2,1,0:T(8,128)(2,1)S(1)}, u32[]{:S(2)}, u32[]{:S(2)}) async-start(bf16[128,32,128]{2,1,0:T(8,128)(2,1)} %bitcast.11), calls=%async_computation.4 | async-start | bytes 2097152 | tf_op jit(solution)/shard_map/all_to_all | solution.py:730
  203.8 2.5 %collective-permute-done.12 = bf16[1,32,32,128]{3,2,1,0:T(8,128)(2,1)S(1)} collective-permute-done((bf16[1,32,32,128]{3,2,1,0:T(8,128)(2,1)S(1)}, bf16[1,32,32,128]{3,2,1,0:T(8,128)(2,1)S(1)}, u32[]{:S(2)}, u32[]{:S(2)}) %collective-permute-start.12) | collective-permute-done | bytes 262176 | tf_op jit(solution)/shard_map/ppermute | solution.py:697
  207.3 1.8 fusion.11
  209.1 8.8 %all-to-all-done.4 = bf16[128,32,128]{2,1,0:T(8,128)(2,1)S(1)} async-done(((bf16[128,32,128]{2,1,0:T(8,128)(2,1)}), bf16[128,32,128]{2,1,0:T(8,128)(2,1)S(1)}, u32[]{:S(2)}, u32[]{:S(2)}) %all-to-all-start.4) | async-done | bytes 1048608 | tf_op jit(solution)/shard_map/all_to_all | solution.py:730
  218.0 2.2 %fusion.10 = f32[128,32,128]{2,1,0:T(8,128)} fusion(bf16[128,32,128]{2,1,0:T(8,128)(2,1)S(1)} %all-to-all-done.4), kind=kLoop, calls=%fused_computation.16 | loop fusion | flops 4718592 | bytes 3145728 | tf_op jit(solution)/shard_map/mul | solution.py:784
  (91 shorter events, 24.5 us)
Async XLA Ops:
  0.6 10.8 %copy-start.20 = (f32[3,32,128]{2,1,0:T(8,128)S(1)}, f32[3,32,128]{2,1,0:T(8,128)}, u32[]{:S(2)}) copy-start(f32[3,32,128]{2,1,0:T(8,128)} %param.10) | copy-start | bytes 147460
  0.6 10.8 %copy-start.21 = (f32[32,128]{1,0:T(8,128)S(1)}, f32[32,128]{1,0:T(8,128)}, u32[]{:S(2)}) copy-start(f32[32,128]{1,0:T(8,128)} %param.9) | copy-start | bytes 49156
  0.6 10.8 %copy-start.18 = (f32[128,32,128]{2,1,0:T(8,128)S(1)}, f32[128,32,128]{2,1,0:T(8,128)}, u32[]{:S(2)}) copy-start(f32[128,32,128]{2,1,0:T(8,128)} %param.7) | copy-start | bytes 6291460
  4.1 36.5 %all-to-all-start = ((bf16[8,128,512]{2,1,0:T(8,128)(2,1)}), bf16[8,128,512]{2,1,0:T(8,128)(2,1)}, u32[]{:S(2)}, u32[]{:S(2)}) async-start(bf16[8,128,512]{2,1,0:T(8,128)(2,1)} %shard_map.86), calls=%async_computation | async-start | bytes 2097152 | tf_op jit(solution)/shard_map/all_to_all | solution.py:725
  13.0 60.2 %copy-start.2 = (f32[1,36,32,128]{3,2,1,0:T(8,128)}, f32[1,36,32,128]{3,2,1,0:T(8,128)S(1)}, u32[]{:S(2)}) copy-start(f32[1,36,32,128]{3,2,1,0:T(8,128)S(1)} %get-tuple-element.26.refs_0_) | copy-start | bytes 1769476
  13.0 15.3 %collective-permute-start = (f32[1,36,32,128]{3,2,1,0:T(8,128)}, f32[1,36,32,128]{3,2,1,0:T(8,128)S(1)}, u32[]{:S(2)}, u32[]{:S(2)}) collective-permute-start(f32[1,36,32,128]{3,2,1,0:T(8,128)} %get-tuple-element.65), channel_id=1, source_target_pairs={{0,1},{1,2},{2,3},{3,0},{4,5},{5,6},{6,7},{7,4},{8,9},{9,10},{10,1... | collective-permute-start | bytes 1769480 | tf_op jit(solution)/shard_map/ppermute | solution.py:697
  13.0 16.5 %collective-permute-start.1 = (f32[1,36,32,128]{3,2,1,0:T(8,128)}, f32[1,36,32,128]{3,2,1,0:T(8,128)}, u32[]{:S(2)}, u32[]{:S(2)}) collective-permute-start(f32[1,36,32,128]{3,2,1,0:T(8,128)} %get-tuple-element.66), channel_id=1, source_target_pairs={{0,2},{1,3},{2,0},{3,1},{4,6},{5,7},{6,4},{7,5},{8,10},{9,11},{10,... | collective-permute-start | bytes 1769480 | tf_op jit(solution)/shard_map/ppermute | solution.py:697
  14.5 26.1 %collective-permute-start.2 = (f32[1,36,32,128]{3,2,1,0:T(8,128)}, f32[1,36,32,128]{3,2,1,0:T(8,128)}, u32[]{:S(2)}, u32[]{:S(2)}) collective-permute-start(f32[1,36,32,128]{3,2,1,0:T(8,128)} %get-tuple-element.64), channel_id=1, source_target_pairs={{0,3},{1,0},{2,1},{3,2},{4,7},{5,4},{6,5},{7,6},{8,11},{9,8},{10,9... | collective-permute-start | bytes 1769480 | tf_op jit(solution)/shard_map/ppermute | solution.py:697
  23.6 49.7 %copy-start.15 = (s32[2]{0:T(128)}, s32[2]{0:T(128)S(1)}, u32[]{:S(2)}) copy-start(s32[2]{0:T(128)S(1)} %pad_add_fusion.place_ref) | copy-start | bytes 28
  24.5 36.6 %copy-start.9 = (bf16[256,256]{1,0:T(8,128)(2,1)}, bf16[256,256]{1,0:T(8,128)(2,1)S(1)}, u32[]{:S(2)}) copy-start(bf16[256,256]{1,0:T(8,128)(2,1)S(1)} %get-tuple-element.63.right_ref.refs_9_) | copy-start | bytes 393220
  24.5 36.7 %slice-start = ((s8[6291456]{0:T(1024)(128)(4,1)}), s8[2097152]{0:T(1024)(128)(4,1)S(1)}, s32[]{:S(2)}) async-start(s8[6291456]{0:T(1024)(128)(4,1)} %bitcast.17), calls=%async_computation.5 | async-start | bytes 4194304
  28.3 45.0 %copy-start.4 = (f32[1,36,32,128]{3,2,1,0:T(8,128)}, f32[1,36,32,128]{3,2,1,0:T(8,128)S(1)}, u32[]{:S(2)}) copy-start(f32[1,36,32,128]{3,2,1,0:T(8,128)S(1)} %collective-permute-done.refs_1_) | copy-start | bytes 1769476
  40.6 25.5 %collective-permute-start.5 = (f32[1,32,32,128]{3,2,1,0:T(8,128)}, f32[1,32,32,128]{3,2,1,0:T(8,128)}, u32[]{:S(2)}, u32[]{:S(2)}) collective-permute-start(f32[1,32,32,128]{3,2,1,0:T(8,128)} %get-tuple-element.32), channel_id=1, source_target_pairs={{0,1},{1,2},{2,3},{3,0},{4,5},{5,6},{6,7},{7,4},{8,9},{9,10},{10,1... | collective-permute-start | bytes 1572872 | tf_op jit(solution)/shard_map/ppermute | solution.py:697
  41.4 24.7 %collective-permute-start.6 = (f32[1,32,32,128]{3,2,1,0:T(8,128)}, f32[1,32,32,128]{3,2,1,0:T(8,128)}, u32[]{:S(2)}, u32[]{:S(2)}) collective-permute-start(f32[1,32,32,128]{3,2,1,0:T(8,128)} %get-tuple-element.33), channel_id=1, source_target_pairs={{0,2},{1,3},{2,0},{3,1},{4,6},{5,7},{6,4},{7,5},{8,10},{9,11},{10,... | collective-permute-start | bytes 1572872 | tf_op jit(solution)/shard_map/ppermute | solution.py:697
  42.9 23.2 %collective-permute-start.7 = (f32[1,32,32,128]{3,2,1,0:T(8,128)}, f32[1,32,32,128]{3,2,1,0:T(8,128)}, u32[]{:S(2)}, u32[]{:S(2)}) collective-permute-start(f32[1,32,32,128]{3,2,1,0:T(8,128)} %get-tuple-element.34), channel_id=1, source_target_pairs={{0,3},{1,0},{2,1},{3,2},{4,7},{5,4},{6,5},{7,6},{8,11},{9,8},{10,9... | collective-permute-start | bytes 1572872 | tf_op jit(solution)/shard_map/ppermute | solution.py:697
  44.0 17.2 %collective-permute-start.3 = (bf16[1024,128]{1,0:T(8,128)(2,1)S(1)}, bf16[1024,128]{1,0:T(8,128)(2,1)S(1)}, u32[]{:S(2)}, u32[]{:S(2)}) collective-permute-start(bf16[1024,128]{1,0:T(8,128)(2,1)S(1)} %get-tuple-element.61), channel_id=1, source_target_pairs={{0,4},{4,8},{8,12},{12,16},{16,20},{20,24},{24,28},{28,1},{1,5},{5... | collective-permute-start | bytes 786440 | tf_op jit(solution)/shard_map/ppermute | solution.py:370
  46.0 15.1 %collective-permute-start.4 = (bf16[1024,128]{1,0:T(8,128)(2,1)S(1)}, bf16[1024,128]{1,0:T(8,128)(2,1)S(1)}, u32[]{:S(2)}, u32[]{:S(2)}) collective-permute-start(bf16[1024,128]{1,0:T(8,128)(2,1)S(1)} %get-tuple-element.60), channel_id=1, source_target_pairs={{4,0},{8,4},{12,8},{16,12},{20,16},{24,20},{28,24},{1,28},{5,1},{9... | collective-permute-start | bytes 786440 | tf_op jit(solution)/shard_map/ppermute | solution.py:371
  53.7 7.5 %slice-start.1 = ((s8[6291456]{0:T(1024)(128)(4,1)}), s8[4194304]{0:T(1024)(128)(4,1)S(1)}, s32[]{:S(2)}) async-start(s8[6291456]{0:T(1024)(128)(4,1)} %bitcast.17), calls=%async_computation.6 | async-start | bytes 8388608
  67.1 38.1 %all-to-all-start.1 = ((bf16[32,32,640]{2,1,0:T(8,128)(2,1)}), bf16[32,32,640]{2,1,0:T(8,128)(2,1)}, u32[]{:S(2)}, u32[]{:S(2)}) async-start(bf16[32,32,640]{2,1,0:T(8,128)(2,1)} %bitcast.21), calls=%async_computation.1 | async-start | bytes 2621440 | tf_op jit(solution)/shard_map/all_to_all | solution.py:769
  75.5 29.7 %copy-start.10 = (bf16[256,256]{1,0:T(8,128)(2,1)S(1)}, bf16[256,256]{1,0:T(8,128)(2,1)}, u32[]{:S(2)}) copy-start(bf16[256,256]{1,0:T(8,128)(2,1)} %copy-done.9) | copy-start | bytes 393220
  75.5 29.7 %copy-start.14 = (bf16[256,256]{1,0:T(8,128)(2,1)S(1)}, bf16[256,256]{1,0:T(8,128)(2,1)}, u32[]{:S(2)}) copy-start(bf16[256,256]{1,0:T(8,128)(2,1)} %get-tuple-element.62.left_ref) | copy-start | bytes 393220
  75.5 71.1 %slice-start.2 = ((s8[6291456]{0:T(1024)(128)(4,1)}), s8[2097152]{0:T(1024)(128)(4,1)S(1)}, s32[]{:S(2)}) async-start(s8[6291456]{0:T(1024)(128)(4,1)} %bitcast.19), calls=%async_computation.7 | async-start | bytes 4194304
  105.2 41.4 %slice-start.3 = ((s8[6291456]{0:T(1024)(128)(4,1)}), s8[4194304]{0:T(1024)(128)(4,1)S(1)}, s32[]{:S(2)}) async-start(s8[6291456]{0:T(1024)(128)(4,1)} %bitcast.19), calls=%async_computation.8 | async-start | bytes 8388608
  111.5 41.2 %copy-start.11 = (f32[4,32,32,128]{3,2,1,0:T(8,128)}, f32[4,32,32,128]{3,2,1,0:T(8,128)S(1)}, u32[]{:S(2)}) copy-start(f32[4,32,32,128]{3,2,1,0:T(8,128)S(1)} %get-tuple-element.42.current_ref) | copy-start | bytes 6291460
  141.2 12.3 %collective-permute-start.8 = (bf16[1024,128]{1,0:T(8,128)(2,1)S(1)}, bf16[1024,128]{1,0:T(8,128)(2,1)S(1)}, u32[]{:S(2)}, u32[]{:S(2)}) collective-permute-start(bf16[1024,128]{1,0:T(8,128)(2,1)S(1)} %get-tuple-element.59), channel_id=1, source_target_pairs={{0,4},{4,8},{8,12},{12,16},{16,20},{20,24},{24,28},{28,1},{1,5},{5... | collective-permute-start | bytes 786440 | tf_op jit(solution)/shard_map/ppermute | solution.py:370
  142.7 13.0 %collective-permute-start.9 = (bf16[1024,128]{1,0:T(8,128)(2,1)S(1)}, bf16[1024,128]{1,0:T(8,128)(2,1)S(1)}, u32[]{:S(2)}, u32[]{:S(2)}) collective-permute-start(bf16[1024,128]{1,0:T(8,128)(2,1)S(1)} %get-tuple-element.58), channel_id=1, source_target_pairs={{4,0},{8,4},{12,8},{16,12},{20,16},{24,20},{28,24},{1,28},{5,1},{9... | collective-permute-start | bytes 786440 | tf_op jit(solution)/shard_map/ppermute | solution.py:371
  159.1 29.3 %all-to-all-start.3 = ((bf16[32,32,512]{2,1,0:T(8,128)(2,1)}), bf16[32,32,512]{2,1,0:T(8,128)(2,1)S(1)}, u32[]{:S(2)}, u32[]{:S(2)}) async-start(bf16[32,32,512]{2,1,0:T(8,128)(2,1)} %bitcast.10), calls=%async_computation.3 | async-start | bytes 2097152 | tf_op jit(solution)/shard_map/all_to_all | solution.py:779
  188.3 7.1 %copy-start.13 = (f32[4,32,32,128]{3,2,1,0:T(8,128)S(1)}, f32[4,32,32,128]{3,2,1,0:T(8,128)}, u32[]{:S(2)}) copy-start(f32[4,32,32,128]{3,2,1,0:T(8,128)} %copy-done.11) | copy-start | bytes 6291460
  192.4 11.2 %collective-permute-start.10 = (bf16[1,32,32,128]{3,2,1,0:T(8,128)(2,1)S(1)}, bf16[1,32,32,128]{3,2,1,0:T(8,128)(2,1)S(1)}, u32[]{:S(2)}, u32[]{:S(2)}) collective-permute-start(bf16[1,32,32,128]{3,2,1,0:T(8,128)(2,1)S(1)} %get-tuple-element.47), channel_id=1, source_target_pairs={{0,1},{1,2},{2,3},{3,0},{4,5},{5,6},{6,7},{7,4},{8,9},{9,10},{10,1... | collective-permute-start | bytes 786440 | tf_op jit(solution)/shard_map/ppermute | solution.py:697
  192.5 11.2 %collective-permute-start.11 = (bf16[1,32,32,128]{3,2,1,0:T(8,128)(2,1)S(1)}, bf16[1,32,32,128]{3,2,1,0:T(8,128)(2,1)S(1)}, u32[]{:S(2)}, u32[]{:S(2)}) collective-permute-start(bf16[1,32,32,128]{3,2,1,0:T(8,128)(2,1)S(1)} %get-tuple-element.48), channel_id=1, source_target_pairs={{0,2},{1,3},{2,0},{3,1},{4,6},{5,7},{6,4},{7,5},{8,10},{9,11},{10,... | collective-permute-start | bytes 786440 | tf_op jit(solution)/shard_map/ppermute | solution.py:697
  194.0 12.3 %collective-permute-start.12 = (bf16[1,32,32,128]{3,2,1,0:T(8,128)(2,1)S(1)}, bf16[1,32,32,128]{3,2,1,0:T(8,128)(2,1)S(1)}, u32[]{:S(2)}, u32[]{:S(2)}) collective-permute-start(bf16[1,32,32,128]{3,2,1,0:T(8,128)(2,1)S(1)} %get-tuple-element.49), channel_id=1, source_target_pairs={{0,3},{1,0},{2,1},{3,2},{4,7},{5,4},{6,5},{7,6},{8,11},{9,8},{10,9... | collective-permute-start | bytes 786440 | tf_op jit(solution)/shard_map/ppermute | solution.py:697
  199.9 18.0 %all-to-all-start.4 = ((bf16[128,32,128]{2,1,0:T(8,128)(2,1)}), bf16[128,32,128]{2,1,0:T(8,128)(2,1)S(1)}, u32[]{:S(2)}, u32[]{:S(2)}) async-start(bf16[128,32,128]{2,1,0:T(8,128)(2,1)} %bitcast.11), calls=%async_computation.4 | async-start | bytes 2097152 | tf_op jit(solution)/shard_map/all_to_all | solution.py:730
  (11 other events, 30.6 us)
